TPU v7x, 128 devices: a whole 4x4x4 slice. The times are simulated.
128 devices in a mesh: feat: 16 (over x, y_lo, core), batch: 8 (over z, y_hi).
Axes of the slice: x: 4, y: 4 (y_hi: 2, y_lo: 2; y = y_hi * 2 + y_lo), z: 4, core: 2. Of those that a mesh axis runs over, the one named last changes fastest.
Arguments:
- embeddings: bfloat16 [8192, 8192], P('batch', 'feat'), may hold values from -6 to 6
- basis: bfloat16 [8192, 1024], P('feat'), may hold values from -0.0625 to 0.0625
- cov_prior: float32 [8192, 8192], P('feat', 'batch'), may hold values from -1 to 2, as said below
Outputs:
- covariance: float32 [8192, 8192], P('feat', 'batch')
- projected: bfloat16 [8192, 1024], P(('batch', 'feat'))
Inputs may be any that keep to these rules, and one draw needn't show every extreme that they name: `cov_prior`: symmetric.
All inputs are finite; a program needn't handle non-finite values.
Results may differ from a plain program's by a relative error of at most 0.011.
Values may be sent and summed in bfloat16 or wider, within the bound.
No kernel may reach another device: no remote copies, remote signals or barrier semaphores. Data moves between devices by JAX's collectives and lax.ppermute only.
A program may use at most 128 MiB of HBM per device.

v0:
```python
import jax
import jax.numpy as jnp
from jax import lax
from jax.sharding import PartitionSpec as P


def cross_product(left, right):
    return lax.dot_general(
        left, right, (((0,), (0,)), ((), ())), preferred_element_type=jnp.float32
    )


def on_device(embeddings, basis, cov_prior):
    batch_count = lax.axis_size("batch")
    items_total = embeddings.shape[0] * batch_count
    partial_gram = cross_product(embeddings, lax.all_gather(embeddings, "feat", axis=1, tiled=True))
    gram = lax.psum_scatter(
        partial_gram.astype(jnp.bfloat16), "batch", scatter_dimension=1, tiled=True
    ).astype(jnp.float32)
    covariance = 0.9 * cov_prior + gram / items_total
    projected = lax.psum_scatter(
        jnp.dot(embeddings, basis, preferred_element_type=jnp.float32),
        "feat",
        scatter_dimension=0,
        tiled=True,
    ).astype(jnp.bfloat16)
    return (covariance, projected)


def solution(mesh):
    placed = (P("batch", "feat"), P("feat", None), P("feat", "batch"))
    return jax.shard_map(
        on_device,
        mesh=mesh,
        in_specs=placed,
        out_specs=(P("feat", "batch"), P(("batch", "feat"), None)),
        check_vma=False,
    )
```

profile of v0, /device:TPU:0, one launch (start us, length us, event | category | flops | bytes accessed | tf_op | source)
XLA Modules:
  0.0 300.5 jit_solution(14117296290041948858)
XLA Ops:
  7.2 0.0 copy-start
  7.2 0.0 all-gather.2.cloned.1.call-start
  7.2 0.7 all-gather.2.cloned.1.call-update
  7.9 0.0 reduce-scatter.5.cloned.1.call-start
  8.0 0.4 copy-done
  8.4 4.4 %fusion = f32[1024,1024]{1,0:T(8,128)} fusion(bf16[1024,512]{1,0:T(8,128)(2,1)} %param.3, bf16[512,1024]{1,0:T(8,128)(2,1)S(1)} %copy-done), kind=kOutput, calls=%fused_computation.2 | convolution fusion | flops 1073741824 | bytes 6291456 | tf_op jit(solution)/shard_map/dot_general | solution.py:22
  12.8 0.0 copy-start.2
  12.8 0.0 reduce-scatter.5.cloned.1.call-update
  12.9 0.0 reduce-scatter.3.cloned.1.call-start
  12.9 90.8 %all-gather.2.cloned.1.call-done = bf16[1024,8192]{1,0:T(8,128)(2,1)} async-done(((bf16[1024,512]{1,0:T(8,128)(2,1)}), bf16[1024,8192]{1,0:T(8,128)(2,1)}) %all-gather.2.cloned.1.call-update) | async-done | bytes 16777232 | tf_op jit(solution)/shard_map/all_gather | solution.py:16
  103.7 0.0 copy-done.2
  103.7 16.9 %convolution_convert_fusion = bf16[512,8192]{1,0:T(8,128)(2,1)} fusion(bf16[1024,512]{1,0:T(8,128)(2,1)S(1)} %copy-done.2, bf16[1024,8192]{1,0:T(8,128)(2,1)} %all-gather.2.cloned.1.call-done), kind=kOutput, calls=%fused_computation | convolution fusion | flops 8594128896 | bytes 26214400 | tf_op jit(solution)/shard_map/dot_general | solution.py:8
  120.7 0.0 copy-start.1
  120.7 0.0 reduce-scatter.3.cloned.1.call-update
  120.7 53.8 %reduce-scatter.5.cloned.1.call-done = f32[64,1024]{1,0:T(8,128)} async-done(((f32[1024,1024]{1,0:T(8,128)}), f32[64,1024]{1,0:T(8,128)}) %reduce-scatter.5.cloned.1.call-update) | async-done | bytes 262160 | tf_op jit(solution)/shard_map/reduce_scatter | solution.py:21
  174.5 1.6 convert_element_type.11
  176.1 114.9 %reduce-scatter.3.cloned.1.call-done = bf16[512,1024]{1,0:T(8,128)(2,1)} async-done(((bf16[512,8192]{1,0:T(8,128)(2,1)}), bf16[512,1024]{1,0:T(8,128)(2,1)}) %reduce-scatter.3.cloned.1.call-update) | async-done | bytes 1048592 | tf_op jit(solution)/shard_map/reduce_scatter | solution.py:17
  291.1 0.0 copy-done.1
  291.1 2.9 multiply_add_fusion
Async XLA Ops:
  7.2 1.2 copy-start
  7.2 96.5 %all-gather.2.cloned.1.call-start = ((), (), s32[]{:S(2)}) async-start(), calls=%async_computation.2 | async-start | bytes 17825792 | tf_op jit(solution)/shard_map/all_gather | solution.py:16
  7.9 166.6 %reduce-scatter.5.cloned.1.call-start = ((), (), s32[]{:S(2)}) async-start(), calls=%async_computation.4 | async-start | bytes 4456448 | tf_op jit(solution)/shard_map/reduce_scatter | solution.py:21
  12.8 90.9 %copy-start.2 = (bf16[1024,512]{1,0:T(8,128)(2,1)S(1)}, bf16[1024,512]{1,0:T(8,128)(2,1)}, u32[]{:S(2)}) copy-start(bf16[1024,512]{1,0:T(8,128)(2,1)} %param.3) | copy-start | bytes 3145732
  12.9 278.2 %reduce-scatter.3.cloned.1.call-start = ((), (), s32[]{:S(2)}) async-start(), calls=%async_computation.3 | async-start | bytes 9437184 | tf_op jit(solution)/shard_map/reduce_scatter | solution.py:17
  120.7 170.4 %copy-start.1 = (f32[512,1024]{1,0:T(8,128)S(1)}, f32[512,1024]{1,0:T(8,128)}, u32[]{:S(2)}) copy-start(f32[512,1024]{1,0:T(8,128)} %param.5) | copy-start | bytes 6291460
Sparse Core Ops, SparseCore 0:
  9.7 94.0 all-gather.1
  106.1 68.3 reduce-scatter.4
  178.3 112.7 reduce-scatter.2
where the time goes:
time: 301 us; the launch traced here: 300 us
  waiting for transfers between devices  260 us (86%)
  matrix products  21.4 us (7%)
  between operations  13.8 us (5%)
  other arithmetic  4.51 us (1%)
    reduce_scatter x1, waiting for transfers between devices, on_device(): lax.psum_scatter(partial_gram.astype(jnp.bfloat16), 'batch', scatter_dime...  115 us
    all_gather x1, waiting for transfers between devices, on_device(): lax.all_gather(embeddings, 'feat', axis=1, tiled=True)  90.8 us
    reduce_scatter x1, waiting for transfers between devices, on_device(): lax.psum_scatter(jnp.dot(embeddings, basis, preferred_element_type=jnp.fl...  53.8 us
    dot_general x1, matrix products, cross_product(): lax.dot_general(left, right, (((0,), (0,)), ((), ())), preferred_element_...  16.9 us
  transfers between devices with their start and end apart: 3, of which 3 were waited for; matrix products, arithmetic and copies ran while one was open for 8% of the time, Pallas kernels for 0%

commit v1 on v0

v1 whole, which is shorter than its diff:
```python
import jax
import jax.numpy as jnp
from jax import lax
from jax.sharding import PartitionSpec as P

CHUNKS = 2
SIZES = (4, 2, 2, 4, 2)
AXES = ("feat", "batch")


def flat(place):
    index = 0
    for value, size in zip(place, SIZES):
        index = index * size + value % size
    return index


def table(move):
    pairs = []
    for x in range(4):
        for yl in range(2):
            for c in range(2):
                for z in range(4):
                    for yh in range(2):
                        pairs.append((flat((x, yl, c, z, yh)), flat(move(x, yl, c, z, yh))))
    return pairs


CORE = table(lambda x, yl, c, z, yh: (x, yl, 1 - c, z, yh))
NEAR = table(lambda x, yl, c, z, yh: (x, 1 - yl, c, z, yh))
FAR = table(lambda x, yl, c, z, yh: (x, 1 - yl, c, z, 1 - yh))
X_STEP = {d: table(lambda x, yl, c, z, yh, d=d: (x + d, yl, c, z, yh)) for d in (1, 2, 3)}
Z_STEP = {d: table(lambda x, yl, c, z, yh, d=d: (x, yl, c, z + d, yh)) for d in (1, 3)}
HOME = {
    (s, t): table(lambda x, yl, c, z, yh, s=s, t=t: (x, yh ^ s, c ^ t, z, 1 - yl))
    for s in range(2)
    for t in range(2)
}


def send(value, pairs):
    return lax.ppermute(value, AXES, pairs)


def columns(array, start, size):
    return lax.dynamic_slice_in_dim(array, start, size, 1)


def pick(array, index):
    return lax.dynamic_index_in_dim(array, index, 0, keepdims=False)


def project(embeddings, basis, x, yl, c):
    total = jnp.dot(embeddings, basis, preferred_element_type=jnp.float32)
    rows, width = total.shape[0] // 16, total.shape[1]
    total = total.reshape(4, 2, 2, rows, width)
    by_core = jnp.moveaxis(total, 2, 0)
    total = pick(by_core, c) + send(
        pick(by_core, 1 - c).astype(jnp.bfloat16), CORE
    ).astype(jnp.float32)
    outgoing = total.astype(jnp.bfloat16)
    mine = pick(total, x)
    for d in (1, 3, 2):
        mine = mine + send(pick(outgoing, (x + d) % 4), X_STEP[d]).astype(jnp.float32)
    mine = pick(mine, yl) + send(pick(mine, 1 - yl).astype(jnp.bfloat16), NEAR).astype(jnp.float32)
    return mine.astype(jnp.bfloat16)


def on_device(embeddings, basis, cov_prior):
    feat, batch = lax.axis_index("feat"), lax.axis_index("batch")
    x, yl, c = feat // 4, feat // 2 % 2, feat % 2
    z, yh = batch // 2, batch % 2
    items, feats = embeddings.shape
    half = feats // 2
    part = half // CHUNKS
    items_total = items * lax.axis_size("batch")

    own = [columns(embeddings, (yh ^ i) * half, half) for i in range(2)]
    near0, far0 = send(own[0], NEAR), send(own[1], FAR)
    right = jnp.concatenate([near0, far0], 0)

    pieces = []
    for k in range(CHUNKS):
        base = right[:, k * part : (k + 1) * part]
        below, above = send(base, X_STEP[1]), send(base, X_STEP[3])
        across = jnp.concatenate(
            [send(below[:items], X_STEP[1]), send(above[items:], X_STEP[3])], 0
        )
        pieces.append(jnp.concatenate([base, above, across, below], 1))

    two0, two1 = send(far0, NEAR), send(near0, FAR)
    near1, far1 = send(own[1], NEAR), send(own[0], FAR)
    groups = [
        jnp.concatenate([own[0], two0], 0),
        jnp.concatenate([own[1], two1], 0),
        right,
        jnp.concatenate([near1, far1], 0),
    ]
    left = jnp.concatenate([g for group in groups for g in (group, send(group, CORE))], 1)

    projected = project(embeddings, basis, x, yl, c)

    arrived = {}
    for k in range(CHUNKS):
        partial = lax.dot_general(
            left, pieces[k], (((0,), (0,)), ((), ())), preferred_element_type=jnp.float32
        ).astype(jnp.bfloat16)
        rows = partial.shape[0] // 2
        block = {d: columns(partial, (z + d - x) % 4 * part, part) for d in range(4)}
        down = send(jnp.stack([block[2][:rows], block[3][rows:]]), Z_STEP[3])
        up = send(jnp.stack([block[1][:rows], block[2][rows:]]), Z_STEP[1])
        first = send(down[0] + block[3][:rows], Z_STEP[3])
        second = send(up[1] + block[1][rows:], Z_STEP[1])

        def total(*terms):
            return sum(t.astype(jnp.float32) for t in terms).astype(jnp.bfloat16)

        whole = jnp.concatenate(
            [
                total(block[0][:rows], up[0], first),
                total(block[0][rows:], down[1], second),
            ],
            0,
        ).reshape(2, 2, 2, half, part)
        for s in range(2):
            chosen = pick(whole, yl ^ yh ^ s)
            for t in range(2):
                outgoing = jnp.concatenate(
                    [pick(chosen[:, t], yh ^ i) for i in range(2)], 0
                )
                arrived[s, t, k] = send(outgoing, HOME[s, t])

    stacked = jnp.stack(
        [
            jnp.concatenate([arrived[s, t, k] for k in range(CHUNKS)], 1)
            for t in range(2)
            for s in range(2)
        ]
    )
    gram = jnp.concatenate(
        [pick(stacked, (q // 2 ^ c) * 2 + (q % 2 ^ yl)) for q in range(4)], 1
    ).astype(jnp.float32)
    covariance = 0.9 * cov_prior + gram / items_total
    return (covariance, projected)


def solution(mesh):
    placed = (P("batch", "feat"), P("feat", None), P("feat", "batch"))
    return jax.shard_map(
        on_device,
        mesh=mesh,
        in_specs=placed,
        out_specs=(P("feat", "batch"), P(("batch", "feat"), None)),
        check_vma=False,
    )
```

time: 301 us -> 207 us (0.69); the launches traced: 300 us -> 203 us
  waiting for transfers between devices: 260 us -> 96.2 us
  starting transfers between devices: 0.12 us -> 61 us
  local copies, waits for them, and re-layouts: 0.45 us -> 20.6 us
  between operations: 13.8 us -> 1.31 us
  matrix products: 21.4 us -> 13.5 us
  other arithmetic: 4.51 us -> 10.7 us
    reduce_scatter x2 -> x0, waiting for transfers between devices: 169 us -> none  [the longest x1 115 us: on_device(): lax.psum_scatter(partial_gram.astype(jnp.bfloat16), 'batch', scatter_dime...]
    ppermute x0 -> x39, waiting for transfers between devices: none -> 96.2 us  [send(): return lax.ppermute(value, AXES, pairs)]
    all_gather x1 -> x0, waiting for transfers between devices: 90.8 us -> none  [on_device(): lax.all_gather(embeddings, 'feat', axis=1, tiled=True)]
    ppermute x0 -> x39, starting transfers between devices: none -> 61 us  [send(): return lax.ppermute(value, AXES, pairs)]
    unnamed x6 -> x28, local copies, waits for them, and re-layouts: 0.45 us -> 9.85 us
    dot_general x2 -> x3, matrix products: 21.4 us -> 13.5 us  [the longest x2 12.3 us: on_device(): lax.dot_general(left, pieces[k], (((0,), (0,)), ((), ())), preferred_elem...]
    slice x0 -> x9, local copies, waits for them, and re-layouts: none -> 5.44 us  [the longest x2 2.39 us: on_device(): above[items:]]
    concatenate x0 -> x13, other arithmetic: none -> 4.72 us  [the longest x1 2.21 us: on_device(): jnp.concatenate([own[1], two1], 0)]
  transfers between devices with their start and end apart: 3 -> 39, of which waited for: 3 -> 18; matrix products, arithmetic and copies ran while one was open for 8% -> 16% of each run, Pallas kernels for 0% -> 0%
where the time goes in v1:
time: 207 us; the launch traced here: 203 us
  waiting for transfers between devices  96.2 us (46%)
  starting transfers between devices  61 us (29%)
  local copies, waits for them, and re-layouts  20.6 us (10%)
  matrix products  13.5 us (7%)
  other arithmetic  10.7 us (5%)
    ppermute x39, waiting for transfers between devices, send(): return lax.ppermute(value, AXES, pairs)  96.2 us
    ppermute x39, starting transfers between devices, send(): return lax.ppermute(value, AXES, pairs)  61 us
    dot_general x2, matrix products, on_device(): lax.dot_general(left, pieces[k], (((0,), (0,)), ((), ())), preferred_elem...  12.3 us
    unnamed x28, local copies, waits for them, and re-layouts  9.85 us
  transfers between devices with their start and end apart: 39, of which 18 were waited for; matrix products, arithmetic and copies ran while one was open for 16% of the time, Pallas kernels for 0%

profile of v1, /device:TPU:0, one launch (start us, length us, event | category | flops | bytes accessed | tf_op | source)
XLA Modules:
  0.0 203.4 jit_solution(10299731398288666831)
XLA Ops:
  0.7 2.3 %constant_dynamic-slice_fusion.1 = (bf16[1024,256]{1,0:T(8,128)(2,1)}, bf16[1024,256]{1,0:T(8,128)(2,1)}) fusion(bf16[1024,512]{1,0:T(8,128)(2,1)} %param.3, s32[]{:T(128)S(6)} %select_n.155, s32[]{:T(128)S(6)} %select_n.156), kind=kLoop, calls=%fused_computation.123 | loop fusion | bytes 2097160 | tf_op jit(solution)/shard_map/dynamic_slice | solution.py:46
  3.0 3.1 %collective-permute-start = (bf16[1024,256]{1,0:T(8,128)(2,1)}, bf16[1024,256]{1,0:T(8,128)(2,1)S(1)}, u32[]{:S(2)}, u32[]{:S(2)}) collective-permute-start(bf16[1024,256]{1,0:T(8,128)(2,1)} %get-tuple-element.32), channel_id=1, source_target_pairs={{0,17},{1,16},{2,19},{3,18},{4,21},{5,20},{6,23},{7,22},{8,25},{9,... | collective-permute-start | bytes 1572872 | tf_op jit(solution)/shard_map/ppermute | solution.py:42
  6.1 12.1 %collective-permute-done = bf16[1024,256]{1,0:T(8,128)(2,1)S(1)} collective-permute-done((bf16[1024,256]{1,0:T(8,128)(2,1)}, bf16[1024,256]{1,0:T(8,128)(2,1)S(1)}, u32[]{:S(2)}, u32[]{:S(2)}) %collective-permute-start) | collective-permute-done | bytes 524320 | tf_op jit(solution)/shard_map/ppermute | solution.py:42
  18.5 12.7 %collective-permute-done.1 = bf16[1024,256]{1,0:T(8,128)(2,1)S(1)} collective-permute-done((bf16[1024,256]{1,0:T(8,128)(2,1)S(1)}, bf16[1024,256]{1,0:T(8,128)(2,1)S(1)}, u32[]{:S(2)}, u32[]{:S(2)}) %collective-permute-start.1) | collective-permute-done | bytes 524320 | tf_op jit(solution)/shard_map/ppermute | solution.py:42
  33.0 14.2 %collective-permute-done.3 = bf16[1024,256]{1,0:T(8,128)(2,1)S(1)} collective-permute-done((bf16[1024,256]{1,0:T(8,128)(2,1)}, bf16[1024,256]{1,0:T(8,128)(2,1)S(1)}, u32[]{:S(2)}, u32[]{:S(2)}) %collective-permute-start.3) | collective-permute-done | bytes 524320 | tf_op jit(solution)/shard_map/ppermute | solution.py:42
  47.2 2.8 %collective-permute-start.4 = (bf16[1024,256]{1,0:T(8,128)(2,1)S(1)}, bf16[1024,256]{1,0:T(8,128)(2,1)S(1)}, u32[]{:S(2)}, u32[]{:S(2)}) collective-permute-start(bf16[1024,256]{1,0:T(8,128)(2,1)S(1)} %collective-permute-done.3), channel_id=1, source_target_pairs={{0,17},{1,16},{2,19},{3,18},{4,21},{5,20},{6,23},{7,22},{8,25},{9,... | collective-permute-start | bytes 1572872 | tf_op jit(solution)/shard_map/ppermute | solution.py:42
  50.1 11.7 %collective-permute-done.4 = bf16[1024,256]{1,0:T(8,128)(2,1)S(1)} collective-permute-done((bf16[1024,256]{1,0:T(8,128)(2,1)S(1)}, bf16[1024,256]{1,0:T(8,128)(2,1)S(1)}, u32[]{:S(2)}, u32[]{:S(2)}) %collective-permute-start.4) | collective-permute-done | bytes 524320 | tf_op jit(solution)/shard_map/ppermute | solution.py:42
  64.1 3.3 %copy-done.9 = bf16[2048,2048]{1,0:T(8,128)(2,1)} copy-done((bf16[2048,2048]{1,0:T(8,128)(2,1)}, bf16[2048,2048]{1,0:T(8,128)(2,1)S(1)}, u32[]{:S(2)}) %copy-start.9) | copy-done | bytes 8388632
  67.4 2.8 %collective-permute-start.8 = (bf16[1024,256]{1,0:T(8,128)(2,1)}, bf16[1024,256]{1,0:T(8,128)(2,1)S(1)}, u32[]{:S(2)}, u32[]{:S(2)}) collective-permute-start(bf16[1024,256]{1,0:T(8,128)(2,1)} %get-tuple-element.31), channel_id=1, source_target_pairs={{0,17},{1,16},{2,19},{3,18},{4,21},{5,20},{6,23},{7,22},{8,25},{9,... | collective-permute-start | bytes 1572872 | tf_op jit(solution)/shard_map/ppermute | solution.py:42
  71.8 3.9 %constant_dynamic-update-slice_fusion.6 = bf16[2048,2048]{1,0:T(8,128)(2,1)} fusion(bf16[2048,2048]{1,0:T(8,128)(2,1)} %copy-done.9, bf16[2048,256]{1,0:T(8,128)(2,1)} %collective-permute-done.5), kind=kLoop, calls=%fused_computation.118 | loop fusion | bytes 2097152
  78.6 2.8 %collective-permute-start.19 = (bf16[2048,128]{1,0:T(8,128)(2,1)}, bf16[2048,128]{1,0:T(8,128)(2,1)}, u32[]{:S(2)}, u32[]{:S(2)}) collective-permute-start(bf16[2048,128]{1,0:T(8,128)(2,1)} %get-tuple-element.26), channel_id=1, source_target_pairs={{0,96},{1,97},{2,98},{3,99},{4,100},{5,101},{6,102},{7,103},{8,104... | collective-permute-start | bytes 1572872 | tf_op jit(solution)/shard_map/ppermute | solution.py:42
  83.8 2.3 %collective-permute-start.10 = (bf16[2048,128]{1,0:T(8,128)(2,1)}, bf16[2048,128]{1,0:T(8,128)(2,1)}, u32[]{:S(2)}, u32[]{:S(2)}) collective-permute-start(bf16[2048,128]{1,0:T(8,128)(2,1)} %get-tuple-element.25), channel_id=1, source_target_pairs={{0,96},{1,97},{2,98},{3,99},{4,100},{5,101},{6,102},{7,103},{8,104... | collective-permute-start | bytes 1572872 | tf_op jit(solution)/shard_map/ppermute | solution.py:42
  86.1 7.9 %collective-permute-done.19 = bf16[2048,128]{1,0:T(8,128)(2,1)} collective-permute-done((bf16[2048,128]{1,0:T(8,128)(2,1)}, bf16[2048,128]{1,0:T(8,128)(2,1)}, u32[]{:S(2)}, u32[]{:S(2)}) %collective-permute-start.19) | collective-permute-done | bytes 524320 | tf_op jit(solution)/shard_map/ppermute | solution.py:42
  99.2 3.7 %collective-permute-start.37 = (bf16[2,64,1024]{2,1,0:T(8,128)(2,1)S(1)}, bf16[2,64,1024]{2,1,0:T(8,128)(2,1)S(1)}, u32[]{:S(2)}, u32[]{:S(2)}) collective-permute-start(bf16[2,64,1024]{2,1,0:T(8,128)(2,1)S(1)} %get-tuple-element.19), channel_id=1, source_target_pairs={{0,64},{1,65},{2,66},{3,67},{4,68},{5,69},{6,70},{7,71},{8,72},{9,... | collective-permute-start | bytes 786440 | tf_op jit(solution)/shard_map/ppermute | solution.py:42
  103.9 5.7 %collective-permute-done.10 = bf16[2048,128]{1,0:T(8,128)(2,1)} collective-permute-done((bf16[2048,128]{1,0:T(8,128)(2,1)}, bf16[2048,128]{1,0:T(8,128)(2,1)}, u32[]{:S(2)}, u32[]{:S(2)}) %collective-permute-start.10) | collective-permute-done | bytes 524320 | tf_op jit(solution)/shard_map/ppermute | solution.py:42
  109.6 3.8 %collective-permute-start.36 = (bf16[2,64,1024]{2,1,0:T(8,128)(2,1)S(1)}, bf16[2,64,1024]{2,1,0:T(8,128)(2,1)S(1)}, u32[]{:S(2)}, u32[]{:S(2)}) collective-permute-start(bf16[2,64,1024]{2,1,0:T(8,128)(2,1)S(1)} %get-tuple-element.20), channel_id=1, source_target_pairs={{0,96},{1,97},{2,98},{3,99},{4,100},{5,101},{6,102},{7,103},{8,104... | collective-permute-start | bytes 786440 | tf_op jit(solution)/shard_map/ppermute | solution.py:42
  122.3 3.7 %collective-permute-start.13 = (bf16[1024,128]{1,0:T(8,128)(2,1)S(1)}, bf16[1024,128]{1,0:T(8,128)(2,1)S(1)}, u32[]{:S(2)}, u32[]{:S(2)}) collective-permute-start(bf16[1024,128]{1,0:T(8,128)(2,1)S(1)} %slice.162), channel_id=1, source_target_pairs={{0,96},{1,97},{2,98},{3,99},{4,100},{5,101},{6,102},{7,103},{8,104... | collective-permute-start | bytes 786440 | tf_op jit(solution)/shard_map/ppermute | solution.py:42
  126.0 6.1 %convolution_convert_fusion = bf16[2048,512]{1,0:T(8,128)(2,1)S(1)} fusion(bf16[2048,2048]{1,0:T(8,128)(2,1)S(1)} %constant_dynamic-update-slice_fusion.2, bf16[2048,128]{1,0:T(8,128)(2,1)} %collective-permute-done.20, bf16[1024,128]{1,0:T(8,128)(2,1)S(1)} %collective-permute-done.22, bf16[1024,128]{1,0:T(8,128)(2,1)S(1)} %collective-permute-done.21, ...), kind=kOutput, calls=%fused_computation | convolution fusion | flops 4306501632 | bytes 12582912 | tf_op jit(solution)/shard_map/dot_general | solution.py:105
  132.3 4.1 %collective-permute-start.24 = (bf16[2,1024,128]{2,1,0:T(8,128)(2,1)S(1)}, bf16[2,1024,128]{2,1,0:T(8,128)(2,1)S(1)}, u32[]{:S(2)}, u32[]{:S(2)}) collective-permute-start(bf16[2,1024,128]{2,1,0:T(8,128)(2,1)S(1)} %pad_maximum_fusion.8), channel_id=1, source_target_pairs={{0,6},{1,7},{2,0},{3,1},{4,2},{5,3},{6,4},{7,5},{8,14},{9,15},{10,... | collective-permute-start | bytes 1572872 | tf_op jit(solution)/shard_map/ppermute | solution.py:42
  136.4 6.1 %convolution_convert_fusion.1 = bf16[2048,512]{1,0:T(8,128)(2,1)S(1)} fusion(bf16[2048,2048]{1,0:T(8,128)(2,1)S(1)} %constant_dynamic-update-slice_fusion.2, bf16[2048,128]{1,0:T(8,128)(2,1)} %collective-permute-done.11, bf16[1024,128]{1,0:T(8,128)(2,1)S(1)} %collective-permute-done.13, bf16[1024,128]{1,0:T(8,128)(2,1)S(1)} %collective-permute-done.12, ...), kind=kOutput, calls=%fused_computation.1 | convolution fusion | flops 4306501632 | bytes 12582912 | tf_op jit(solution)/shard_map/dot_general | solution.py:105
  144.0 3.3 %collective-permute-done.24 = bf16[2,1024,128]{2,1,0:T(8,128)(2,1)S(1)} collective-permute-done((bf16[2,1024,128]{2,1,0:T(8,128)(2,1)S(1)}, bf16[2,1024,128]{2,1,0:T(8,128)(2,1)S(1)}, u32[]{:S(2)}, u32[]{:S(2)}) %collective-permute-start.24) | collective-permute-done | bytes 524320 | tf_op jit(solution)/shard_map/ppermute | solution.py:42
  147.9 6.5 %collective-permute-done.15 = bf16[2,1024,128]{2,1,0:T(8,128)(2,1)S(1)} collective-permute-done((bf16[2,1024,128]{2,1,0:T(8,128)(2,1)S(1)}, bf16[2,1024,128]{2,1,0:T(8,128)(2,1)S(1)}, u32[]{:S(2)}, u32[]{:S(2)}) %collective-permute-start.15) | collective-permute-done | bytes 524320 | tf_op jit(solution)/shard_map/ppermute | solution.py:42
  156.2 3.4 %collective-permute-start.25 = (bf16[1024,128]{1,0:T(8,128)(2,1)S(1)}, bf16[1024,128]{1,0:T(8,128)(2,1)S(1)}, u32[]{:S(2)}, u32[]{:S(2)}) collective-permute-start(bf16[1024,128]{1,0:T(8,128)(2,1)S(1)} %get-tuple-element.13), channel_id=1, source_target_pairs={{0,6},{1,7},{2,0},{3,1},{4,2},{5,3},{6,4},{7,5},{8,14},{9,15},{10,... | collective-permute-start | bytes 786440 | tf_op jit(solution)/shard_map/ppermute | solution.py:42
  162.4 3.2 %collective-permute-start.16 = (bf16[1024,128]{1,0:T(8,128)(2,1)S(1)}, bf16[1024,128]{1,0:T(8,128)(2,1)S(1)}, u32[]{:S(2)}, u32[]{:S(2)}) collective-permute-start(bf16[1024,128]{1,0:T(8,128)(2,1)S(1)} %get-tuple-element.6), channel_id=1, source_target_pairs={{0,6},{1,7},{2,0},{3,1},{4,2},{5,3},{6,4},{7,5},{8,14},{9,15},{10,... | collective-permute-start | bytes 786440 | tf_op jit(solution)/shard_map/ppermute | solution.py:42
  165.6 7.2 %collective-permute-done.14 = bf16[2,1024,128]{2,1,0:T(8,128)(2,1)S(1)} collective-permute-done((bf16[2,1024,128]{2,1,0:T(8,128)(2,1)S(1)}, bf16[2,1024,128]{2,1,0:T(8,128)(2,1)S(1)}, u32[]{:S(2)}, u32[]{:S(2)}) %collective-permute-start.14) | collective-permute-done | bytes 524320 | tf_op jit(solution)/shard_map/ppermute | solution.py:42
  173.0 5.1 %collective-permute-done.26 = bf16[1024,128]{1,0:T(8,128)(2,1)S(1)} collective-permute-done((bf16[1024,128]{1,0:T(8,128)(2,1)S(1)}, bf16[1024,128]{1,0:T(8,128)(2,1)S(1)}, u32[]{:S(2)}, u32[]{:S(2)}) %collective-permute-start.26) | collective-permute-done | bytes 262176 | tf_op jit(solution)/shard_map/ppermute | solution.py:42
  178.3 2.5 %collective-permute-done.17 = bf16[1024,128]{1,0:T(8,128)(2,1)S(1)} collective-permute-done((bf16[1024,128]{1,0:T(8,128)(2,1)S(1)}, bf16[1024,128]{1,0:T(8,128)(2,1)S(1)}, u32[]{:S(2)}, u32[]{:S(2)}) %collective-permute-start.17) | collective-permute-done | bytes 262176 | tf_op jit(solution)/shard_map/ppermute | solution.py:42
  181.5 3.0 %collective-permute-start.32 = (bf16[512,128]{1,0:T(8,128)(2,1)S(1)}, bf16[512,128]{1,0:T(8,128)(2,1)S(1)}, u32[]{:S(2)}, u32[]{:S(2)}) collective-permute-start(bf16[512,128]{1,0:T(8,128)(2,1)S(1)} %pad_maximum_fusion.16), channel_id=1, source_target_pairs={{0,25},{1,9},{2,27},{3,11},{4,29},{5,13},{6,31},{7,15},{8,17},{9,1... | collective-permute-start | bytes 393224 | tf_op jit(solution)/shard_map/ppermute | solution.py:42
  184.7 2.7 %collective-permute-start.30 = (bf16[512,128]{1,0:T(8,128)(2,1)S(1)}, bf16[512,128]{1,0:T(8,128)(2,1)S(1)}, u32[]{:S(2)}, u32[]{:S(2)}) collective-permute-start(bf16[512,128]{1,0:T(8,128)(2,1)S(1)} %pad_maximum_fusion.14), channel_id=1, source_target_pairs={{0,9},{1,25},{2,11},{3,27},{4,13},{5,29},{6,15},{7,31},{8,1},{9,17... | collective-permute-start | bytes 393224 | tf_op jit(solution)/shard_map/ppermute | solution.py:42
  187.5 3.8 %collective-permute-start.29 = (bf16[512,128]{1,0:T(8,128)(2,1)S(1)}, bf16[512,128]{1,0:T(8,128)(2,1)S(1)}, u32[]{:S(2)}, u32[]{:S(2)}) collective-permute-start(bf16[512,128]{1,0:T(8,128)(2,1)S(1)} %pad_maximum_fusion.13), channel_id=1, source_target_pairs={{0,17},{1,1},{2,19},{3,3},{4,21},{5,5},{6,23},{7,7},{8,25},{9,9},{... | collective-permute-start | bytes 393224 | tf_op jit(solution)/shard_map/ppermute | solution.py:42
  191.4 3.4 %collective-permute-start.28 = (bf16[512,128]{1,0:T(8,128)(2,1)S(1)}, bf16[512,128]{1,0:T(8,128)(2,1)S(1)}, u32[]{:S(2)}, u32[]{:S(2)}) collective-permute-start(bf16[512,128]{1,0:T(8,128)(2,1)S(1)} %pad_maximum_fusion.12), channel_id=1, source_target_pairs={{0,17},{1,1},{2,19},{3,3},{4,21},{5,5},{6,23},{7,7},{8,25},{9,9},{... | collective-permute-start | bytes 393224 | tf_op jit(solution)/shard_map/ppermute | solution.py:42
  195.0 3.2 %collective-permute-start.18 = (bf16[512,128]{1,0:T(8,128)(2,1)S(1)}, bf16[512,128]{1,0:T(8,128)(2,1)S(1)}, u32[]{:S(2)}, u32[]{:S(2)}) collective-permute-start(bf16[512,128]{1,0:T(8,128)(2,1)S(1)} %pad_maximum_fusion.10), channel_id=1, source_target_pairs={{0,1},{1,17},{2,3},{3,19},{4,5},{5,21},{6,7},{7,23},{8,9},{9,25},{... | collective-permute-start | bytes 393224 | tf_op jit(solution)/shard_map/ppermute | solution.py:42
  (136 shorter events, 39.6 us)
Async XLA Ops:
  3.0 15.2 %collective-permute-start = (bf16[1024,256]{1,0:T(8,128)(2,1)}, bf16[1024,256]{1,0:T(8,128)(2,1)S(1)}, u32[]{:S(2)}, u32[]{:S(2)}) collective-permute-start(bf16[1024,256]{1,0:T(8,128)(2,1)} %get-tuple-element.32), channel_id=1, source_target_pairs={{0,17},{1,16},{2,19},{3,18},{4,21},{5,20},{6,23},{7,22},{8,25},{9,... | collective-permute-start | bytes 1572872 | tf_op jit(solution)/shard_map/ppermute | solution.py:42
  18.2 13.0 %collective-permute-start.1 = (bf16[1024,256]{1,0:T(8,128)(2,1)S(1)}, bf16[1024,256]{1,0:T(8,128)(2,1)S(1)}, u32[]{:S(2)}, u32[]{:S(2)}) collective-permute-start(bf16[1024,256]{1,0:T(8,128)(2,1)S(1)} %collective-permute-done), channel_id=1, source_target_pairs={{0,16},{1,17},{2,18},{3,19},{4,20},{5,21},{6,22},{7,23},{8,24},{9,... | collective-permute-start | bytes 1572872 | tf_op jit(solution)/shard_map/ppermute | solution.py:42
  32.5 17.4 %collective-permute-start.2 = (bf16[2048,256]{1,0:T(8,128)(2,1)S(1)}, bf16[2048,256]{1,0:T(8,128)(2,1)S(1)}, u32[]{:S(2)}, u32[]{:S(2)}) collective-permute-start(bf16[2048,256]{1,0:T(8,128)(2,1)S(1)} %get-tuple-element.29), channel_id=1, source_target_pairs={{0,8},{1,9},{2,10},{3,11},{4,12},{5,13},{6,14},{7,15},{8,0},{9,1},... | collective-permute-start | bytes 3145736 | tf_op jit(solution)/shard_map/ppermute | solution.py:42
  32.6 14.6 %collective-permute-start.3 = (bf16[1024,256]{1,0:T(8,128)(2,1)}, bf16[1024,256]{1,0:T(8,128)(2,1)S(1)}, u32[]{:S(2)}, u32[]{:S(2)}) collective-permute-start(bf16[1024,256]{1,0:T(8,128)(2,1)} %get-tuple-element.31), channel_id=1, source_target_pairs={{0,16},{1,17},{2,18},{3,19},{4,20},{5,21},{6,22},{7,23},{8,24},{9,... | collective-permute-start | bytes 1572872 | tf_op jit(solution)/shard_map/ppermute | solution.py:42
  47.2 14.7 %collective-permute-start.4 = (bf16[1024,256]{1,0:T(8,128)(2,1)S(1)}, bf16[1024,256]{1,0:T(8,128)(2,1)S(1)}, u32[]{:S(2)}, u32[]{:S(2)}) collective-permute-start(bf16[1024,256]{1,0:T(8,128)(2,1)S(1)} %collective-permute-done.3), channel_id=1, source_target_pairs={{0,17},{1,16},{2,19},{3,18},{4,21},{5,20},{6,23},{7,22},{8,25},{9,... | collective-permute-start | bytes 1572872 | tf_op jit(solution)/shard_map/ppermute | solution.py:42
  67.4 13.9 %collective-permute-start.7 = (bf16[1024,256]{1,0:T(8,128)(2,1)}, bf16[1024,256]{1,0:T(8,128)(2,1)S(1)}, u32[]{:S(2)}, u32[]{:S(2)}) collective-permute-start(bf16[1024,256]{1,0:T(8,128)(2,1)} %get-tuple-element.32), channel_id=1, source_target_pairs={{0,16},{1,17},{2,18},{3,19},{4,20},{5,21},{6,22},{7,23},{8,24},{9,... | collective-permute-start | bytes 1572872 | tf_op jit(solution)/shard_map/ppermute | solution.py:42
  67.4 14.0 %collective-permute-start.8 = (bf16[1024,256]{1,0:T(8,128)(2,1)}, bf16[1024,256]{1,0:T(8,128)(2,1)S(1)}, u32[]{:S(2)}, u32[]{:S(2)}) collective-permute-start(bf16[1024,256]{1,0:T(8,128)(2,1)} %get-tuple-element.31), channel_id=1, source_target_pairs={{0,17},{1,16},{2,19},{3,18},{4,21},{5,20},{6,23},{7,22},{8,25},{9,... | collective-permute-start | bytes 1572872 | tf_op jit(solution)/shard_map/ppermute | solution.py:42
  71.7 12.2 %collective-permute-start.34 = (bf16[4,2,64,1024]{3,2,1,0:T(8,128)(2,1)S(1)}, bf16[4,2,64,1024]{3,2,1,0:T(8,128)(2,1)S(1)}, u32[]{:S(2)}, u32[]{:S(2)}) collective-permute-start(bf16[4,2,64,1024]{3,2,1,0:T(8,128)(2,1)S(1)} %fusion.18), channel_id=1, source_target_pairs={{0,8},{1,9},{2,10},{3,11},{4,12},{5,13},{6,14},{7,15},{8,0},{9,1},... | collective-permute-start | bytes 3145736 | tf_op jit(solution)/shard_map/ppermute | solution.py:42
  78.6 15.5 %collective-permute-start.19 = (bf16[2048,128]{1,0:T(8,128)(2,1)}, bf16[2048,128]{1,0:T(8,128)(2,1)}, u32[]{:S(2)}, u32[]{:S(2)}) collective-permute-start(bf16[2048,128]{1,0:T(8,128)(2,1)} %get-tuple-element.26), channel_id=1, source_target_pairs={{0,96},{1,97},{2,98},{3,99},{4,100},{5,101},{6,102},{7,103},{8,104... | collective-permute-start | bytes 1572872 | tf_op jit(solution)/shard_map/ppermute | solution.py:42
  81.3 34.2 %collective-permute-start.6 = (bf16[2048,256]{1,0:T(8,128)(2,1)S(1)}, bf16[2048,256]{1,0:T(8,128)(2,1)}, u32[]{:S(2)}, u32[]{:S(2)}) collective-permute-start(bf16[2048,256]{1,0:T(8,128)(2,1)S(1)} %get-tuple-element.37), channel_id=1, source_target_pairs={{0,8},{1,9},{2,10},{3,11},{4,12},{5,13},{6,14},{7,15},{8,0},{9,1},... | collective-permute-start | bytes 3145736 | tf_op jit(solution)/shard_map/ppermute | solution.py:42
  82.4 36.7 %collective-permute-start.9 = (bf16[2048,256]{1,0:T(8,128)(2,1)}, bf16[2048,256]{1,0:T(8,128)(2,1)}, u32[]{:S(2)}, u32[]{:S(2)}) collective-permute-start(bf16[2048,256]{1,0:T(8,128)(2,1)} %pad_maximum_fusion), channel_id=1, source_target_pairs={{0,8},{1,9},{2,10},{3,11},{4,12},{5,13},{6,14},{7,15},{8,0},{9,1},... | collective-permute-start | bytes 3145736 | tf_op jit(solution)/shard_map/ppermute | solution.py:42
  82.9 16.3 %collective-permute-start.20 = (bf16[2048,128]{1,0:T(8,128)(2,1)}, bf16[2048,128]{1,0:T(8,128)(2,1)}, u32[]{:S(2)}, u32[]{:S(2)}) collective-permute-start(bf16[2048,128]{1,0:T(8,128)(2,1)} %get-tuple-element.26), channel_id=1, source_target_pairs={{0,32},{1,33},{2,34},{3,35},{4,36},{5,37},{6,38},{7,39},{8,40},{9,... | collective-permute-start | bytes 1572872 | tf_op jit(solution)/shard_map/ppermute | solution.py:42
  83.8 25.8 %collective-permute-start.10 = (bf16[2048,128]{1,0:T(8,128)(2,1)}, bf16[2048,128]{1,0:T(8,128)(2,1)}, u32[]{:S(2)}, u32[]{:S(2)}) collective-permute-start(bf16[2048,128]{1,0:T(8,128)(2,1)} %get-tuple-element.25), channel_id=1, source_target_pairs={{0,96},{1,97},{2,98},{3,99},{4,100},{5,101},{6,102},{7,103},{8,104... | collective-permute-start | bytes 1572872 | tf_op jit(solution)/shard_map/ppermute | solution.py:42
  94.0 20.4 %collective-permute-start.11 = (bf16[2048,128]{1,0:T(8,128)(2,1)}, bf16[2048,128]{1,0:T(8,128)(2,1)}, u32[]{:S(2)}, u32[]{:S(2)}) collective-permute-start(bf16[2048,128]{1,0:T(8,128)(2,1)} %get-tuple-element.25), channel_id=1, source_target_pairs={{0,32},{1,33},{2,34},{3,35},{4,36},{5,37},{6,38},{7,39},{8,40},{9,... | collective-permute-start | bytes 1572872 | tf_op jit(solution)/shard_map/ppermute | solution.py:42
  99.2 48.5 %collective-permute-start.37 = (bf16[2,64,1024]{2,1,0:T(8,128)(2,1)S(1)}, bf16[2,64,1024]{2,1,0:T(8,128)(2,1)S(1)}, u32[]{:S(2)}, u32[]{:S(2)}) collective-permute-start(bf16[2,64,1024]{2,1,0:T(8,128)(2,1)S(1)} %get-tuple-element.19), channel_id=1, source_target_pairs={{0,64},{1,65},{2,66},{3,67},{4,68},{5,69},{6,70},{7,71},{8,72},{9,... | collective-permute-start | bytes 786440 | tf_op jit(solution)/shard_map/ppermute | solution.py:42
  109.6 38.1 %collective-permute-start.36 = (bf16[2,64,1024]{2,1,0:T(8,128)(2,1)S(1)}, bf16[2,64,1024]{2,1,0:T(8,128)(2,1)S(1)}, u32[]{:S(2)}, u32[]{:S(2)}) collective-permute-start(bf16[2,64,1024]{2,1,0:T(8,128)(2,1)S(1)} %get-tuple-element.20), channel_id=1, source_target_pairs={{0,96},{1,97},{2,98},{3,99},{4,100},{5,101},{6,102},{7,103},{8,104... | collective-permute-start | bytes 786440 | tf_op jit(solution)/shard_map/ppermute | solution.py:42
  115.5 10.5 %collective-permute-start.21 = (bf16[1024,128]{1,0:T(8,128)(2,1)S(1)}, bf16[1024,128]{1,0:T(8,128)(2,1)S(1)}, u32[]{:S(2)}, u32[]{:S(2)}) collective-permute-start(bf16[1024,128]{1,0:T(8,128)(2,1)S(1)} %slice.169), channel_id=1, source_target_pairs={{0,32},{1,33},{2,34},{3,35},{4,36},{5,37},{6,38},{7,39},{8,40},{9,... | collective-permute-start | bytes 786440 | tf_op jit(solution)/shard_map/ppermute | solution.py:42
  119.1 28.6 %collective-permute-start.35 = (bf16[2,64,1024]{2,1,0:T(8,128)(2,1)S(1)}, bf16[2,64,1024]{2,1,0:T(8,128)(2,1)S(1)}, u32[]{:S(2)}, u32[]{:S(2)}) collective-permute-start(bf16[2,64,1024]{2,1,0:T(8,128)(2,1)S(1)} %get-tuple-element.18), channel_id=1, source_target_pairs={{0,32},{1,33},{2,34},{3,35},{4,36},{5,37},{6,38},{7,39},{8,40},{9,... | collective-permute-start | bytes 786440 | tf_op jit(solution)/shard_map/ppermute | solution.py:42
  122.3 10.0 %collective-permute-start.13 = (bf16[1024,128]{1,0:T(8,128)(2,1)S(1)}, bf16[1024,128]{1,0:T(8,128)(2,1)S(1)}, u32[]{:S(2)}, u32[]{:S(2)}) collective-permute-start(bf16[1024,128]{1,0:T(8,128)(2,1)S(1)} %slice.162), channel_id=1, source_target_pairs={{0,96},{1,97},{2,98},{3,99},{4,100},{5,101},{6,102},{7,103},{8,104... | collective-permute-start | bytes 786440 | tf_op jit(solution)/shard_map/ppermute | solution.py:42
  126.0 10.4 %collective-permute-start.12 = (bf16[1024,128]{1,0:T(8,128)(2,1)S(1)}, bf16[1024,128]{1,0:T(8,128)(2,1)S(1)}, u32[]{:S(2)}, u32[]{:S(2)}) collective-permute-start(bf16[1024,128]{1,0:T(8,128)(2,1)S(1)} %slice.161), channel_id=1, source_target_pairs={{0,32},{1,33},{2,34},{3,35},{4,36},{5,37},{6,38},{7,39},{8,40},{9,... | collective-permute-start | bytes 786440 | tf_op jit(solution)/shard_map/ppermute | solution.py:42
  132.3 14.9 %collective-permute-start.24 = (bf16[2,1024,128]{2,1,0:T(8,128)(2,1)S(1)}, bf16[2,1024,128]{2,1,0:T(8,128)(2,1)S(1)}, u32[]{:S(2)}, u32[]{:S(2)}) collective-permute-start(bf16[2,1024,128]{2,1,0:T(8,128)(2,1)S(1)} %pad_maximum_fusion.8), channel_id=1, source_target_pairs={{0,6},{1,7},{2,0},{3,1},{4,2},{5,3},{6,4},{7,5},{8,14},{9,15},{10,... | collective-permute-start | bytes 1572872 | tf_op jit(solution)/shard_map/ppermute | solution.py:42
  142.7 11.6 %collective-permute-start.15 = (bf16[2,1024,128]{2,1,0:T(8,128)(2,1)S(1)}, bf16[2,1024,128]{2,1,0:T(8,128)(2,1)S(1)}, u32[]{:S(2)}, u32[]{:S(2)}) collective-permute-start(bf16[2,1024,128]{2,1,0:T(8,128)(2,1)S(1)} %pad_maximum_fusion.5), channel_id=1, source_target_pairs={{0,6},{1,7},{2,0},{3,1},{4,2},{5,3},{6,4},{7,5},{8,14},{9,15},{10,... | collective-permute-start | bytes 1572872 | tf_op jit(solution)/shard_map/ppermute | solution.py:42
  147.5 14.1 %collective-permute-start.23 = (bf16[2,1024,128]{2,1,0:T(8,128)(2,1)S(1)}, bf16[2,1024,128]{2,1,0:T(8,128)(2,1)S(1)}, u32[]{:S(2)}, u32[]{:S(2)}) collective-permute-start(bf16[2,1024,128]{2,1,0:T(8,128)(2,1)S(1)} %pad_maximum_fusion.7), channel_id=1, source_target_pairs={{0,2},{1,3},{2,4},{3,5},{4,6},{5,7},{6,0},{7,1},{8,10},{9,11},{10,... | collective-permute-start | bytes 1572872 | tf_op jit(solution)/shard_map/ppermute | solution.py:42
  154.6 18.2 %collective-permute-start.14 = (bf16[2,1024,128]{2,1,0:T(8,128)(2,1)S(1)}, bf16[2,1024,128]{2,1,0:T(8,128)(2,1)S(1)}, u32[]{:S(2)}, u32[]{:S(2)}) collective-permute-start(bf16[2,1024,128]{2,1,0:T(8,128)(2,1)S(1)} %pad_maximum_fusion.4), channel_id=1, source_target_pairs={{0,2},{1,3},{2,4},{3,5},{4,6},{5,7},{6,0},{7,1},{8,10},{9,11},{10,... | collective-permute-start | bytes 1572872 | tf_op jit(solution)/shard_map/ppermute | solution.py:42
  156.2 16.8 %collective-permute-start.25 = (bf16[1024,128]{1,0:T(8,128)(2,1)S(1)}, bf16[1024,128]{1,0:T(8,128)(2,1)S(1)}, u32[]{:S(2)}, u32[]{:S(2)}) collective-permute-start(bf16[1024,128]{1,0:T(8,128)(2,1)S(1)} %get-tuple-element.13), channel_id=1, source_target_pairs={{0,6},{1,7},{2,0},{3,1},{4,2},{5,3},{6,4},{7,5},{8,14},{9,15},{10,... | collective-permute-start | bytes 786440 | tf_op jit(solution)/shard_map/ppermute | solution.py:42
  161.6 16.4 %collective-permute-start.26 = (bf16[1024,128]{1,0:T(8,128)(2,1)S(1)}, bf16[1024,128]{1,0:T(8,128)(2,1)S(1)}, u32[]{:S(2)}, u32[]{:S(2)}) collective-permute-start(bf16[1024,128]{1,0:T(8,128)(2,1)S(1)} %dynamic-slice_add_fusion), channel_id=1, source_target_pairs={{0,2},{1,3},{2,4},{3,5},{4,6},{5,7},{6,0},{7,1},{8,10},{9,11},{10,... | collective-permute-start | bytes 786440 | tf_op jit(solution)/shard_map/ppermute | solution.py:42
  162.4 15.9 %collective-permute-start.16 = (bf16[1024,128]{1,0:T(8,128)(2,1)S(1)}, bf16[1024,128]{1,0:T(8,128)(2,1)S(1)}, u32[]{:S(2)}, u32[]{:S(2)}) collective-permute-start(bf16[1024,128]{1,0:T(8,128)(2,1)S(1)} %get-tuple-element.6), channel_id=1, source_target_pairs={{0,6},{1,7},{2,0},{3,1},{4,2},{5,3},{6,4},{7,5},{8,14},{9,15},{10,... | collective-permute-start | bytes 786440 | tf_op jit(solution)/shard_map/ppermute | solution.py:42
  181.3 10.1 %collective-permute-start.33 = (bf16[512,128]{1,0:T(8,128)(2,1)S(1)}, bf16[512,128]{1,0:T(8,128)(2,1)S(1)}, u32[]{:S(2)}, u32[]{:S(2)}) collective-permute-start(bf16[512,128]{1,0:T(8,128)(2,1)S(1)} %pad_maximum_fusion.17), channel_id=1, source_target_pairs={{0,25},{1,9},{2,27},{3,11},{4,29},{5,13},{6,31},{7,15},{8,17},{9,1... | collective-permute-start | bytes 393224 | tf_op jit(solution)/shard_map/ppermute | solution.py:42
  181.5 13.4 %collective-permute-start.32 = (bf16[512,128]{1,0:T(8,128)(2,1)S(1)}, bf16[512,128]{1,0:T(8,128)(2,1)S(1)}, u32[]{:S(2)}, u32[]{:S(2)}) collective-permute-start(bf16[512,128]{1,0:T(8,128)(2,1)S(1)} %pad_maximum_fusion.16), channel_id=1, source_target_pairs={{0,25},{1,9},{2,27},{3,11},{4,29},{5,13},{6,31},{7,15},{8,17},{9,1... | collective-permute-start | bytes 393224 | tf_op jit(solution)/shard_map/ppermute | solution.py:42
  184.6 10.4 %collective-permute-start.31 = (bf16[512,128]{1,0:T(8,128)(2,1)S(1)}, bf16[512,128]{1,0:T(8,128)(2,1)S(1)}, u32[]{:S(2)}, u32[]{:S(2)}) collective-permute-start(bf16[512,128]{1,0:T(8,128)(2,1)S(1)} %pad_maximum_fusion.15), channel_id=1, source_target_pairs={{0,9},{1,25},{2,11},{3,27},{4,13},{5,29},{6,15},{7,31},{8,1},{9,17... | collective-permute-start | bytes 393224 | tf_op jit(solution)/shard_map/ppermute | solution.py:42
  184.7 13.5 %collective-permute-start.30 = (bf16[512,128]{1,0:T(8,128)(2,1)S(1)}, bf16[512,128]{1,0:T(8,128)(2,1)S(1)}, u32[]{:S(2)}, u32[]{:S(2)}) collective-permute-start(bf16[512,128]{1,0:T(8,128)(2,1)S(1)} %pad_maximum_fusion.14), channel_id=1, source_target_pairs={{0,9},{1,25},{2,11},{3,27},{4,13},{5,29},{6,15},{7,31},{8,1},{9,17... | collective-permute-start | bytes 393224 | tf_op jit(solution)/shard_map/ppermute | solution.py:42
  187.5 10.8 %collective-permute-start.29 = (bf16[512,128]{1,0:T(8,128)(2,1)S(1)}, bf16[512,128]{1,0:T(8,128)(2,1)S(1)}, u32[]{:S(2)}, u32[]{:S(2)}) collective-permute-start(bf16[512,128]{1,0:T(8,128)(2,1)S(1)} %pad_maximum_fusion.13), channel_id=1, source_target_pairs={{0,17},{1,1},{2,19},{3,3},{4,21},{5,5},{6,23},{7,7},{8,25},{9,9},{... | collective-permute-start | bytes 393224 | tf_op jit(solution)/shard_map/ppermute | solution.py:42
  (18 other events, 232.9 us)

commit v2 on v0

v2 whole, which is shorter than its diff:
```python
import jax
import jax.numpy as jnp
from jax import lax
from jax.sharding import PartitionSpec as P

SIZES = (4, 2, 2, 4, 2)
AXES = ("feat", "batch")


def flat(place):
    index = 0
    for value, size in zip(place, SIZES):
        index = index * size + value % size
    return index


def table(move):
    pairs = []
    for x in range(4):
        for yl in range(2):
            for c in range(2):
                for z in range(4):
                    for yh in range(2):
                        pairs.append((flat((x, yl, c, z, yh)), flat(move(x, yl, c, z, yh))))
    return pairs


CORE = table(lambda x, yl, c, z, yh: (x, yl, 1 - c, z, yh))
NEAR = table(lambda x, yl, c, z, yh: (x, 1 - yl, c, z, yh))
FAR = table(lambda x, yl, c, z, yh: (x, 1 - yl, c, z, 1 - yh))
X_STEP = {d: table(lambda x, yl, c, z, yh, d=d: (x + d, yl, c, z, yh)) for d in (1, 2, 3)}
Z_STEP = {d: table(lambda x, yl, c, z, yh, d=d: (x, yl, c, z + d, yh)) for d in (1, 3)}
HOME = {
    (s, t): table(lambda x, yl, c, z, yh, s=s, t=t: (x, yh ^ s, c ^ t, z, 1 - yl))
    for s in range(2)
    for t in range(2)
}


def send(value, pairs):
    return lax.ppermute(value, AXES, pairs)


def columns(array, start, size):
    return lax.dynamic_slice_in_dim(array, start, size, 1)


def pick(array, index):
    return lax.dynamic_index_in_dim(array, index, 0, keepdims=False)


def wide(value):
    return value.astype(jnp.float32)


def narrow(value):
    return value.astype(jnp.bfloat16)


def together(sends, held):
    values, held = lax.optimization_barrier(([value for value, _ in sends], held))
    results = [send(value, pairs) for value, (_, pairs) in zip(values, sends)]
    return lax.optimization_barrier((results, held))


def on_device(embeddings, basis, cov_prior):
    feat, batch = lax.axis_index("feat"), lax.axis_index("batch")
    x, yl, c = feat // 4, feat // 2 % 2, feat % 2
    z, yh = batch // 2, batch % 2
    items, feats = embeddings.shape
    half = feats // 2
    items_total = items * lax.axis_size("batch")

    own = [columns(embeddings, (yh ^ i) * half, half) for i in range(2)]
    (near, far), own = together([(own[0], NEAR), (own[1], FAR)], own)

    share = jnp.dot(embeddings, basis, preferred_element_type=jnp.float32)
    rows, width = share.shape[0] // 16, share.shape[1]
    share = jnp.moveaxis(share.reshape(4, 2, 2, rows, width), 2, 0)
    share_mine, share_sent = pick(share, c), narrow(pick(share, 1 - c))

    right = jnp.concatenate([near, far], 0)
    (below, above, to_near, to_far, share_got), (right, own, share_mine) = together(
        [
            (right, X_STEP[1]),
            (right, X_STEP[3]),
            (jnp.concatenate([own[1], far], 1), NEAR),
            (jnp.concatenate([own[0], near], 1), FAR),
            (share_sent, CORE),
        ],
        (right, own, share_mine),
    )
    groups = [
        jnp.concatenate([own[0], to_near[:, half:]], 0),
        jnp.concatenate([own[1], to_far[:, half:]], 0),
        right,
        jnp.concatenate([to_near[:, :half], to_far[:, :half]], 0),
    ]
    group = jnp.concatenate(groups, 1)
    share = share_mine + wide(share_got)
    (up_half, down_half, other), (right, above, below, group, share) = together(
        [(below[:items], X_STEP[1]), (above[items:], X_STEP[3]), (group, CORE)],
        (right, above, below, group, share),
    )
    across = jnp.concatenate([up_half, down_half], 0)
    blocks = jnp.stack([right, above, across, below])
    rhs = jnp.concatenate([pick(blocks, (z + d - x) % 4) for d in range(4)], 1)
    partial = [
        narrow(
            lax.dot_general(lhs, rhs, (((0,), (0,)), ((), ())), preferred_element_type=jnp.float32)
        )
        for lhs in (group, other)
    ]
    block = [[p[:, d * half : (d + 1) * half] for p in partial] for d in range(4)]
    outgoing = narrow(share)
    (down, up, *shares), (block, share) = together(
        [
            (jnp.stack([block[2][0], block[3][1]]), Z_STEP[3]),
            (jnp.stack([block[1][0], block[2][1]]), Z_STEP[1]),
        ]
        + [(pick(outgoing, (x + d) % 4), X_STEP[d]) for d in (1, 2, 3)],
        (block, share),
    )
    share = pick(share, x) + sum(wide(s) for s in shares)
    (first, second, share_got), (block, up, down, share) = together(
        [
            (narrow(wide(down[0]) + wide(block[3][0])), Z_STEP[3]),
            (narrow(wide(up[1]) + wide(block[1][1])), Z_STEP[1]),
            (narrow(pick(share, 1 - yl)), NEAR),
        ],
        (block, up, down, share),
    )
    projected = narrow(pick(share, yl) + wide(share_got))
    whole = jnp.stack(
        [
            narrow(wide(block[0][0]) + wide(up[0]) + wide(first)),
            narrow(wide(block[0][1]) + wide(down[1]) + wide(second)),
        ]
    ).reshape(2, 2, 2, half, half)
    homeward = []
    for s in range(2):
        for t in range(2):
            chosen = pick(whole[t], yl ^ yh ^ s)
            value = jnp.concatenate([pick(chosen, yh ^ i) for i in range(2)], 0)
            homeward.append((value, HOME[s, t]))
    arrived, projected = together(homeward, projected)
    arrived = jnp.stack(arrived)
    gram = jnp.concatenate(
        [pick(arrived, (q % 2 ^ yl) * 2 + (q // 2 ^ c)) for q in range(4)], 1
    )
    covariance = 0.9 * cov_prior + wide(gram) / items_total
    return (covariance, projected)


def solution(mesh):
    placed = (P("batch", "feat"), P("feat", None), P("feat", "batch"))
    return jax.shard_map(
        on_device,
        mesh=mesh,
        in_specs=placed,
        out_specs=(P("feat", "batch"), P(("batch", "feat"), None)),
        check_vma=False,
    )
```

time: 301 us -> 186 us (0.62)
  waiting for transfers between devices: 260 us -> 88.2 us
  other arithmetic: 4.51 us -> 39 us
  starting transfers between devices: 0.12 us -> 32.1 us
  between operations: 13.8 us -> 0.99 us
  local copies, waits for them, and re-layouts: 0.45 us -> 7.64 us
  matrix products: 21.4 us -> 16.9 us
    reduce_scatter x2 -> x0, waiting for transfers between devices: 169 us -> none  [the longest x1 115 us: on_device(): lax.psum_scatter(partial_gram.astype(jnp.bfloat16), 'batch', scatter_dime...]
    all_gather x1 -> x0, waiting for transfers between devices: 90.8 us -> none  [on_device(): lax.all_gather(embeddings, 'feat', axis=1, tiled=True)]
    ppermute x0 -> x22, waiting for transfers between devices: none -> 88.2 us  [send(): return lax.ppermute(value, AXES, pairs)]
    ppermute x0 -> x22, starting transfers between devices: none -> 32.1 us  [send(): return lax.ppermute(value, AXES, pairs)]
    concatenate x0 -> x7, other arithmetic: none -> 22.6 us  [the longest x1 19.9 us: on_device(): group = jnp.concatenate(groups, 1)]
    another operation x0 -> x5, other arithmetic: none -> 5.35 us  [the longest x2 3.08 us: on_device(): blocks = jnp.stack([right, above, across, below])]
    dot_general x2 -> x3, matrix products: 21.4 us -> 16.9 us  [the longest x2 14.4 us: on_device(): lax.dot_general(lhs, rhs, (((0,), (0,)), ((), ())), preferred_element_typ...]
    convert_element_type x1 -> x6, other arithmetic: 1.62 us -> 6.02 us  [narrow(): return value.astype(jnp.bfloat16)]
  transfers between devices with their start and end apart: 3 -> 22, of which waited for: 3 -> 16; matrix products, arithmetic and copies ran while one was open for 8% -> 2% of each run, Pallas kernels for 0% -> 0%
where the time goes in v2:
time: 186 us; the launch traced here: 185 us
  waiting for transfers between devices  88.2 us (47%)
  other arithmetic  39 us (21%)
  starting transfers between devices  32.1 us (17%)
  matrix products  16.9 us (9%)
  local copies, waits for them, and re-layouts  7.64 us (4%)
    ppermute x22, waiting for transfers between devices, send(): return lax.ppermute(value, AXES, pairs)  88.2 us
    ppermute x22, starting transfers between devices, send(): return lax.ppermute(value, AXES, pairs)  32.1 us
    concatenate x1, other arithmetic, on_device(): group = jnp.concatenate(groups, 1)  19.9 us
    dot_general x2, matrix products, on_device(): lax.dot_general(lhs, rhs, (((0,), (0,)), ((), ())), preferred_element_typ...  14.4 us
    convert_element_type x6, other arithmetic, narrow(): return value.astype(jnp.bfloat16)  6.02 us
  transfers between devices with their start and end apart: 22, of which 16 were waited for; matrix products, arithmetic and copies ran while one was open for 2% of the time, Pallas kernels for 0%

profile of v2, /device:TPU:0, one launch (start us, length us, event | category | flops | bytes accessed | tf_op | source)
XLA Modules:
  0.0 184.8 jit_solution(4793775281091116290)
XLA Ops:
  2.0 1.7 collective-permute-start
  3.8 2.2 %collective-permute-start.1 = (bf16[1024,256]{1,0:T(8,128)(2,1)S(1)}, bf16[1024,256]{1,0:T(8,128)(2,1)}, u32[]{:S(2)}, u32[]{:S(2)}) collective-permute-start(bf16[1024,256]{1,0:T(8,128)(2,1)S(1)} %get-tuple-element.111), channel_id=1, source_target_pairs={{0,17},{1,16},{2,19},{3,18},{4,21},{5,20},{6,23},{7,22},{8,25},{9,... | collective-permute-start | bytes 1572872 | tf_op jit(solution)/shard_map/ppermute | solution.py:41
  6.0 2.5 %fusion.15 = f32[1024,1024]{1,0:T(8,128)S(1)} fusion(bf16[1024,512]{1,0:T(8,128)(2,1)} %param.3, bf16[512,1024]{1,0:T(8,128)(2,1)S(1)} %copy-done), kind=kOutput, calls=%fused_computation.67 | convolution fusion | flops 1073741824 | bytes 6291456 | tf_op jit(solution)/shard_map/dot_general | solution.py:77
  8.9 6.8 %collective-permute-done = bf16[1024,256]{1,0:T(8,128)(2,1)S(1)} collective-permute-done((bf16[1024,256]{1,0:T(8,128)(2,1)S(1)}, bf16[1024,256]{1,0:T(8,128)(2,1)S(1)}, u32[]{:S(2)}, u32[]{:S(2)}) %collective-permute-start) | collective-permute-done | bytes 524320 | tf_op jit(solution)/shard_map/ppermute | solution.py:41
  16.5 2.0 %collective-permute-done.1 = bf16[1024,256]{1,0:T(8,128)(2,1)} collective-permute-done((bf16[1024,256]{1,0:T(8,128)(2,1)S(1)}, bf16[1024,256]{1,0:T(8,128)(2,1)}, u32[]{:S(2)}, u32[]{:S(2)}) %collective-permute-start.1) | collective-permute-done | bytes 524320 | tf_op jit(solution)/shard_map/ppermute | solution.py:41
  21.1 1.6 collective-permute-start.2
  22.7 1.7 collective-permute-start.3
  24.4 2.3 %collective-permute-start.5 = (bf16[1024,512]{1,0:T(8,128)(2,1)S(1)}, bf16[1024,512]{1,0:T(8,128)(2,1)S(1)}, u32[]{:S(2)}, u32[]{:S(2)}) collective-permute-start(bf16[1024,512]{1,0:T(8,128)(2,1)S(1)} %get-tuple-element.101), channel_id=1, source_target_pairs={{0,17},{1,16},{2,19},{3,18},{4,21},{5,20},{6,23},{7,22},{8,25},{9,... | collective-permute-start | bytes 3145736 | tf_op jit(solution)/shard_map/ppermute | solution.py:41
  26.7 19.4 %collective-permute-done.2 = bf16[2048,256]{1,0:T(8,128)(2,1)S(1)} collective-permute-done((bf16[2048,256]{1,0:T(8,128)(2,1)S(1)}, bf16[2048,256]{1,0:T(8,128)(2,1)S(1)}, u32[]{:S(2)}, u32[]{:S(2)}) %collective-permute-start.2) | collective-permute-done | bytes 1048608 | tf_op jit(solution)/shard_map/ppermute | solution.py:41
  51.0 19.9 %maximum_maximum_fusion = bf16[2048,1024]{1,0:T(8,128)(2,1)} fusion(bf16[1024,256]{1,0:T(8,128)(2,1)S(1)} %get-tuple-element.200, bf16[1024,256]{1,0:T(8,128)(2,1)S(1)} %get-tuple-element.198, bf16[2048,256]{1,0:T(8,128)(2,1)S(1)} %pad_maximum_fusion.2, bf16[1024,256]{1,0:T(8,128)(2,1)S(1)} %get-tuple-element.199, bf16[1024,256]{1,0:T(8,128)(2,1)S(1)} %copy-done.3, ...), kind=kLoop, calls=%fused_computation | loop fusion | flops 29360128 | bytes 8388608 | tf_op jit(solution)/shard_map/concatenate | solution.py:99
  71.2 3.0 %collective-permute-start.8 = (bf16[1024,256]{1,0:T(8,128)(2,1)}, bf16[1024,256]{1,0:T(8,128)(2,1)}, u32[]{:S(2)}, u32[]{:S(2)}) collective-permute-start(bf16[1024,256]{1,0:T(8,128)(2,1)} %slice.61), channel_id=1, source_target_pairs={{0,96},{1,97},{2,98},{3,99},{4,100},{5,101},{6,102},{7,103},{8,104... | collective-permute-start | bytes 1572872 | tf_op jit(solution)/shard_map/ppermute | solution.py:41
  74.2 12.6 %collective-permute-done.7 = bf16[1024,256]{1,0:T(8,128)(2,1)} collective-permute-done((bf16[1024,256]{1,0:T(8,128)(2,1)}, bf16[1024,256]{1,0:T(8,128)(2,1)}, u32[]{:S(2)}, u32[]{:S(2)}) %collective-permute-start.7) | collective-permute-done | bytes 524320 | tf_op jit(solution)/shard_map/ppermute | solution.py:41
  88.1 1.8 pad_maximum_fusion
  90.2 7.2 %convolution_convert_fusion.1 = bf16[1024,1024]{1,0:T(8,128)(2,1)S(1)} fusion(bf16[2048,1024]{1,0:T(8,128)(2,1)} %maximum_maximum_fusion, bf16[2048,256]{1,0:T(8,128)(2,1)S(1)} %get-tuple-element.179, bf16[2048,256]{1,0:T(8,128)(2,1)S(1)} %get-tuple-element.180, bf16[2048,256]{1,0:T(8,128)(2,1)S(1)} %get-tuple-element.181, ...), kind=kOutput, calls=%fused_computation.8 | convolution fusion | flops 4312793088 | bytes 10485760 | tf_op jit(solution)/shard_map/dot_general | solution.py:110
  98.3 7.2 %convolution_convert_fusion = bf16[1024,1024]{1,0:T(8,128)(2,1)S(1)} fusion(bf16[2048,1024]{1,0:T(8,128)(2,1)} %collective-permute-done.9, bf16[2048,256]{1,0:T(8,128)(2,1)S(1)} %get-tuple-element.179, bf16[2048,256]{1,0:T(8,128)(2,1)S(1)} %get-tuple-element.180, bf16[2048,256]{1,0:T(8,128)(2,1)S(1)} %get-tuple-element.181, ...), kind=kOutput, calls=%fused_computation.7 | convolution fusion | flops 4312793088 | bytes 10485760 | tf_op jit(solution)/shard_map/dot_general | solution.py:110
  109.6 4.0 %collective-permute-start.10 = (bf16[2,1024,256]{2,1,0:T(8,128)(2,1)}, bf16[2,1024,256]{2,1,0:T(8,128)(2,1)}, u32[]{:S(2)}, u32[]{:S(2)}) collective-permute-start(bf16[2,1024,256]{2,1,0:T(8,128)(2,1)} %pad_maximum_fusion.5), channel_id=1, source_target_pairs={{0,6},{1,7},{2,0},{3,1},{4,2},{5,3},{6,4},{7,5},{8,14},{9,15},{10,... | collective-permute-start | bytes 3145736 | tf_op jit(solution)/shard_map/ppermute | solution.py:41
  113.9 4.1 %collective-permute-start.13 = (bf16[2,64,1024]{2,1,0:T(8,128)(2,1)}, bf16[2,64,1024]{2,1,0:T(8,128)(2,1)}, u32[]{:S(2)}, u32[]{:S(2)}) collective-permute-start(bf16[2,64,1024]{2,1,0:T(8,128)(2,1)} %get-tuple-element.135), channel_id=1, source_target_pairs={{0,64},{1,65},{2,66},{3,67},{4,68},{5,69},{6,70},{7,71},{8,72},{9,... | collective-permute-start | bytes 786440 | tf_op jit(solution)/shard_map/ppermute | solution.py:41
  118.1 5.8 %collective-permute-done.12 = bf16[2,64,1024]{2,1,0:T(8,128)(2,1)} collective-permute-done((bf16[2,64,1024]{2,1,0:T(8,128)(2,1)}, bf16[2,64,1024]{2,1,0:T(8,128)(2,1)}, u32[]{:S(2)}, u32[]{:S(2)}) %collective-permute-start.12) | collective-permute-done | bytes 262176 | tf_op jit(solution)/shard_map/ppermute | solution.py:41
  123.9 5.4 %collective-permute-done.13 = bf16[2,64,1024]{2,1,0:T(8,128)(2,1)} collective-permute-done((bf16[2,64,1024]{2,1,0:T(8,128)(2,1)}, bf16[2,64,1024]{2,1,0:T(8,128)(2,1)}, u32[]{:S(2)}, u32[]{:S(2)}) %collective-permute-start.13) | collective-permute-done | bytes 262176 | tf_op jit(solution)/shard_map/ppermute | solution.py:41
  129.3 7.0 %collective-permute-done.10 = bf16[2,1024,256]{2,1,0:T(8,128)(2,1)} collective-permute-done((bf16[2,1024,256]{2,1,0:T(8,128)(2,1)}, bf16[2,1024,256]{2,1,0:T(8,128)(2,1)}, u32[]{:S(2)}, u32[]{:S(2)}) %collective-permute-start.10) | collective-permute-done | bytes 1048608 | tf_op jit(solution)/shard_map/ppermute | solution.py:41
  136.3 3.4 %collective-permute-done.11 = bf16[2,1024,256]{2,1,0:T(8,128)(2,1)} collective-permute-done((bf16[2,1024,256]{2,1,0:T(8,128)(2,1)}, bf16[2,1024,256]{2,1,0:T(8,128)(2,1)}, u32[]{:S(2)}, u32[]{:S(2)}) %collective-permute-start.11) | collective-permute-done | bytes 1048608 | tf_op jit(solution)/shard_map/ppermute | solution.py:41
  143.9 1.7 collective-permute-start.16
  146.2 4.4 %collective-permute-done.17 = bf16[64,1024]{1,0:T(8,128)(2,1)S(1)} collective-permute-done((bf16[64,1024]{1,0:T(8,128)(2,1)S(1)}, bf16[64,1024]{1,0:T(8,128)(2,1)S(1)}, u32[]{:S(2)}, u32[]{:S(2)}) %collective-permute-start.17) | collective-permute-done | bytes 131104 | tf_op jit(solution)/shard_map/ppermute | solution.py:41
  150.6 5.4 %collective-permute-done.15 = bf16[1024,256]{1,0:T(8,128)(2,1)S(1)} collective-permute-done((bf16[1024,256]{1,0:T(8,128)(2,1)S(1)}, bf16[1024,256]{1,0:T(8,128)(2,1)S(1)}, u32[]{:S(2)}, u32[]{:S(2)}) %collective-permute-start.15) | collective-permute-done | bytes 524320 | tf_op jit(solution)/shard_map/ppermute | solution.py:41
  156.0 1.5 collective-permute-done.16
  161.1 2.1 %collective-permute-start.18 = (bf16[512,256]{1,0:T(8,128)(2,1)S(1)}, bf16[512,256]{1,0:T(8,128)(2,1)S(1)}, u32[]{:S(2)}, u32[]{:S(2)}) collective-permute-start(bf16[512,256]{1,0:T(8,128)(2,1)S(1)} %pad_maximum_fusion.10), channel_id=1, source_target_pairs={{0,1},{1,17},{2,3},{3,19},{4,5},{5,21},{6,7},{7,23},{8,9},{9,25},{... | collective-permute-start | bytes 786440 | tf_op jit(solution)/shard_map/ppermute | solution.py:41
  163.2 3.0 %collective-permute-start.20 = (bf16[512,256]{1,0:T(8,128)(2,1)S(1)}, bf16[512,256]{1,0:T(8,128)(2,1)S(1)}, u32[]{:S(2)}, u32[]{:S(2)}) collective-permute-start(bf16[512,256]{1,0:T(8,128)(2,1)S(1)} %pad_maximum_fusion.12), channel_id=1, source_target_pairs={{0,17},{1,1},{2,19},{3,3},{4,21},{5,5},{6,23},{7,7},{8,25},{9,9},{... | collective-permute-start | bytes 786440 | tf_op jit(solution)/shard_map/ppermute | solution.py:41
  166.2 3.2 %collective-permute-start.21 = (bf16[512,256]{1,0:T(8,128)(2,1)S(1)}, bf16[512,256]{1,0:T(8,128)(2,1)S(1)}, u32[]{:S(2)}, u32[]{:S(2)}) collective-permute-start(bf16[512,256]{1,0:T(8,128)(2,1)S(1)} %pad_maximum_fusion.13), channel_id=1, source_target_pairs={{0,25},{1,9},{2,27},{3,11},{4,29},{5,13},{6,31},{7,15},{8,17},{9,1... | collective-permute-start | bytes 786440 | tf_op jit(solution)/shard_map/ppermute | solution.py:41
  169.4 3.4 %collective-permute-done.19 = bf16[512,256]{1,0:T(8,128)(2,1)S(1)} collective-permute-done((bf16[512,256]{1,0:T(8,128)(2,1)S(1)}, bf16[512,256]{1,0:T(8,128)(2,1)S(1)}, u32[]{:S(2)}, u32[]{:S(2)}) %collective-permute-start.19) | collective-permute-done | bytes 262176 | tf_op jit(solution)/shard_map/ppermute | solution.py:41
  172.7 2.2 %collective-permute-done.20 = bf16[512,256]{1,0:T(8,128)(2,1)S(1)} collective-permute-done((bf16[512,256]{1,0:T(8,128)(2,1)S(1)}, bf16[512,256]{1,0:T(8,128)(2,1)S(1)}, u32[]{:S(2)}, u32[]{:S(2)}) %collective-permute-start.20) | collective-permute-done | bytes 262176 | tf_op jit(solution)/shard_map/ppermute | solution.py:41
  174.9 6.2 %collective-permute-done.21 = bf16[512,256]{1,0:T(8,128)(2,1)S(1)} collective-permute-done((bf16[512,256]{1,0:T(8,128)(2,1)S(1)}, bf16[512,256]{1,0:T(8,128)(2,1)S(1)}, u32[]{:S(2)}, u32[]{:S(2)}) %collective-permute-start.21) | collective-permute-done | bytes 262176 | tf_op jit(solution)/shard_map/ppermute | solution.py:41
  181.3 3.5 %multiply_add_fusion = f32[512,1024]{1,0:T(8,128)} fusion(f32[512,1024]{1,0:T(8,128)} %param.5, bf16[512,256]{1,0:T(8,128)(2,1)S(1)} %get-tuple-element.191, bf16[512,256]{1,0:T(8,128)(2,1)S(1)} %get-tuple-element.192, bf16[512,256]{1,0:T(8,128)(2,1)S(1)} %get-tuple-element.193, bf16[512,256]{1,0:T(8,128)(2,1)S(1)} %get-tuple-element.190), kind=kLoop, calls=%fused_computation.3 | loop fusion | flops 5767168 | bytes 5242880 | tf_op jit(solution)/shard_map/add | solution.py:151
  (75 shorter events, 25.6 us)
Async XLA Ops:
  0.6 5.3 %copy-start = (bf16[512,1024]{1,0:T(8,128)(2,1)S(1)}, bf16[512,1024]{1,0:T(8,128)(2,1)}, u32[]{:S(2)}) copy-start(bf16[512,1024]{1,0:T(8,128)(2,1)} %param.4) | copy-start | bytes 3145732
  2.0 17.7 %copy-start.2 = (bf16[1024,256]{1,0:T(8,128)(2,1)}, bf16[1024,256]{1,0:T(8,128)(2,1)S(1)}, u32[]{:S(2)}) copy-start(bf16[1024,256]{1,0:T(8,128)(2,1)S(1)} %get-tuple-element.111) | copy-start | bytes 1572868
  2.0 17.7 %copy-start.4 = (bf16[1024,256]{1,0:T(8,128)(2,1)}, bf16[1024,256]{1,0:T(8,128)(2,1)S(1)}, u32[]{:S(2)}) copy-start(bf16[1024,256]{1,0:T(8,128)(2,1)S(1)} %get-tuple-element.109) | copy-start | bytes 1572868
  2.0 13.7 %collective-permute-start = (bf16[1024,256]{1,0:T(8,128)(2,1)S(1)}, bf16[1024,256]{1,0:T(8,128)(2,1)S(1)}, u32[]{:S(2)}, u32[]{:S(2)}) collective-permute-start(bf16[1024,256]{1,0:T(8,128)(2,1)S(1)} %get-tuple-element.109), channel_id=1, source_target_pairs={{0,16},{1,17},{2,18},{3,19},{4,20},{5,21},{6,22},{7,23},{8,24},{9,... | collective-permute-start | bytes 1572872 | tf_op jit(solution)/shard_map/ppermute | solution.py:41
  3.8 14.7 %collective-permute-start.1 = (bf16[1024,256]{1,0:T(8,128)(2,1)S(1)}, bf16[1024,256]{1,0:T(8,128)(2,1)}, u32[]{:S(2)}, u32[]{:S(2)}) collective-permute-start(bf16[1024,256]{1,0:T(8,128)(2,1)S(1)} %get-tuple-element.111), channel_id=1, source_target_pairs={{0,17},{1,16},{2,19},{3,18},{4,21},{5,20},{6,23},{7,22},{8,25},{9,... | collective-permute-start | bytes 1572872 | tf_op jit(solution)/shard_map/ppermute | solution.py:41
  21.1 25.0 %collective-permute-start.2 = (bf16[2048,256]{1,0:T(8,128)(2,1)S(1)}, bf16[2048,256]{1,0:T(8,128)(2,1)S(1)}, u32[]{:S(2)}, u32[]{:S(2)}) collective-permute-start(bf16[2048,256]{1,0:T(8,128)(2,1)S(1)} %pad_maximum_fusion.2), channel_id=1, source_target_pairs={{0,32},{1,33},{2,34},{3,35},{4,36},{5,37},{6,38},{7,39},{8,40},{9,... | collective-permute-start | bytes 3145736 | tf_op jit(solution)/shard_map/ppermute | solution.py:41
  22.7 23.4 %collective-permute-start.3 = (bf16[2048,256]{1,0:T(8,128)(2,1)S(1)}, bf16[2048,256]{1,0:T(8,128)(2,1)S(1)}, u32[]{:S(2)}, u32[]{:S(2)}) collective-permute-start(bf16[2048,256]{1,0:T(8,128)(2,1)S(1)} %pad_maximum_fusion.2), channel_id=1, source_target_pairs={{0,96},{1,97},{2,98},{3,99},{4,100},{5,101},{6,102},{7,103},{8,104... | collective-permute-start | bytes 3145736 | tf_op jit(solution)/shard_map/ppermute | solution.py:41
  24.4 23.1 %collective-permute-start.4 = (bf16[1024,512]{1,0:T(8,128)(2,1)S(1)}, bf16[1024,512]{1,0:T(8,128)(2,1)S(1)}, u32[]{:S(2)}, u32[]{:S(2)}) collective-permute-start(bf16[1024,512]{1,0:T(8,128)(2,1)S(1)} %get-tuple-element.100), channel_id=1, source_target_pairs={{0,16},{1,17},{2,18},{3,19},{4,20},{5,21},{6,22},{7,23},{8,24},{9,... | collective-permute-start | bytes 3145736 | tf_op jit(solution)/shard_map/ppermute | solution.py:41
  24.4 24.4 %collective-permute-start.5 = (bf16[1024,512]{1,0:T(8,128)(2,1)S(1)}, bf16[1024,512]{1,0:T(8,128)(2,1)S(1)}, u32[]{:S(2)}, u32[]{:S(2)}) collective-permute-start(bf16[1024,512]{1,0:T(8,128)(2,1)S(1)} %get-tuple-element.101), channel_id=1, source_target_pairs={{0,17},{1,16},{2,19},{3,18},{4,21},{5,20},{6,23},{7,22},{8,25},{9,... | collective-permute-start | bytes 3145736 | tf_op jit(solution)/shard_map/ppermute | solution.py:41
  26.7 22.1 %collective-permute-start.6 = (bf16[4,2,64,1024]{3,2,1,0:T(8,128)(2,1)S(1)}, bf16[4,2,64,1024]{3,2,1,0:T(8,128)(2,1)S(1)}, u32[]{:S(2)}, u32[]{:S(2)}) collective-permute-start(bf16[4,2,64,1024]{3,2,1,0:T(8,128)(2,1)S(1)} %fusion), channel_id=1, source_target_pairs={{0,8},{1,9},{2,10},{3,11},{4,12},{5,13},{6,14},{7,15},{8,0},{9,1},... | collective-permute-start | bytes 3145736 | tf_op jit(solution)/shard_map/ppermute | solution.py:41
  46.1 3.7 %copy-start.6 = (bf16[2048,256]{1,0:T(8,128)(2,1)}, bf16[2048,256]{1,0:T(8,128)(2,1)S(1)}, u32[]{:S(2)}) copy-start(bf16[2048,256]{1,0:T(8,128)(2,1)S(1)} %collective-permute-done.2) | copy-start | bytes 3145732
  46.1 3.7 %copy-start.7 = (bf16[2048,256]{1,0:T(8,128)(2,1)}, bf16[2048,256]{1,0:T(8,128)(2,1)S(1)}, u32[]{:S(2)}) copy-start(bf16[2048,256]{1,0:T(8,128)(2,1)S(1)} %collective-permute-done.3) | copy-start | bytes 3145732
  49.0 2.0 %copy-start.3 = (bf16[1024,256]{1,0:T(8,128)(2,1)S(1)}, bf16[1024,256]{1,0:T(8,128)(2,1)}, u32[]{:S(2)}) copy-start(bf16[1024,256]{1,0:T(8,128)(2,1)} %copy-done.2) | copy-start | bytes 1572868
  70.9 15.9 %collective-permute-start.9 = (bf16[2048,1024]{1,0:T(8,128)(2,1)}, bf16[2048,1024]{1,0:T(8,128)(2,1)}, u32[]{:S(2)}, u32[]{:S(2)}) collective-permute-start(bf16[2048,1024]{1,0:T(8,128)(2,1)} %maximum_maximum_fusion), channel_id=1, source_target_pairs={{0,8},{1,9},{2,10},{3,11},{4,12},{5,13},{6,14},{7,15},{8,0},{9,1},... | collective-permute-start | bytes 12582920 | tf_op jit(solution)/shard_map/ppermute | solution.py:41
  70.9 15.9 %collective-permute-start.7 = (bf16[1024,256]{1,0:T(8,128)(2,1)}, bf16[1024,256]{1,0:T(8,128)(2,1)}, u32[]{:S(2)}, u32[]{:S(2)}) collective-permute-start(bf16[1024,256]{1,0:T(8,128)(2,1)} %slice.60), channel_id=1, source_target_pairs={{0,32},{1,33},{2,34},{3,35},{4,36},{5,37},{6,38},{7,39},{8,40},{9,... | collective-permute-start | bytes 1572872 | tf_op jit(solution)/shard_map/ppermute | solution.py:41
  71.2 15.6 %collective-permute-start.8 = (bf16[1024,256]{1,0:T(8,128)(2,1)}, bf16[1024,256]{1,0:T(8,128)(2,1)}, u32[]{:S(2)}, u32[]{:S(2)}) collective-permute-start(bf16[1024,256]{1,0:T(8,128)(2,1)} %slice.61), channel_id=1, source_target_pairs={{0,96},{1,97},{2,98},{3,99},{4,100},{5,101},{6,102},{7,103},{8,104... | collective-permute-start | bytes 1572872 | tf_op jit(solution)/shard_map/ppermute | solution.py:41
  109.6 26.7 %collective-permute-start.10 = (bf16[2,1024,256]{2,1,0:T(8,128)(2,1)}, bf16[2,1024,256]{2,1,0:T(8,128)(2,1)}, u32[]{:S(2)}, u32[]{:S(2)}) collective-permute-start(bf16[2,1024,256]{2,1,0:T(8,128)(2,1)} %pad_maximum_fusion.5), channel_id=1, source_target_pairs={{0,6},{1,7},{2,0},{3,1},{4,2},{5,3},{6,4},{7,5},{8,14},{9,15},{10,... | collective-permute-start | bytes 3145736 | tf_op jit(solution)/shard_map/ppermute | solution.py:41
  113.7 26.0 %collective-permute-start.11 = (bf16[2,1024,256]{2,1,0:T(8,128)(2,1)}, bf16[2,1024,256]{2,1,0:T(8,128)(2,1)}, u32[]{:S(2)}, u32[]{:S(2)}) collective-permute-start(bf16[2,1024,256]{2,1,0:T(8,128)(2,1)} %pad_maximum_fusion.6), channel_id=1, source_target_pairs={{0,2},{1,3},{2,4},{3,5},{4,6},{5,7},{6,0},{7,1},{8,10},{9,11},{10,... | collective-permute-start | bytes 3145736 | tf_op jit(solution)/shard_map/ppermute | solution.py:41
  113.7 10.2 %collective-permute-start.12 = (bf16[2,64,1024]{2,1,0:T(8,128)(2,1)}, bf16[2,64,1024]{2,1,0:T(8,128)(2,1)}, u32[]{:S(2)}, u32[]{:S(2)}) collective-permute-start(bf16[2,64,1024]{2,1,0:T(8,128)(2,1)} %get-tuple-element.134), channel_id=1, source_target_pairs={{0,32},{1,33},{2,34},{3,35},{4,36},{5,37},{6,38},{7,39},{8,40},{9,... | collective-permute-start | bytes 786440 | tf_op jit(solution)/shard_map/ppermute | solution.py:41
  113.9 15.4 %collective-permute-start.13 = (bf16[2,64,1024]{2,1,0:T(8,128)(2,1)}, bf16[2,64,1024]{2,1,0:T(8,128)(2,1)}, u32[]{:S(2)}, u32[]{:S(2)}) collective-permute-start(bf16[2,64,1024]{2,1,0:T(8,128)(2,1)} %get-tuple-element.135), channel_id=1, source_target_pairs={{0,64},{1,65},{2,66},{3,67},{4,68},{5,69},{6,70},{7,71},{8,72},{9,... | collective-permute-start | bytes 786440 | tf_op jit(solution)/shard_map/ppermute | solution.py:41
  118.1 11.2 %collective-permute-start.14 = (bf16[2,64,1024]{2,1,0:T(8,128)(2,1)S(1)}, bf16[2,64,1024]{2,1,0:T(8,128)(2,1)}, u32[]{:S(2)}, u32[]{:S(2)}) collective-permute-start(bf16[2,64,1024]{2,1,0:T(8,128)(2,1)S(1)} %get-tuple-element.136), channel_id=1, source_target_pairs={{0,96},{1,97},{2,98},{3,99},{4,100},{5,101},{6,102},{7,103},{8,104... | collective-permute-start | bytes 786440 | tf_op jit(solution)/shard_map/ppermute | solution.py:41
  140.9 2.6 %copy-start.10 = (f32[2,64,1024]{2,1,0:T(8,128)}, f32[2,64,1024]{2,1,0:T(8,128)S(1)}, u32[]{:S(2)}) copy-start(f32[2,64,1024]{2,1,0:T(8,128)S(1)} %bitcast_add_fusion) | copy-start | bytes 1572868
  141.0 18.0 %copy-start.8 = (bf16[1024,256]{1,0:T(8,128)(2,1)S(1)}, bf16[1024,256]{1,0:T(8,128)(2,1)}, u32[]{:S(2)}) copy-start(bf16[1024,256]{1,0:T(8,128)(2,1)} %get-tuple-element.160) | copy-start | bytes 1572868
  143.6 12.4 %collective-permute-start.15 = (bf16[1024,256]{1,0:T(8,128)(2,1)S(1)}, bf16[1024,256]{1,0:T(8,128)(2,1)S(1)}, u32[]{:S(2)}, u32[]{:S(2)}) collective-permute-start(bf16[1024,256]{1,0:T(8,128)(2,1)S(1)} %fusion.6), channel_id=1, source_target_pairs={{0,6},{1,7},{2,0},{3,1},{4,2},{5,3},{6,4},{7,5},{8,14},{9,15},{10,... | collective-permute-start | bytes 1572872 | tf_op jit(solution)/shard_map/ppermute | solution.py:41
  143.9 13.6 %collective-permute-start.16 = (bf16[1024,256]{1,0:T(8,128)(2,1)S(1)}, bf16[1024,256]{1,0:T(8,128)(2,1)S(1)}, u32[]{:S(2)}, u32[]{:S(2)}) collective-permute-start(bf16[1024,256]{1,0:T(8,128)(2,1)S(1)} %fusion.5), channel_id=1, source_target_pairs={{0,2},{1,3},{2,4},{3,5},{4,6},{5,7},{6,0},{7,1},{8,10},{9,11},{10,... | collective-permute-start | bytes 1572872 | tf_op jit(solution)/shard_map/ppermute | solution.py:41
  145.7 5.0 %collective-permute-start.17 = (bf16[64,1024]{1,0:T(8,128)(2,1)S(1)}, bf16[64,1024]{1,0:T(8,128)(2,1)S(1)}, u32[]{:S(2)}, u32[]{:S(2)}) collective-permute-start(bf16[64,1024]{1,0:T(8,128)(2,1)S(1)} %fusion.8), channel_id=1, source_target_pairs={{0,16},{1,17},{2,18},{3,19},{4,20},{5,21},{6,22},{7,23},{8,24},{9,... | collective-permute-start | bytes 393224 | tf_op jit(solution)/shard_map/ppermute | solution.py:41
  146.2 14.2 %copy-start.11 = (f32[2,64,1024]{2,1,0:T(8,128)S(1)}, f32[2,64,1024]{2,1,0:T(8,128)}, u32[]{:S(2)}) copy-start(f32[2,64,1024]{2,1,0:T(8,128)} %copy-done.10) | copy-start | bytes 1572868
  161.1 8.3 %collective-permute-start.18 = (bf16[512,256]{1,0:T(8,128)(2,1)S(1)}, bf16[512,256]{1,0:T(8,128)(2,1)S(1)}, u32[]{:S(2)}, u32[]{:S(2)}) collective-permute-start(bf16[512,256]{1,0:T(8,128)(2,1)S(1)} %pad_maximum_fusion.10), channel_id=1, source_target_pairs={{0,1},{1,17},{2,3},{3,19},{4,5},{5,21},{6,7},{7,23},{8,9},{9,25},{... | collective-permute-start | bytes 786440 | tf_op jit(solution)/shard_map/ppermute | solution.py:41
  163.2 9.5 %collective-permute-start.19 = (bf16[512,256]{1,0:T(8,128)(2,1)S(1)}, bf16[512,256]{1,0:T(8,128)(2,1)S(1)}, u32[]{:S(2)}, u32[]{:S(2)}) collective-permute-start(bf16[512,256]{1,0:T(8,128)(2,1)S(1)} %pad_maximum_fusion.11), channel_id=1, source_target_pairs={{0,9},{1,25},{2,11},{3,27},{4,13},{5,29},{6,15},{7,31},{8,1},{9,17... | collective-permute-start | bytes 786440 | tf_op jit(solution)/shard_map/ppermute | solution.py:41
  163.2 11.7 %collective-permute-start.20 = (bf16[512,256]{1,0:T(8,128)(2,1)S(1)}, bf16[512,256]{1,0:T(8,128)(2,1)S(1)}, u32[]{:S(2)}, u32[]{:S(2)}) collective-permute-start(bf16[512,256]{1,0:T(8,128)(2,1)S(1)} %pad_maximum_fusion.12), channel_id=1, source_target_pairs={{0,17},{1,1},{2,19},{3,3},{4,21},{5,5},{6,23},{7,7},{8,25},{9,9},{... | collective-permute-start | bytes 786440 | tf_op jit(solution)/shard_map/ppermute | solution.py:41
  166.2 14.9 %collective-permute-start.21 = (bf16[512,256]{1,0:T(8,128)(2,1)S(1)}, bf16[512,256]{1,0:T(8,128)(2,1)S(1)}, u32[]{:S(2)}, u32[]{:S(2)}) collective-permute-start(bf16[512,256]{1,0:T(8,128)(2,1)S(1)} %pad_maximum_fusion.13), channel_id=1, source_target_pairs={{0,25},{1,9},{2,27},{3,11},{4,29},{5,13},{6,31},{7,15},{8,17},{9,1... | collective-permute-start | bytes 786440 | tf_op jit(solution)/shard_map/ppermute | solution.py:41
  181.1 3.7 %copy-start.1 = (bf16[512,1024]{1,0:T(8,128)(2,1)S(1)}, bf16[512,1024]{1,0:T(8,128)(2,1)}, u32[]{:S(2)}) copy-start(bf16[512,1024]{1,0:T(8,128)(2,1)} %param.4) | copy-start | bytes 3145732
  (2 other events, 2.8 us)

commit v3 on v2

v3 whole, which is shorter than its diff:
```python
import jax
import jax.numpy as jnp
from jax import lax
from jax.experimental import pallas as pl
from jax.experimental.pallas import tpu as pltpu
from jax.sharding import PartitionSpec as P

SIZES = (4, 2, 2, 4, 2)
AXES = ("feat", "batch")


def flat(place):
    index = 0
    for value, size in zip(place, SIZES):
        index = index * size + value % size
    return index


def table(move):
    pairs = []
    for x in range(4):
        for yl in range(2):
            for c in range(2):
                for z in range(4):
                    for yh in range(2):
                        pairs.append((flat((x, yl, c, z, yh)), flat(move(x, yl, c, z, yh))))
    return pairs


CORE = table(lambda x, yl, c, z, yh: (x, yl, 1 - c, z, yh))
NEAR = table(lambda x, yl, c, z, yh: (x, 1 - yl, c, z, yh))
FAR = table(lambda x, yl, c, z, yh: (x, 1 - yl, c, z, 1 - yh))
X_STEP = {d: table(lambda x, yl, c, z, yh, d=d: (x + d, yl, c, z, yh)) for d in (1, 2, 3)}
Z_STEP = {d: table(lambda x, yl, c, z, yh, d=d: (x, yl, c, z + d, yh)) for d in (1, 3)}
HOME = {
    (s, t): table(lambda x, yl, c, z, yh, s=s, t=t: (x, yh ^ s, c ^ t, z, 1 - yl))
    for s in range(2)
    for t in range(2)
}


def send(value, pairs):
    return lax.ppermute(value, AXES, pairs)


def pick(array, index):
    return lax.dynamic_index_in_dim(array, index, 0, keepdims=False)


def wide(value):
    return value.astype(jnp.float32)


def narrow(value):
    return value.astype(jnp.bfloat16)


def together(sends, held):
    values, held = lax.optimization_barrier(([value for value, _ in sends], held))
    results = [send(value, pairs) for value, (_, pairs) in zip(values, sends)]
    return lax.optimization_barrier((results, held))


def block_kernel(
    shift_ref,
    own, right, to_near, to_far,
    own_c, right_c, to_near_c, to_far_c,
    above, below, across_up, across_down,
    down, up, middle, home,
    left, columns_in, result, left_sem, column_sem, out_sem,
):
    shift = shift_ref[0]
    rights = []
    sources = ((right, 0), (above, 1), (below, 3), (across_up, 2), (across_down, 2))
    for n, (source, dx) in enumerate(sources):
        dz = (shift + dx) % 4
        target = columns_in.at[dz] if n < 3 else columns_in.at[dz, n - 3]
        rights.append(pltpu.make_async_copy(source, target, column_sem.at[n]))
    lefts = [
        pltpu.make_async_copy(source, left.at[n // 4, n % 4], left_sem.at[n])
        for n, source in enumerate(
            (own, right, to_near, to_far, own_c, right_c, to_near_c, to_far_c)
        )
    ]
    for copy in lefts[:4] + rights + lefts[4:]:
        copy.start()
    for copy in lefts[:4] + rights:
        copy.wait()
    rows = own.shape[1]

    def multiply(cc):
        pairs = (((0, 0), (2, 1)), ((0, 1), (3, 1)), ((1, 0), (1, 1)), ((2, 0), (3, 0)))

        def step(dz, carry):
            for g, pair in enumerate(pairs):
                total = None
                for i, (piece, half) in enumerate(pair):
                    term = lax.dot_general(
                        left[cc, piece, half],
                        columns_in[dz, i],
                        (((1,), (1,)), ((), ())),
                        preferred_element_type=jnp.float32,
                    )
                    total = term if total is None else total + term
                result[cc, dz, g * rows : (g + 1) * rows, :] = total.astype(jnp.bfloat16)
            return carry

        lax.fori_loop(0, 4, step, 0)

    outs = []
    for cc, targets in enumerate(((home, up, down, middle), (home, middle, up, down))):
        if cc:
            for copy in lefts[4:]:
                copy.wait()
        multiply(cc)
        for dz, target in enumerate(targets):
            copy = pltpu.make_async_copy(
                result.at[cc, dz], target.at[cc], out_sem.at[cc * 4 + dz]
            )
            copy.start()
            outs.append(copy)
    for copy in outs:
        copy.wait()


def block_product(shift, left, left_c, above, below, across_up, across_down):
    _, half, items = left[0].shape
    anywhere = pl.BlockSpec(memory_space=pl.ANY)
    message = jax.ShapeDtypeStruct((2, 4 * half, half), jnp.bfloat16)
    operands = (*left, *left_c, above, below, across_up, across_down)
    return pl.pallas_call(
        block_kernel,
        out_shape=[message] * 4,
        in_specs=[pl.BlockSpec(memory_space=pltpu.SMEM)] + [anywhere] * len(operands),
        out_specs=[anywhere] * 4,
        scratch_shapes=[
            pltpu.VMEM((2, 4, 2, half, items), jnp.bfloat16),
            pltpu.VMEM((4, 2, half, items), jnp.bfloat16),
            pltpu.VMEM((2, 4, 4 * half, half), jnp.bfloat16),
            pltpu.SemaphoreType.DMA((8,)),
            pltpu.SemaphoreType.DMA((5,)),
            pltpu.SemaphoreType.DMA((8,)),
        ],
        compiler_params=pltpu.CompilerParams(vmem_limit_bytes=24 * 1024 * 1024),
        cost_estimate=pl.CostEstimate(
            flops=2 * 8 * half * 4 * half * 2 * items,
            bytes_accessed=32 * half * items * 2 + 32 * half * half * 2,
            transcendentals=0,
        ),
    )(shift, *operands)


def on_device(embeddings, basis, cov_prior):
    feat, batch = lax.axis_index("feat"), lax.axis_index("batch")
    x, yl, c = feat // 4, feat // 2 % 2, feat % 2
    z, yh = batch // 2, batch % 2
    items, feats = embeddings.shape
    half = feats // 2
    items_total = items * lax.axis_size("batch")

    halves = embeddings.T.reshape(2, half, items)
    own = jnp.stack([pick(halves, yh), pick(halves, 1 - yh)])
    (near, far, own_c), own = together([(own[0], NEAR), (own[1], FAR), (own, CORE)], own)

    share = jnp.dot(embeddings, basis, preferred_element_type=jnp.float32)
    rows, width = share.shape[0] // 16, share.shape[1]
    share = jnp.moveaxis(share.reshape(4, 2, 2, rows, width), 2, 0)
    share_mine, share_sent = pick(share, c), narrow(pick(share, 1 - c))

    right = jnp.stack([near, far])
    (below, above, to_near, to_far, right_c), (right, own, own_c, share_mine) = together(
        [
            (right, X_STEP[1]),
            (right, X_STEP[3]),
            (jnp.stack([own[1], far]), NEAR),
            (jnp.stack([own[0], near]), FAR),
            (right, CORE),
        ],
        (right, own, own_c, share_mine),
    )
    (across_up, across_down, to_near_c, to_far_c, share_got), held = together(
        [
            (below[0], X_STEP[1]),
            (above[1], X_STEP[3]),
            (to_near, CORE),
            (to_far, CORE),
            (share_sent, CORE),
        ],
        (right, above, below, own, own_c, right_c, to_near, to_far, share_mine),
    )
    right, above, below, own, own_c, right_c, to_near, to_far, share_mine = held
    share = share_mine + wide(share_got)
    down, up, middle, home = block_product(
        ((x - z) % 4).astype(jnp.int32).reshape(1),
        (own, right, to_near, to_far),
        (own_c, right_c, to_near_c, to_far_c),
        above, below, across_up, across_down,
    )
    outgoing = narrow(share)
    (down, up, *shares), (middle, home, share) = together(
        [(down, Z_STEP[3]), (up, Z_STEP[1])]
        + [(pick(outgoing, (x + d) % 4), X_STEP[d]) for d in (1, 2, 3)],
        (middle, home, share),
    )
    share = pick(share, x) + sum(wide(s) for s in shares)
    (first, second, share_got), (home, up, down, share) = together(
        [
            (narrow(wide(down[0]) + wide(middle[0])), Z_STEP[3]),
            (narrow(wide(up[1]) + wide(middle[1])), Z_STEP[1]),
            (narrow(pick(share, 1 - yl)), NEAR),
        ],
        (home, up, down, share),
    )
    projected = narrow(pick(share, yl) + wide(share_got))
    whole = [
        narrow(wide(home[0]) + wide(up[0]) + wide(first)).reshape(2, 2, half, half),
        narrow(wide(home[1]) + wide(down[1]) + wide(second)).reshape(2, 2, half, half),
    ]
    homeward = []
    for s in range(2):
        for t in range(2):
            chosen = pick(whole[t], yl ^ yh ^ s)
            value = jnp.concatenate([pick(chosen, yh ^ i) for i in range(2)], 0)
            homeward.append((value, HOME[s, t]))
    arrived, projected = together(homeward, projected)
    arrived = jnp.stack(arrived)
    gram = jnp.concatenate(
        [pick(arrived, (q % 2 ^ yl) * 2 + (q // 2 ^ c)) for q in range(4)], 1
    )
    covariance = 0.9 * cov_prior + wide(gram) / items_total
    return (covariance, projected)


def solution(mesh):
    placed = (P("batch", "feat"), P("feat", None), P("feat", "batch"))
    return jax.shard_map(
        on_device,
        mesh=mesh,
        in_specs=placed,
        out_specs=(P("feat", "batch"), P(("batch", "feat"), None)),
        check_vma=False,
    )
```

time: 186 us -> 171 us (0.919)
  other arithmetic: 39 us -> 16.1 us
  matrix products: 16.9 us -> 2.47 us
  Pallas kernels: 0 us -> 14.3 us
  local copies, waits for them, and re-layouts: 7.64 us -> 17.3 us
    concatenate x3 -> x0, other arithmetic: 22.6 us -> none  [the longest x1 19.9 us: on_device(): group = jnp.concatenate(groups, 1)]
    dot_general x2 -> x0, matrix products: 14.4 us -> none  [on_device(): lax.dot_general(lhs, rhs, (((0,), (0,)), ((), ())), preferred_element_typ...]
    pallas_call x0 -> x1, Pallas kernels: none -> 14.3 us  [block_product(): pl.pallas_call(block_kernel, out_shape=[message] * 4, in_specs=[pl.BlockS...]
    unnamed x24, local copies, waits for them, and re-layouts: 0.85 us -> 6.94 us
    slice x6 -> x1, local copies, waits for them, and re-layouts: 3.68 us -> 0.07 us  [on_device(): own[0]]
    convert_element_type x2, local copies, waits for them, and re-layouts: 0.19 us -> 2.75 us  [narrow(): return value.astype(jnp.bfloat16)]
    convert_element_type x6 -> x4, other arithmetic: 6.02 us -> 8.56 us  [narrow(): return value.astype(jnp.bfloat16)]
    squeeze x0 -> x1, local copies, waits for them, and re-layouts: none -> 2.24 us  [on_device(): above[1]]
  transfers between devices with their start and end apart: 22 -> 25, of which waited for: 16 -> 16; matrix products, arithmetic and copies ran while one was open for 2% -> 4% of each run, Pallas kernels for 0% -> 0%
where the time goes in v3:
time: 171 us
  waiting for transfers between devices  86.9 us (51%)
  starting transfers between devices  32.6 us (19%)
  local copies, waits for them, and re-layouts  17.3 us (10%)
  other arithmetic  16.1 us (9%)
  Pallas kernels  14.3 us (8%)
  matrix products  2.47 us (1%)
    ppermute x25, waiting for transfers between devices, send(): return lax.ppermute(value, AXES, pairs)  86.9 us
    ppermute x25, starting transfers between devices, send(): return lax.ppermute(value, AXES, pairs)  32.6 us
    pallas_call x1, Pallas kernels, block_product(): pl.pallas_call(block_kernel, out_shape=[message] * 4, in_specs=[pl.BlockS...  14.3 us
    convert_element_type x4, other arithmetic, narrow(): return value.astype(jnp.bfloat16)  8.56 us
    unnamed x24, local copies, waits for them, and re-layouts  6.94 us
  transfers between devices with their start and end apart: 25, of which 16 were waited for; matrix products, arithmetic and copies ran while one was open for 4% of the time, Pallas kernels for 0%

profile of v3, /device:TPU:0, one launch (start us, length us, event | category | flops | bytes accessed | tf_op | source)
XLA Modules:
  0.0 170.5 jit_solution(12696032043579915805)
XLA Ops:
  4.7 1.7 %collective-permute-start = (bf16[256,1024]{1,0:T(8,128)(2,1)}, bf16[256,1024]{1,0:T(8,128)(2,1)}, u32[]{:S(2)}, u32[]{:S(2)}) collective-permute-start(bf16[256,1024]{1,0:T(8,128)(2,1)} %bitcast.3), channel_id=1, source_target_pairs={{0,16},{1,17},{2,18},{3,19},{4,20},{5,21},{6,22},{7,23},{8,24},{9,... | collective-permute-start | bytes 1572872 | tf_op jit(solution)/shard_map/ppermute | solution.py:43
  6.5 2.2 %collective-permute-start.1 = (bf16[256,1024]{1,0:T(8,128)(2,1)}, bf16[256,1024]{1,0:T(8,128)(2,1)}, u32[]{:S(2)}, u32[]{:S(2)}) collective-permute-start(bf16[256,1024]{1,0:T(8,128)(2,1)} %bitcast.4), channel_id=1, source_target_pairs={{0,17},{1,16},{2,19},{3,18},{4,21},{5,20},{6,23},{7,22},{8,25},{9,... | collective-permute-start | bytes 1572872 | tf_op jit(solution)/shard_map/ppermute | solution.py:43
  8.6 2.5 %fusion.9 = f32[1024,1024]{1,0:T(8,128)S(1)} fusion(bf16[1024,512]{1,0:T(8,128)(2,1)} %param.3, bf16[512,1024]{1,0:T(8,128)(2,1)S(1)} %copy-done), kind=kOutput, calls=%fused_computation.48 | convolution fusion | flops 1073741824 | bytes 6291456 | tf_op jit(solution)/shard_map/dot_general | solution.py:165
  13.8 5.6 %collective-permute-done = bf16[256,1024]{1,0:T(8,128)(2,1)} collective-permute-done((bf16[256,1024]{1,0:T(8,128)(2,1)}, bf16[256,1024]{1,0:T(8,128)(2,1)}, u32[]{:S(2)}, u32[]{:S(2)}) %collective-permute-start) | collective-permute-done | bytes 524320 | tf_op jit(solution)/shard_map/ppermute | solution.py:43
  19.4 2.6 %collective-permute-done.1 = bf16[256,1024]{1,0:T(8,128)(2,1)} collective-permute-done((bf16[256,1024]{1,0:T(8,128)(2,1)}, bf16[256,1024]{1,0:T(8,128)(2,1)}, u32[]{:S(2)}, u32[]{:S(2)}) %collective-permute-start.1) | collective-permute-done | bytes 524320 | tf_op jit(solution)/shard_map/ppermute | solution.py:43
  23.0 3.0 %pad_maximum_fusion.3 = (bf16[2,256,1024]{2,1,0:T(8,128)(2,1)}, bf16[2,256,1024]{2,1,0:T(8,128)(2,1)S(1)}, bf16[2,256,1024]{2,1,0:T(8,128)(2,1)}) fusion(bf16[1,256,1024]{2,1,0:T(8,128)(2,1)} %bitcast.5, bf16[1,256,1024]{2,1,0:T(8,128)(2,1)S(1)} %get-tuple-element.211, bf16[1,256,1024]{2,1,0:T(8,128)(2,1)} %bitcast.6, ...), kind=kLoop, calls=%fused_computation.8 | loop fusion | flops 1572864 | bytes 5242880 | tf_op jit(solution)/shard_map/stack | solution.py:176
  27.4 1.7 %collective-permute-start.4 = (bf16[2,256,1024]{2,1,0:T(8,128)(2,1)S(1)}, bf16[2,256,1024]{2,1,0:T(8,128)(2,1)}, u32[]{:S(2)}, u32[]{:S(2)}) collective-permute-start(bf16[2,256,1024]{2,1,0:T(8,128)(2,1)S(1)} %get-tuple-element.141.right), channel_id=1, source_target_pairs={{0,96},{1,97},{2,98},{3,99},{4,100},{5,101},{6,102},{7,103},{8,104... | collective-permute-start | bytes 3145736 | tf_op jit(solution)/shard_map/ppermute | solution.py:43
  29.2 2.3 %collective-permute-start.6 = (bf16[2,256,1024]{2,1,0:T(8,128)(2,1)}, bf16[2,256,1024]{2,1,0:T(8,128)(2,1)}, u32[]{:S(2)}, u32[]{:S(2)}) collective-permute-start(bf16[2,256,1024]{2,1,0:T(8,128)(2,1)} %get-tuple-element.111), channel_id=1, source_target_pairs={{0,17},{1,16},{2,19},{3,18},{4,21},{5,20},{6,23},{7,22},{8,25},{9,... | collective-permute-start | bytes 3145736 | tf_op jit(solution)/shard_map/ppermute | solution.py:43
  31.4 2.7 %fusion = bf16[4,2,64,1024]{3,2,1,0:T(8,128)(2,1)} fusion(f32[4,2,2,64,1024]{4,3,2,1,0:T(8,128)} %bitcast.76, s32[]{:T(128)S(6)} %select_n.125), kind=kLoop, calls=%fused_computation.6 | loop fusion | bytes 2097156 | tf_op jit(solution)/shard_map/convert_element_type | solution.py:55
  34.2 17.5 %collective-permute-done.3.below = bf16[2,256,1024]{2,1,0:T(8,128)(2,1)} collective-permute-done((bf16[2,256,1024]{2,1,0:T(8,128)(2,1)S(1)}, bf16[2,256,1024]{2,1,0:T(8,128)(2,1)}, u32[]{:S(2)}, u32[]{:S(2)}) %collective-permute-start.3) | collective-permute-done | bytes 1048608 | tf_op jit(solution)/shard_map/ppermute | solution.py:43
  51.6 1.7 collective-permute-done.5.to_near
  54.5 2.2 %slice_bitcast_fusion = (bf16[256,1024]{1,0:T(8,128)(2,1)}, bf16[256,1024]{1,0:T(8,128)(2,1)}) fusion(bf16[2,256,1024]{2,1,0:T(8,128)(2,1)} %collective-permute-done.4.above, bf16[2,256,1024]{2,1,0:T(8,128)(2,1)} %collective-permute-done.3.below), kind=kLoop, calls=%fused_computation.19 | loop fusion | bytes 2097152 | tf_op jit(solution)/shard_map/squeeze | solution.py:184
  57.6 3.0 %collective-permute-start.9 = (bf16[256,1024]{1,0:T(8,128)(2,1)}, bf16[256,1024]{1,0:T(8,128)(2,1)}, u32[]{:S(2)}, u32[]{:S(2)}) collective-permute-start(bf16[256,1024]{1,0:T(8,128)(2,1)} %get-tuple-element.127), channel_id=1, source_target_pairs={{0,96},{1,97},{2,98},{3,99},{4,100},{5,101},{6,102},{7,103},{8,104... | collective-permute-start | bytes 1572872 | tf_op jit(solution)/shard_map/ppermute | solution.py:43
  60.5 12.6 %collective-permute-done.8.across_up = bf16[256,1024]{1,0:T(8,128)(2,1)} collective-permute-done((bf16[256,1024]{1,0:T(8,128)(2,1)}, bf16[256,1024]{1,0:T(8,128)(2,1)}, u32[]{:S(2)}, u32[]{:S(2)}) %collective-permute-start.8) | collective-permute-done | bytes 524320 | tf_op jit(solution)/shard_map/ppermute | solution.py:43
  73.2 3.7 %fusion.7 = (bf16[4,2,64,1024]{3,2,1,0:T(8,128)(2,1)S(1)}, f32[4,2,64,1024]{3,2,1,0:T(8,128)}) fusion(f32[4,2,64,1024]{3,2,1,0:T(8,128)} %dynamic-slice_bitcast_fusion, bf16[4,2,64,1024]{3,2,1,0:T(8,128)(2,1)} %collective-permute-done.12), kind=kLoop, calls=%fused_computation.46 | loop fusion | flops 1572864 | bytes 6291456 | tf_op jit(solution)/shard_map/convert_element_type | solution.py:55
  77.8 14.3 %shard_map.50 = (bf16[2,1024,256]{2,1,0:T(8,128)(2,1)}, bf16[2,1024,256]{2,1,0:T(8,128)(2,1)}, bf16[2,1024,256]{2,1,0:T(8,128)(2,1)S(1)}, bf16[2,1024,256]{2,1,0:T(8,128)(2,1)S(1)}) custom-call(s32[1]{0:T(128)} %bitcast.shift_ref, bf16[2,256,1024]{2,1,0:T(8,128)(2,1)S(1)} %pad_maximum_fusion.2.own, bf16[2,256,1024]{2,1,0:T(8,128)(2,1)S(1)} %get-tuple-element.141.right, ...), custom_call_target="tpu_custom_call" | custom-call | flops 8589934592 | bytes 20971520 | tf_op jit(solution)/shard_map/pallas_call | solution.py:131
  94.1 4.0 %collective-permute-start.13 = (bf16[2,1024,256]{2,1,0:T(8,128)(2,1)}, bf16[2,1024,256]{2,1,0:T(8,128)(2,1)S(1)}, u32[]{:S(2)}, u32[]{:S(2)}) collective-permute-start(bf16[2,1024,256]{2,1,0:T(8,128)(2,1)} %get-tuple-element.158), channel_id=1, source_target_pairs={{0,6},{1,7},{2,0},{3,1},{4,2},{5,3},{6,4},{7,5},{8,14},{9,15},{10,... | collective-permute-start | bytes 3145736 | tf_op jit(solution)/shard_map/ppermute | solution.py:43
  98.4 4.1 %collective-permute-start.16 = (bf16[2,64,1024]{2,1,0:T(8,128)(2,1)}, bf16[2,64,1024]{2,1,0:T(8,128)(2,1)}, u32[]{:S(2)}, u32[]{:S(2)}) collective-permute-start(bf16[2,64,1024]{2,1,0:T(8,128)(2,1)} %get-tuple-element.161), channel_id=1, source_target_pairs={{0,64},{1,65},{2,66},{3,67},{4,68},{5,69},{6,70},{7,71},{8,72},{9,... | collective-permute-start | bytes 786440 | tf_op jit(solution)/shard_map/ppermute | solution.py:43
  102.5 5.8 %collective-permute-done.15 = bf16[2,64,1024]{2,1,0:T(8,128)(2,1)} collective-permute-done((bf16[2,64,1024]{2,1,0:T(8,128)(2,1)}, bf16[2,64,1024]{2,1,0:T(8,128)(2,1)}, u32[]{:S(2)}, u32[]{:S(2)}) %collective-permute-start.15) | collective-permute-done | bytes 262176 | tf_op jit(solution)/shard_map/ppermute | solution.py:43
  108.3 5.4 %collective-permute-done.16 = bf16[2,64,1024]{2,1,0:T(8,128)(2,1)} collective-permute-done((bf16[2,64,1024]{2,1,0:T(8,128)(2,1)}, bf16[2,64,1024]{2,1,0:T(8,128)(2,1)}, u32[]{:S(2)}, u32[]{:S(2)}) %collective-permute-start.16) | collective-permute-done | bytes 262176 | tf_op jit(solution)/shard_map/ppermute | solution.py:43
  113.8 7.0 %collective-permute-done.13 = bf16[2,1024,256]{2,1,0:T(8,128)(2,1)S(1)} collective-permute-done((bf16[2,1024,256]{2,1,0:T(8,128)(2,1)}, bf16[2,1024,256]{2,1,0:T(8,128)(2,1)S(1)}, u32[]{:S(2)}, u32[]{:S(2)}) %collective-permute-start.13) | collective-permute-done | bytes 1048608 | tf_op jit(solution)/shard_map/ppermute | solution.py:43
  120.7 3.4 %collective-permute-done.14 = bf16[2,1024,256]{2,1,0:T(8,128)(2,1)} collective-permute-done((bf16[2,1024,256]{2,1,0:T(8,128)(2,1)}, bf16[2,1024,256]{2,1,0:T(8,128)(2,1)}, u32[]{:S(2)}, u32[]{:S(2)}) %collective-permute-start.14) | collective-permute-done | bytes 1048608 | tf_op jit(solution)/shard_map/ppermute | solution.py:43
  126.4 2.5 %fusion.4 = (bf16[1024,256]{1,0:T(8,128)(2,1)}, bf16[1024,256]{1,0:T(8,128)(2,1)}) fusion(bf16[2,1024,256]{2,1,0:T(8,128)(2,1)S(1)} %copy-done.2, bf16[2,1024,256]{2,1,0:T(8,128)(2,1)} %collective-permute-done.14, bf16[2,1024,256]{2,1,0:T(8,128)(2,1)} %copy-done.11), kind=kLoop, calls=%fused_computation.17 | loop fusion | flops 2097152 | bytes 3145728 | tf_op jit(solution)/shard_map/convert_element_type | solution.py:55
  131.5 4.4 %collective-permute-done.20 = bf16[64,1024]{1,0:T(8,128)(2,1)S(1)} collective-permute-done((bf16[64,1024]{1,0:T(8,128)(2,1)S(1)}, bf16[64,1024]{1,0:T(8,128)(2,1)S(1)}, u32[]{:S(2)}, u32[]{:S(2)}) %collective-permute-start.20) | collective-permute-done | bytes 131104 | tf_op jit(solution)/shard_map/ppermute | solution.py:43
  135.9 5.6 %collective-permute-done.18 = bf16[1024,256]{1,0:T(8,128)(2,1)S(1)} collective-permute-done((bf16[1024,256]{1,0:T(8,128)(2,1)}, bf16[1024,256]{1,0:T(8,128)(2,1)S(1)}, u32[]{:S(2)}, u32[]{:S(2)}) %collective-permute-start.18) | collective-permute-done | bytes 524320 | tf_op jit(solution)/shard_map/ppermute | solution.py:43
  141.5 2.4 %collective-permute-done.19 = bf16[1024,256]{1,0:T(8,128)(2,1)S(1)} collective-permute-done((bf16[1024,256]{1,0:T(8,128)(2,1)}, bf16[1024,256]{1,0:T(8,128)(2,1)S(1)}, u32[]{:S(2)}, u32[]{:S(2)}) %collective-permute-start.19) | collective-permute-done | bytes 524320 | tf_op jit(solution)/shard_map/ppermute | solution.py:43
  147.2 2.2 %collective-permute-start.21 = (bf16[512,256]{1,0:T(8,128)(2,1)S(1)}, bf16[512,256]{1,0:T(8,128)(2,1)S(1)}, u32[]{:S(2)}, u32[]{:S(2)}) collective-permute-start(bf16[512,256]{1,0:T(8,128)(2,1)S(1)} %pad_maximum_fusion.5), channel_id=1, source_target_pairs={{0,1},{1,17},{2,3},{3,19},{4,5},{5,21},{6,7},{7,23},{8,9},{9,25},{... | collective-permute-start | bytes 786440 | tf_op jit(solution)/shard_map/ppermute | solution.py:43
  149.4 2.9 %collective-permute-start.23 = (bf16[512,256]{1,0:T(8,128)(2,1)S(1)}, bf16[512,256]{1,0:T(8,128)(2,1)S(1)}, u32[]{:S(2)}, u32[]{:S(2)}) collective-permute-start(bf16[512,256]{1,0:T(8,128)(2,1)S(1)} %pad_maximum_fusion.7), channel_id=1, source_target_pairs={{0,17},{1,1},{2,19},{3,3},{4,21},{5,5},{6,23},{7,7},{8,25},{9,9},{... | collective-permute-start | bytes 786440 | tf_op jit(solution)/shard_map/ppermute | solution.py:43
  152.3 3.2 %collective-permute-start.24 = (bf16[512,256]{1,0:T(8,128)(2,1)S(1)}, bf16[512,256]{1,0:T(8,128)(2,1)S(1)}, u32[]{:S(2)}, u32[]{:S(2)}) collective-permute-start(bf16[512,256]{1,0:T(8,128)(2,1)S(1)} %pad_maximum_fusion.8), channel_id=1, source_target_pairs={{0,25},{1,9},{2,27},{3,11},{4,29},{5,13},{6,31},{7,15},{8,17},{9,1... | collective-permute-start | bytes 786440 | tf_op jit(solution)/shard_map/ppermute | solution.py:43
  155.5 3.4 %collective-permute-done.22 = bf16[512,256]{1,0:T(8,128)(2,1)S(1)} collective-permute-done((bf16[512,256]{1,0:T(8,128)(2,1)S(1)}, bf16[512,256]{1,0:T(8,128)(2,1)S(1)}, u32[]{:S(2)}, u32[]{:S(2)}) %collective-permute-start.22) | collective-permute-done | bytes 262176 | tf_op jit(solution)/shard_map/ppermute | solution.py:43
  158.9 2.2 %collective-permute-done.23 = bf16[512,256]{1,0:T(8,128)(2,1)S(1)} collective-permute-done((bf16[512,256]{1,0:T(8,128)(2,1)S(1)}, bf16[512,256]{1,0:T(8,128)(2,1)S(1)}, u32[]{:S(2)}, u32[]{:S(2)}) %collective-permute-start.23) | collective-permute-done | bytes 262176 | tf_op jit(solution)/shard_map/ppermute | solution.py:43
  161.1 6.2 %collective-permute-done.24 = bf16[512,256]{1,0:T(8,128)(2,1)S(1)} collective-permute-done((bf16[512,256]{1,0:T(8,128)(2,1)S(1)}, bf16[512,256]{1,0:T(8,128)(2,1)S(1)}, u32[]{:S(2)}, u32[]{:S(2)}) %collective-permute-start.24) | collective-permute-done | bytes 262176 | tf_op jit(solution)/shard_map/ppermute | solution.py:43
  (68 shorter events, 25.6 us)
Async XLA Ops:
  0.6 8.0 %copy-start = (bf16[512,1024]{1,0:T(8,128)(2,1)S(1)}, bf16[512,1024]{1,0:T(8,128)(2,1)}, u32[]{:S(2)}) copy-start(bf16[512,1024]{1,0:T(8,128)(2,1)} %param.4) | copy-start | bytes 3145732
  4.6 17.3 %collective-permute-start.2 = (bf16[2,256,1024]{2,1,0:T(8,128)(2,1)S(1)}, bf16[2,256,1024]{2,1,0:T(8,128)(2,1)S(1)}, u32[]{:S(2)}, u32[]{:S(2)}) collective-permute-start(bf16[2,256,1024]{2,1,0:T(8,128)(2,1)S(1)} %pad_maximum_fusion.2.own), channel_id=1, source_target_pairs={{0,8},{1,9},{2,10},{3,11},{4,12},{5,13},{6,14},{7,15},{8,0},{9,1},... | collective-permute-start | bytes 3145736 | tf_op jit(solution)/shard_map/ppermute | solution.py:43
  4.7 14.7 %collective-permute-start = (bf16[256,1024]{1,0:T(8,128)(2,1)}, bf16[256,1024]{1,0:T(8,128)(2,1)}, u32[]{:S(2)}, u32[]{:S(2)}) collective-permute-start(bf16[256,1024]{1,0:T(8,128)(2,1)} %bitcast.3), channel_id=1, source_target_pairs={{0,16},{1,17},{2,18},{3,19},{4,20},{5,21},{6,22},{7,23},{8,24},{9,... | collective-permute-start | bytes 1572872 | tf_op jit(solution)/shard_map/ppermute | solution.py:43
  6.5 15.5 %collective-permute-start.1 = (bf16[256,1024]{1,0:T(8,128)(2,1)}, bf16[256,1024]{1,0:T(8,128)(2,1)}, u32[]{:S(2)}, u32[]{:S(2)}) collective-permute-start(bf16[256,1024]{1,0:T(8,128)(2,1)} %bitcast.4), channel_id=1, source_target_pairs={{0,17},{1,16},{2,19},{3,18},{4,21},{5,20},{6,23},{7,22},{8,25},{9,... | collective-permute-start | bytes 1572872 | tf_op jit(solution)/shard_map/ppermute | solution.py:43
  11.1 2.7 %copy-start.7 = (f32[1024,1024]{1,0:T(8,128)}, f32[1024,1024]{1,0:T(8,128)S(1)}, u32[]{:S(2)}) copy-start(f32[1024,1024]{1,0:T(8,128)S(1)} %fusion.9) | copy-start | bytes 12582916
  25.9 25.7 %collective-permute-start.3 = (bf16[2,256,1024]{2,1,0:T(8,128)(2,1)S(1)}, bf16[2,256,1024]{2,1,0:T(8,128)(2,1)}, u32[]{:S(2)}, u32[]{:S(2)}) collective-permute-start(bf16[2,256,1024]{2,1,0:T(8,128)(2,1)S(1)} %get-tuple-element.141.right), channel_id=1, source_target_pairs={{0,32},{1,33},{2,34},{3,35},{4,36},{5,37},{6,38},{7,39},{8,40},{9,... | collective-permute-start | bytes 3145736 | tf_op jit(solution)/shard_map/ppermute | solution.py:43
  27.4 24.2 %collective-permute-start.4 = (bf16[2,256,1024]{2,1,0:T(8,128)(2,1)S(1)}, bf16[2,256,1024]{2,1,0:T(8,128)(2,1)}, u32[]{:S(2)}, u32[]{:S(2)}) collective-permute-start(bf16[2,256,1024]{2,1,0:T(8,128)(2,1)S(1)} %get-tuple-element.141.right), channel_id=1, source_target_pairs={{0,96},{1,97},{2,98},{3,99},{4,100},{5,101},{6,102},{7,103},{8,104... | collective-permute-start | bytes 3145736 | tf_op jit(solution)/shard_map/ppermute | solution.py:43
  29.2 24.1 %collective-permute-start.5 = (bf16[2,256,1024]{2,1,0:T(8,128)(2,1)}, bf16[2,256,1024]{2,1,0:T(8,128)(2,1)}, u32[]{:S(2)}, u32[]{:S(2)}) collective-permute-start(bf16[2,256,1024]{2,1,0:T(8,128)(2,1)} %get-tuple-element.110), channel_id=1, source_target_pairs={{0,16},{1,17},{2,18},{3,19},{4,20},{5,21},{6,22},{7,23},{8,24},{9,... | collective-permute-start | bytes 3145736 | tf_op jit(solution)/shard_map/ppermute | solution.py:43
  29.2 25.4 %collective-permute-start.6 = (bf16[2,256,1024]{2,1,0:T(8,128)(2,1)}, bf16[2,256,1024]{2,1,0:T(8,128)(2,1)}, u32[]{:S(2)}, u32[]{:S(2)}) collective-permute-start(bf16[2,256,1024]{2,1,0:T(8,128)(2,1)} %get-tuple-element.111), channel_id=1, source_target_pairs={{0,17},{1,16},{2,19},{3,18},{4,21},{5,20},{6,23},{7,22},{8,25},{9,... | collective-permute-start | bytes 3145736 | tf_op jit(solution)/shard_map/ppermute | solution.py:43
  31.4 23.1 %collective-permute-start.7 = (bf16[2,256,1024]{2,1,0:T(8,128)(2,1)S(1)}, bf16[2,256,1024]{2,1,0:T(8,128)(2,1)}, u32[]{:S(2)}, u32[]{:S(2)}) collective-permute-start(bf16[2,256,1024]{2,1,0:T(8,128)(2,1)S(1)} %get-tuple-element.141.right), channel_id=1, source_target_pairs={{0,8},{1,9},{2,10},{3,11},{4,12},{5,13},{6,14},{7,15},{8,0},{9,1},... | collective-permute-start | bytes 3145736 | tf_op jit(solution)/shard_map/ppermute | solution.py:43
  56.8 16.4 %collective-permute-start.10 = (bf16[2,256,1024]{2,1,0:T(8,128)(2,1)}, bf16[2,256,1024]{2,1,0:T(8,128)(2,1)}, u32[]{:S(2)}, u32[]{:S(2)}) collective-permute-start(bf16[2,256,1024]{2,1,0:T(8,128)(2,1)} %collective-permute-done.5.to_near), channel_id=1, source_target_pairs={{0,8},{1,9},{2,10},{3,11},{4,12},{5,13},{6,14},{7,15},{8,0},{9,1},... | collective-permute-start | bytes 3145736 | tf_op jit(solution)/shard_map/ppermute | solution.py:43
  56.8 16.4 %collective-permute-start.11 = (bf16[2,256,1024]{2,1,0:T(8,128)(2,1)}, bf16[2,256,1024]{2,1,0:T(8,128)(2,1)}, u32[]{:S(2)}, u32[]{:S(2)}) collective-permute-start(bf16[2,256,1024]{2,1,0:T(8,128)(2,1)} %collective-permute-done.6.to_far), channel_id=1, source_target_pairs={{0,8},{1,9},{2,10},{3,11},{4,12},{5,13},{6,14},{7,15},{8,0},{9,1},... | collective-permute-start | bytes 3145736 | tf_op jit(solution)/shard_map/ppermute | solution.py:43
  57.3 15.9 %collective-permute-start.12 = (bf16[4,2,64,1024]{3,2,1,0:T(8,128)(2,1)}, bf16[4,2,64,1024]{3,2,1,0:T(8,128)(2,1)}, u32[]{:S(2)}, u32[]{:S(2)}) collective-permute-start(bf16[4,2,64,1024]{3,2,1,0:T(8,128)(2,1)} %fusion), channel_id=1, source_target_pairs={{0,8},{1,9},{2,10},{3,11},{4,12},{5,13},{6,14},{7,15},{8,0},{9,1},... | collective-permute-start | bytes 3145736 | tf_op jit(solution)/shard_map/ppermute | solution.py:43
  57.3 15.9 %collective-permute-start.8 = (bf16[256,1024]{1,0:T(8,128)(2,1)}, bf16[256,1024]{1,0:T(8,128)(2,1)}, u32[]{:S(2)}, u32[]{:S(2)}) collective-permute-start(bf16[256,1024]{1,0:T(8,128)(2,1)} %get-tuple-element.126), channel_id=1, source_target_pairs={{0,32},{1,33},{2,34},{3,35},{4,36},{5,37},{6,38},{7,39},{8,40},{9,... | collective-permute-start | bytes 1572872 | tf_op jit(solution)/shard_map/ppermute | solution.py:43
  57.6 15.6 %collective-permute-start.9 = (bf16[256,1024]{1,0:T(8,128)(2,1)}, bf16[256,1024]{1,0:T(8,128)(2,1)}, u32[]{:S(2)}, u32[]{:S(2)}) collective-permute-start(bf16[256,1024]{1,0:T(8,128)(2,1)} %get-tuple-element.127), channel_id=1, source_target_pairs={{0,96},{1,97},{2,98},{3,99},{4,100},{5,101},{6,102},{7,103},{8,104... | collective-permute-start | bytes 1572872 | tf_op jit(solution)/shard_map/ppermute | solution.py:43
  60.5 17.2 %copy-start.6 = (bf16[2,256,1024]{2,1,0:T(8,128)(2,1)S(1)}, bf16[2,256,1024]{2,1,0:T(8,128)(2,1)}, u32[]{:S(2)}) copy-start(bf16[2,256,1024]{2,1,0:T(8,128)(2,1)} %copy-done.5) | copy-start | bytes 3145732
  94.1 32.3 %copy-start.2 = (bf16[2,1024,256]{2,1,0:T(8,128)(2,1)S(1)}, bf16[2,1024,256]{2,1,0:T(8,128)(2,1)}, u32[]{:S(2)}) copy-start(bf16[2,1024,256]{2,1,0:T(8,128)(2,1)} %copy-done.1) | copy-start | bytes 3145732
  94.1 26.7 %collective-permute-start.13 = (bf16[2,1024,256]{2,1,0:T(8,128)(2,1)}, bf16[2,1024,256]{2,1,0:T(8,128)(2,1)S(1)}, u32[]{:S(2)}, u32[]{:S(2)}) collective-permute-start(bf16[2,1024,256]{2,1,0:T(8,128)(2,1)} %get-tuple-element.158), channel_id=1, source_target_pairs={{0,6},{1,7},{2,0},{3,1},{4,2},{5,3},{6,4},{7,5},{8,14},{9,15},{10,... | collective-permute-start | bytes 3145736 | tf_op jit(solution)/shard_map/ppermute | solution.py:43
  98.1 26.0 %collective-permute-start.14 = (bf16[2,1024,256]{2,1,0:T(8,128)(2,1)}, bf16[2,1024,256]{2,1,0:T(8,128)(2,1)}, u32[]{:S(2)}, u32[]{:S(2)}) collective-permute-start(bf16[2,1024,256]{2,1,0:T(8,128)(2,1)} %get-tuple-element.159), channel_id=1, source_target_pairs={{0,2},{1,3},{2,4},{3,5},{4,6},{5,7},{6,0},{7,1},{8,10},{9,11},{10,... | collective-permute-start | bytes 3145736 | tf_op jit(solution)/shard_map/ppermute | solution.py:43
  98.1 10.2 %collective-permute-start.15 = (bf16[2,64,1024]{2,1,0:T(8,128)(2,1)}, bf16[2,64,1024]{2,1,0:T(8,128)(2,1)}, u32[]{:S(2)}, u32[]{:S(2)}) collective-permute-start(bf16[2,64,1024]{2,1,0:T(8,128)(2,1)} %get-tuple-element.160), channel_id=1, source_target_pairs={{0,32},{1,33},{2,34},{3,35},{4,36},{5,37},{6,38},{7,39},{8,40},{9,... | collective-permute-start | bytes 786440 | tf_op jit(solution)/shard_map/ppermute | solution.py:43
  98.4 15.4 %collective-permute-start.16 = (bf16[2,64,1024]{2,1,0:T(8,128)(2,1)}, bf16[2,64,1024]{2,1,0:T(8,128)(2,1)}, u32[]{:S(2)}, u32[]{:S(2)}) collective-permute-start(bf16[2,64,1024]{2,1,0:T(8,128)(2,1)} %get-tuple-element.161), channel_id=1, source_target_pairs={{0,64},{1,65},{2,66},{3,67},{4,68},{5,69},{6,70},{7,71},{8,72},{9,... | collective-permute-start | bytes 786440 | tf_op jit(solution)/shard_map/ppermute | solution.py:43
  102.5 11.2 %collective-permute-start.17 = (bf16[2,64,1024]{2,1,0:T(8,128)(2,1)S(1)}, bf16[2,64,1024]{2,1,0:T(8,128)(2,1)}, u32[]{:S(2)}, u32[]{:S(2)}) collective-permute-start(bf16[2,64,1024]{2,1,0:T(8,128)(2,1)S(1)} %get-tuple-element.162), channel_id=1, source_target_pairs={{0,96},{1,97},{2,98},{3,99},{4,100},{5,101},{6,102},{7,103},{8,104... | collective-permute-start | bytes 786440 | tf_op jit(solution)/shard_map/ppermute | solution.py:43
  120.7 3.4 %copy-start.11 = (bf16[2,1024,256]{2,1,0:T(8,128)(2,1)}, bf16[2,1024,256]{2,1,0:T(8,128)(2,1)S(1)}, u32[]{:S(2)}) copy-start(bf16[2,1024,256]{2,1,0:T(8,128)(2,1)S(1)} %collective-permute-done.13) | copy-start | bytes 3145732
  126.4 17.5 %copy-start.4 = (bf16[2,1024,256]{2,1,0:T(8,128)(2,1)S(1)}, bf16[2,1024,256]{2,1,0:T(8,128)(2,1)}, u32[]{:S(2)}) copy-start(bf16[2,1024,256]{2,1,0:T(8,128)(2,1)} %copy-done.3) | copy-start | bytes 3145732
  128.9 12.6 %collective-permute-start.18 = (bf16[1024,256]{1,0:T(8,128)(2,1)}, bf16[1024,256]{1,0:T(8,128)(2,1)S(1)}, u32[]{:S(2)}, u32[]{:S(2)}) collective-permute-start(bf16[1024,256]{1,0:T(8,128)(2,1)} %get-tuple-element.174), channel_id=1, source_target_pairs={{0,6},{1,7},{2,0},{3,1},{4,2},{5,3},{6,4},{7,5},{8,14},{9,15},{10,... | collective-permute-start | bytes 1572872 | tf_op jit(solution)/shard_map/ppermute | solution.py:43
  130.1 13.8 %collective-permute-start.19 = (bf16[1024,256]{1,0:T(8,128)(2,1)}, bf16[1024,256]{1,0:T(8,128)(2,1)S(1)}, u32[]{:S(2)}, u32[]{:S(2)}) collective-permute-start(bf16[1024,256]{1,0:T(8,128)(2,1)} %get-tuple-element.175), channel_id=1, source_target_pairs={{0,2},{1,3},{2,4},{3,5},{4,6},{5,7},{6,0},{7,1},{8,10},{9,11},{10,... | collective-permute-start | bytes 1572872 | tf_op jit(solution)/shard_map/ppermute | solution.py:43
  131.0 5.0 %collective-permute-start.20 = (bf16[64,1024]{1,0:T(8,128)(2,1)S(1)}, bf16[64,1024]{1,0:T(8,128)(2,1)S(1)}, u32[]{:S(2)}, u32[]{:S(2)}) collective-permute-start(bf16[64,1024]{1,0:T(8,128)(2,1)S(1)} %fusion.6), channel_id=1, source_target_pairs={{0,16},{1,17},{2,18},{3,19},{4,20},{5,21},{6,22},{7,23},{8,24},{9,... | collective-permute-start | bytes 393224 | tf_op jit(solution)/shard_map/ppermute | solution.py:43
  147.2 8.3 %collective-permute-start.21 = (bf16[512,256]{1,0:T(8,128)(2,1)S(1)}, bf16[512,256]{1,0:T(8,128)(2,1)S(1)}, u32[]{:S(2)}, u32[]{:S(2)}) collective-permute-start(bf16[512,256]{1,0:T(8,128)(2,1)S(1)} %pad_maximum_fusion.5), channel_id=1, source_target_pairs={{0,1},{1,17},{2,3},{3,19},{4,5},{5,21},{6,7},{7,23},{8,9},{9,25},{... | collective-permute-start | bytes 786440 | tf_op jit(solution)/shard_map/ppermute | solution.py:43
  149.4 9.5 %collective-permute-start.22 = (bf16[512,256]{1,0:T(8,128)(2,1)S(1)}, bf16[512,256]{1,0:T(8,128)(2,1)S(1)}, u32[]{:S(2)}, u32[]{:S(2)}) collective-permute-start(bf16[512,256]{1,0:T(8,128)(2,1)S(1)} %pad_maximum_fusion.6), channel_id=1, source_target_pairs={{0,9},{1,25},{2,11},{3,27},{4,13},{5,29},{6,15},{7,31},{8,1},{9,17... | collective-permute-start | bytes 786440 | tf_op jit(solution)/shard_map/ppermute | solution.py:43
  149.4 11.7 %collective-permute-start.23 = (bf16[512,256]{1,0:T(8,128)(2,1)S(1)}, bf16[512,256]{1,0:T(8,128)(2,1)S(1)}, u32[]{:S(2)}, u32[]{:S(2)}) collective-permute-start(bf16[512,256]{1,0:T(8,128)(2,1)S(1)} %pad_maximum_fusion.7), channel_id=1, source_target_pairs={{0,17},{1,1},{2,19},{3,3},{4,21},{5,5},{6,23},{7,7},{8,25},{9,9},{... | collective-permute-start | bytes 786440 | tf_op jit(solution)/shard_map/ppermute | solution.py:43
  152.3 14.9 %collective-permute-start.24 = (bf16[512,256]{1,0:T(8,128)(2,1)S(1)}, bf16[512,256]{1,0:T(8,128)(2,1)S(1)}, u32[]{:S(2)}, u32[]{:S(2)}) collective-permute-start(bf16[512,256]{1,0:T(8,128)(2,1)S(1)} %pad_maximum_fusion.8), channel_id=1, source_target_pairs={{0,25},{1,9},{2,27},{3,11},{4,29},{5,13},{6,31},{7,15},{8,17},{9,1... | collective-permute-start | bytes 786440 | tf_op jit(solution)/shard_map/ppermute | solution.py:43
  167.3 1.6 copy-start.8
  (5 other events, 4.8 us)

commit v4 on v2

v4 whole, which is shorter than its diff:
```python
import functools

import jax
import jax.numpy as jnp
from jax import lax
from jax.experimental import pallas as pl
from jax.experimental.pallas import tpu as pltpu
from jax.sharding import PartitionSpec as P

SIZES = (4, 2, 2, 4, 2)
AXES = ("feat", "batch")


def flat(place):
    index = 0
    for value, size in zip(place, SIZES):
        index = index * size + value % size
    return index


def table(move):
    pairs = []
    for x in range(4):
        for yl in range(2):
            for c in range(2):
                for z in range(4):
                    for yh in range(2):
                        pairs.append((flat((x, yl, c, z, yh)), flat(move(x, yl, c, z, yh))))
    return pairs


CORE = table(lambda x, yl, c, z, yh: (x, yl, 1 - c, z, yh))
NEAR = table(lambda x, yl, c, z, yh: (x, 1 - yl, c, z, yh))
FAR = table(lambda x, yl, c, z, yh: (x, 1 - yl, c, z, 1 - yh))
X_STEP = {d: table(lambda x, yl, c, z, yh, d=d: (x + d, yl, c, z, yh)) for d in (1, 2, 3)}
Z_STEP = {d: table(lambda x, yl, c, z, yh, d=d: (x, yl, c, z + d, yh)) for d in (1, 3)}
HOME = {
    (s, t): table(lambda x, yl, c, z, yh, s=s, t=t: (x, yh ^ s, c ^ t, z, 1 - yl))
    for s in range(2)
    for t in range(2)
}


def send(value, pairs):
    return lax.ppermute(value, AXES, pairs)


def pick(array, index):
    return lax.dynamic_index_in_dim(array, index, 0, keepdims=False)


def wide(value):
    return value.astype(jnp.float32)


def narrow(value):
    return value.astype(jnp.bfloat16)


def together(sends, after=()):
    values, _ = lax.optimization_barrier(([value for value, _ in sends], after))
    results = [send(value, pairs) for value, (_, pairs) in zip(values, sends)]
    return lax.optimization_barrier(results)


def block_kernel(plan, sides, offsets, *refs):
    place, refs = refs[0], refs[1:]
    n_in = plan["inputs"]
    inputs, refs = refs[:n_in], refs[n_in + plan["kept"] :]
    targets, refs = refs[: plan["targets"]], refs[plan["targets"] :]
    left, columns_in, result, left_sem, column_sem, out_sem = refs
    shift, high = place[0], place[1]

    def view(name):
        index, part = name
        if part is None:
            return inputs[index]
        return inputs[index].at[part if isinstance(part, int) else (high ^ int(part))]

    rights = [
        pltpu.make_async_copy(view(name), columns_in.at[n, i], column_sem.at[2 * n + i])
        for n, names in enumerate(plan["blocks"])
        for i, name in enumerate(names)
    ]
    lefts = [
        pltpu.make_async_copy(view(name), left.at[k, i], left_sem.at[2 * k + i])
        for k, names in enumerate(sides)
        for i, name in enumerate(names)
    ]
    for copy in rights[:2] + lefts[:2] + rights[2:] + lefts[2:]:
        copy.start()
    for copy in rights:
        copy.wait()
    rows = columns_in.shape[2]
    outs = []
    for k in range(len(sides)):
        for copy in lefts[2 * k : 2 * k + 2]:
            copy.wait()
        side, group = divmod(k, 4)
        for n in range(len(offsets)):
            total = None
            for i in range(2):
                term = lax.dot_general(
                    left[k, i],
                    columns_in[n, i],
                    (((1,), (1,)), ((), ())),
                    preferred_element_type=jnp.float32,
                )
                total = term if total is None else total + term
            result[side, n, group * rows : (group + 1) * rows, :] = total.astype(jnp.bfloat16)
        if group == 3:
            for n, dx in enumerate(offsets):
                dz = (shift + dx) % 4
                for d in range(4):
                    copy = pltpu.make_async_copy(
                        result.at[side, n],
                        targets[side * 4 + d],
                        out_sem.at[side * len(offsets) + n],
                    )
                    outs.append((dz == d, copy))
                    pl.when(dz == d)(copy.start)
    for here, copy in outs:
        pl.when(here)(copy.wait)


def block_product(place, sides, blocks, kept=()):
    inputs = []

    def enter(piece):
        array, part = piece if isinstance(piece, tuple) else (piece, None)
        for index, known in enumerate(inputs):
            if known is array:
                return index, part
        inputs.append(array)
        return len(inputs) - 1, part

    groups = [[enter(piece) for piece in pair] for side in sides for pair in side]
    names = [[enter(piece) for piece in pair] for pair in blocks.values()]
    half, items = inputs[0].shape[-2:]
    n_targets = 4 * len(sides)
    plan = {"inputs": len(inputs), "kept": len(kept), "targets": n_targets, "blocks": names}
    anywhere = pl.BlockSpec(memory_space=pl.ANY)
    n_blocks = len(blocks)
    return pl.pallas_call(
        functools.partial(block_kernel, plan, groups, tuple(blocks)),
        out_shape=[jax.ShapeDtypeStruct((4 * half, half), jnp.bfloat16)] * n_targets,
        in_specs=[pl.BlockSpec(memory_space=pltpu.SMEM)]
        + [anywhere] * (len(inputs) + len(kept)),
        out_specs=[anywhere] * n_targets,
        input_output_aliases={1 + len(inputs) + n: n for n in range(len(kept))},
        scratch_shapes=[
            pltpu.VMEM((len(groups), 2, half, items), jnp.bfloat16),
            pltpu.VMEM((n_blocks, 2, half, items), jnp.bfloat16),
            pltpu.VMEM((len(sides), n_blocks, 4 * half, half), jnp.bfloat16),
            pltpu.SemaphoreType.DMA((2 * len(groups),)),
            pltpu.SemaphoreType.DMA((2 * n_blocks,)),
            pltpu.SemaphoreType.DMA((len(sides) * n_blocks,)),
        ],
        compiler_params=pltpu.CompilerParams(vmem_limit_bytes=20 * 1024 * 1024),
        cost_estimate=pl.CostEstimate(
            flops=2 * len(sides) * 4 * half * n_blocks * half * 2 * items,
            bytes_accessed=(len(groups) + n_blocks) * 4 * half * items,
            transcendentals=0,
        ),
    )(place, *inputs, *kept)


def on_device(embeddings, basis, cov_prior):
    feat, batch = lax.axis_index("feat"), lax.axis_index("batch")
    x, yl, c = feat // 4, feat // 2 % 2, feat % 2
    z, yh = batch // 2, batch % 2
    items, feats = embeddings.shape
    half = feats // 2
    items_total = items * lax.axis_size("batch")
    place = jnp.stack([(x - z) % 4, yh]).astype(jnp.int32)

    whole = embeddings.T.reshape(2, half, items)
    inner, outer = pick(whole, yh), pick(whole, 1 - yh)
    near, far = together([(inner, NEAR), (outer, FAR)])
    right = jnp.stack([near, far])

    below_n, above_f, near1, far1, whole_c = together(
        [(near, X_STEP[1]), (far, X_STEP[3]), (outer, NEAR), (inner, FAR), (whole, CORE)]
    )
    share = jnp.dot(embeddings, basis, preferred_element_type=jnp.float32)
    rows, width = share.shape[0] // 16, share.shape[1]
    share = jnp.moveaxis(share.reshape(4, 2, 2, rows, width), 2, 0)
    share_sent = narrow(pick(share, 1 - c))
    rim = jnp.stack([near1, far1])

    below_f, above_n, two0, two1, right_c = together(
        [(far, X_STEP[1]), (near, X_STEP[3]), (far, NEAR), (near, FAR), (right, CORE)],
        (below_n, above_f),
    )
    two = jnp.stack([two0, two1])
    rim_c, two_c = together([(rim, CORE), (two, CORE)], (below_f, above_n))
    across = together([(below_n, X_STEP[1]), (above_f, X_STEP[3])], (below_f, above_n))
    (share_got,) = together([(share_sent, CORE)], (below_f, above_n))
    side = (
        ((whole, "0"), two0),
        ((whole, "1"), two1),
        (near, far),
        (near1, far1),
    )
    side_c = (
        ((whole_c, "0"), (two_c, 0)),
        ((whole_c, "1"), (two_c, 1)),
        ((right_c, 0), (right_c, 1)),
        ((rim_c, 0), (rim_c, 1)),
    )
    early = {0: (near, far), 1: (above_n, above_f), 3: (below_n, below_f)}
    a = block_product(place, [side], early)
    b = block_product(place, [side_c], early)
    across, a, b = lax.optimization_barrier((across, a, b))
    a0, a1, a2, a3, b0, b1, b2, b3 = block_product(
        place, [side, side_c], {2: tuple(across)}, (*a, *b)
    )

    down_a, up_b, down_b, up_a = together(
        [(a2, Z_STEP[3]), (b2, Z_STEP[1]), (b3, Z_STEP[3]), (a1, Z_STEP[1])]
    )
    share = pick(share, c) + wide(share_got)
    outgoing = narrow(share)
    first, second, *shares = together(
        [(narrow(wide(down_a) + wide(a3)), Z_STEP[3]), (narrow(wide(up_b) + wide(b1)), Z_STEP[1])]
        + [(pick(outgoing, (x + d) % 4), X_STEP[d]) for d in (1, 3, 2)]
    )
    share = pick(share, x) + sum(wide(s) for s in shares)
    total = [
        narrow(wide(a0) + wide(up_a) + wide(first)).reshape(2, 2, half, half),
        narrow(wide(b0) + wide(down_b) + wide(second)).reshape(2, 2, half, half),
    ]
    homeward = []
    for s in range(2):
        for t in range(2):
            chosen = pick(total[t], yl ^ yh ^ s)
            value = jnp.concatenate([pick(chosen, yh ^ i) for i in range(2)], 0)
            homeward.append((value, HOME[s, t]))
    *arrived, share_got = together(homeward + [(narrow(pick(share, 1 - yl)), NEAR)])
    projected = narrow(pick(share, yl) + wide(share_got))
    arrived = jnp.stack(arrived)
    gram = jnp.concatenate(
        [pick(arrived, (q % 2 ^ yl) * 2 + (q // 2 ^ c)) for q in range(4)], 1
    )
    covariance = 0.9 * cov_prior + wide(gram) / items_total
    return (covariance, projected)


def solution(mesh):
    placed = (P("batch", "feat"), P("feat", None), P("feat", "batch"))
    return jax.shard_map(
        on_device,
        mesh=mesh,
        in_specs=placed,
        out_specs=(P("feat", "batch"), P(("batch", "feat"), None)),
        check_vma=False,
    )
```

time: 186 us -> 181 us (0.973)
  Pallas kernels: 0 us -> 25.2 us
  other arithmetic: 39 us -> 15.3 us
  matrix products: 16.9 us -> 2.47 us
  local copies, waits for them, and re-layouts: 7.64 us -> 18.5 us
  waiting for transfers between devices: 88.2 us -> 77.5 us
  starting transfers between devices: 32.1 us -> 40.3 us
    pallas_call x0 -> x3, Pallas kernels: none -> 25.2 us  [block_product(): pl.pallas_call(functools.partial(block_kernel, plan, groups, tuple(blocks...]
    concatenate x3 -> x0, other arithmetic: 22.6 us -> none  [the longest x1 19.9 us: on_device(): group = jnp.concatenate(groups, 1)]
    dot_general x2 -> x0, matrix products: 14.4 us -> none  [on_device(): lax.dot_general(lhs, rhs, (((0,), (0,)), ((), ())), preferred_element_typ...]
    unnamed x24 -> x66, local copies, waits for them, and re-layouts: 0.85 us -> 14 us
    ppermute x22 -> x31, waiting for transfers between devices: 88.2 us -> 77.5 us  [send(): return lax.ppermute(value, AXES, pairs)]
    ppermute x22 -> x31, starting transfers between devices: 32.1 us -> 40.3 us  [send(): return lax.ppermute(value, AXES, pairs)]
    slice x6 -> x0, local copies, waits for them, and re-layouts: 3.68 us -> none  [the longest x2 1.86 us: on_device(): block = [[p[:, d * half:(d + 1) * half] for p in partial] for d in range(4)]]
    another operation x4 -> x3, other arithmetic: 5.21 us -> 1.7 us  [the longest x1 1.52 us: on_device(): rim = jnp.stack([near1, far1])]
  transfers between devices with their start and end apart: 22 -> 31, of which waited for: 16 -> 14; matrix products, arithmetic and copies ran while one was open for 2% -> 5% of each run, Pallas kernels for 0% -> 14%
where the time goes in v4:
time: 181 us; the launch traced here: 180 us
  waiting for transfers between devices  77.5 us (43%)
  starting transfers between devices  40.3 us (22%)
  Pallas kernels  25.2 us (14%)
  local copies, waits for them, and re-layouts  18.5 us (10%)
  other arithmetic  15.3 us (8%)
  matrix products  2.47 us (1%)
    ppermute x31, waiting for transfers between devices, send(): return lax.ppermute(value, AXES, pairs)  77.5 us
    ppermute x31, starting transfers between devices, send(): return lax.ppermute(value, AXES, pairs)  40.3 us
    pallas_call x3, Pallas kernels, block_product(): pl.pallas_call(functools.partial(block_kernel, plan, groups, tuple(blocks...  25.2 us
    unnamed x66, local copies, waits for them, and re-layouts  14 us
    convert_element_type x6, other arithmetic, narrow(): return value.astype(jnp.bfloat16)  9.24 us
  transfers between devices with their start and end apart: 31, of which 14 were waited for; matrix products, arithmetic and copies ran while one was open for 5% of the time, Pallas kernels for 14%

profile of v4, /device:TPU:0, one launch (start us, length us, event | category | flops | bytes accessed | tf_op | source)
XLA Modules:
  0.0 180.2 jit_solution(18135344107380752503)
XLA Ops:
  0.7 1.6 copy.13
  2.3 1.7 collective-permute-start
  4.1 2.2 %collective-permute-start.1 = (bf16[256,1024]{1,0:T(8,128)(2,1)S(1)}, bf16[256,1024]{1,0:T(8,128)(2,1)S(1)}, u32[]{:S(2)}, u32[]{:S(2)}) collective-permute-start(bf16[256,1024]{1,0:T(8,128)(2,1)S(1)} %get-tuple-element.95), channel_id=1, source_target_pairs={{0,17},{1,16},{2,19},{3,18},{4,21},{5,20},{6,23},{7,22},{8,25},{9,... | collective-permute-start | bytes 1572872 | tf_op jit(solution)/shard_map/ppermute | solution.py:45
  6.3 9.7 %collective-permute-done.refs_4_.refs_5_ = bf16[256,1024]{1,0:T(8,128)(2,1)S(1)} collective-permute-done((bf16[256,1024]{1,0:T(8,128)(2,1)S(1)}, bf16[256,1024]{1,0:T(8,128)(2,1)S(1)}, u32[]{:S(2)}, u32[]{:S(2)}) %collective-permute-start) | collective-permute-done | bytes 524320 | tf_op jit(solution)/shard_map/ppermute | solution.py:45
  16.0 2.7 %collective-permute-done.1.refs_5_.refs_6_ = bf16[256,1024]{1,0:T(8,128)(2,1)S(1)} collective-permute-done((bf16[256,1024]{1,0:T(8,128)(2,1)S(1)}, bf16[256,1024]{1,0:T(8,128)(2,1)S(1)}, u32[]{:S(2)}, u32[]{:S(2)}) %collective-permute-start.1) | collective-permute-done | bytes 524320 | tf_op jit(solution)/shard_map/ppermute | solution.py:45
  20.2 1.7 collective-permute-start.3
  21.9 2.3 %collective-permute-start.5 = (bf16[256,1024]{1,0:T(8,128)(2,1)S(1)}, bf16[256,1024]{1,0:T(8,128)(2,1)S(1)}, u32[]{:S(2)}, u32[]{:S(2)}) collective-permute-start(bf16[256,1024]{1,0:T(8,128)(2,1)S(1)} %get-tuple-element.96), channel_id=1, source_target_pairs={{0,17},{1,16},{2,19},{3,18},{4,21},{5,20},{6,23},{7,22},{8,25},{9,... | collective-permute-start | bytes 1572872 | tf_op jit(solution)/shard_map/ppermute | solution.py:45
  24.3 10.1 %collective-permute-done.2.refs_10_.refs_9_ = bf16[256,1024]{1,0:T(8,128)(2,1)} collective-permute-done((bf16[256,1024]{1,0:T(8,128)(2,1)S(1)}, bf16[256,1024]{1,0:T(8,128)(2,1)}, u32[]{:S(2)}, u32[]{:S(2)}) %collective-permute-start.2) | collective-permute-done | bytes 524320 | tf_op jit(solution)/shard_map/ppermute | solution.py:45
  38.2 3.0 %collective-permute-start.8 = (bf16[256,1024]{1,0:T(8,128)(2,1)S(1)}, bf16[256,1024]{1,0:T(8,128)(2,1)S(1)}, u32[]{:S(2)}, u32[]{:S(2)}) collective-permute-start(bf16[256,1024]{1,0:T(8,128)(2,1)S(1)} %collective-permute-done.refs_4_.refs_5_), channel_id=1, source_target_pairs={{0,96},{1,97},{2,98},{3,99},{4,100},{5,101},{6,102},{7,103},{8,104... | collective-permute-start | bytes 1572872 | tf_op jit(solution)/shard_map/ppermute | solution.py:45
  41.7 2.2 %collective-permute-start.10 = (bf16[256,1024]{1,0:T(8,128)(2,1)S(1)}, bf16[256,1024]{1,0:T(8,128)(2,1)S(1)}, u32[]{:S(2)}, u32[]{:S(2)}) collective-permute-start(bf16[256,1024]{1,0:T(8,128)(2,1)S(1)} %collective-permute-done.refs_4_.refs_5_), channel_id=1, source_target_pairs={{0,17},{1,16},{2,19},{3,18},{4,21},{5,20},{6,23},{7,22},{8,25},{9,... | collective-permute-start | bytes 1572872 | tf_op jit(solution)/shard_map/ppermute | solution.py:45
  43.9 9.6 %collective-permute-done.7.refs_11_.refs_10_ = bf16[256,1024]{1,0:T(8,128)(2,1)S(1)} collective-permute-done((bf16[256,1024]{1,0:T(8,128)(2,1)S(1)}, bf16[256,1024]{1,0:T(8,128)(2,1)S(1)}, u32[]{:S(2)}, u32[]{:S(2)}) %collective-permute-start.7) | collective-permute-done | bytes 524320 | tf_op jit(solution)/shard_map/ppermute | solution.py:45
  59.5 2.5 %fusion.4 = f32[1024,1024]{1,0:T(8,128)S(1)} fusion(bf16[1024,512]{1,0:T(8,128)(2,1)} %param.3, bf16[512,1024]{1,0:T(8,128)(2,1)S(1)} %copy-done), kind=kOutput, calls=%fused_computation.40 | convolution fusion | flops 1073741824 | bytes 6291456 | tf_op jit(solution)/shard_map/dot_general | solution.py:185
  62.1 3.2 %collective-permute-start.15 = (bf16[256,1024]{1,0:T(8,128)(2,1)}, bf16[256,1024]{1,0:T(8,128)(2,1)}, u32[]{:S(2)}, u32[]{:S(2)}) collective-permute-start(bf16[256,1024]{1,0:T(8,128)(2,1)} %collective-permute-done.3.refs_9_.refs_8_), channel_id=1, source_target_pairs={{0,96},{1,97},{2,98},{3,99},{4,100},{5,101},{6,102},{7,103},{8,104... | collective-permute-start | bytes 1572872 | tf_op jit(solution)/shard_map/ppermute | solution.py:45
  73.9 8.4 %shard_map.50 = (bf16[1024,256]{1,0:T(8,128)(2,1)S(1)}, bf16[1024,256]{1,0:T(8,128)(2,1)}, bf16[1024,256]{1,0:T(8,128)(2,1)}, bf16[1024,256]{1,0:T(8,128)(2,1)S(1)}) custom-call(s32[2]{0:T(128)S(1)} %pad_add_fusion.refs_0_, bf16[2,256,1024]{2,1,0:T(8,128)(2,1)S(1)} %bitcast.68, bf16[256,1024]{1,0:T(8,128)(2,1)S(1)} %copy-done.17, ...), custom_call_target="tpu_custom_call" | custom-call | flops 3221225472 | bytes 7340032 | tf_op jit(solution)/shard_map/pallas_call | solution.py:144
  83.5 8.2 %shard_map.51 = (bf16[1024,256]{1,0:T(8,128)(2,1)S(1)}, bf16[1024,256]{1,0:T(8,128)(2,1)S(1)}, bf16[1024,256]{1,0:T(8,128)(2,1)}, bf16[1024,256]{1,0:T(8,128)(2,1)}) custom-call(s32[2]{0:T(128)S(1)} %pad_add_fusion.refs_0_, bf16[2,256,1024]{2,1,0:T(8,128)(2,1)S(1)} %copy-done.23, bf16[2,256,1024]{2,1,0:T(8,128)(2,1)} %collective-permute-done.13.refs_2_.refs_9_, ...), custom_call_target="tpu_custom_call" | custom-call | flops 3221225472 | bytes 7340032 | tf_op jit(solution)/shard_map/pallas_call | solution.py:144
  91.7 8.6 %shard_map.52 = (bf16[1024,256]{1,0:T(8,128)(2,1)S(1)}, bf16[1024,256]{1,0:T(8,128)(2,1)}, bf16[1024,256]{1,0:T(8,128)(2,1)}, bf16[1024,256]{1,0:T(8,128)(2,1)S(...) custom-call(s32[2]{0:T(128)S(1)} %pad_add_fusion.refs_0_, ...), custom_call_target="tpu_custom_call", output_to_operand_aliasing={{0}: (14, {}), {1}: (15, {}), {2}: (16, {}), {3}: (17, {}),... | custom-call | flops 2147483648 | bytes 9437184 | tf_op jit(solution)/shard_map/pallas_call | solution.py:144
  101.9 4.2 %collective-permute-start.16 = (bf16[1024,256]{1,0:T(8,128)(2,1)}, bf16[1024,256]{1,0:T(8,128)(2,1)S(1)}, u32[]{:S(2)}, u32[]{:S(2)}) collective-permute-start(bf16[1024,256]{1,0:T(8,128)(2,1)} %get-tuple-element.144), channel_id=1, source_target_pairs={{0,6},{1,7},{2,0},{3,1},{4,2},{5,3},{6,4},{7,5},{8,14},{9,15},{10,... | collective-permute-start | bytes 1572872 | tf_op jit(solution)/shard_map/ppermute | solution.py:45
  106.1 3.2 %collective-permute-start.18 = (bf16[1024,256]{1,0:T(8,128)(2,1)}, bf16[1024,256]{1,0:T(8,128)(2,1)}, u32[]{:S(2)}, u32[]{:S(2)}) collective-permute-start(bf16[1024,256]{1,0:T(8,128)(2,1)} %get-tuple-element.146), channel_id=1, source_target_pairs={{0,6},{1,7},{2,0},{3,1},{4,2},{5,3},{6,4},{7,5},{8,14},{9,15},{10,... | collective-permute-start | bytes 1572872 | tf_op jit(solution)/shard_map/ppermute | solution.py:45
  109.3 3.8 %fusion.3 = (bf16[4,2,64,1024]{3,2,1,0:T(8,128)(2,1)S(1)}, f32[4,2,64,1024]{3,2,1,0:T(8,128)}) fusion(bf16[4,2,64,1024]{3,2,1,0:T(8,128)(2,1)} %collective-permute-done.20, f32[4,2,2,64,1024]{4,3,2,1,0:T(8,128)} %bitcast.77, s32[]{:T(128)S(6)} %select_n.124), kind=kLoop, calls=%fused_computation.39 | loop fusion | flops 1572864 | bytes 6291460 | tf_op jit(solution)/shard_map/convert_element_type | solution.py:57
  113.9 4.7 %collective-permute-done.16 = bf16[1024,256]{1,0:T(8,128)(2,1)S(1)} collective-permute-done((bf16[1024,256]{1,0:T(8,128)(2,1)}, bf16[1024,256]{1,0:T(8,128)(2,1)S(1)}, u32[]{:S(2)}, u32[]{:S(2)}) %collective-permute-start.16) | collective-permute-done | bytes 524320 | tf_op jit(solution)/shard_map/ppermute | solution.py:45
  118.6 3.7 %collective-permute-done.17 = bf16[1024,256]{1,0:T(8,128)(2,1)} collective-permute-done((bf16[1024,256]{1,0:T(8,128)(2,1)}, bf16[1024,256]{1,0:T(8,128)(2,1)}, u32[]{:S(2)}, u32[]{:S(2)}) %collective-permute-start.17) | collective-permute-done | bytes 524320 | tf_op jit(solution)/shard_map/ppermute | solution.py:45
  122.3 7.1 %collective-permute-done.18 = bf16[1024,256]{1,0:T(8,128)(2,1)} collective-permute-done((bf16[1024,256]{1,0:T(8,128)(2,1)}, bf16[1024,256]{1,0:T(8,128)(2,1)}, u32[]{:S(2)}, u32[]{:S(2)}) %collective-permute-start.18) | collective-permute-done | bytes 524320 | tf_op jit(solution)/shard_map/ppermute | solution.py:45
  129.5 3.4 %collective-permute-done.19 = bf16[1024,256]{1,0:T(8,128)(2,1)} collective-permute-done((bf16[1024,256]{1,0:T(8,128)(2,1)}, bf16[1024,256]{1,0:T(8,128)(2,1)}, u32[]{:S(2)}, u32[]{:S(2)}) %collective-permute-start.19) | collective-permute-done | bytes 524320 | tf_op jit(solution)/shard_map/ppermute | solution.py:45
  135.4 1.7 collective-permute-start.22
  137.1 3.2 %collective-permute-start.24 = (bf16[2,64,1024]{2,1,0:T(8,128)(2,1)}, bf16[2,64,1024]{2,1,0:T(8,128)(2,1)}, u32[]{:S(2)}, u32[]{:S(2)}) collective-permute-start(bf16[2,64,1024]{2,1,0:T(8,128)(2,1)} %get-tuple-element.157), channel_id=1, source_target_pairs={{0,96},{1,97},{2,98},{3,99},{4,100},{5,101},{6,102},{7,103},{8,104... | collective-permute-start | bytes 786440 | tf_op jit(solution)/shard_map/ppermute | solution.py:45
  140.4 11.0 %collective-permute-done.23 = bf16[2,64,1024]{2,1,0:T(8,128)(2,1)} collective-permute-done((bf16[2,64,1024]{2,1,0:T(8,128)(2,1)}, bf16[2,64,1024]{2,1,0:T(8,128)(2,1)}, u32[]{:S(2)}, u32[]{:S(2)}) %collective-permute-start.23) | collective-permute-done | bytes 262176 | tf_op jit(solution)/shard_map/ppermute | solution.py:45
  156.3 1.9 %collective-permute-start.26 = (bf16[512,256]{1,0:T(8,128)(2,1)S(1)}, bf16[512,256]{1,0:T(8,128)(2,1)S(1)}, u32[]{:S(2)}, u32[]{:S(2)}) collective-permute-start(bf16[512,256]{1,0:T(8,128)(2,1)S(1)} %pad_maximum_fusion.4), channel_id=1, source_target_pairs={{0,1},{1,17},{2,3},{3,19},{4,5},{5,21},{6,7},{7,23},{8,9},{9,25},{... | collective-permute-start | bytes 786440 | tf_op jit(solution)/shard_map/ppermute | solution.py:45
  158.2 2.9 %collective-permute-start.28 = (bf16[512,256]{1,0:T(8,128)(2,1)S(1)}, bf16[512,256]{1,0:T(8,128)(2,1)S(1)}, u32[]{:S(2)}, u32[]{:S(2)}) collective-permute-start(bf16[512,256]{1,0:T(8,128)(2,1)S(1)} %pad_maximum_fusion.6), channel_id=1, source_target_pairs={{0,17},{1,1},{2,19},{3,3},{4,21},{5,5},{6,23},{7,7},{8,25},{9,9},{... | collective-permute-start | bytes 786440 | tf_op jit(solution)/shard_map/ppermute | solution.py:45
  161.2 3.5 %collective-permute-start.29 = (bf16[512,256]{1,0:T(8,128)(2,1)S(1)}, bf16[512,256]{1,0:T(8,128)(2,1)}, u32[]{:S(2)}, u32[]{:S(2)}) collective-permute-start(bf16[512,256]{1,0:T(8,128)(2,1)S(1)} %pad_maximum_fusion.7), channel_id=1, source_target_pairs={{0,25},{1,9},{2,27},{3,11},{4,29},{5,13},{6,31},{7,15},{8,17},{9,1... | collective-permute-start | bytes 786440 | tf_op jit(solution)/shard_map/ppermute | solution.py:45
  164.6 6.5 %collective-permute-done.30 = bf16[64,1024]{1,0:T(8,128)(2,1)S(1)} collective-permute-done((bf16[64,1024]{1,0:T(8,128)(2,1)}, bf16[64,1024]{1,0:T(8,128)(2,1)S(1)}, u32[]{:S(2)}, u32[]{:S(2)}) %collective-permute-start.30) | collective-permute-done | bytes 131104 | tf_op jit(solution)/shard_map/ppermute | solution.py:45
  171.1 5.1 %collective-permute-done.29 = bf16[512,256]{1,0:T(8,128)(2,1)} collective-permute-done((bf16[512,256]{1,0:T(8,128)(2,1)S(1)}, bf16[512,256]{1,0:T(8,128)(2,1)}, u32[]{:S(2)}, u32[]{:S(2)}) %collective-permute-start.29) | collective-permute-done | bytes 262176 | tf_op jit(solution)/shard_map/ppermute | solution.py:45
  178.6 1.7 multiply_add_fusion
  (124 shorter events, 34.0 us)
Async XLA Ops:
  0.6 58.9 %copy-start = (bf16[512,1024]{1,0:T(8,128)(2,1)S(1)}, bf16[512,1024]{1,0:T(8,128)(2,1)}, u32[]{:S(2)}) copy-start(bf16[512,1024]{1,0:T(8,128)(2,1)} %param.4) | copy-start | bytes 3145732
  2.3 13.7 %collective-permute-start = (bf16[256,1024]{1,0:T(8,128)(2,1)S(1)}, bf16[256,1024]{1,0:T(8,128)(2,1)S(1)}, u32[]{:S(2)}, u32[]{:S(2)}) collective-permute-start(bf16[256,1024]{1,0:T(8,128)(2,1)S(1)} %get-tuple-element.96), channel_id=1, source_target_pairs={{0,16},{1,17},{2,18},{3,19},{4,20},{5,21},{6,22},{7,23},{8,24},{9,... | collective-permute-start | bytes 1572872 | tf_op jit(solution)/shard_map/ppermute | solution.py:45
  4.1 14.6 %collective-permute-start.1 = (bf16[256,1024]{1,0:T(8,128)(2,1)S(1)}, bf16[256,1024]{1,0:T(8,128)(2,1)S(1)}, u32[]{:S(2)}, u32[]{:S(2)}) collective-permute-start(bf16[256,1024]{1,0:T(8,128)(2,1)S(1)} %get-tuple-element.95), channel_id=1, source_target_pairs={{0,17},{1,16},{2,19},{3,18},{4,21},{5,20},{6,23},{7,22},{8,25},{9,... | collective-permute-start | bytes 1572872 | tf_op jit(solution)/shard_map/ppermute | solution.py:45
  18.7 18.2 %collective-permute-start.6 = (bf16[2,256,1024]{2,1,0:T(8,128)(2,1)S(1)}, bf16[2,256,1024]{2,1,0:T(8,128)(2,1)S(1)}, u32[]{:S(2)}, u32[]{:S(2)}) collective-permute-start(bf16[2,256,1024]{2,1,0:T(8,128)(2,1)S(1)} %bitcast.67), channel_id=1, source_target_pairs={{0,8},{1,9},{2,10},{3,11},{4,12},{5,13},{6,14},{7,15},{8,0},{9,1},... | collective-permute-start | bytes 3145736 | tf_op jit(solution)/shard_map/ppermute | solution.py:45
  18.7 15.7 %collective-permute-start.2 = (bf16[256,1024]{1,0:T(8,128)(2,1)S(1)}, bf16[256,1024]{1,0:T(8,128)(2,1)}, u32[]{:S(2)}, u32[]{:S(2)}) collective-permute-start(bf16[256,1024]{1,0:T(8,128)(2,1)S(1)} %collective-permute-done.refs_4_.refs_5_), channel_id=1, source_target_pairs={{0,32},{1,33},{2,34},{3,35},{4,36},{5,37},{6,38},{7,39},{8,40},{9,... | collective-permute-start | bytes 1572872 | tf_op jit(solution)/shard_map/ppermute | solution.py:45
  20.2 14.2 %collective-permute-start.3 = (bf16[256,1024]{1,0:T(8,128)(2,1)S(1)}, bf16[256,1024]{1,0:T(8,128)(2,1)}, u32[]{:S(2)}, u32[]{:S(2)}) collective-permute-start(bf16[256,1024]{1,0:T(8,128)(2,1)S(1)} %collective-permute-done.1.refs_5_.refs_6_), channel_id=1, source_target_pairs={{0,96},{1,97},{2,98},{3,99},{4,100},{5,101},{6,102},{7,103},{8,104... | collective-permute-start | bytes 1572872 | tf_op jit(solution)/shard_map/ppermute | solution.py:45
  21.9 13.8 %collective-permute-start.4 = (bf16[256,1024]{1,0:T(8,128)(2,1)S(1)}, bf16[256,1024]{1,0:T(8,128)(2,1)S(1)}, u32[]{:S(2)}, u32[]{:S(2)}) collective-permute-start(bf16[256,1024]{1,0:T(8,128)(2,1)S(1)} %get-tuple-element.95), channel_id=1, source_target_pairs={{0,16},{1,17},{2,18},{3,19},{4,20},{5,21},{6,22},{7,23},{8,24},{9,... | collective-permute-start | bytes 1572872 | tf_op jit(solution)/shard_map/ppermute | solution.py:45
  21.9 15.0 %collective-permute-start.5 = (bf16[256,1024]{1,0:T(8,128)(2,1)S(1)}, bf16[256,1024]{1,0:T(8,128)(2,1)S(1)}, u32[]{:S(2)}, u32[]{:S(2)}) collective-permute-start(bf16[256,1024]{1,0:T(8,128)(2,1)S(1)} %get-tuple-element.96), channel_id=1, source_target_pairs={{0,17},{1,16},{2,19},{3,18},{4,21},{5,20},{6,23},{7,22},{8,25},{9,... | collective-permute-start | bytes 1572872 | tf_op jit(solution)/shard_map/ppermute | solution.py:45
  37.9 18.5 %collective-permute-start.11 = (bf16[2,256,1024]{2,1,0:T(8,128)(2,1)S(1)}, bf16[2,256,1024]{2,1,0:T(8,128)(2,1)S(1)}, u32[]{:S(2)}, u32[]{:S(2)}) collective-permute-start(bf16[2,256,1024]{2,1,0:T(8,128)(2,1)S(1)} %pad_maximum_fusion), channel_id=1, source_target_pairs={{0,8},{1,9},{2,10},{3,11},{4,12},{5,13},{6,14},{7,15},{8,0},{9,1},... | collective-permute-start | bytes 3145736 | tf_op jit(solution)/shard_map/ppermute | solution.py:45
  37.9 15.5 %collective-permute-start.7 = (bf16[256,1024]{1,0:T(8,128)(2,1)S(1)}, bf16[256,1024]{1,0:T(8,128)(2,1)S(1)}, u32[]{:S(2)}, u32[]{:S(2)}) collective-permute-start(bf16[256,1024]{1,0:T(8,128)(2,1)S(1)} %collective-permute-done.1.refs_5_.refs_6_), channel_id=1, source_target_pairs={{0,32},{1,33},{2,34},{3,35},{4,36},{5,37},{6,38},{7,39},{8,40},{9,... | collective-permute-start | bytes 1572872 | tf_op jit(solution)/shard_map/ppermute | solution.py:45
  38.2 16.1 %collective-permute-start.8 = (bf16[256,1024]{1,0:T(8,128)(2,1)S(1)}, bf16[256,1024]{1,0:T(8,128)(2,1)S(1)}, u32[]{:S(2)}, u32[]{:S(2)}) collective-permute-start(bf16[256,1024]{1,0:T(8,128)(2,1)S(1)} %collective-permute-done.refs_4_.refs_5_), channel_id=1, source_target_pairs={{0,96},{1,97},{2,98},{3,99},{4,100},{5,101},{6,102},{7,103},{8,104... | collective-permute-start | bytes 1572872 | tf_op jit(solution)/shard_map/ppermute | solution.py:45
  41.1 13.9 %collective-permute-start.9 = (bf16[256,1024]{1,0:T(8,128)(2,1)S(1)}, bf16[256,1024]{1,0:T(8,128)(2,1)S(1)}, u32[]{:S(2)}, u32[]{:S(2)}) collective-permute-start(bf16[256,1024]{1,0:T(8,128)(2,1)S(1)} %collective-permute-done.1.refs_5_.refs_6_), channel_id=1, source_target_pairs={{0,16},{1,17},{2,18},{3,19},{4,20},{5,21},{6,22},{7,23},{8,24},{9,... | collective-permute-start | bytes 1572872 | tf_op jit(solution)/shard_map/ppermute | solution.py:45
  41.7 14.7 %collective-permute-start.10 = (bf16[256,1024]{1,0:T(8,128)(2,1)S(1)}, bf16[256,1024]{1,0:T(8,128)(2,1)S(1)}, u32[]{:S(2)}, u32[]{:S(2)}) collective-permute-start(bf16[256,1024]{1,0:T(8,128)(2,1)S(1)} %collective-permute-done.refs_4_.refs_5_), channel_id=1, source_target_pairs={{0,17},{1,16},{2,19},{3,18},{4,21},{5,20},{6,23},{7,22},{8,25},{9,... | collective-permute-start | bytes 1572872 | tf_op jit(solution)/shard_map/ppermute | solution.py:45
  58.9 23.4 %collective-permute-start.12 = (bf16[2,256,1024]{2,1,0:T(8,128)(2,1)}, bf16[2,256,1024]{2,1,0:T(8,128)(2,1)}, u32[]{:S(2)}, u32[]{:S(2)}) collective-permute-start(bf16[2,256,1024]{2,1,0:T(8,128)(2,1)} %get-tuple-element.112), channel_id=1, source_target_pairs={{0,8},{1,9},{2,10},{3,11},{4,12},{5,13},{6,14},{7,15},{8,0},{9,1},... | collective-permute-start | bytes 3145736 | tf_op jit(solution)/shard_map/ppermute | solution.py:45
  59.0 23.4 %collective-permute-start.13 = (bf16[2,256,1024]{2,1,0:T(8,128)(2,1)}, bf16[2,256,1024]{2,1,0:T(8,128)(2,1)}, u32[]{:S(2)}, u32[]{:S(2)}) collective-permute-start(bf16[2,256,1024]{2,1,0:T(8,128)(2,1)} %get-tuple-element.113), channel_id=1, source_target_pairs={{0,8},{1,9},{2,10},{3,11},{4,12},{5,13},{6,14},{7,15},{8,0},{9,1},... | collective-permute-start | bytes 3145736 | tf_op jit(solution)/shard_map/ppermute | solution.py:45
  62.0 20.3 %collective-permute-start.14 = (bf16[256,1024]{1,0:T(8,128)(2,1)}, bf16[256,1024]{1,0:T(8,128)(2,1)}, u32[]{:S(2)}, u32[]{:S(2)}) collective-permute-start(bf16[256,1024]{1,0:T(8,128)(2,1)} %collective-permute-done.2.refs_10_.refs_9_), channel_id=1, source_target_pairs={{0,32},{1,33},{2,34},{3,35},{4,36},{5,37},{6,38},{7,39},{8,40},{9,... | collective-permute-start | bytes 1572872 | tf_op jit(solution)/shard_map/ppermute | solution.py:45
  62.1 20.3 %collective-permute-start.15 = (bf16[256,1024]{1,0:T(8,128)(2,1)}, bf16[256,1024]{1,0:T(8,128)(2,1)}, u32[]{:S(2)}, u32[]{:S(2)}) collective-permute-start(bf16[256,1024]{1,0:T(8,128)(2,1)} %collective-permute-done.3.refs_9_.refs_8_), channel_id=1, source_target_pairs={{0,96},{1,97},{2,98},{3,99},{4,100},{5,101},{6,102},{7,103},{8,104... | collective-permute-start | bytes 1572872 | tf_op jit(solution)/shard_map/ppermute | solution.py:45
  66.5 42.8 %collective-permute-start.20 = (bf16[4,2,64,1024]{3,2,1,0:T(8,128)(2,1)}, bf16[4,2,64,1024]{3,2,1,0:T(8,128)(2,1)}, u32[]{:S(2)}, u32[]{:S(2)}) collective-permute-start(bf16[4,2,64,1024]{3,2,1,0:T(8,128)(2,1)} %fusion), channel_id=1, source_target_pairs={{0,8},{1,9},{2,10},{3,11},{4,12},{5,13},{6,14},{7,15},{8,0},{9,1},... | collective-permute-start | bytes 3145736 | tf_op jit(solution)/shard_map/ppermute | solution.py:45
  101.9 16.7 %collective-permute-start.16 = (bf16[1024,256]{1,0:T(8,128)(2,1)}, bf16[1024,256]{1,0:T(8,128)(2,1)S(1)}, u32[]{:S(2)}, u32[]{:S(2)}) collective-permute-start(bf16[1024,256]{1,0:T(8,128)(2,1)} %get-tuple-element.144), channel_id=1, source_target_pairs={{0,6},{1,7},{2,0},{3,1},{4,2},{5,3},{6,4},{7,5},{8,14},{9,15},{10,... | collective-permute-start | bytes 1572872 | tf_op jit(solution)/shard_map/ppermute | solution.py:45
  106.0 16.3 %collective-permute-start.17 = (bf16[1024,256]{1,0:T(8,128)(2,1)}, bf16[1024,256]{1,0:T(8,128)(2,1)}, u32[]{:S(2)}, u32[]{:S(2)}) collective-permute-start(bf16[1024,256]{1,0:T(8,128)(2,1)} %get-tuple-element.145), channel_id=1, source_target_pairs={{0,2},{1,3},{2,4},{3,5},{4,6},{5,7},{6,0},{7,1},{8,10},{9,11},{10,... | collective-permute-start | bytes 1572872 | tf_op jit(solution)/shard_map/ppermute | solution.py:45
  106.1 23.4 %collective-permute-start.18 = (bf16[1024,256]{1,0:T(8,128)(2,1)}, bf16[1024,256]{1,0:T(8,128)(2,1)}, u32[]{:S(2)}, u32[]{:S(2)}) collective-permute-start(bf16[1024,256]{1,0:T(8,128)(2,1)} %get-tuple-element.146), channel_id=1, source_target_pairs={{0,6},{1,7},{2,0},{3,1},{4,2},{5,3},{6,4},{7,5},{8,14},{9,15},{10,... | collective-permute-start | bytes 1572872 | tf_op jit(solution)/shard_map/ppermute | solution.py:45
  109.3 23.6 %collective-permute-start.19 = (bf16[1024,256]{1,0:T(8,128)(2,1)}, bf16[1024,256]{1,0:T(8,128)(2,1)}, u32[]{:S(2)}, u32[]{:S(2)}) collective-permute-start(bf16[1024,256]{1,0:T(8,128)(2,1)} %get-tuple-element.147), channel_id=1, source_target_pairs={{0,2},{1,3},{2,4},{3,5},{4,6},{5,7},{6,0},{7,1},{8,10},{9,11},{10,... | collective-permute-start | bytes 1572872 | tf_op jit(solution)/shard_map/ppermute | solution.py:45
  135.0 16.3 %collective-permute-start.21 = (bf16[1024,256]{1,0:T(8,128)(2,1)}, bf16[1024,256]{1,0:T(8,128)(2,1)}, u32[]{:S(2)}, u32[]{:S(2)}) collective-permute-start(bf16[1024,256]{1,0:T(8,128)(2,1)} %add_convert_fusion.3), channel_id=1, source_target_pairs={{0,6},{1,7},{2,0},{3,1},{4,2},{5,3},{6,4},{7,5},{8,14},{9,15},{10,... | collective-permute-start | bytes 1572872 | tf_op jit(solution)/shard_map/ppermute | solution.py:45
  135.4 16.0 %collective-permute-start.22 = (bf16[1024,256]{1,0:T(8,128)(2,1)S(1)}, bf16[1024,256]{1,0:T(8,128)(2,1)S(1)}, u32[]{:S(2)}, u32[]{:S(2)}) collective-permute-start(bf16[1024,256]{1,0:T(8,128)(2,1)S(1)} %add_convert_fusion.2), channel_id=1, source_target_pairs={{0,2},{1,3},{2,4},{3,5},{4,6},{5,7},{6,0},{7,1},{8,10},{9,11},{10,... | collective-permute-start | bytes 1572872 | tf_op jit(solution)/shard_map/ppermute | solution.py:45
  137.1 14.2 %collective-permute-start.23 = (bf16[2,64,1024]{2,1,0:T(8,128)(2,1)}, bf16[2,64,1024]{2,1,0:T(8,128)(2,1)}, u32[]{:S(2)}, u32[]{:S(2)}) collective-permute-start(bf16[2,64,1024]{2,1,0:T(8,128)(2,1)} %get-tuple-element.156), channel_id=1, source_target_pairs={{0,32},{1,33},{2,34},{3,35},{4,36},{5,37},{6,38},{7,39},{8,40},{9,... | collective-permute-start | bytes 786440 | tf_op jit(solution)/shard_map/ppermute | solution.py:45
  137.1 14.2 %collective-permute-start.24 = (bf16[2,64,1024]{2,1,0:T(8,128)(2,1)}, bf16[2,64,1024]{2,1,0:T(8,128)(2,1)}, u32[]{:S(2)}, u32[]{:S(2)}) collective-permute-start(bf16[2,64,1024]{2,1,0:T(8,128)(2,1)} %get-tuple-element.157), channel_id=1, source_target_pairs={{0,96},{1,97},{2,98},{3,99},{4,100},{5,101},{6,102},{7,103},{8,104... | collective-permute-start | bytes 786440 | tf_op jit(solution)/shard_map/ppermute | solution.py:45
  140.4 11.0 %collective-permute-start.25 = (bf16[2,64,1024]{2,1,0:T(8,128)(2,1)S(1)}, bf16[2,64,1024]{2,1,0:T(8,128)(2,1)}, u32[]{:S(2)}, u32[]{:S(2)}) collective-permute-start(bf16[2,64,1024]{2,1,0:T(8,128)(2,1)S(1)} %get-tuple-element.158), channel_id=1, source_target_pairs={{0,64},{1,65},{2,66},{3,67},{4,68},{5,69},{6,70},{7,71},{8,72},{9,... | collective-permute-start | bytes 786440 | tf_op jit(solution)/shard_map/ppermute | solution.py:45
  156.3 14.8 %collective-permute-start.26 = (bf16[512,256]{1,0:T(8,128)(2,1)S(1)}, bf16[512,256]{1,0:T(8,128)(2,1)S(1)}, u32[]{:S(2)}, u32[]{:S(2)}) collective-permute-start(bf16[512,256]{1,0:T(8,128)(2,1)S(1)} %pad_maximum_fusion.4), channel_id=1, source_target_pairs={{0,1},{1,17},{2,3},{3,19},{4,5},{5,21},{6,7},{7,23},{8,9},{9,25},{... | collective-permute-start | bytes 786440 | tf_op jit(solution)/shard_map/ppermute | solution.py:45
  158.2 12.9 %collective-permute-start.27 = (bf16[512,256]{1,0:T(8,128)(2,1)S(1)}, bf16[512,256]{1,0:T(8,128)(2,1)S(1)}, u32[]{:S(2)}, u32[]{:S(2)}) collective-permute-start(bf16[512,256]{1,0:T(8,128)(2,1)S(1)} %pad_maximum_fusion.5), channel_id=1, source_target_pairs={{0,9},{1,25},{2,11},{3,27},{4,13},{5,29},{6,15},{7,31},{8,1},{9,17... | collective-permute-start | bytes 786440 | tf_op jit(solution)/shard_map/ppermute | solution.py:45
  158.2 12.9 %collective-permute-start.28 = (bf16[512,256]{1,0:T(8,128)(2,1)S(1)}, bf16[512,256]{1,0:T(8,128)(2,1)S(1)}, u32[]{:S(2)}, u32[]{:S(2)}) collective-permute-start(bf16[512,256]{1,0:T(8,128)(2,1)S(1)} %pad_maximum_fusion.6), channel_id=1, source_target_pairs={{0,17},{1,1},{2,19},{3,3},{4,21},{5,5},{6,23},{7,7},{8,25},{9,9},{... | collective-permute-start | bytes 786440 | tf_op jit(solution)/shard_map/ppermute | solution.py:45
  161.2 15.0 %collective-permute-start.29 = (bf16[512,256]{1,0:T(8,128)(2,1)S(1)}, bf16[512,256]{1,0:T(8,128)(2,1)}, u32[]{:S(2)}, u32[]{:S(2)}) collective-permute-start(bf16[512,256]{1,0:T(8,128)(2,1)S(1)} %pad_maximum_fusion.7), channel_id=1, source_target_pairs={{0,25},{1,9},{2,27},{3,11},{4,29},{5,13},{6,31},{7,15},{8,17},{9,1... | collective-permute-start | bytes 786440 | tf_op jit(solution)/shard_map/ppermute | solution.py:45
  164.6 6.5 %collective-permute-start.30 = (bf16[64,1024]{1,0:T(8,128)(2,1)}, bf16[64,1024]{1,0:T(8,128)(2,1)S(1)}, u32[]{:S(2)}, u32[]{:S(2)}) collective-permute-start(bf16[64,1024]{1,0:T(8,128)(2,1)} %fusion.2), channel_id=1, source_target_pairs={{0,16},{1,17},{2,18},{3,19},{4,20},{5,21},{6,22},{7,23},{8,24},{9,... | collective-permute-start | bytes 393224 | tf_op jit(solution)/shard_map/ppermute | solution.py:45
  (32 other events, 323.7 us)

commit v5 on v4

--- a/solution.py
+++ b/solution.py
@@ -67,7 +67,8 @@
     place, refs = refs[0], refs[1:]
     n_in = plan["inputs"]
     inputs, refs = refs[:n_in], refs[n_in + plan["kept"] :]
-    targets, refs = refs[: plan["targets"]], refs[plan["targets"] :]
+    home, up, down, middle = refs[:4]
+    targets, refs = ((home, up, down, middle), (home, middle, up, down)), refs[4:]
     left, columns_in, result, left_sem, column_sem, out_sem = refs
     shift, high = place[0], place[1]
 
@@ -112,9 +113,10 @@
             for n, dx in enumerate(offsets):
                 dz = (shift + dx) % 4
                 for d in range(4):
+                    cc = plan["sides"][side]
                     copy = pltpu.make_async_copy(
                         result.at[side, n],
-                        targets[side * 4 + d],
+                        targets[cc][d].at[cc],
                         out_sem.at[side * len(offsets) + n],
                     )
                     outs.append((dz == d, copy))
@@ -134,19 +136,18 @@
         inputs.append(array)
         return len(inputs) - 1, part
 
-    groups = [[enter(piece) for piece in pair] for side in sides for pair in side]
+    groups = [[enter(piece) for piece in pair] for side in sides.values() for pair in side]
     names = [[enter(piece) for piece in pair] for pair in blocks.values()]
     half, items = inputs[0].shape[-2:]
-    n_targets = 4 * len(sides)
-    plan = {"inputs": len(inputs), "kept": len(kept), "targets": n_targets, "blocks": names}
-    anywhere = pl.BlockSpec(memory_space=pl.ANY)
+    plan = {"inputs": len(inputs), "kept": len(kept), "sides": tuple(sides), "blocks": names}
+    outside = pl.BlockSpec(memory_space=pltpu.HBM)
     n_blocks = len(blocks)
     return pl.pallas_call(
         functools.partial(block_kernel, plan, groups, tuple(blocks)),
-        out_shape=[jax.ShapeDtypeStruct((4 * half, half), jnp.bfloat16)] * n_targets,
+        out_shape=[jax.ShapeDtypeStruct((2, 4 * half, half), jnp.bfloat16)] * 4,
         in_specs=[pl.BlockSpec(memory_space=pltpu.SMEM)]
-        + [anywhere] * (len(inputs) + len(kept)),
-        out_specs=[anywhere] * n_targets,
+        + [outside] * (len(inputs) + len(kept)),
+        out_specs=[outside] * 4,
         input_output_aliases={1 + len(inputs) + n: n for n in range(len(kept))},
         scratch_shapes=[
             pltpu.VMEM((len(groups), 2, half, items), jnp.bfloat16),
@@ -156,11 +157,9 @@
             pltpu.SemaphoreType.DMA((2 * n_blocks,)),
             pltpu.SemaphoreType.DMA((len(sides) * n_blocks,)),
         ],
-        compiler_params=pltpu.CompilerParams(vmem_limit_bytes=20 * 1024 * 1024),
+        compiler_params=pltpu.CompilerParams(vmem_limit_bytes=60 * 1024 * 1024),
         cost_estimate=pl.CostEstimate(
-            flops=2 * len(sides) * 4 * half * n_blocks * half * 2 * items,
-            bytes_accessed=(len(groups) + n_blocks) * 4 * half * items,
-            transcendentals=0,
+            flops=half * half, bytes_accessed=half * items, transcendentals=0
         ),
     )(place, *inputs, *kept)
 
@@ -176,26 +175,33 @@
 
     whole = embeddings.T.reshape(2, half, items)
     inner, outer = pick(whole, yh), pick(whole, 1 - yh)
-    near, far = together([(inner, NEAR), (outer, FAR)])
+    near, far, whole_c = together([(inner, NEAR), (outer, FAR), (whole, CORE)])
     right = jnp.stack([near, far])
-
-    below_n, above_f, near1, far1, whole_c = together(
-        [(near, X_STEP[1]), (far, X_STEP[3]), (outer, NEAR), (inner, FAR), (whole, CORE)]
-    )
     share = jnp.dot(embeddings, basis, preferred_element_type=jnp.float32)
     rows, width = share.shape[0] // 16, share.shape[1]
     share = jnp.moveaxis(share.reshape(4, 2, 2, rows, width), 2, 0)
     share_sent = narrow(pick(share, 1 - c))
-    rim = jnp.stack([near1, far1])
-
+
+    below_n, above_f, near1, far1, share_got = together(
+        [
+            (near, X_STEP[1]),
+            (far, X_STEP[3]),
+            (outer, NEAR),
+            (inner, FAR),
+            (share_sent, CORE),
+        ]
+    )
     below_f, above_n, two0, two1, right_c = together(
         [(far, X_STEP[1]), (near, X_STEP[3]), (far, NEAR), (near, FAR), (right, CORE)],
         (below_n, above_f),
     )
-    two = jnp.stack([two0, two1])
-    rim_c, two_c = together([(rim, CORE), (two, CORE)], (below_f, above_n))
+    rim = jnp.stack([near1, far1])
+    share = pick(share, c) + wide(share_got)
+    outgoing = narrow(share)
+    rim_c, two0_c, two1_c = together(
+        [(rim, CORE), (two0, CORE), (two1, CORE)], (below_f, above_n)
+    )
     across = together([(below_n, X_STEP[1]), (above_f, X_STEP[3])], (below_f, above_n))
-    (share_got,) = together([(share_sent, CORE)], (below_f, above_n))
     side = (
         ((whole, "0"), two0),
         ((whole, "1"), two1),
@@ -203,32 +209,33 @@
         (near1, far1),
     )
     side_c = (
-        ((whole_c, "0"), (two_c, 0)),
-        ((whole_c, "1"), (two_c, 1)),
+        ((whole_c, "0"), two0_c),
+        ((whole_c, "1"), two1_c),
         ((right_c, 0), (right_c, 1)),
         ((rim_c, 0), (rim_c, 1)),
     )
     early = {0: (near, far), 1: (above_n, above_f), 3: (below_n, below_f)}
-    a = block_product(place, [side], early)
-    b = block_product(place, [side_c], early)
-    across, a, b = lax.optimization_barrier((across, a, b))
-    a0, a1, a2, a3, b0, b1, b2, b3 = block_product(
-        place, [side, side_c], {2: tuple(across)}, (*a, *b)
-    )
-
-    down_a, up_b, down_b, up_a = together(
-        [(a2, Z_STEP[3]), (b2, Z_STEP[1]), (b3, Z_STEP[3]), (a1, Z_STEP[1])]
-    )
-    share = pick(share, c) + wide(share_got)
-    outgoing = narrow(share)
-    first, second, *shares = together(
-        [(narrow(wide(down_a) + wide(a3)), Z_STEP[3]), (narrow(wide(up_b) + wide(b1)), Z_STEP[1])]
-        + [(pick(outgoing, (x + d) % 4), X_STEP[d]) for d in (1, 3, 2)]
+    kept = block_product(place, {0: side}, early)
+    kept = block_product(place, {1: side_c}, early, kept)
+    across, kept = lax.optimization_barrier((across, kept))
+    home, up, down, middle = block_product(
+        place, {0: side, 1: side_c}, {2: tuple(across)}, kept
+    )
+
+    down, up, *shares = together(
+        [(down, Z_STEP[3]), (up, Z_STEP[1])]
+        + [(pick(outgoing, (x + d) % 4), X_STEP[d]) for d in (1, 2, 3)]
+    )
+    first, second = together(
+        [
+            (narrow(wide(down[0]) + wide(middle[0])), Z_STEP[3]),
+            (narrow(wide(up[1]) + wide(middle[1])), Z_STEP[1]),
+        ]
     )
     share = pick(share, x) + sum(wide(s) for s in shares)
     total = [
-        narrow(wide(a0) + wide(up_a) + wide(first)).reshape(2, 2, half, half),
-        narrow(wide(b0) + wide(down_b) + wide(second)).reshape(2, 2, half, half),
+        narrow(wide(home[0]) + wide(up[0]) + wide(first)).reshape(2, 2, half, half),
+        narrow(wide(home[1]) + wide(down[1]) + wide(second)).reshape(2, 2, half, half),
     ]
     homeward = []
     for s in range(2):

time: 181 us -> 174 us (0.961)
  local copies, waits for them, and re-layouts: 18.5 us -> 7.18 us
  Pallas kernels: 25.2 us -> 31.1 us
  starting transfers between devices: 40.3 us -> 36.8 us
  waiting for transfers between devices: 77.5 us -> 80.1 us
    unnamed x66 -> x48, local copies, waits for them, and re-layouts: 14 us -> 3.38 us
    pallas_call x3, Pallas kernels: 25.2 us -> 31.1 us  [block_product(): pl.pallas_call(functools.partial(block_kernel, plan, groups, tuple(blocks...]
    ppermute x31 -> x30, starting transfers between devices: 40.3 us -> 36.8 us  [send(): return lax.ppermute(value, AXES, pairs)]
    ppermute x31 -> x30, waiting for transfers between devices: 77.5 us -> 80.1 us  [send(): return lax.ppermute(value, AXES, pairs)]
    convert_element_type x6 -> x4, other arithmetic: 9.24 us -> 8.8 us  [narrow(): return value.astype(jnp.bfloat16)]
  transfers between devices with their start and end apart: 31 -> 30, of which waited for: 14 -> 16; matrix products, arithmetic and copies ran while one was open for 5% -> 6% of each run, Pallas kernels for 14% -> 6%
where the time goes in v5:
time: 174 us
  waiting for transfers between devices  80.1 us (46%)
  starting transfers between devices  36.8 us (21%)
  Pallas kernels  31.1 us (18%)
  other arithmetic  15.1 us (9%)
  local copies, waits for them, and re-layouts  7.18 us (4%)
  matrix products  2.47 us (1%)
    ppermute x30, waiting for transfers between devices, send(): return lax.ppermute(value, AXES, pairs)  80.1 us
    ppermute x30, starting transfers between devices, send(): return lax.ppermute(value, AXES, pairs)  36.8 us
    pallas_call x3, Pallas kernels, block_product(): pl.pallas_call(functools.partial(block_kernel, plan, groups, tuple(blocks...  31.1 us
    convert_element_type x4, other arithmetic, narrow(): return value.astype(jnp.bfloat16)  8.8 us
  transfers between devices with their start and end apart: 30, of which 16 were waited for; matrix products, arithmetic and copies ran while one was open for 6% of the time, Pallas kernels for 6%

profile of v5, /device:TPU:0, one launch (start us, length us, event | category | flops | bytes accessed | tf_op | source)
XLA Modules:
  0.0 173.7 jit_solution(8729007253404063638)
XLA Ops:
  3.4 1.7 collective-permute-start
  5.1 2.2 %collective-permute-start.1 = (bf16[256,1024]{1,0:T(8,128)(2,1)}, bf16[256,1024]{1,0:T(8,128)(2,1)S(1)}, u32[]{:S(2)}, u32[]{:S(2)}) collective-permute-start(bf16[256,1024]{1,0:T(8,128)(2,1)} %get-tuple-element.87), channel_id=1, source_target_pairs={{0,17},{1,16},{2,19},{3,18},{4,21},{5,20},{6,23},{7,22},{8,25},{9,... | collective-permute-start | bytes 1572872 | tf_op jit(solution)/shard_map/ppermute | solution.py:45
  7.3 2.5 %fusion.8 = f32[1024,1024]{1,0:T(8,128)S(1)} fusion(bf16[1024,512]{1,0:T(8,128)(2,1)} %param.3, bf16[512,1024]{1,0:T(8,128)(2,1)S(1)} %copy-done), kind=kOutput, calls=%fused_computation.43 | convolution fusion | flops 1073741824 | bytes 6291456 | tf_op jit(solution)/shard_map/dot_general | solution.py:180
  10.0 8.0 %collective-permute-done.refs_4_.refs_6_ = bf16[256,1024]{1,0:T(8,128)(2,1)S(1)} collective-permute-done((bf16[256,1024]{1,0:T(8,128)(2,1)}, bf16[256,1024]{1,0:T(8,128)(2,1)S(1)}, u32[]{:S(2)}, u32[]{:S(2)}) %collective-permute-start) | collective-permute-done | bytes 524320 | tf_op jit(solution)/shard_map/ppermute | solution.py:45
  18.0 2.6 %collective-permute-done.1.refs_5_.refs_7_ = bf16[256,1024]{1,0:T(8,128)(2,1)S(1)} collective-permute-done((bf16[256,1024]{1,0:T(8,128)(2,1)}, bf16[256,1024]{1,0:T(8,128)(2,1)S(1)}, u32[]{:S(2)}, u32[]{:S(2)}) %collective-permute-start.1) | collective-permute-done | bytes 524320 | tf_op jit(solution)/shard_map/ppermute | solution.py:45
  22.1 1.7 %collective-permute-start.4 = (bf16[256,1024]{1,0:T(8,128)(2,1)S(1)}, bf16[256,1024]{1,0:T(8,128)(2,1)S(1)}, u32[]{:S(2)}, u32[]{:S(2)}) collective-permute-start(bf16[256,1024]{1,0:T(8,128)(2,1)S(1)} %collective-permute-done.1.refs_5_.refs_7_), channel_id=1, source_target_pairs={{0,96},{1,97},{2,98},{3,99},{4,100},{5,101},{6,102},{7,103},{8,104... | collective-permute-start | bytes 1572872 | tf_op jit(solution)/shard_map/ppermute | solution.py:45
  23.9 2.3 %collective-permute-start.6 = (bf16[256,1024]{1,0:T(8,128)(2,1)}, bf16[256,1024]{1,0:T(8,128)(2,1)S(1)}, u32[]{:S(2)}, u32[]{:S(2)}) collective-permute-start(bf16[256,1024]{1,0:T(8,128)(2,1)} %get-tuple-element.88), channel_id=1, source_target_pairs={{0,17},{1,16},{2,19},{3,18},{4,21},{5,20},{6,23},{7,22},{8,25},{9,... | collective-permute-start | bytes 1572872 | tf_op jit(solution)/shard_map/ppermute | solution.py:45
  26.3 9.9 %collective-permute-done.3.refs_10_ = bf16[256,1024]{1,0:T(8,128)(2,1)S(1)} collective-permute-done((bf16[256,1024]{1,0:T(8,128)(2,1)S(1)}, bf16[256,1024]{1,0:T(8,128)(2,1)S(1)}, u32[]{:S(2)}, u32[]{:S(2)}) %collective-permute-start.3) | collective-permute-done | bytes 524320 | tf_op jit(solution)/shard_map/ppermute | solution.py:45
  36.1 1.7 collective-permute-done.5.refs_6_
  40.3 3.0 %collective-permute-start.9 = (bf16[256,1024]{1,0:T(8,128)(2,1)S(1)}, bf16[256,1024]{1,0:T(8,128)(2,1)S(1)}, u32[]{:S(2)}, u32[]{:S(2)}) collective-permute-start(bf16[256,1024]{1,0:T(8,128)(2,1)S(1)} %collective-permute-done.refs_4_.refs_6_), channel_id=1, source_target_pairs={{0,96},{1,97},{2,98},{3,99},{4,100},{5,101},{6,102},{7,103},{8,104... | collective-permute-start | bytes 1572872 | tf_op jit(solution)/shard_map/ppermute | solution.py:45
  43.8 2.2 %collective-permute-start.11 = (bf16[256,1024]{1,0:T(8,128)(2,1)S(1)}, bf16[256,1024]{1,0:T(8,128)(2,1)S(1)}, u32[]{:S(2)}, u32[]{:S(2)}) collective-permute-start(bf16[256,1024]{1,0:T(8,128)(2,1)S(1)} %collective-permute-done.refs_4_.refs_6_), channel_id=1, source_target_pairs={{0,17},{1,16},{2,19},{3,18},{4,21},{5,20},{6,23},{7,22},{8,25},{9,... | collective-permute-start | bytes 1572872 | tf_op jit(solution)/shard_map/ppermute | solution.py:45
  47.1 8.4 %collective-permute-done.8.refs_11_ = bf16[256,1024]{1,0:T(8,128)(2,1)S(1)} collective-permute-done((bf16[256,1024]{1,0:T(8,128)(2,1)S(1)}, bf16[256,1024]{1,0:T(8,128)(2,1)S(1)}, u32[]{:S(2)}, u32[]{:S(2)}) %collective-permute-start.8) | collective-permute-done | bytes 524320 | tf_op jit(solution)/shard_map/ppermute | solution.py:45
  59.4 3.2 %collective-permute-start.17 = (bf16[256,1024]{1,0:T(8,128)(2,1)}, bf16[256,1024]{1,0:T(8,128)(2,1)}, u32[]{:S(2)}, u32[]{:S(2)}) collective-permute-start(bf16[256,1024]{1,0:T(8,128)(2,1)} %copy-done.10), channel_id=1, source_target_pairs={{0,96},{1,97},{2,98},{3,99},{4,100},{5,101},{6,102},{7,103},{8,104... | collective-permute-start | bytes 1572872 | tf_op jit(solution)/shard_map/ppermute | solution.py:45
  63.7 3.8 %fusion.7 = (bf16[4,2,64,1024]{3,2,1,0:T(8,128)(2,1)S(1)}, f32[4,2,64,1024]{3,2,1,0:T(8,128)}) fusion(bf16[4,2,64,1024]{3,2,1,0:T(8,128)(2,1)} %copy-done.17, f32[4,2,2,64,1024]{4,3,2,1,0:T(8,128)} %bitcast.85, s32[]{:T(128)S(6)} %select_n.125), kind=kLoop, calls=%fused_computation.42 | loop fusion | flops 1572864 | bytes 6291460 | tf_op jit(solution)/shard_map/convert_element_type | solution.py:57
  67.5 10.0 %shard_map.50 = (bf16[2,1024,256]{2,1,0:T(8,128)(2,1)}, bf16[2,1024,256]{2,1,0:T(8,128)(2,1)}, bf16[2,1024,256]{2,1,0:T(8,128)(2,1)}, bf16[2,1024,256]{2,1,0:T(8,128)(2,1)}) custom-call(s32[2]{0:T(128)} %pad_add_fusion.refs_0_, bf16[2,256,1024]{2,1,0:T(8,128)(2,1)} %bitcast.78, bf16[256,1024]{1,0:T(8,128)(2,1)} %copy-done.14, bf16[256,1024]{1,0:T(8,128)(2,1)} %copy-done.15, ...), custom_call_target="tpu_custom_call" | custom-call | flops 65536 | bytes 262144 | tf_op jit(solution)/shard_map/pallas_call | solution.py:145
  78.8 10.0 %shard_map.51 = (bf16[2,1024,256]{2,1,0:T(8,128)(2,1)}, bf16[2,1024,256]{2,1,0:T(8,128)(2,1)}, bf16[2,1024,256]{2,1,0:T(8,128)(2,1)}, bf16[2,1024,256]{2,1,0:T(8,128)(2,1)}) custom-call(s32[2]{0:T(128)} %pad_add_fusion.refs_0_, ...), custom_call_target="tpu_custom_call", output_to_operand_aliasing={{0}: (12, {}), {1}: (13, {}), {2}: (14, {}), {3}: (15, {})} | custom-call | flops 65536 | bytes 262144 | tf_op jit(solution)/shard_map/pallas_call | solution.py:145
  88.9 11.0 %shard_map.52 = (bf16[2,1024,256]{2,1,0:T(8,128)(2,1)}, bf16[2,1024,256]{2,1,0:T(8,128)(2,1)}, bf16[2,1024,256]{2,1,0:T(8,128)(2,1)}, bf16[2,1024,256]{2,1,0:T(8,128)(2,1)}) custom-call(s32[2]{0:T(128)} %pad_add_fusion.refs_0_, bf16[2,256,1024]{2,1,0:T(8,128)(2,1)} %bitcast.79, ...), custom_call_target="tpu_custom_call", output_to_operand_aliasing={{0}: (15, {}), {1}: (16, {}), {2}: (17, {}), {3}: (18, {})} | custom-call | flops 65536 | bytes 262144 | tf_op jit(solution)/shard_map/pallas_call | solution.py:145
  99.9 4.1 %collective-permute-start.18 = (bf16[2,1024,256]{2,1,0:T(8,128)(2,1)}, bf16[2,1024,256]{2,1,0:T(8,128)(2,1)S(1)}, u32[]{:S(2)}, u32[]{:S(2)}) collective-permute-start(bf16[2,1024,256]{2,1,0:T(8,128)(2,1)} %get-tuple-element.133), channel_id=1, source_target_pairs={{0,6},{1,7},{2,0},{3,1},{4,2},{5,3},{6,4},{7,5},{8,14},{9,15},{10,... | collective-permute-start | bytes 3145736 | tf_op jit(solution)/shard_map/ppermute | solution.py:45
  103.9 2.1 %collective-permute-start.21 = (bf16[2,64,1024]{2,1,0:T(8,128)(2,1)S(1)}, bf16[2,64,1024]{2,1,0:T(8,128)(2,1)S(1)}, u32[]{:S(2)}, u32[]{:S(2)}) collective-permute-start(bf16[2,64,1024]{2,1,0:T(8,128)(2,1)S(1)} %get-tuple-element.136), channel_id=1, source_target_pairs={{0,64},{1,65},{2,66},{3,67},{4,68},{5,69},{6,70},{7,71},{8,72},{9,... | collective-permute-start | bytes 786440 | tf_op jit(solution)/shard_map/ppermute | solution.py:45
  107.2 11.5 %collective-permute-done.20 = bf16[2,64,1024]{2,1,0:T(8,128)(2,1)S(1)} collective-permute-done((bf16[2,64,1024]{2,1,0:T(8,128)(2,1)S(1)}, bf16[2,64,1024]{2,1,0:T(8,128)(2,1)S(1)}, u32[]{:S(2)}, u32[]{:S(2)}) %collective-permute-start.20) | collective-permute-done | bytes 262176 | tf_op jit(solution)/shard_map/ppermute | solution.py:45
  119.3 7.5 %collective-permute-done.18 = bf16[2,1024,256]{2,1,0:T(8,128)(2,1)S(1)} collective-permute-done((bf16[2,1024,256]{2,1,0:T(8,128)(2,1)}, bf16[2,1024,256]{2,1,0:T(8,128)(2,1)S(1)}, u32[]{:S(2)}, u32[]{:S(2)}) %collective-permute-start.18) | collective-permute-done | bytes 1048608 | tf_op jit(solution)/shard_map/ppermute | solution.py:45
  126.8 3.3 %collective-permute-done.19 = bf16[2,1024,256]{2,1,0:T(8,128)(2,1)S(1)} collective-permute-done((bf16[2,1024,256]{2,1,0:T(8,128)(2,1)}, bf16[2,1024,256]{2,1,0:T(8,128)(2,1)S(1)}, u32[]{:S(2)}, u32[]{:S(2)}) %collective-permute-start.19) | collective-permute-done | bytes 1048608 | tf_op jit(solution)/shard_map/ppermute | solution.py:45
  130.2 2.7 %fusion.4 = (bf16[1024,256]{1,0:T(8,128)(2,1)S(1)}, bf16[1024,256]{1,0:T(8,128)(2,1)}) fusion(bf16[2,1024,256]{2,1,0:T(8,128)(2,1)} %get-tuple-element.140, bf16[2,1024,256]{2,1,0:T(8,128)(2,1)S(1)} %collective-permute-done.19, bf16[2,1024,256]{2,1,0:T(8,128)(2,1)S(1)} %collective-permute-done.18), kind=kLoop, calls=%fused_computation.14 | loop fusion | flops 2097152 | bytes 3145728 | tf_op jit(solution)/shard_map/convert_element_type | solution.py:57
  137.1 8.8 %collective-permute-done.23 = bf16[1024,256]{1,0:T(8,128)(2,1)} collective-permute-done((bf16[1024,256]{1,0:T(8,128)(2,1)}, bf16[1024,256]{1,0:T(8,128)(2,1)}, u32[]{:S(2)}, u32[]{:S(2)}) %collective-permute-start.23) | collective-permute-done | bytes 524320 | tf_op jit(solution)/shard_map/ppermute | solution.py:45
  145.8 2.0 %collective-permute-done.24 = bf16[1024,256]{1,0:T(8,128)(2,1)} collective-permute-done((bf16[1024,256]{1,0:T(8,128)(2,1)S(1)}, bf16[1024,256]{1,0:T(8,128)(2,1)}, u32[]{:S(2)}, u32[]{:S(2)}) %collective-permute-start.24) | collective-permute-done | bytes 524320 | tf_op jit(solution)/shard_map/ppermute | solution.py:45
  147.9 1.6 fusion.1
  149.7 2.0 %collective-permute-start.25 = (bf16[512,256]{1,0:T(8,128)(2,1)S(1)}, bf16[512,256]{1,0:T(8,128)(2,1)S(1)}, u32[]{:S(2)}, u32[]{:S(2)}) collective-permute-start(bf16[512,256]{1,0:T(8,128)(2,1)S(1)} %pad_maximum_fusion.3), channel_id=1, source_target_pairs={{0,1},{1,17},{2,3},{3,19},{4,5},{5,21},{6,7},{7,23},{8,9},{9,25},{... | collective-permute-start | bytes 786440 | tf_op jit(solution)/shard_map/ppermute | solution.py:45
  151.7 2.9 %collective-permute-start.27 = (bf16[512,256]{1,0:T(8,128)(2,1)S(1)}, bf16[512,256]{1,0:T(8,128)(2,1)S(1)}, u32[]{:S(2)}, u32[]{:S(2)}) collective-permute-start(bf16[512,256]{1,0:T(8,128)(2,1)S(1)} %pad_maximum_fusion.5), channel_id=1, source_target_pairs={{0,17},{1,1},{2,19},{3,3},{4,21},{5,5},{6,23},{7,7},{8,25},{9,9},{... | collective-permute-start | bytes 786440 | tf_op jit(solution)/shard_map/ppermute | solution.py:45
  154.6 3.4 %collective-permute-start.28 = (bf16[512,256]{1,0:T(8,128)(2,1)S(1)}, bf16[512,256]{1,0:T(8,128)(2,1)}, u32[]{:S(2)}, u32[]{:S(2)}) collective-permute-start(bf16[512,256]{1,0:T(8,128)(2,1)S(1)} %pad_maximum_fusion.6), channel_id=1, source_target_pairs={{0,25},{1,9},{2,27},{3,11},{4,29},{5,13},{6,31},{7,15},{8,17},{9,1... | collective-permute-start | bytes 786440 | tf_op jit(solution)/shard_map/ppermute | solution.py:45
  158.1 6.5 %collective-permute-done.29 = bf16[64,1024]{1,0:T(8,128)(2,1)S(1)} collective-permute-done((bf16[64,1024]{1,0:T(8,128)(2,1)}, bf16[64,1024]{1,0:T(8,128)(2,1)S(1)}, u32[]{:S(2)}, u32[]{:S(2)}) %collective-permute-start.29) | collective-permute-done | bytes 131104 | tf_op jit(solution)/shard_map/ppermute | solution.py:45
  164.6 5.1 %collective-permute-done.28 = bf16[512,256]{1,0:T(8,128)(2,1)} collective-permute-done((bf16[512,256]{1,0:T(8,128)(2,1)S(1)}, bf16[512,256]{1,0:T(8,128)(2,1)}, u32[]{:S(2)}, u32[]{:S(2)}) %collective-permute-start.28) | collective-permute-done | bytes 262176 | tf_op jit(solution)/shard_map/ppermute | solution.py:45
  172.0 1.7 multiply_add_fusion
  (101 shorter events, 23.4 us)
Async XLA Ops:
  3.4 17.1 %collective-permute-start.2 = (bf16[2,256,1024]{2,1,0:T(8,128)(2,1)S(1)}, bf16[2,256,1024]{2,1,0:T(8,128)(2,1)}, u32[]{:S(2)}, u32[]{:S(2)}) collective-permute-start(bf16[2,256,1024]{2,1,0:T(8,128)(2,1)S(1)} %bitcast.77), channel_id=1, source_target_pairs={{0,8},{1,9},{2,10},{3,11},{4,12},{5,13},{6,14},{7,15},{8,0},{9,1},... | collective-permute-start | bytes 3145736 | tf_op jit(solution)/shard_map/ppermute | solution.py:45
  3.4 14.5 %collective-permute-start = (bf16[256,1024]{1,0:T(8,128)(2,1)}, bf16[256,1024]{1,0:T(8,128)(2,1)S(1)}, u32[]{:S(2)}, u32[]{:S(2)}) collective-permute-start(bf16[256,1024]{1,0:T(8,128)(2,1)} %get-tuple-element.88), channel_id=1, source_target_pairs={{0,16},{1,17},{2,18},{3,19},{4,20},{5,21},{6,22},{7,23},{8,24},{9,... | collective-permute-start | bytes 1572872 | tf_op jit(solution)/shard_map/ppermute | solution.py:45
  5.1 15.5 %collective-permute-start.1 = (bf16[256,1024]{1,0:T(8,128)(2,1)}, bf16[256,1024]{1,0:T(8,128)(2,1)S(1)}, u32[]{:S(2)}, u32[]{:S(2)}) collective-permute-start(bf16[256,1024]{1,0:T(8,128)(2,1)} %get-tuple-element.87), channel_id=1, source_target_pairs={{0,17},{1,16},{2,19},{3,18},{4,21},{5,20},{6,23},{7,22},{8,25},{9,... | collective-permute-start | bytes 1572872 | tf_op jit(solution)/shard_map/ppermute | solution.py:45
  18.0 29.2 %copy-start.3 = (bf16[256,1024]{1,0:T(8,128)(2,1)}, bf16[256,1024]{1,0:T(8,128)(2,1)S(1)}, u32[]{:S(2)}) copy-start(bf16[256,1024]{1,0:T(8,128)(2,1)S(1)} %collective-permute-done.refs_4_.refs_6_) | copy-start | bytes 1572868
  20.6 18.4 %collective-permute-start.7 = (bf16[4,2,64,1024]{3,2,1,0:T(8,128)(2,1)S(1)}, bf16[4,2,64,1024]{3,2,1,0:T(8,128)(2,1)S(1)}, u32[]{:S(2)}, u32[]{:S(2)}) collective-permute-start(bf16[4,2,64,1024]{3,2,1,0:T(8,128)(2,1)S(1)} %fusion), channel_id=1, source_target_pairs={{0,8},{1,9},{2,10},{3,11},{4,12},{5,13},{6,14},{7,15},{8,0},{9,1},... | collective-permute-start | bytes 3145736 | tf_op jit(solution)/shard_map/ppermute | solution.py:45
  20.6 15.5 %collective-permute-start.3 = (bf16[256,1024]{1,0:T(8,128)(2,1)S(1)}, bf16[256,1024]{1,0:T(8,128)(2,1)S(1)}, u32[]{:S(2)}, u32[]{:S(2)}) collective-permute-start(bf16[256,1024]{1,0:T(8,128)(2,1)S(1)} %collective-permute-done.refs_4_.refs_6_), channel_id=1, source_target_pairs={{0,32},{1,33},{2,34},{3,35},{4,36},{5,37},{6,38},{7,39},{8,40},{9,... | collective-permute-start | bytes 1572872 | tf_op jit(solution)/shard_map/ppermute | solution.py:45
  22.1 14.0 %collective-permute-start.4 = (bf16[256,1024]{1,0:T(8,128)(2,1)S(1)}, bf16[256,1024]{1,0:T(8,128)(2,1)S(1)}, u32[]{:S(2)}, u32[]{:S(2)}) collective-permute-start(bf16[256,1024]{1,0:T(8,128)(2,1)S(1)} %collective-permute-done.1.refs_5_.refs_7_), channel_id=1, source_target_pairs={{0,96},{1,97},{2,98},{3,99},{4,100},{5,101},{6,102},{7,103},{8,104... | collective-permute-start | bytes 1572872 | tf_op jit(solution)/shard_map/ppermute | solution.py:45
  23.9 13.9 %collective-permute-start.5 = (bf16[256,1024]{1,0:T(8,128)(2,1)}, bf16[256,1024]{1,0:T(8,128)(2,1)S(1)}, u32[]{:S(2)}, u32[]{:S(2)}) collective-permute-start(bf16[256,1024]{1,0:T(8,128)(2,1)} %get-tuple-element.87), channel_id=1, source_target_pairs={{0,16},{1,17},{2,18},{3,19},{4,20},{5,21},{6,22},{7,23},{8,24},{9,... | collective-permute-start | bytes 1572872 | tf_op jit(solution)/shard_map/ppermute | solution.py:45
  23.9 15.1 %collective-permute-start.6 = (bf16[256,1024]{1,0:T(8,128)(2,1)}, bf16[256,1024]{1,0:T(8,128)(2,1)S(1)}, u32[]{:S(2)}, u32[]{:S(2)}) collective-permute-start(bf16[256,1024]{1,0:T(8,128)(2,1)} %get-tuple-element.88), channel_id=1, source_target_pairs={{0,17},{1,16},{2,19},{3,18},{4,21},{5,20},{6,23},{7,22},{8,25},{9,... | collective-permute-start | bytes 1572872 | tf_op jit(solution)/shard_map/ppermute | solution.py:45
  37.8 29.7 %copy-start.5 = (bf16[256,1024]{1,0:T(8,128)(2,1)}, bf16[256,1024]{1,0:T(8,128)(2,1)S(1)}, u32[]{:S(2)}) copy-start(bf16[256,1024]{1,0:T(8,128)(2,1)S(1)} %collective-permute-done.5.refs_6_) | copy-start | bytes 1572868
  40.0 18.5 %collective-permute-start.12 = (bf16[2,256,1024]{2,1,0:T(8,128)(2,1)S(1)}, bf16[2,256,1024]{2,1,0:T(8,128)(2,1)}, u32[]{:S(2)}, u32[]{:S(2)}) collective-permute-start(bf16[2,256,1024]{2,1,0:T(8,128)(2,1)S(1)} %pad_maximum_fusion), channel_id=1, source_target_pairs={{0,8},{1,9},{2,10},{3,11},{4,12},{5,13},{6,14},{7,15},{8,0},{9,1},... | collective-permute-start | bytes 3145736 | tf_op jit(solution)/shard_map/ppermute | solution.py:45
  40.0 15.5 %collective-permute-start.8 = (bf16[256,1024]{1,0:T(8,128)(2,1)S(1)}, bf16[256,1024]{1,0:T(8,128)(2,1)S(1)}, u32[]{:S(2)}, u32[]{:S(2)}) collective-permute-start(bf16[256,1024]{1,0:T(8,128)(2,1)S(1)} %collective-permute-done.1.refs_5_.refs_7_), channel_id=1, source_target_pairs={{0,32},{1,33},{2,34},{3,35},{4,36},{5,37},{6,38},{7,39},{8,40},{9,... | collective-permute-start | bytes 1572872 | tf_op jit(solution)/shard_map/ppermute | solution.py:45
  40.3 15.3 %collective-permute-start.9 = (bf16[256,1024]{1,0:T(8,128)(2,1)S(1)}, bf16[256,1024]{1,0:T(8,128)(2,1)S(1)}, u32[]{:S(2)}, u32[]{:S(2)}) collective-permute-start(bf16[256,1024]{1,0:T(8,128)(2,1)S(1)} %collective-permute-done.refs_4_.refs_6_), channel_id=1, source_target_pairs={{0,96},{1,97},{2,98},{3,99},{4,100},{5,101},{6,102},{7,103},{8,104... | collective-permute-start | bytes 1572872 | tf_op jit(solution)/shard_map/ppermute | solution.py:45
  43.3 13.8 %collective-permute-start.10 = (bf16[256,1024]{1,0:T(8,128)(2,1)S(1)}, bf16[256,1024]{1,0:T(8,128)(2,1)S(1)}, u32[]{:S(2)}, u32[]{:S(2)}) collective-permute-start(bf16[256,1024]{1,0:T(8,128)(2,1)S(1)} %collective-permute-done.1.refs_5_.refs_7_), channel_id=1, source_target_pairs={{0,16},{1,17},{2,18},{3,19},{4,20},{5,21},{6,22},{7,23},{8,24},{9,... | collective-permute-start | bytes 1572872 | tf_op jit(solution)/shard_map/ppermute | solution.py:45
  43.8 14.7 %collective-permute-start.11 = (bf16[256,1024]{1,0:T(8,128)(2,1)S(1)}, bf16[256,1024]{1,0:T(8,128)(2,1)S(1)}, u32[]{:S(2)}, u32[]{:S(2)}) collective-permute-start(bf16[256,1024]{1,0:T(8,128)(2,1)S(1)} %collective-permute-done.refs_4_.refs_6_), channel_id=1, source_target_pairs={{0,17},{1,16},{2,19},{3,18},{4,21},{5,20},{6,23},{7,22},{8,25},{9,... | collective-permute-start | bytes 1572872 | tf_op jit(solution)/shard_map/ppermute | solution.py:45
  59.4 18.3 %collective-permute-start.13 = (bf16[2,256,1024]{2,1,0:T(8,128)(2,1)}, bf16[2,256,1024]{2,1,0:T(8,128)(2,1)S(1)}, u32[]{:S(2)}, u32[]{:S(2)}) collective-permute-start(bf16[2,256,1024]{2,1,0:T(8,128)(2,1)} %pad_maximum_fusion.1), channel_id=1, source_target_pairs={{0,8},{1,9},{2,10},{3,11},{4,12},{5,13},{6,14},{7,15},{8,0},{9,1},... | collective-permute-start | bytes 3145736 | tf_op jit(solution)/shard_map/ppermute | solution.py:45
  59.4 18.2 %collective-permute-start.16 = (bf16[256,1024]{1,0:T(8,128)(2,1)}, bf16[256,1024]{1,0:T(8,128)(2,1)}, u32[]{:S(2)}, u32[]{:S(2)}) collective-permute-start(bf16[256,1024]{1,0:T(8,128)(2,1)} %copy-done.9), channel_id=1, source_target_pairs={{0,32},{1,33},{2,34},{3,35},{4,36},{5,37},{6,38},{7,39},{8,40},{9,... | collective-permute-start | bytes 1572872 | tf_op jit(solution)/shard_map/ppermute | solution.py:45
  59.4 18.2 %collective-permute-start.17 = (bf16[256,1024]{1,0:T(8,128)(2,1)}, bf16[256,1024]{1,0:T(8,128)(2,1)}, u32[]{:S(2)}, u32[]{:S(2)}) collective-permute-start(bf16[256,1024]{1,0:T(8,128)(2,1)} %copy-done.10), channel_id=1, source_target_pairs={{0,96},{1,97},{2,98},{3,99},{4,100},{5,101},{6,102},{7,103},{8,104... | collective-permute-start | bytes 1572872 | tf_op jit(solution)/shard_map/ppermute | solution.py:45
  62.6 15.0 %collective-permute-start.14 = (bf16[256,1024]{1,0:T(8,128)(2,1)}, bf16[256,1024]{1,0:T(8,128)(2,1)S(1)}, u32[]{:S(2)}, u32[]{:S(2)}) collective-permute-start(bf16[256,1024]{1,0:T(8,128)(2,1)} %copy-done.14), channel_id=1, source_target_pairs={{0,8},{1,9},{2,10},{3,11},{4,12},{5,13},{6,14},{7,15},{8,0},{9,1},... | collective-permute-start | bytes 1572872 | tf_op jit(solution)/shard_map/ppermute | solution.py:45
  62.6 15.0 %collective-permute-start.15 = (bf16[256,1024]{1,0:T(8,128)(2,1)}, bf16[256,1024]{1,0:T(8,128)(2,1)}, u32[]{:S(2)}, u32[]{:S(2)}) collective-permute-start(bf16[256,1024]{1,0:T(8,128)(2,1)} %copy-done.15), channel_id=1, source_target_pairs={{0,8},{1,9},{2,10},{3,11},{4,12},{5,13},{6,14},{7,15},{8,0},{9,1},... | collective-permute-start | bytes 1572872 | tf_op jit(solution)/shard_map/ppermute | solution.py:45
  99.9 27.0 %collective-permute-start.18 = (bf16[2,1024,256]{2,1,0:T(8,128)(2,1)}, bf16[2,1024,256]{2,1,0:T(8,128)(2,1)S(1)}, u32[]{:S(2)}, u32[]{:S(2)}) collective-permute-start(bf16[2,1024,256]{2,1,0:T(8,128)(2,1)} %get-tuple-element.133), channel_id=1, source_target_pairs={{0,6},{1,7},{2,0},{3,1},{4,2},{5,3},{6,4},{7,5},{8,14},{9,15},{10,... | collective-permute-start | bytes 3145736 | tf_op jit(solution)/shard_map/ppermute | solution.py:45
  103.9 26.2 %collective-permute-start.19 = (bf16[2,1024,256]{2,1,0:T(8,128)(2,1)}, bf16[2,1024,256]{2,1,0:T(8,128)(2,1)S(1)}, u32[]{:S(2)}, u32[]{:S(2)}) collective-permute-start(bf16[2,1024,256]{2,1,0:T(8,128)(2,1)} %get-tuple-element.134), channel_id=1, source_target_pairs={{0,2},{1,3},{2,4},{3,5},{4,6},{5,7},{6,0},{7,1},{8,10},{9,11},{10,... | collective-permute-start | bytes 3145736 | tf_op jit(solution)/shard_map/ppermute | solution.py:45
  103.9 14.8 %collective-permute-start.20 = (bf16[2,64,1024]{2,1,0:T(8,128)(2,1)S(1)}, bf16[2,64,1024]{2,1,0:T(8,128)(2,1)S(1)}, u32[]{:S(2)}, u32[]{:S(2)}) collective-permute-start(bf16[2,64,1024]{2,1,0:T(8,128)(2,1)S(1)} %get-tuple-element.135), channel_id=1, source_target_pairs={{0,32},{1,33},{2,34},{3,35},{4,36},{5,37},{6,38},{7,39},{8,40},{9,... | collective-permute-start | bytes 786440 | tf_op jit(solution)/shard_map/ppermute | solution.py:45
  103.9 14.8 %collective-permute-start.21 = (bf16[2,64,1024]{2,1,0:T(8,128)(2,1)S(1)}, bf16[2,64,1024]{2,1,0:T(8,128)(2,1)S(1)}, u32[]{:S(2)}, u32[]{:S(2)}) collective-permute-start(bf16[2,64,1024]{2,1,0:T(8,128)(2,1)S(1)} %get-tuple-element.136), channel_id=1, source_target_pairs={{0,64},{1,65},{2,66},{3,67},{4,68},{5,69},{6,70},{7,71},{8,72},{9,... | collective-permute-start | bytes 786440 | tf_op jit(solution)/shard_map/ppermute | solution.py:45
  106.0 13.3 %collective-permute-start.22 = (bf16[2,64,1024]{2,1,0:T(8,128)(2,1)S(1)}, bf16[2,64,1024]{2,1,0:T(8,128)(2,1)S(1)}, u32[]{:S(2)}, u32[]{:S(2)}) collective-permute-start(bf16[2,64,1024]{2,1,0:T(8,128)(2,1)S(1)} %get-tuple-element.137), channel_id=1, source_target_pairs={{0,96},{1,97},{2,98},{3,99},{4,100},{5,101},{6,102},{7,103},{8,104... | collective-permute-start | bytes 786440 | tf_op jit(solution)/shard_map/ppermute | solution.py:45
  132.9 13.0 %collective-permute-start.23 = (bf16[1024,256]{1,0:T(8,128)(2,1)}, bf16[1024,256]{1,0:T(8,128)(2,1)}, u32[]{:S(2)}, u32[]{:S(2)}) collective-permute-start(bf16[1024,256]{1,0:T(8,128)(2,1)} %get-tuple-element.141), channel_id=1, source_target_pairs={{0,6},{1,7},{2,0},{3,1},{4,2},{5,3},{6,4},{7,5},{8,14},{9,15},{10,... | collective-permute-start | bytes 1572872 | tf_op jit(solution)/shard_map/ppermute | solution.py:45
  133.8 14.0 %collective-permute-start.24 = (bf16[1024,256]{1,0:T(8,128)(2,1)S(1)}, bf16[1024,256]{1,0:T(8,128)(2,1)}, u32[]{:S(2)}, u32[]{:S(2)}) collective-permute-start(bf16[1024,256]{1,0:T(8,128)(2,1)S(1)} %get-tuple-element.142), channel_id=1, source_target_pairs={{0,2},{1,3},{2,4},{3,5},{4,6},{5,7},{6,0},{7,1},{8,10},{9,11},{10,... | collective-permute-start | bytes 1572872 | tf_op jit(solution)/shard_map/ppermute | solution.py:45
  149.7 14.9 %collective-permute-start.25 = (bf16[512,256]{1,0:T(8,128)(2,1)S(1)}, bf16[512,256]{1,0:T(8,128)(2,1)S(1)}, u32[]{:S(2)}, u32[]{:S(2)}) collective-permute-start(bf16[512,256]{1,0:T(8,128)(2,1)S(1)} %pad_maximum_fusion.3), channel_id=1, source_target_pairs={{0,1},{1,17},{2,3},{3,19},{4,5},{5,21},{6,7},{7,23},{8,9},{9,25},{... | collective-permute-start | bytes 786440 | tf_op jit(solution)/shard_map/ppermute | solution.py:45
  151.7 12.9 %collective-permute-start.26 = (bf16[512,256]{1,0:T(8,128)(2,1)S(1)}, bf16[512,256]{1,0:T(8,128)(2,1)S(1)}, u32[]{:S(2)}, u32[]{:S(2)}) collective-permute-start(bf16[512,256]{1,0:T(8,128)(2,1)S(1)} %pad_maximum_fusion.4), channel_id=1, source_target_pairs={{0,9},{1,25},{2,11},{3,27},{4,13},{5,29},{6,15},{7,31},{8,1},{9,17... | collective-permute-start | bytes 786440 | tf_op jit(solution)/shard_map/ppermute | solution.py:45
  151.7 12.9 %collective-permute-start.27 = (bf16[512,256]{1,0:T(8,128)(2,1)S(1)}, bf16[512,256]{1,0:T(8,128)(2,1)S(1)}, u32[]{:S(2)}, u32[]{:S(2)}) collective-permute-start(bf16[512,256]{1,0:T(8,128)(2,1)S(1)} %pad_maximum_fusion.5), channel_id=1, source_target_pairs={{0,17},{1,1},{2,19},{3,3},{4,21},{5,5},{6,23},{7,7},{8,25},{9,9},{... | collective-permute-start | bytes 786440 | tf_op jit(solution)/shard_map/ppermute | solution.py:45
  154.6 15.0 %collective-permute-start.28 = (bf16[512,256]{1,0:T(8,128)(2,1)S(1)}, bf16[512,256]{1,0:T(8,128)(2,1)}, u32[]{:S(2)}, u32[]{:S(2)}) collective-permute-start(bf16[512,256]{1,0:T(8,128)(2,1)S(1)} %pad_maximum_fusion.6), channel_id=1, source_target_pairs={{0,25},{1,9},{2,27},{3,11},{4,29},{5,13},{6,31},{7,15},{8,17},{9,1... | collective-permute-start | bytes 786440 | tf_op jit(solution)/shard_map/ppermute | solution.py:45
  158.1 6.5 %collective-permute-start.29 = (bf16[64,1024]{1,0:T(8,128)(2,1)}, bf16[64,1024]{1,0:T(8,128)(2,1)S(1)}, u32[]{:S(2)}, u32[]{:S(2)}) collective-permute-start(bf16[64,1024]{1,0:T(8,128)(2,1)} %fusion.6), channel_id=1, source_target_pairs={{0,16},{1,17},{2,18},{3,19},{4,20},{5,21},{6,22},{7,23},{8,24},{9,... | collective-permute-start | bytes 393224 | tf_op jit(solution)/shard_map/ppermute | solution.py:45
  (22 other events, 215.3 us)

commit v6 on v5

--- a/solution.py
+++ b/solution.py
@@ -93,34 +93,43 @@
     for copy in rights:
         copy.wait()
     rows = columns_in.shape[2]
+    n_offsets = len(offsets)
     outs = []
-    for k in range(len(sides)):
-        for copy in lefts[2 * k : 2 * k + 2]:
-            copy.wait()
-        side, group = divmod(k, 4)
-        for n in range(len(offsets)):
-            total = None
+
+    def multiply(step, carry):
+        k, n = step // n_offsets, step % n_offsets
+
+        @pl.when(n == 0)
+        def _():
             for i in range(2):
-                term = lax.dot_general(
-                    left[k, i],
-                    columns_in[n, i],
-                    (((1,), (1,)), ((), ())),
-                    preferred_element_type=jnp.float32,
+                piece = left.at[k, i]
+                pltpu.make_async_copy(piece, piece, left_sem.at[2 * k + i]).wait()
+
+        total = sum(
+            lax.dot_general(
+                left[k, i],
+                columns_in[n, i],
+                (((1,), (1,)), ((), ())),
+                preferred_element_type=jnp.float32,
+            )
+            for i in range(2)
+        )
+        place_in = pl.ds(pl.multiple_of(k % 4 * rows, rows), rows)
+        result[k // 4, n, place_in, :] = total.astype(jnp.bfloat16)
+        return carry
+
+    for side, cc in enumerate(plan["sides"]):
+        lax.fori_loop(4 * n_offsets * side, 4 * n_offsets * (side + 1), multiply, 0)
+        for n, dx in enumerate(offsets):
+            dz = (shift + dx) % 4
+            for d in range(4):
+                copy = pltpu.make_async_copy(
+                    result.at[side, n],
+                    targets[cc][d].at[cc],
+                    out_sem.at[side * n_offsets + n],
                 )
-                total = term if total is None else total + term
-            result[side, n, group * rows : (group + 1) * rows, :] = total.astype(jnp.bfloat16)
-        if group == 3:
-            for n, dx in enumerate(offsets):
-                dz = (shift + dx) % 4
-                for d in range(4):
-                    cc = plan["sides"][side]
-                    copy = pltpu.make_async_copy(
-                        result.at[side, n],
-                        targets[cc][d].at[cc],
-                        out_sem.at[side * len(offsets) + n],
-                    )
-                    outs.append((dz == d, copy))
-                    pl.when(dz == d)(copy.start)
+                outs.append((dz == d, copy))
+                pl.when(dz == d)(copy.start)
     for here, copy in outs:
         pl.when(here)(copy.wait)
 
@@ -177,18 +186,16 @@
     inner, outer = pick(whole, yh), pick(whole, 1 - yh)
     near, far, whole_c = together([(inner, NEAR), (outer, FAR), (whole, CORE)])
     right = jnp.stack([near, far])
-    share = jnp.dot(embeddings, basis, preferred_element_type=jnp.float32)
-    rows, width = share.shape[0] // 16, share.shape[1]
-    share = jnp.moveaxis(share.reshape(4, 2, 2, rows, width), 2, 0)
-    share_sent = narrow(pick(share, 1 - c))
-
-    below_n, above_f, near1, far1, share_got = together(
+    share = narrow(jnp.dot(embeddings, basis, preferred_element_type=jnp.float32))
+    width = share.shape[1]
+    share = share.reshape(16, items // 16, width)
+
+    below_n, above_f, near1, far1 = together(
         [
             (near, X_STEP[1]),
             (far, X_STEP[3]),
             (outer, NEAR),
             (inner, FAR),
-            (share_sent, CORE),
         ]
     )
     below_f, above_n, two0, two1, right_c = together(
@@ -196,8 +203,6 @@
         (below_n, above_f),
     )
     rim = jnp.stack([near1, far1])
-    share = pick(share, c) + wide(share_got)
-    outgoing = narrow(share)
     rim_c, two0_c, two1_c = together(
         [(rim, CORE), (two0, CORE), (two1, CORE)], (below_f, above_n)
     )
@@ -222,17 +227,15 @@
         place, {0: side, 1: side_c}, {2: tuple(across)}, kept
     )
 
-    down, up, *shares = together(
-        [(down, Z_STEP[3]), (up, Z_STEP[1])]
-        + [(pick(outgoing, (x + d) % 4), X_STEP[d]) for d in (1, 2, 3)]
-    )
+    share, down, up = lax.optimization_barrier((share, down, up))
+    shares = lax.all_to_all(share, "feat", 0, 0)
+    down, up = together([(down, Z_STEP[3]), (up, Z_STEP[1])])
     first, second = together(
         [
             (narrow(wide(down[0]) + wide(middle[0])), Z_STEP[3]),
             (narrow(wide(up[1]) + wide(middle[1])), Z_STEP[1]),
         ]
     )
-    share = pick(share, x) + sum(wide(s) for s in shares)
     total = [
         narrow(wide(home[0]) + wide(up[0]) + wide(first)).reshape(2, 2, half, half),
         narrow(wide(home[1]) + wide(down[1]) + wide(second)).reshape(2, 2, half, half),
@@ -242,9 +245,11 @@
         for t in range(2):
             chosen = pick(total[t], yl ^ yh ^ s)
             value = jnp.concatenate([pick(chosen, yh ^ i) for i in range(2)], 0)
-            homeward.append((value, HOME[s, t]))
-    *arrived, share_got = together(homeward + [(narrow(pick(share, 1 - yl)), NEAR)])
-    projected = narrow(pick(share, yl) + wide(share_got))
+            homeward.append(value)
+    shares, homeward = lax.optimization_barrier((shares, homeward))
+    projected = narrow(jnp.sum(wide(shares), 0))
+    arrived = [send(v, HOME[s // 2, s % 2]) for s, v in enumerate(homeward)]
+    *arrived, projected = lax.optimization_barrier((*arrived, projected))
     arrived = jnp.stack(arrived)
     gram = jnp.concatenate(
         [pick(arrived, (q % 2 ^ yl) * 2 + (q // 2 ^ c)) for q in range(4)], 1

time: 174 us -> 167 us (0.960)
  other arithmetic: 15.1 us -> 10.4 us
  local copies, waits for them, and re-layouts: 7.18 us -> 4.21 us
    convert_element_type x4 -> x2, other arithmetic: 8.8 us -> 4.05 us  [narrow(): return value.astype(jnp.bfloat16)]
    ppermute x30 -> x25, starting transfers between devices: 36.8 us -> 32.2 us  [send(): return lax.ppermute(value, AXES, pairs)]
    all_to_all x0 -> x1, starting transfers between devices: none -> 4.44 us  [on_device(): shares = lax.all_to_all(share, 'feat', 0, 0)]
    reduce_sum x0 -> x1, other arithmetic: none -> 2.68 us  [on_device(): projected = narrow(jnp.sum(wide(shares), 0))]
    ppermute x30 -> x25, waiting for transfers between devices: 80.1 us -> 80 us  [send(): return lax.ppermute(value, AXES, pairs)]
  transfers between devices with their start and end apart: 30 -> 26, of which waited for: 16 -> 15; matrix products, arithmetic and copies ran while one was open for 6% -> 8% of each run, Pallas kernels for 6% -> 6%
where the time goes in v6:
time: 167 us; the launch traced here: 166 us
  waiting for transfers between devices  80 us (48%)
  starting transfers between devices  36.6 us (22%)
  Pallas kernels  30.3 us (18%)
  other arithmetic  10.4 us (6%)
  local copies, waits for them, and re-layouts  4.21 us (3%)
  matrix products  3.8 us (2%)
    ppermute x25, waiting for transfers between devices, send(): return lax.ppermute(value, AXES, pairs)  80 us
    ppermute x25, starting transfers between devices, send(): return lax.ppermute(value, AXES, pairs)  32.2 us
    pallas_call x3, Pallas kernels, block_product(): pl.pallas_call(functools.partial(block_kernel, plan, groups, tuple(blocks...  30.3 us
    all_to_all x1, starting transfers between devices, on_device(): shares = lax.all_to_all(share, 'feat', 0, 0)  4.44 us
    convert_element_type x2, other arithmetic, narrow(): return value.astype(jnp.bfloat16)  4.05 us
    dot_general x1, matrix products, on_device(): jnp.dot(embeddings, basis, preferred_element_type=jnp.float32)  3.8 us
  transfers between devices with their start and end apart: 26, of which 15 were waited for; matrix products, arithmetic and copies ran while one was open for 8% of the time, Pallas kernels for 6%

profile of v6, /device:TPU:0, one launch (start us, length us, event | category | flops | bytes accessed | tf_op | source)
XLA Modules:
  0.0 166.4 jit_solution(2599398541717395182)
XLA Ops:
  0.7 1.6 copy.13
  2.4 1.7 %collective-permute-start = (bf16[256,1024]{1,0:T(8,128)(2,1)S(1)}, bf16[256,1024]{1,0:T(8,128)(2,1)S(1)}, u32[]{:S(2)}, u32[]{:S(2)}) collective-permute-start(bf16[256,1024]{1,0:T(8,128)(2,1)S(1)} %get-tuple-element.83), channel_id=1, source_target_pairs={{0,16},{1,17},{2,18},{3,19},{4,20},{5,21},{6,22},{7,23},{8,24},{9,... | collective-permute-start | bytes 1572872 | tf_op jit(solution)/shard_map/ppermute | solution.py:45
  4.2 2.2 %collective-permute-start.1 = (bf16[256,1024]{1,0:T(8,128)(2,1)S(1)}, bf16[256,1024]{1,0:T(8,128)(2,1)S(1)}, u32[]{:S(2)}, u32[]{:S(2)}) collective-permute-start(bf16[256,1024]{1,0:T(8,128)(2,1)S(1)} %get-tuple-element.82), channel_id=1, source_target_pairs={{0,17},{1,16},{2,19},{3,18},{4,21},{5,20},{6,23},{7,22},{8,25},{9,... | collective-permute-start | bytes 1572872 | tf_op jit(solution)/shard_map/ppermute | solution.py:45
  6.4 10.4 %collective-permute-done.refs_4_.refs_6_ = bf16[256,1024]{1,0:T(8,128)(2,1)S(1)} collective-permute-done((bf16[256,1024]{1,0:T(8,128)(2,1)S(1)}, bf16[256,1024]{1,0:T(8,128)(2,1)S(1)}, u32[]{:S(2)}, u32[]{:S(2)}) %collective-permute-start) | collective-permute-done | bytes 524320 | tf_op jit(solution)/shard_map/ppermute | solution.py:45
  16.8 2.6 %collective-permute-done.1.refs_5_.refs_7_ = bf16[256,1024]{1,0:T(8,128)(2,1)S(1)} collective-permute-done((bf16[256,1024]{1,0:T(8,128)(2,1)S(1)}, bf16[256,1024]{1,0:T(8,128)(2,1)S(1)}, u32[]{:S(2)}, u32[]{:S(2)}) %collective-permute-start.1) | collective-permute-done | bytes 524320 | tf_op jit(solution)/shard_map/ppermute | solution.py:45
  20.9 1.7 %collective-permute-start.4 = (bf16[256,1024]{1,0:T(8,128)(2,1)S(1)}, bf16[256,1024]{1,0:T(8,128)(2,1)}, u32[]{:S(2)}, u32[]{:S(2)}) collective-permute-start(bf16[256,1024]{1,0:T(8,128)(2,1)S(1)} %collective-permute-done.1.refs_5_.refs_7_), channel_id=1, source_target_pairs={{0,96},{1,97},{2,98},{3,99},{4,100},{5,101},{6,102},{7,103},{8,104... | collective-permute-start | bytes 1572872 | tf_op jit(solution)/shard_map/ppermute | solution.py:45
  22.7 2.3 %collective-permute-start.6 = (bf16[256,1024]{1,0:T(8,128)(2,1)S(1)}, bf16[256,1024]{1,0:T(8,128)(2,1)S(1)}, u32[]{:S(2)}, u32[]{:S(2)}) collective-permute-start(bf16[256,1024]{1,0:T(8,128)(2,1)S(1)} %get-tuple-element.83), channel_id=1, source_target_pairs={{0,17},{1,16},{2,19},{3,18},{4,21},{5,20},{6,23},{7,22},{8,25},{9,... | collective-permute-start | bytes 1572872 | tf_op jit(solution)/shard_map/ppermute | solution.py:45
  25.0 8.9 %collective-permute-done.3.refs_10_ = bf16[256,1024]{1,0:T(8,128)(2,1)} collective-permute-done((bf16[256,1024]{1,0:T(8,128)(2,1)S(1)}, bf16[256,1024]{1,0:T(8,128)(2,1)}, u32[]{:S(2)}, u32[]{:S(2)}) %collective-permute-start.3) | collective-permute-done | bytes 524320 | tf_op jit(solution)/shard_map/ppermute | solution.py:45
  36.5 2.2 %collective-permute-start.10 = (bf16[256,1024]{1,0:T(8,128)(2,1)S(1)}, bf16[256,1024]{1,0:T(8,128)(2,1)}, u32[]{:S(2)}, u32[]{:S(2)}) collective-permute-start(bf16[256,1024]{1,0:T(8,128)(2,1)S(1)} %collective-permute-done.refs_4_.refs_6_), channel_id=1, source_target_pairs={{0,17},{1,16},{2,19},{3,18},{4,21},{5,20},{6,23},{7,22},{8,25},{9,... | collective-permute-start | bytes 1572872 | tf_op jit(solution)/shard_map/ppermute | solution.py:45
  39.0 3.0 %collective-permute-start.8 = (bf16[256,1024]{1,0:T(8,128)(2,1)S(1)}, bf16[256,1024]{1,0:T(8,128)(2,1)S(1)}, u32[]{:S(2)}, u32[]{:S(2)}) collective-permute-start(bf16[256,1024]{1,0:T(8,128)(2,1)S(1)} %collective-permute-done.refs_4_.refs_6_), channel_id=1, source_target_pairs={{0,96},{1,97},{2,98},{3,99},{4,100},{5,101},{6,102},{7,103},{8,104... | collective-permute-start | bytes 1572872 | tf_op jit(solution)/shard_map/ppermute | solution.py:45
  43.0 9.1 %collective-permute-done.10.refs_3_ = bf16[256,1024]{1,0:T(8,128)(2,1)} collective-permute-done((bf16[256,1024]{1,0:T(8,128)(2,1)S(1)}, bf16[256,1024]{1,0:T(8,128)(2,1)}, u32[]{:S(2)}, u32[]{:S(2)}) %collective-permute-start.10) | collective-permute-done | bytes 524320 | tf_op jit(solution)/shard_map/ppermute | solution.py:45
  52.1 1.8 %collective-permute-done.7.refs_11_ = bf16[256,1024]{1,0:T(8,128)(2,1)S(1)} collective-permute-done((bf16[256,1024]{1,0:T(8,128)(2,1)S(1)}, bf16[256,1024]{1,0:T(8,128)(2,1)S(1)}, u32[]{:S(2)}, u32[]{:S(2)}) %collective-permute-start.7) | collective-permute-done | bytes 524320 | tf_op jit(solution)/shard_map/ppermute | solution.py:45
  53.9 1.6 collective-permute-done.9.refs_2_
  55.7 3.2 %collective-permute-start.16 = (bf16[256,1024]{1,0:T(8,128)(2,1)}, bf16[256,1024]{1,0:T(8,128)(2,1)}, u32[]{:S(2)}, u32[]{:S(2)}) collective-permute-start(bf16[256,1024]{1,0:T(8,128)(2,1)} %collective-permute-done.4.refs_9_), channel_id=1, source_target_pairs={{0,96},{1,97},{2,98},{3,99},{4,100},{5,101},{6,102},{7,103},{8,104... | collective-permute-start | bytes 1572872 | tf_op jit(solution)/shard_map/ppermute | solution.py:45
  60.1 3.8 %convolution_convert_fusion = bf16[1024,1024]{1,0:T(8,128)(2,1)} fusion(bf16[1024,512]{1,0:T(8,128)(2,1)} %param.3, bf16[512,1024]{1,0:T(8,128)(2,1)S(1)} %copy-done), kind=kOutput, calls=%fused_computation.1 | convolution fusion | flops 1074790400 | bytes 4194304 | tf_op jit(solution)/shard_map/dot_general | solution.py:189
  63.9 10.7 %shard_map.50 = (bf16[2,1024,256]{2,1,0:T(8,128)(2,1)}, bf16[2,1024,256]{2,1,0:T(8,128)(2,1)}, bf16[2,1024,256]{2,1,0:T(8,128)(2,1)}, bf16[2,1024,256]{2,1,0:T(8,128)(2,1)}) custom-call(s32[2]{0:T(128)} %pad_add_fusion.refs_0_, bf16[2,256,1024]{2,1,0:T(8,128)(2,1)} %bitcast.59, bf16[256,1024]{1,0:T(8,128)(2,1)} %collective-permute-done.9.refs_2_, ...), custom_call_target="tpu_custom_call" | custom-call | flops 65536 | bytes 262144 | tf_op jit(solution)/shard_map/pallas_call | solution.py:154
  75.7 10.7 %shard_map.51 = (bf16[2,1024,256]{2,1,0:T(8,128)(2,1)}, bf16[2,1024,256]{2,1,0:T(8,128)(2,1)}, bf16[2,1024,256]{2,1,0:T(8,128)(2,1)}, bf16[2,1024,256]{2,1,0:T(8,128)(2,1)}) custom-call(s32[2]{0:T(128)} %pad_add_fusion.refs_0_, bf16[2,256,1024]{2,1,0:T(8,128)(2,1)} %copy-done.8, ...), custom_call_target="tpu_custom_call", output_to_operand_aliasing={{0}: (12, {}), {1}: (13, {}), {2}: (14, {}), {3}: (15, {})} | custom-call | flops 65536 | bytes 262144 | tf_op jit(solution)/shard_map/pallas_call | solution.py:154
  86.4 9.0 %shard_map.52 = (bf16[2,1024,256]{2,1,0:T(8,128)(2,1)}, bf16[2,1024,256]{2,1,0:T(8,128)(2,1)}, bf16[2,1024,256]{2,1,0:T(8,128)(2,1)}, bf16[2,1024,256]{2,1,0:T(8,128)(2,1)}) custom-call(s32[2]{0:T(128)} %pad_add_fusion.refs_0_, bf16[2,256,1024]{2,1,0:T(8,128)(2,1)} %bitcast.60, ...), custom_call_target="tpu_custom_call", output_to_operand_aliasing={{0}: (15, {}), {1}: (16, {}), {2}: (17, {}), {3}: (18, {})} | custom-call | flops 65536 | bytes 262144 | tf_op jit(solution)/shard_map/pallas_call | solution.py:154
  95.3 4.1 %collective-permute-start.17 = (bf16[2,1024,256]{2,1,0:T(8,128)(2,1)}, bf16[2,1024,256]{2,1,0:T(8,128)(2,1)}, u32[]{:S(2)}, u32[]{:S(2)}) collective-permute-start(bf16[2,1024,256]{2,1,0:T(8,128)(2,1)} %get-tuple-element.129), channel_id=1, source_target_pairs={{0,6},{1,7},{2,0},{3,1},{4,2},{5,3},{6,4},{7,5},{8,14},{9,15},{10,... | collective-permute-start | bytes 3145736 | tf_op jit(solution)/shard_map/ppermute | solution.py:45
  99.4 4.4 %all-to-all-start = ((bf16[16,64,1024]{2,1,0:T(8,128)(2,1)}), bf16[16,64,1024]{2,1,0:T(8,128)(2,1)}, u32[]{:S(2)}, u32[]{:S(2)}) async-start(bf16[16,64,1024]{2,1,0:T(8,128)(2,1)} %bitcast.65), calls=%async_computation | async-start | bytes 4194304 | tf_op jit(solution)/shard_map/all_to_all | solution.py:231
  103.9 18.4 %collective-permute-done.17 = bf16[2,1024,256]{2,1,0:T(8,128)(2,1)} collective-permute-done((bf16[2,1024,256]{2,1,0:T(8,128)(2,1)}, bf16[2,1024,256]{2,1,0:T(8,128)(2,1)}, u32[]{:S(2)}, u32[]{:S(2)}) %collective-permute-start.17) | collective-permute-done | bytes 1048608 | tf_op jit(solution)/shard_map/ppermute | solution.py:45
  122.3 3.4 %collective-permute-done.18 = bf16[2,1024,256]{2,1,0:T(8,128)(2,1)} collective-permute-done((bf16[2,1024,256]{2,1,0:T(8,128)(2,1)}, bf16[2,1024,256]{2,1,0:T(8,128)(2,1)}, u32[]{:S(2)}, u32[]{:S(2)}) %collective-permute-start.18) | collective-permute-done | bytes 1048608 | tf_op jit(solution)/shard_map/ppermute | solution.py:45
  125.7 2.4 %fusion.3 = (bf16[1024,256]{1,0:T(8,128)(2,1)}, bf16[1024,256]{1,0:T(8,128)(2,1)}) fusion(bf16[2,1024,256]{2,1,0:T(8,128)(2,1)S(1)} %copy-done.2, bf16[2,1024,256]{2,1,0:T(8,128)(2,1)} %collective-permute-done.18, bf16[2,1024,256]{2,1,0:T(8,128)(2,1)} %collective-permute-done.17), kind=kLoop, calls=%fused_computation.12 | loop fusion | flops 2097152 | bytes 3145728 | tf_op jit(solution)/shard_map/convert_element_type | solution.py:57
  128.4 1.7 %collective-permute-start.20 = (bf16[1024,256]{1,0:T(8,128)(2,1)}, bf16[1024,256]{1,0:T(8,128)(2,1)S(1)}, u32[]{:S(2)}, u32[]{:S(2)}) collective-permute-start(bf16[1024,256]{1,0:T(8,128)(2,1)} %get-tuple-element.135), channel_id=1, source_target_pairs={{0,2},{1,3},{2,4},{3,5},{4,6},{5,7},{6,0},{7,1},{8,10},{9,11},{10,... | collective-permute-start | bytes 1572872 | tf_op jit(solution)/shard_map/ppermute | solution.py:45
  130.2 10.8 %collective-permute-done.19 = bf16[1024,256]{1,0:T(8,128)(2,1)S(1)} collective-permute-done((bf16[1024,256]{1,0:T(8,128)(2,1)}, bf16[1024,256]{1,0:T(8,128)(2,1)S(1)}, u32[]{:S(2)}, u32[]{:S(2)}) %collective-permute-start.19) | collective-permute-done | bytes 524320 | tf_op jit(solution)/shard_map/ppermute | solution.py:45
  142.6 1.6 fusion
  145.2 4.1 %collective-permute-start.23 = (bf16[512,256]{1,0:T(8,128)(2,1)S(1)}, bf16[512,256]{1,0:T(8,128)(2,1)S(1)}, u32[]{:S(2)}, u32[]{:S(2)}) collective-permute-start(bf16[512,256]{1,0:T(8,128)(2,1)S(1)} %pad_maximum_fusion.5), channel_id=1, source_target_pairs={{0,17},{1,1},{2,19},{3,3},{4,21},{5,5},{6,23},{7,7},{8,25},{9,9},{... | collective-permute-start | bytes 786440 | tf_op jit(solution)/shard_map/ppermute | solution.py:45
  149.3 2.3 %collective-permute-start.24 = (bf16[512,256]{1,0:T(8,128)(2,1)S(1)}, bf16[512,256]{1,0:T(8,128)(2,1)S(1)}, u32[]{:S(2)}, u32[]{:S(2)}) collective-permute-start(bf16[512,256]{1,0:T(8,128)(2,1)S(1)} %pad_maximum_fusion.6), channel_id=1, source_target_pairs={{0,25},{1,9},{2,27},{3,11},{4,29},{5,13},{6,31},{7,15},{8,17},{9,1... | collective-permute-start | bytes 786440 | tf_op jit(solution)/shard_map/ppermute | solution.py:45
  151.6 2.7 %reduce_sum.12 = bf16[64,1024]{1,0:T(8,128)(2,1)} reduce(bf16[16,64,1024]{2,1,0:T(8,128)(2,1)} %all-to-all-done, bf16[]{:T(256)} %constant.278.clone.1), dimensions={0}, to_apply=%region_0.1 | reduce | flops 983040 | bytes 2228226 | tf_op jit(solution)/shard_map/reduce_sum | solution.py:250
  154.7 1.9 %collective-permute-done.23 = bf16[512,256]{1,0:T(8,128)(2,1)S(1)} collective-permute-done((bf16[512,256]{1,0:T(8,128)(2,1)S(1)}, bf16[512,256]{1,0:T(8,128)(2,1)S(1)}, u32[]{:S(2)}, u32[]{:S(2)}) %collective-permute-start.23) | collective-permute-done | bytes 262176 | tf_op jit(solution)/shard_map/ppermute | solution.py:45
  156.6 6.5 %collective-permute-done.24 = bf16[512,256]{1,0:T(8,128)(2,1)S(1)} collective-permute-done((bf16[512,256]{1,0:T(8,128)(2,1)S(1)}, bf16[512,256]{1,0:T(8,128)(2,1)S(1)}, u32[]{:S(2)}, u32[]{:S(2)}) %collective-permute-start.24) | collective-permute-done | bytes 262176 | tf_op jit(solution)/shard_map/ppermute | solution.py:45
  164.7 1.7 multiply_add_fusion
  (68 shorter events, 13.0 us)
Async XLA Ops:
  0.6 59.5 %copy-start = (bf16[512,1024]{1,0:T(8,128)(2,1)S(1)}, bf16[512,1024]{1,0:T(8,128)(2,1)}, u32[]{:S(2)}) copy-start(bf16[512,1024]{1,0:T(8,128)(2,1)} %param.4) | copy-start | bytes 3145732
  2.2 22.8 %copy-start.1 = (bf16[512,1024]{1,0:T(8,128)(2,1)}, bf16[512,1024]{1,0:T(8,128)(2,1)S(1)}, u32[]{:S(2)}) copy-start(bf16[512,1024]{1,0:T(8,128)(2,1)S(1)} %copy.13) | copy-start | bytes 3145732
  2.3 17.0 %collective-permute-start.2 = (bf16[2,256,1024]{2,1,0:T(8,128)(2,1)S(1)}, bf16[2,256,1024]{2,1,0:T(8,128)(2,1)S(1)}, u32[]{:S(2)}, u32[]{:S(2)}) collective-permute-start(bf16[2,256,1024]{2,1,0:T(8,128)(2,1)S(1)} %bitcast.58), channel_id=1, source_target_pairs={{0,8},{1,9},{2,10},{3,11},{4,12},{5,13},{6,14},{7,15},{8,0},{9,1},... | collective-permute-start | bytes 3145736 | tf_op jit(solution)/shard_map/ppermute | solution.py:45
  2.4 14.3 %collective-permute-start = (bf16[256,1024]{1,0:T(8,128)(2,1)S(1)}, bf16[256,1024]{1,0:T(8,128)(2,1)S(1)}, u32[]{:S(2)}, u32[]{:S(2)}) collective-permute-start(bf16[256,1024]{1,0:T(8,128)(2,1)S(1)} %get-tuple-element.83), channel_id=1, source_target_pairs={{0,16},{1,17},{2,18},{3,19},{4,20},{5,21},{6,22},{7,23},{8,24},{9,... | collective-permute-start | bytes 1572872 | tf_op jit(solution)/shard_map/ppermute | solution.py:45
  4.2 15.2 %collective-permute-start.1 = (bf16[256,1024]{1,0:T(8,128)(2,1)S(1)}, bf16[256,1024]{1,0:T(8,128)(2,1)S(1)}, u32[]{:S(2)}, u32[]{:S(2)}) collective-permute-start(bf16[256,1024]{1,0:T(8,128)(2,1)S(1)} %get-tuple-element.82), channel_id=1, source_target_pairs={{0,17},{1,16},{2,19},{3,18},{4,21},{5,20},{6,23},{7,22},{8,25},{9,... | collective-permute-start | bytes 1572872 | tf_op jit(solution)/shard_map/ppermute | solution.py:45
  16.8 26.2 %copy-start.4 = (bf16[256,1024]{1,0:T(8,128)(2,1)}, bf16[256,1024]{1,0:T(8,128)(2,1)S(1)}, u32[]{:S(2)}) copy-start(bf16[256,1024]{1,0:T(8,128)(2,1)S(1)} %collective-permute-done.refs_4_.refs_6_) | copy-start | bytes 1572868
  19.4 23.6 %copy-start.5 = (bf16[256,1024]{1,0:T(8,128)(2,1)}, bf16[256,1024]{1,0:T(8,128)(2,1)S(1)}, u32[]{:S(2)}) copy-start(bf16[256,1024]{1,0:T(8,128)(2,1)S(1)} %collective-permute-done.1.refs_5_.refs_7_) | copy-start | bytes 1572868
  19.4 14.5 %collective-permute-start.3 = (bf16[256,1024]{1,0:T(8,128)(2,1)S(1)}, bf16[256,1024]{1,0:T(8,128)(2,1)}, u32[]{:S(2)}, u32[]{:S(2)}) collective-permute-start(bf16[256,1024]{1,0:T(8,128)(2,1)S(1)} %collective-permute-done.refs_4_.refs_6_), channel_id=1, source_target_pairs={{0,32},{1,33},{2,34},{3,35},{4,36},{5,37},{6,38},{7,39},{8,40},{9,... | collective-permute-start | bytes 1572872 | tf_op jit(solution)/shard_map/ppermute | solution.py:45
  20.9 13.0 %collective-permute-start.4 = (bf16[256,1024]{1,0:T(8,128)(2,1)S(1)}, bf16[256,1024]{1,0:T(8,128)(2,1)}, u32[]{:S(2)}, u32[]{:S(2)}) collective-permute-start(bf16[256,1024]{1,0:T(8,128)(2,1)S(1)} %collective-permute-done.1.refs_5_.refs_7_), channel_id=1, source_target_pairs={{0,96},{1,97},{2,98},{3,99},{4,100},{5,101},{6,102},{7,103},{8,104... | collective-permute-start | bytes 1572872 | tf_op jit(solution)/shard_map/ppermute | solution.py:45
  22.7 12.6 %collective-permute-start.5 = (bf16[256,1024]{1,0:T(8,128)(2,1)S(1)}, bf16[256,1024]{1,0:T(8,128)(2,1)S(1)}, u32[]{:S(2)}, u32[]{:S(2)}) collective-permute-start(bf16[256,1024]{1,0:T(8,128)(2,1)S(1)} %get-tuple-element.82), channel_id=1, source_target_pairs={{0,16},{1,17},{2,18},{3,19},{4,20},{5,21},{6,22},{7,23},{8,24},{9,... | collective-permute-start | bytes 1572872 | tf_op jit(solution)/shard_map/ppermute | solution.py:45
  22.7 13.8 %collective-permute-start.6 = (bf16[256,1024]{1,0:T(8,128)(2,1)S(1)}, bf16[256,1024]{1,0:T(8,128)(2,1)S(1)}, u32[]{:S(2)}, u32[]{:S(2)}) collective-permute-start(bf16[256,1024]{1,0:T(8,128)(2,1)S(1)} %get-tuple-element.83), channel_id=1, source_target_pairs={{0,17},{1,16},{2,19},{3,18},{4,21},{5,20},{6,23},{7,22},{8,25},{9,... | collective-permute-start | bytes 1572872 | tf_op jit(solution)/shard_map/ppermute | solution.py:45
  36.5 19.0 %collective-permute-start.11 = (bf16[2,256,1024]{2,1,0:T(8,128)(2,1)S(1)}, bf16[2,256,1024]{2,1,0:T(8,128)(2,1)S(1)}, u32[]{:S(2)}, u32[]{:S(2)}) collective-permute-start(bf16[2,256,1024]{2,1,0:T(8,128)(2,1)S(1)} %pad_maximum_fusion), channel_id=1, source_target_pairs={{0,8},{1,9},{2,10},{3,11},{4,12},{5,13},{6,14},{7,15},{8,0},{9,1},... | collective-permute-start | bytes 3145736 | tf_op jit(solution)/shard_map/ppermute | solution.py:45
  36.5 15.7 %collective-permute-start.10 = (bf16[256,1024]{1,0:T(8,128)(2,1)S(1)}, bf16[256,1024]{1,0:T(8,128)(2,1)}, u32[]{:S(2)}, u32[]{:S(2)}) collective-permute-start(bf16[256,1024]{1,0:T(8,128)(2,1)S(1)} %collective-permute-done.refs_4_.refs_6_), channel_id=1, source_target_pairs={{0,17},{1,16},{2,19},{3,18},{4,21},{5,20},{6,23},{7,22},{8,25},{9,... | collective-permute-start | bytes 1572872 | tf_op jit(solution)/shard_map/ppermute | solution.py:45
  38.7 15.3 %collective-permute-start.7 = (bf16[256,1024]{1,0:T(8,128)(2,1)S(1)}, bf16[256,1024]{1,0:T(8,128)(2,1)S(1)}, u32[]{:S(2)}, u32[]{:S(2)}) collective-permute-start(bf16[256,1024]{1,0:T(8,128)(2,1)S(1)} %collective-permute-done.1.refs_5_.refs_7_), channel_id=1, source_target_pairs={{0,32},{1,33},{2,34},{3,35},{4,36},{5,37},{6,38},{7,39},{8,40},{9,... | collective-permute-start | bytes 1572872 | tf_op jit(solution)/shard_map/ppermute | solution.py:45
  39.0 15.0 %collective-permute-start.8 = (bf16[256,1024]{1,0:T(8,128)(2,1)S(1)}, bf16[256,1024]{1,0:T(8,128)(2,1)S(1)}, u32[]{:S(2)}, u32[]{:S(2)}) collective-permute-start(bf16[256,1024]{1,0:T(8,128)(2,1)S(1)} %collective-permute-done.refs_4_.refs_6_), channel_id=1, source_target_pairs={{0,96},{1,97},{2,98},{3,99},{4,100},{5,101},{6,102},{7,103},{8,104... | collective-permute-start | bytes 1572872 | tf_op jit(solution)/shard_map/ppermute | solution.py:45
  41.9 13.6 %collective-permute-start.9 = (bf16[256,1024]{1,0:T(8,128)(2,1)S(1)}, bf16[256,1024]{1,0:T(8,128)(2,1)}, u32[]{:S(2)}, u32[]{:S(2)}) collective-permute-start(bf16[256,1024]{1,0:T(8,128)(2,1)S(1)} %collective-permute-done.1.refs_5_.refs_7_), channel_id=1, source_target_pairs={{0,16},{1,17},{2,18},{3,19},{4,20},{5,21},{6,22},{7,23},{8,24},{9,... | collective-permute-start | bytes 1572872 | tf_op jit(solution)/shard_map/ppermute | solution.py:45
  55.5 19.2 %collective-permute-start.12 = (bf16[2,256,1024]{2,1,0:T(8,128)(2,1)}, bf16[2,256,1024]{2,1,0:T(8,128)(2,1)S(1)}, u32[]{:S(2)}, u32[]{:S(2)}) collective-permute-start(bf16[2,256,1024]{2,1,0:T(8,128)(2,1)} %pad_maximum_fusion.1), channel_id=1, source_target_pairs={{0,8},{1,9},{2,10},{3,11},{4,12},{5,13},{6,14},{7,15},{8,0},{9,1},... | collective-permute-start | bytes 3145736 | tf_op jit(solution)/shard_map/ppermute | solution.py:45
  55.6 19.0 %collective-permute-start.15 = (bf16[256,1024]{1,0:T(8,128)(2,1)}, bf16[256,1024]{1,0:T(8,128)(2,1)}, u32[]{:S(2)}, u32[]{:S(2)}) collective-permute-start(bf16[256,1024]{1,0:T(8,128)(2,1)} %collective-permute-done.3.refs_10_), channel_id=1, source_target_pairs={{0,32},{1,33},{2,34},{3,35},{4,36},{5,37},{6,38},{7,39},{8,40},{9,... | collective-permute-start | bytes 1572872 | tf_op jit(solution)/shard_map/ppermute | solution.py:45
  55.7 18.9 %collective-permute-start.16 = (bf16[256,1024]{1,0:T(8,128)(2,1)}, bf16[256,1024]{1,0:T(8,128)(2,1)}, u32[]{:S(2)}, u32[]{:S(2)}) collective-permute-start(bf16[256,1024]{1,0:T(8,128)(2,1)} %collective-permute-done.4.refs_9_), channel_id=1, source_target_pairs={{0,96},{1,97},{2,98},{3,99},{4,100},{5,101},{6,102},{7,103},{8,104... | collective-permute-start | bytes 1572872 | tf_op jit(solution)/shard_map/ppermute | solution.py:45
  58.9 15.7 %collective-permute-start.13 = (bf16[256,1024]{1,0:T(8,128)(2,1)}, bf16[256,1024]{1,0:T(8,128)(2,1)}, u32[]{:S(2)}, u32[]{:S(2)}) collective-permute-start(bf16[256,1024]{1,0:T(8,128)(2,1)} %collective-permute-done.9.refs_2_), channel_id=1, source_target_pairs={{0,8},{1,9},{2,10},{3,11},{4,12},{5,13},{6,14},{7,15},{8,0},{9,1},... | collective-permute-start | bytes 1572872 | tf_op jit(solution)/shard_map/ppermute | solution.py:45
  58.9 15.7 %collective-permute-start.14 = (bf16[256,1024]{1,0:T(8,128)(2,1)}, bf16[256,1024]{1,0:T(8,128)(2,1)}, u32[]{:S(2)}, u32[]{:S(2)}) collective-permute-start(bf16[256,1024]{1,0:T(8,128)(2,1)} %collective-permute-done.10.refs_3_), channel_id=1, source_target_pairs={{0,8},{1,9},{2,10},{3,11},{4,12},{5,13},{6,14},{7,15},{8,0},{9,1},... | collective-permute-start | bytes 1572872 | tf_op jit(solution)/shard_map/ppermute | solution.py:45
  95.3 30.4 %copy-start.2 = (bf16[2,1024,256]{2,1,0:T(8,128)(2,1)S(1)}, bf16[2,1024,256]{2,1,0:T(8,128)(2,1)}, u32[]{:S(2)}) copy-start(bf16[2,1024,256]{2,1,0:T(8,128)(2,1)} %get-tuple-element.133) | copy-start | bytes 3145732
  95.3 27.0 %collective-permute-start.17 = (bf16[2,1024,256]{2,1,0:T(8,128)(2,1)}, bf16[2,1024,256]{2,1,0:T(8,128)(2,1)}, u32[]{:S(2)}, u32[]{:S(2)}) collective-permute-start(bf16[2,1024,256]{2,1,0:T(8,128)(2,1)} %get-tuple-element.129), channel_id=1, source_target_pairs={{0,6},{1,7},{2,0},{3,1},{4,2},{5,3},{6,4},{7,5},{8,14},{9,15},{10,... | collective-permute-start | bytes 3145736 | tf_op jit(solution)/shard_map/ppermute | solution.py:45
  99.4 26.3 %collective-permute-start.18 = (bf16[2,1024,256]{2,1,0:T(8,128)(2,1)}, bf16[2,1024,256]{2,1,0:T(8,128)(2,1)}, u32[]{:S(2)}, u32[]{:S(2)}) collective-permute-start(bf16[2,1024,256]{2,1,0:T(8,128)(2,1)} %get-tuple-element.130), channel_id=1, source_target_pairs={{0,2},{1,3},{2,4},{3,5},{4,6},{5,7},{6,0},{7,1},{8,10},{9,11},{10,... | collective-permute-start | bytes 3145736 | tf_op jit(solution)/shard_map/ppermute | solution.py:45
  99.4 45.0 %all-to-all-start = ((bf16[16,64,1024]{2,1,0:T(8,128)(2,1)}), bf16[16,64,1024]{2,1,0:T(8,128)(2,1)}, u32[]{:S(2)}, u32[]{:S(2)}) async-start(bf16[16,64,1024]{2,1,0:T(8,128)(2,1)} %bitcast.65), calls=%async_computation | async-start | bytes 4194304 | tf_op jit(solution)/shard_map/all_to_all | solution.py:231
  103.8 38.7 %copy-start.3 = (bf16[2,1024,256]{2,1,0:T(8,128)(2,1)S(1)}, bf16[2,1024,256]{2,1,0:T(8,128)(2,1)}, u32[]{:S(2)}) copy-start(bf16[2,1024,256]{2,1,0:T(8,128)(2,1)} %get-tuple-element.126) | copy-start | bytes 3145732
  128.2 12.9 %collective-permute-start.19 = (bf16[1024,256]{1,0:T(8,128)(2,1)}, bf16[1024,256]{1,0:T(8,128)(2,1)S(1)}, u32[]{:S(2)}, u32[]{:S(2)}) collective-permute-start(bf16[1024,256]{1,0:T(8,128)(2,1)} %get-tuple-element.134), channel_id=1, source_target_pairs={{0,6},{1,7},{2,0},{3,1},{4,2},{5,3},{6,4},{7,5},{8,14},{9,15},{10,... | collective-permute-start | bytes 1572872 | tf_op jit(solution)/shard_map/ppermute | solution.py:45
  128.4 14.1 %collective-permute-start.20 = (bf16[1024,256]{1,0:T(8,128)(2,1)}, bf16[1024,256]{1,0:T(8,128)(2,1)S(1)}, u32[]{:S(2)}, u32[]{:S(2)}) collective-permute-start(bf16[1024,256]{1,0:T(8,128)(2,1)} %get-tuple-element.135), channel_id=1, source_target_pairs={{0,2},{1,3},{2,4},{3,5},{4,6},{5,7},{6,0},{7,1},{8,10},{9,11},{10,... | collective-permute-start | bytes 1572872 | tf_op jit(solution)/shard_map/ppermute | solution.py:45
  144.4 9.9 %collective-permute-start.21 = (bf16[512,256]{1,0:T(8,128)(2,1)S(1)}, bf16[512,256]{1,0:T(8,128)(2,1)S(1)}, u32[]{:S(2)}, u32[]{:S(2)}) collective-permute-start(bf16[512,256]{1,0:T(8,128)(2,1)S(1)} %pad_maximum_fusion.3), channel_id=1, source_target_pairs={{0,1},{1,17},{2,3},{3,19},{4,5},{5,21},{6,7},{7,23},{8,9},{9,25},{... | collective-permute-start | bytes 786440 | tf_op jit(solution)/shard_map/ppermute | solution.py:45
  145.2 9.5 %collective-permute-start.22 = (bf16[512,256]{1,0:T(8,128)(2,1)S(1)}, bf16[512,256]{1,0:T(8,128)(2,1)S(1)}, u32[]{:S(2)}, u32[]{:S(2)}) collective-permute-start(bf16[512,256]{1,0:T(8,128)(2,1)S(1)} %pad_maximum_fusion.4), channel_id=1, source_target_pairs={{0,9},{1,25},{2,11},{3,27},{4,13},{5,29},{6,15},{7,31},{8,1},{9,17... | collective-permute-start | bytes 786440 | tf_op jit(solution)/shard_map/ppermute | solution.py:45
  145.2 11.4 %collective-permute-start.23 = (bf16[512,256]{1,0:T(8,128)(2,1)S(1)}, bf16[512,256]{1,0:T(8,128)(2,1)S(1)}, u32[]{:S(2)}, u32[]{:S(2)}) collective-permute-start(bf16[512,256]{1,0:T(8,128)(2,1)S(1)} %pad_maximum_fusion.5), channel_id=1, source_target_pairs={{0,17},{1,1},{2,19},{3,3},{4,21},{5,5},{6,23},{7,7},{8,25},{9,9},{... | collective-permute-start | bytes 786440 | tf_op jit(solution)/shard_map/ppermute | solution.py:45
  149.3 13.8 %collective-permute-start.24 = (bf16[512,256]{1,0:T(8,128)(2,1)S(1)}, bf16[512,256]{1,0:T(8,128)(2,1)S(1)}, u32[]{:S(2)}, u32[]{:S(2)}) collective-permute-start(bf16[512,256]{1,0:T(8,128)(2,1)S(1)} %pad_maximum_fusion.6), channel_id=1, source_target_pairs={{0,25},{1,9},{2,27},{3,11},{4,29},{5,13},{6,31},{7,15},{8,17},{9,1... | collective-permute-start | bytes 786440 | tf_op jit(solution)/shard_map/ppermute | solution.py:45
  (8 other events, 57.0 us)

commit v7 on v6

--- a/solution.py
+++ b/solution.py
@@ -63,7 +63,7 @@
     return lax.optimization_barrier(results)
 
 
-def block_kernel(plan, sides, offsets, *refs):
+def block_kernel(plan, sides, *refs):
     place, refs = refs[0], refs[1:]
     n_in = plan["inputs"]
     inputs, refs = refs[:n_in], refs[n_in + plan["kept"] :]
@@ -71,6 +71,7 @@
     targets, refs = ((home, up, down, middle), (home, middle, up, down)), refs[4:]
     left, columns_in, result, left_sem, column_sem, out_sem = refs
     shift, high = place[0], place[1]
+    rows = columns_in.shape[2]
 
     def view(name):
         index, part = name
@@ -84,49 +85,41 @@
         for i, name in enumerate(names)
     ]
     lefts = [
-        pltpu.make_async_copy(view(name), left.at[k, i], left_sem.at[2 * k + i])
+        pltpu.make_async_copy(
+            view(name),
+            left.at[k // 4, i, pl.ds(k % 4 * rows, rows)],
+            left_sem.at[2 * k + i],
+        )
         for k, names in enumerate(sides)
         for i, name in enumerate(names)
     ]
-    for copy in rights[:2] + lefts[:2] + rights[2:] + lefts[2:]:
+    for copy in rights[:2] + lefts[:8] + rights[2:] + lefts[8:]:
         copy.start()
-    for copy in rights:
-        copy.wait()
-    rows = columns_in.shape[2]
-    n_offsets = len(offsets)
     outs = []
-
-    def multiply(step, carry):
-        k, n = step // n_offsets, step % n_offsets
-
-        @pl.when(n == 0)
-        def _():
+    arrived = set()
+    for side, (cc, wanted) in enumerate(plan["sides"]):
+        for copy in lefts[8 * side : 8 * side + 8]:
+            copy.wait()
+        for n, dx in wanted:
+            if n not in arrived:
+                arrived.add(n)
+                for copy in rights[2 * n : 2 * n + 2]:
+                    copy.wait()
+            total = None
             for i in range(2):
-                piece = left.at[k, i]
-                pltpu.make_async_copy(piece, piece, left_sem.at[2 * k + i]).wait()
-
-        total = sum(
-            lax.dot_general(
-                left[k, i],
-                columns_in[n, i],
-                (((1,), (1,)), ((), ())),
-                preferred_element_type=jnp.float32,
-            )
-            for i in range(2)
-        )
-        place_in = pl.ds(pl.multiple_of(k % 4 * rows, rows), rows)
-        result[k // 4, n, place_in, :] = total.astype(jnp.bfloat16)
-        return carry
-
-    for side, cc in enumerate(plan["sides"]):
-        lax.fori_loop(4 * n_offsets * side, 4 * n_offsets * (side + 1), multiply, 0)
-        for n, dx in enumerate(offsets):
+                term = lax.dot_general(
+                    left[side, i],
+                    columns_in[n, i],
+                    (((1,), (1,)), ((), ())),
+                    preferred_element_type=jnp.float32,
+                )
+                total = term if total is None else total + term
+            slot = len(outs) // 4
+            result[slot] = total.astype(jnp.bfloat16)
             dz = (shift + dx) % 4
             for d in range(4):
                 copy = pltpu.make_async_copy(
-                    result.at[side, n],
-                    targets[cc][d].at[cc],
-                    out_sem.at[side * n_offsets + n],
+                    result.at[slot], targets[cc][d].at[cc], out_sem.at[slot]
                 )
                 outs.append((dz == d, copy))
                 pl.when(dz == d)(copy.start)
@@ -145,26 +138,29 @@
         inputs.append(array)
         return len(inputs) - 1, part
 
-    groups = [[enter(piece) for piece in pair] for side in sides.values() for pair in side]
+    groups = [[enter(piece) for piece in pair] for side, _ in sides.values() for pair in side]
     names = [[enter(piece) for piece in pair] for pair in blocks.values()]
     half, items = inputs[0].shape[-2:]
-    plan = {"inputs": len(inputs), "kept": len(kept), "sides": tuple(sides), "blocks": names}
+    order = list(blocks)
+    wanted = tuple((cc, tuple((order.index(dx), dx) for dx in dxs)) for cc, (_, dxs) in sides.items())
+    n_results = sum(len(dxs) for _, dxs in wanted)
+    plan = {"inputs": len(inputs), "kept": len(kept), "sides": wanted, "blocks": names}
     outside = pl.BlockSpec(memory_space=pltpu.HBM)
     n_blocks = len(blocks)
     return pl.pallas_call(
-        functools.partial(block_kernel, plan, groups, tuple(blocks)),
+        functools.partial(block_kernel, plan, groups),
         out_shape=[jax.ShapeDtypeStruct((2, 4 * half, half), jnp.bfloat16)] * 4,
         in_specs=[pl.BlockSpec(memory_space=pltpu.SMEM)]
         + [outside] * (len(inputs) + len(kept)),
         out_specs=[outside] * 4,
         input_output_aliases={1 + len(inputs) + n: n for n in range(len(kept))},
         scratch_shapes=[
-            pltpu.VMEM((len(groups), 2, half, items), jnp.bfloat16),
+            pltpu.VMEM((len(sides), 2, 4 * half, items), jnp.bfloat16),
             pltpu.VMEM((n_blocks, 2, half, items), jnp.bfloat16),
-            pltpu.VMEM((len(sides), n_blocks, 4 * half, half), jnp.bfloat16),
+            pltpu.VMEM((n_results, 4 * half, half), jnp.bfloat16),
             pltpu.SemaphoreType.DMA((2 * len(groups),)),
             pltpu.SemaphoreType.DMA((2 * n_blocks,)),
-            pltpu.SemaphoreType.DMA((len(sides) * n_blocks,)),
+            pltpu.SemaphoreType.DMA((n_results,)),
         ],
         compiler_params=pltpu.CompilerParams(vmem_limit_bytes=60 * 1024 * 1024),
         cost_estimate=pl.CostEstimate(
@@ -196,7 +192,8 @@
             (far, X_STEP[3]),
             (outer, NEAR),
             (inner, FAR),
-        ]
+        ],
+        (share,),
     )
     below_f, above_n, two0, two1, right_c = together(
         [(far, X_STEP[1]), (near, X_STEP[3]), (far, NEAR), (near, FAR), (right, CORE)],
@@ -220,11 +217,9 @@
         ((rim_c, 0), (rim_c, 1)),
     )
     early = {0: (near, far), 1: (above_n, above_f), 3: (below_n, below_f)}
-    kept = block_product(place, {0: side}, early)
-    kept = block_product(place, {1: side_c}, early, kept)
-    across, kept = lax.optimization_barrier((across, kept))
+    kept = block_product(place, {0: (side, (0, 1, 3))}, early)
     home, up, down, middle = block_product(
-        place, {0: side, 1: side_c}, {2: tuple(across)}, kept
+        place, {1: (side_c, (0, 1, 3, 2)), 0: (side, (2,))}, {**early, 2: tuple(across)}, kept
     )
 
     share, down, up = lax.optimization_barrier((share, down, up))

time: 167 us -> 161 us (0.964)
  Pallas kernels: 30.3 us -> 25.9 us
  other arithmetic: 10.4 us -> 13.1 us
  local copies, waits for them, and re-layouts: 4.21 us -> 2.27 us
    pallas_call x3 -> x2, Pallas kernels: 30.3 us -> 25.9 us  [block_product(): pl.pallas_call(functools.partial(block_kernel, plan, groups), out_shape=[...]
    concatenate x4, other arithmetic: 0.08 us -> 2.17 us  [on_device(): value = jnp.concatenate([pick(chosen, yh ^ i) for i in range(2)], 0)]
    unnamed x28, local copies, waits for them, and re-layouts: 2.39 us -> 0.4 us
  transfers between devices with their start and end apart: 26 -> 26, of which waited for: 15 -> 17; matrix products, arithmetic and copies ran while one was open for 8% -> 8% of each run, Pallas kernels for 6% -> 7%
where the time goes in v7:
time: 161 us
  waiting for transfers between devices  79.6 us (49%)
  starting transfers between devices  36.4 us (23%)
  Pallas kernels  25.9 us (16%)
  other arithmetic  13.1 us (8%)
  matrix products  2.57 us (2%)
  local copies, waits for them, and re-layouts  2.27 us (1%)
    ppermute x25, waiting for transfers between devices, send(): return lax.ppermute(value, AXES, pairs)  79.6 us
    ppermute x25, starting transfers between devices, send(): return lax.ppermute(value, AXES, pairs)  32.2 us
    pallas_call x2, Pallas kernels, block_product(): pl.pallas_call(functools.partial(block_kernel, plan, groups), out_shape=[...  25.9 us
    convert_element_type x2, other arithmetic, narrow(): return value.astype(jnp.bfloat16)  4.99 us
    all_to_all x1, starting transfers between devices, on_device(): shares = lax.all_to_all(share, 'feat', 0, 0)  4.27 us
  transfers between devices with their start and end apart: 26, of which 17 were waited for; matrix products, arithmetic and copies ran while one was open for 8% of the time, Pallas kernels for 7%

profile of v7, /device:TPU:0, one launch (start us, length us, event | category | flops | bytes accessed | tf_op | source)
XLA Modules:
  0.0 160.8 jit_solution(4830937082792461955)
XLA Ops:
  0.7 1.6 %copy.9 = bf16[512,1024]{1,0:T(8,128)(2,1)S(1)} copy(bf16[512,1024]{0,1:T(8,128)(2,1)} %bitcast.68) | data formatting | bytes 2097152 | tf_op jit(solution)/shard_map/transpose | solution.py:181
  2.5 1.7 %collective-permute-start = (bf16[256,1024]{1,0:T(8,128)(2,1)S(1)}, bf16[256,1024]{1,0:T(8,128)(2,1)S(1)}, u32[]{:S(2)}, u32[]{:S(2)}) collective-permute-start(bf16[256,1024]{1,0:T(8,128)(2,1)S(1)} %get-tuple-element.74), channel_id=1, source_target_pairs={{0,16},{1,17},{2,18},{3,19},{4,20},{5,21},{6,22},{7,23},{8,24},{9,... | collective-permute-start | bytes 1572872 | tf_op jit(solution)/shard_map/ppermute | solution.py:45
  4.2 2.2 %collective-permute-start.1 = (bf16[256,1024]{1,0:T(8,128)(2,1)S(1)}, bf16[256,1024]{1,0:T(8,128)(2,1)S(1)}, u32[]{:S(2)}, u32[]{:S(2)}) collective-permute-start(bf16[256,1024]{1,0:T(8,128)(2,1)S(1)} %get-tuple-element.73), channel_id=1, source_target_pairs={{0,17},{1,16},{2,19},{3,18},{4,21},{5,20},{6,23},{7,22},{8,25},{9,... | collective-permute-start | bytes 1572872 | tf_op jit(solution)/shard_map/ppermute | solution.py:45
  6.4 2.6 %convolution_convert_fusion = bf16[1024,1024]{1,0:T(8,128)(2,1)} fusion(bf16[1024,512]{1,0:T(8,128)(2,1)S(1)} %copy-done.13, bf16[512,1024]{1,0:T(8,128)(2,1)S(1)} %copy-done), kind=kOutput, calls=%fused_computation.1 | convolution fusion | flops 1074790400 | bytes 4194304 | tf_op jit(solution)/shard_map/dot_general | solution.py:185
  9.0 7.8 %collective-permute-done.refs_4_.refs_9_ = bf16[256,1024]{1,0:T(8,128)(2,1)S(1)} collective-permute-done((bf16[256,1024]{1,0:T(8,128)(2,1)S(1)}, bf16[256,1024]{1,0:T(8,128)(2,1)S(1)}, u32[]{:S(2)}, u32[]{:S(2)}) %collective-permute-start) | collective-permute-done | bytes 524320 | tf_op jit(solution)/shard_map/ppermute | solution.py:45
  16.9 2.6 %collective-permute-done.1.refs_5_.refs_10_ = bf16[256,1024]{1,0:T(8,128)(2,1)S(1)} collective-permute-done((bf16[256,1024]{1,0:T(8,128)(2,1)S(1)}, bf16[256,1024]{1,0:T(8,128)(2,1)S(1)}, u32[]{:S(2)}, u32[]{:S(2)}) %collective-permute-start.1) | collective-permute-done | bytes 524320 | tf_op jit(solution)/shard_map/ppermute | solution.py:45
  19.4 1.6 collective-permute-start.3
  21.0 1.7 %collective-permute-start.4 = (bf16[256,1024]{1,0:T(8,128)(2,1)S(1)}, bf16[256,1024]{1,0:T(8,128)(2,1)S(1)}, u32[]{:S(2)}, u32[]{:S(2)}) collective-permute-start(bf16[256,1024]{1,0:T(8,128)(2,1)S(1)} %collective-permute-done.1.refs_5_.refs_10_), channel_id=1, source_target_pairs={{0,96},{1,97},{2,98},{3,99},{4,100},{5,101},{6,102},{7,103},{8,104... | collective-permute-start | bytes 1572872 | tf_op jit(solution)/shard_map/ppermute | solution.py:45
  22.8 2.3 %collective-permute-start.6 = (bf16[256,1024]{1,0:T(8,128)(2,1)S(1)}, bf16[256,1024]{1,0:T(8,128)(2,1)S(1)}, u32[]{:S(2)}, u32[]{:S(2)}) collective-permute-start(bf16[256,1024]{1,0:T(8,128)(2,1)S(1)} %get-tuple-element.74), channel_id=1, source_target_pairs={{0,17},{1,16},{2,19},{3,18},{4,21},{5,20},{6,23},{7,22},{8,25},{9,... | collective-permute-start | bytes 1572872 | tf_op jit(solution)/shard_map/ppermute | solution.py:45
  25.1 8.8 %collective-permute-done.3.refs_10_.refs_15_ = bf16[256,1024]{1,0:T(8,128)(2,1)S(1)} collective-permute-done((bf16[256,1024]{1,0:T(8,128)(2,1)S(1)}, bf16[256,1024]{1,0:T(8,128)(2,1)S(1)}, u32[]{:S(2)}, u32[]{:S(2)}) %collective-permute-start.3) | collective-permute-done | bytes 524320 | tf_op jit(solution)/shard_map/ppermute | solution.py:45
  36.6 2.2 %collective-permute-start.10 = (bf16[256,1024]{1,0:T(8,128)(2,1)S(1)}, bf16[256,1024]{1,0:T(8,128)(2,1)}, u32[]{:S(2)}, u32[]{:S(2)}) collective-permute-start(bf16[256,1024]{1,0:T(8,128)(2,1)S(1)} %collective-permute-done.refs_4_.refs_9_), channel_id=1, source_target_pairs={{0,17},{1,16},{2,19},{3,18},{4,21},{5,20},{6,23},{7,22},{8,25},{9,... | collective-permute-start | bytes 1572872 | tf_op jit(solution)/shard_map/ppermute | solution.py:45
  39.0 3.0 %collective-permute-start.8 = (bf16[256,1024]{1,0:T(8,128)(2,1)S(1)}, bf16[256,1024]{1,0:T(8,128)(2,1)S(1)}, u32[]{:S(2)}, u32[]{:S(2)}) collective-permute-start(bf16[256,1024]{1,0:T(8,128)(2,1)S(1)} %collective-permute-done.refs_4_.refs_9_), channel_id=1, source_target_pairs={{0,96},{1,97},{2,98},{3,99},{4,100},{5,101},{6,102},{7,103},{8,104... | collective-permute-start | bytes 1572872 | tf_op jit(solution)/shard_map/ppermute | solution.py:45
  43.1 9.2 %collective-permute-done.10.refs_3_.refs_8_ = bf16[256,1024]{1,0:T(8,128)(2,1)} collective-permute-done((bf16[256,1024]{1,0:T(8,128)(2,1)S(1)}, bf16[256,1024]{1,0:T(8,128)(2,1)}, u32[]{:S(2)}, u32[]{:S(2)}) %collective-permute-start.10) | collective-permute-done | bytes 524320 | tf_op jit(solution)/shard_map/ppermute | solution.py:45
  52.2 1.8 %collective-permute-done.7.refs_11_.refs_16_ = bf16[256,1024]{1,0:T(8,128)(2,1)S(1)} collective-permute-done((bf16[256,1024]{1,0:T(8,128)(2,1)S(1)}, bf16[256,1024]{1,0:T(8,128)(2,1)S(1)}, u32[]{:S(2)}, u32[]{:S(2)}) %collective-permute-start.7) | collective-permute-done | bytes 524320 | tf_op jit(solution)/shard_map/ppermute | solution.py:45
  54.0 1.6 collective-permute-done.9.refs_2_.refs_7_
  55.7 3.2 %collective-permute-start.16 = (bf16[256,1024]{1,0:T(8,128)(2,1)S(1)}, bf16[256,1024]{1,0:T(8,128)(2,1)}, u32[]{:S(2)}, u32[]{:S(2)}) collective-permute-start(bf16[256,1024]{1,0:T(8,128)(2,1)S(1)} %collective-permute-done.4.refs_9_.refs_14_), channel_id=1, source_target_pairs={{0,96},{1,97},{2,98},{3,99},{4,100},{5,101},{6,102},{7,103},{8,104... | collective-permute-start | bytes 1572872 | tf_op jit(solution)/shard_map/ppermute | solution.py:45
  60.0 10.6 %shard_map.50 = (bf16[2,1024,256]{2,1,0:T(8,128)(2,1)}, bf16[2,1024,256]{2,1,0:T(8,128)(2,1)}, bf16[2,1024,256]{2,1,0:T(8,128)(2,1)}, bf16[2,1024,256]{2,1,0:T(8,128)(2,1)}) custom-call(s32[2]{0:T(128)} %pad_add_fusion.refs_0_, bf16[2,256,1024]{2,1,0:T(8,128)(2,1)} %bitcast.59, bf16[256,1024]{1,0:T(8,128)(2,1)} %collective-permute-done.9.refs_2_.refs_7_, ...), custom_call_target="tpu_custom_call" | custom-call | flops 65536 | bytes 262144 | tf_op jit(solution)/shard_map/pallas_call | solution.py:150
  71.3 15.4 %shard_map.51 = (bf16[2,1024,256]{2,1,0:T(8,128)(2,1)}, bf16[2,1024,256]{2,1,0:T(8,128)(2,1)}, bf16[2,1024,256]{2,1,0:T(8,128)(2,1)}, bf16[2,1024,256]{2,1,0:T(8,128)(2,1)}) custom-call(s32[2]{0:T(128)} %pad_add_fusion.refs_0_, bf16[2,256,1024]{2,1,0:T(8,128)(2,1)} %copy-done.11, ...), custom_call_target="tpu_custom_call", output_to_operand_aliasing={{0}: (19, {}), {1}: (20, {}), {2}: (21, {}), {3}: (22, {})} | custom-call | flops 65536 | bytes 262144 | tf_op jit(solution)/shard_map/pallas_call | solution.py:150
  86.7 4.2 %collective-permute-start.17 = (bf16[2,1024,256]{2,1,0:T(8,128)(2,1)}, bf16[2,1024,256]{2,1,0:T(8,128)(2,1)}, u32[]{:S(2)}, u32[]{:S(2)}) collective-permute-start(bf16[2,1024,256]{2,1,0:T(8,128)(2,1)} %get-tuple-element.109), channel_id=1, source_target_pairs={{0,6},{1,7},{2,0},{3,1},{4,2},{5,3},{6,4},{7,5},{8,14},{9,15},{10,... | collective-permute-start | bytes 3145736 | tf_op jit(solution)/shard_map/ppermute | solution.py:45
  90.8 4.3 %all-to-all-start = ((bf16[16,64,1024]{2,1,0:T(8,128)(2,1)}), bf16[16,64,1024]{2,1,0:T(8,128)(2,1)S(1)}, u32[]{:S(2)}, u32[]{:S(2)}) async-start(bf16[16,64,1024]{2,1,0:T(8,128)(2,1)} %bitcast.65), calls=%async_computation | async-start | bytes 4194304 | tf_op jit(solution)/shard_map/all_to_all | solution.py:226
  95.1 18.3 %collective-permute-done.17 = bf16[2,1024,256]{2,1,0:T(8,128)(2,1)} collective-permute-done((bf16[2,1024,256]{2,1,0:T(8,128)(2,1)}, bf16[2,1024,256]{2,1,0:T(8,128)(2,1)}, u32[]{:S(2)}, u32[]{:S(2)}) %collective-permute-start.17) | collective-permute-done | bytes 1048608 | tf_op jit(solution)/shard_map/ppermute | solution.py:45
  113.4 3.4 %collective-permute-done.18 = bf16[2,1024,256]{2,1,0:T(8,128)(2,1)} collective-permute-done((bf16[2,1024,256]{2,1,0:T(8,128)(2,1)}, bf16[2,1024,256]{2,1,0:T(8,128)(2,1)}, u32[]{:S(2)}, u32[]{:S(2)}) %collective-permute-start.18) | collective-permute-done | bytes 1048608 | tf_op jit(solution)/shard_map/ppermute | solution.py:45
  116.8 2.8 %fusion.3 = (bf16[1024,256]{1,0:T(8,128)(2,1)}, bf16[1024,256]{1,0:T(8,128)(2,1)}) fusion(bf16[2,1024,256]{2,1,0:T(8,128)(2,1)} %get-tuple-element.113, bf16[2,1024,256]{2,1,0:T(8,128)(2,1)} %collective-permute-done.18, bf16[2,1024,256]{2,1,0:T(8,128)(2,1)} %collective-permute-done.17), kind=kLoop, calls=%fused_computation.12 | loop fusion | flops 2097152 | bytes 3145728 | tf_op jit(solution)/shard_map/convert_element_type | solution.py:57
  119.8 1.7 %collective-permute-start.20 = (bf16[1024,256]{1,0:T(8,128)(2,1)}, bf16[1024,256]{1,0:T(8,128)(2,1)}, u32[]{:S(2)}, u32[]{:S(2)}) collective-permute-start(bf16[1024,256]{1,0:T(8,128)(2,1)} %get-tuple-element.115), channel_id=1, source_target_pairs={{0,2},{1,3},{2,4},{3,5},{4,6},{5,7},{6,0},{7,1},{8,10},{9,11},{10,... | collective-permute-start | bytes 1572872 | tf_op jit(solution)/shard_map/ppermute | solution.py:45
  121.6 10.6 %collective-permute-done.19 = bf16[1024,256]{1,0:T(8,128)(2,1)} collective-permute-done((bf16[1024,256]{1,0:T(8,128)(2,1)}, bf16[1024,256]{1,0:T(8,128)(2,1)}, u32[]{:S(2)}, u32[]{:S(2)}) %collective-permute-start.19) | collective-permute-done | bytes 524320 | tf_op jit(solution)/shard_map/ppermute | solution.py:45
  132.2 1.5 collective-permute-done.20
  133.7 2.2 %fusion = (bf16[1024,256]{1,0:T(8,128)(2,1)S(1)}, bf16[1024,256]{1,0:T(8,128)(2,1)S(1)}) fusion(bf16[1024,256]{1,0:T(8,128)(2,1)} %collective-permute-done.20, bf16[2,1024,256]{2,1,0:T(8,128)(2,1)} %collective-permute-done.17, bf16[2,1024,256]{2,1,0:T(8,128)(2,1)} %get-tuple-element.106, bf16[1024,256]{1,0:T(8,128)(2,1)} %collective-permute-done.19, ...), kind=kLoop, calls=%fused_computation.6 | loop fusion | flops 3145728 | bytes 4194304 | tf_op jit(solution)/shard_map/convert_element_type | solution.py:57
  139.0 4.1 %collective-permute-start.23 = (bf16[512,256]{1,0:T(8,128)(2,1)}, bf16[512,256]{1,0:T(8,128)(2,1)}, u32[]{:S(2)}, u32[]{:S(2)}) collective-permute-start(bf16[512,256]{1,0:T(8,128)(2,1)} %pad_maximum_fusion.5), channel_id=1, source_target_pairs={{0,17},{1,1},{2,19},{3,3},{4,21},{5,5},{6,23},{7,7},{8,25},{9,9},{... | collective-permute-start | bytes 786440 | tf_op jit(solution)/shard_map/ppermute | solution.py:45
  143.1 2.3 %collective-permute-start.24 = (bf16[512,256]{1,0:T(8,128)(2,1)S(1)}, bf16[512,256]{1,0:T(8,128)(2,1)}, u32[]{:S(2)}, u32[]{:S(2)}) collective-permute-start(bf16[512,256]{1,0:T(8,128)(2,1)S(1)} %pad_maximum_fusion.6), channel_id=1, source_target_pairs={{0,25},{1,9},{2,27},{3,11},{4,29},{5,13},{6,31},{7,15},{8,17},{9,1... | collective-permute-start | bytes 786440 | tf_op jit(solution)/shard_map/ppermute | solution.py:45
  148.8 1.9 %collective-permute-done.23 = bf16[512,256]{1,0:T(8,128)(2,1)} collective-permute-done((bf16[512,256]{1,0:T(8,128)(2,1)}, bf16[512,256]{1,0:T(8,128)(2,1)}, u32[]{:S(2)}, u32[]{:S(2)}) %collective-permute-start.23) | collective-permute-done | bytes 262176 | tf_op jit(solution)/shard_map/ppermute | solution.py:45
  150.7 6.5 %collective-permute-done.24 = bf16[512,256]{1,0:T(8,128)(2,1)} collective-permute-done((bf16[512,256]{1,0:T(8,128)(2,1)S(1)}, bf16[512,256]{1,0:T(8,128)(2,1)}, u32[]{:S(2)}, u32[]{:S(2)}) %collective-permute-start.24) | collective-permute-done | bytes 262176 | tf_op jit(solution)/shard_map/ppermute | solution.py:45
  159.1 1.7 %multiply_add_fusion = f32[512,1024]{1,0:T(8,128)} fusion(f32[512,1024]{1,0:T(8,128)S(1)} %copy-done.10, bf16[512,256]{1,0:T(8,128)(2,1)S(1)} %get-tuple-element.129, bf16[512,256]{1,0:T(8,128)(2,1)S(1)} %get-tuple-element.130, bf16[512,256]{1,0:T(8,128)(2,1)S(1)} %get-tuple-element.131, bf16[512,256]{1,0:T(8,128)(2,1)S(1)} %get-tuple-element.128), kind=kLoop, calls=%fused_computation | loop fusion | flops 5767168 | bytes 5242880 | tf_op jit(solution)/shard_map/add | solution.py:252
  (67 shorter events, 14.9 us)
Async XLA Ops:
  2.4 17.0 %collective-permute-start.2 = (bf16[2,256,1024]{2,1,0:T(8,128)(2,1)S(1)}, bf16[2,256,1024]{2,1,0:T(8,128)(2,1)S(1)}, u32[]{:S(2)}, u32[]{:S(2)}) collective-permute-start(bf16[2,256,1024]{2,1,0:T(8,128)(2,1)S(1)} %bitcast.58), channel_id=1, source_target_pairs={{0,8},{1,9},{2,10},{3,11},{4,12},{5,13},{6,14},{7,15},{8,0},{9,1},... | collective-permute-start | bytes 3145736 | tf_op jit(solution)/shard_map/ppermute | solution.py:45
  2.5 14.3 %collective-permute-start = (bf16[256,1024]{1,0:T(8,128)(2,1)S(1)}, bf16[256,1024]{1,0:T(8,128)(2,1)S(1)}, u32[]{:S(2)}, u32[]{:S(2)}) collective-permute-start(bf16[256,1024]{1,0:T(8,128)(2,1)S(1)} %get-tuple-element.74), channel_id=1, source_target_pairs={{0,16},{1,17},{2,18},{3,19},{4,20},{5,21},{6,22},{7,23},{8,24},{9,... | collective-permute-start | bytes 1572872 | tf_op jit(solution)/shard_map/ppermute | solution.py:45
  4.2 15.2 %collective-permute-start.1 = (bf16[256,1024]{1,0:T(8,128)(2,1)S(1)}, bf16[256,1024]{1,0:T(8,128)(2,1)S(1)}, u32[]{:S(2)}, u32[]{:S(2)}) collective-permute-start(bf16[256,1024]{1,0:T(8,128)(2,1)S(1)} %get-tuple-element.73), channel_id=1, source_target_pairs={{0,17},{1,16},{2,19},{3,18},{4,21},{5,20},{6,23},{7,22},{8,25},{9,... | collective-permute-start | bytes 1572872 | tf_op jit(solution)/shard_map/ppermute | solution.py:45
  16.9 26.2 %copy-start.2 = (bf16[256,1024]{1,0:T(8,128)(2,1)}, bf16[256,1024]{1,0:T(8,128)(2,1)S(1)}, u32[]{:S(2)}) copy-start(bf16[256,1024]{1,0:T(8,128)(2,1)S(1)} %collective-permute-done.refs_4_.refs_9_) | copy-start | bytes 1572868
  19.4 23.6 %copy-start.3 = (bf16[256,1024]{1,0:T(8,128)(2,1)}, bf16[256,1024]{1,0:T(8,128)(2,1)S(1)}, u32[]{:S(2)}) copy-start(bf16[256,1024]{1,0:T(8,128)(2,1)S(1)} %collective-permute-done.1.refs_5_.refs_10_) | copy-start | bytes 1572868
  19.4 23.6 %copy-start.11 = (bf16[2,256,1024]{2,1,0:T(8,128)(2,1)}, bf16[2,256,1024]{2,1,0:T(8,128)(2,1)S(1)}, u32[]{:S(2)}) copy-start(bf16[2,256,1024]{2,1,0:T(8,128)(2,1)S(1)} %collective-permute-done.2.refs_1_) | copy-start | bytes 3145732
  19.4 14.4 %collective-permute-start.3 = (bf16[256,1024]{1,0:T(8,128)(2,1)S(1)}, bf16[256,1024]{1,0:T(8,128)(2,1)S(1)}, u32[]{:S(2)}, u32[]{:S(2)}) collective-permute-start(bf16[256,1024]{1,0:T(8,128)(2,1)S(1)} %collective-permute-done.refs_4_.refs_9_), channel_id=1, source_target_pairs={{0,32},{1,33},{2,34},{3,35},{4,36},{5,37},{6,38},{7,39},{8,40},{9,... | collective-permute-start | bytes 1572872 | tf_op jit(solution)/shard_map/ppermute | solution.py:45
  21.0 12.9 %collective-permute-start.4 = (bf16[256,1024]{1,0:T(8,128)(2,1)S(1)}, bf16[256,1024]{1,0:T(8,128)(2,1)S(1)}, u32[]{:S(2)}, u32[]{:S(2)}) collective-permute-start(bf16[256,1024]{1,0:T(8,128)(2,1)S(1)} %collective-permute-done.1.refs_5_.refs_10_), channel_id=1, source_target_pairs={{0,96},{1,97},{2,98},{3,99},{4,100},{5,101},{6,102},{7,103},{8,104... | collective-permute-start | bytes 1572872 | tf_op jit(solution)/shard_map/ppermute | solution.py:45
  22.8 12.6 %collective-permute-start.5 = (bf16[256,1024]{1,0:T(8,128)(2,1)S(1)}, bf16[256,1024]{1,0:T(8,128)(2,1)S(1)}, u32[]{:S(2)}, u32[]{:S(2)}) collective-permute-start(bf16[256,1024]{1,0:T(8,128)(2,1)S(1)} %get-tuple-element.73), channel_id=1, source_target_pairs={{0,16},{1,17},{2,18},{3,19},{4,20},{5,21},{6,22},{7,23},{8,24},{9,... | collective-permute-start | bytes 1572872 | tf_op jit(solution)/shard_map/ppermute | solution.py:45
  22.8 13.8 %collective-permute-start.6 = (bf16[256,1024]{1,0:T(8,128)(2,1)S(1)}, bf16[256,1024]{1,0:T(8,128)(2,1)S(1)}, u32[]{:S(2)}, u32[]{:S(2)}) collective-permute-start(bf16[256,1024]{1,0:T(8,128)(2,1)S(1)} %get-tuple-element.74), channel_id=1, source_target_pairs={{0,17},{1,16},{2,19},{3,18},{4,21},{5,20},{6,23},{7,22},{8,25},{9,... | collective-permute-start | bytes 1572872 | tf_op jit(solution)/shard_map/ppermute | solution.py:45
  33.9 26.1 %copy-start.6 = (bf16[256,1024]{1,0:T(8,128)(2,1)}, bf16[256,1024]{1,0:T(8,128)(2,1)S(1)}, u32[]{:S(2)}) copy-start(bf16[256,1024]{1,0:T(8,128)(2,1)S(1)} %collective-permute-done.3.refs_10_.refs_15_) | copy-start | bytes 1572868
  33.9 26.1 %copy-start.7 = (bf16[256,1024]{1,0:T(8,128)(2,1)}, bf16[256,1024]{1,0:T(8,128)(2,1)S(1)}, u32[]{:S(2)}) copy-start(bf16[256,1024]{1,0:T(8,128)(2,1)S(1)} %collective-permute-done.4.refs_9_.refs_14_) | copy-start | bytes 1572868
  35.3 24.6 %copy-start.4 = (bf16[256,1024]{1,0:T(8,128)(2,1)}, bf16[256,1024]{1,0:T(8,128)(2,1)S(1)}, u32[]{:S(2)}) copy-start(bf16[256,1024]{1,0:T(8,128)(2,1)S(1)} %collective-permute-done.5.refs_6_.refs_11_) | copy-start | bytes 1572868
  36.6 19.0 %collective-permute-start.11 = (bf16[2,256,1024]{2,1,0:T(8,128)(2,1)S(1)}, bf16[2,256,1024]{2,1,0:T(8,128)(2,1)S(1)}, u32[]{:S(2)}, u32[]{:S(2)}) collective-permute-start(bf16[2,256,1024]{2,1,0:T(8,128)(2,1)S(1)} %pad_maximum_fusion.1), channel_id=1, source_target_pairs={{0,8},{1,9},{2,10},{3,11},{4,12},{5,13},{6,14},{7,15},{8,0},{9,1},... | collective-permute-start | bytes 3145736 | tf_op jit(solution)/shard_map/ppermute | solution.py:45
  36.6 15.7 %collective-permute-start.10 = (bf16[256,1024]{1,0:T(8,128)(2,1)S(1)}, bf16[256,1024]{1,0:T(8,128)(2,1)}, u32[]{:S(2)}, u32[]{:S(2)}) collective-permute-start(bf16[256,1024]{1,0:T(8,128)(2,1)S(1)} %collective-permute-done.refs_4_.refs_9_), channel_id=1, source_target_pairs={{0,17},{1,16},{2,19},{3,18},{4,21},{5,20},{6,23},{7,22},{8,25},{9,... | collective-permute-start | bytes 1572872 | tf_op jit(solution)/shard_map/ppermute | solution.py:45
  38.7 15.3 %collective-permute-start.7 = (bf16[256,1024]{1,0:T(8,128)(2,1)S(1)}, bf16[256,1024]{1,0:T(8,128)(2,1)S(1)}, u32[]{:S(2)}, u32[]{:S(2)}) collective-permute-start(bf16[256,1024]{1,0:T(8,128)(2,1)S(1)} %collective-permute-done.1.refs_5_.refs_10_), channel_id=1, source_target_pairs={{0,32},{1,33},{2,34},{3,35},{4,36},{5,37},{6,38},{7,39},{8,40},{9,... | collective-permute-start | bytes 1572872 | tf_op jit(solution)/shard_map/ppermute | solution.py:45
  39.0 15.0 %collective-permute-start.8 = (bf16[256,1024]{1,0:T(8,128)(2,1)S(1)}, bf16[256,1024]{1,0:T(8,128)(2,1)S(1)}, u32[]{:S(2)}, u32[]{:S(2)}) collective-permute-start(bf16[256,1024]{1,0:T(8,128)(2,1)S(1)} %collective-permute-done.refs_4_.refs_9_), channel_id=1, source_target_pairs={{0,96},{1,97},{2,98},{3,99},{4,100},{5,101},{6,102},{7,103},{8,104... | collective-permute-start | bytes 1572872 | tf_op jit(solution)/shard_map/ppermute | solution.py:45
  42.0 13.6 %collective-permute-start.9 = (bf16[256,1024]{1,0:T(8,128)(2,1)S(1)}, bf16[256,1024]{1,0:T(8,128)(2,1)}, u32[]{:S(2)}, u32[]{:S(2)}) collective-permute-start(bf16[256,1024]{1,0:T(8,128)(2,1)S(1)} %collective-permute-done.1.refs_5_.refs_10_), channel_id=1, source_target_pairs={{0,16},{1,17},{2,18},{3,19},{4,20},{5,21},{6,22},{7,23},{8,24},{9,... | collective-permute-start | bytes 1572872 | tf_op jit(solution)/shard_map/ppermute | solution.py:45
  55.6 15.7 %collective-permute-start.12 = (bf16[2,256,1024]{2,1,0:T(8,128)(2,1)}, bf16[2,256,1024]{2,1,0:T(8,128)(2,1)}, u32[]{:S(2)}, u32[]{:S(2)}) collective-permute-start(bf16[2,256,1024]{2,1,0:T(8,128)(2,1)} %pad_maximum_fusion), channel_id=1, source_target_pairs={{0,8},{1,9},{2,10},{3,11},{4,12},{5,13},{6,14},{7,15},{8,0},{9,1},... | collective-permute-start | bytes 3145736 | tf_op jit(solution)/shard_map/ppermute | solution.py:45
  55.6 15.7 %collective-permute-start.15 = (bf16[256,1024]{1,0:T(8,128)(2,1)S(1)}, bf16[256,1024]{1,0:T(8,128)(2,1)}, u32[]{:S(2)}, u32[]{:S(2)}) collective-permute-start(bf16[256,1024]{1,0:T(8,128)(2,1)S(1)} %collective-permute-done.3.refs_10_.refs_15_), channel_id=1, source_target_pairs={{0,32},{1,33},{2,34},{3,35},{4,36},{5,37},{6,38},{7,39},{8,40},{9,... | collective-permute-start | bytes 1572872 | tf_op jit(solution)/shard_map/ppermute | solution.py:45
  55.7 15.6 %collective-permute-start.16 = (bf16[256,1024]{1,0:T(8,128)(2,1)S(1)}, bf16[256,1024]{1,0:T(8,128)(2,1)}, u32[]{:S(2)}, u32[]{:S(2)}) collective-permute-start(bf16[256,1024]{1,0:T(8,128)(2,1)S(1)} %collective-permute-done.4.refs_9_.refs_14_), channel_id=1, source_target_pairs={{0,96},{1,97},{2,98},{3,99},{4,100},{5,101},{6,102},{7,103},{8,104... | collective-permute-start | bytes 1572872 | tf_op jit(solution)/shard_map/ppermute | solution.py:45
  58.9 12.4 %collective-permute-start.13 = (bf16[256,1024]{1,0:T(8,128)(2,1)}, bf16[256,1024]{1,0:T(8,128)(2,1)}, u32[]{:S(2)}, u32[]{:S(2)}) collective-permute-start(bf16[256,1024]{1,0:T(8,128)(2,1)} %collective-permute-done.9.refs_2_.refs_7_), channel_id=1, source_target_pairs={{0,8},{1,9},{2,10},{3,11},{4,12},{5,13},{6,14},{7,15},{8,0},{9,1},... | collective-permute-start | bytes 1572872 | tf_op jit(solution)/shard_map/ppermute | solution.py:45
  58.9 12.4 %collective-permute-start.14 = (bf16[256,1024]{1,0:T(8,128)(2,1)}, bf16[256,1024]{1,0:T(8,128)(2,1)}, u32[]{:S(2)}, u32[]{:S(2)}) collective-permute-start(bf16[256,1024]{1,0:T(8,128)(2,1)} %collective-permute-done.10.refs_3_.refs_8_), channel_id=1, source_target_pairs={{0,8},{1,9},{2,10},{3,11},{4,12},{5,13},{6,14},{7,15},{8,0},{9,1},... | collective-permute-start | bytes 1572872 | tf_op jit(solution)/shard_map/ppermute | solution.py:45
  86.7 26.7 %collective-permute-start.17 = (bf16[2,1024,256]{2,1,0:T(8,128)(2,1)}, bf16[2,1024,256]{2,1,0:T(8,128)(2,1)}, u32[]{:S(2)}, u32[]{:S(2)}) collective-permute-start(bf16[2,1024,256]{2,1,0:T(8,128)(2,1)} %get-tuple-element.109), channel_id=1, source_target_pairs={{0,6},{1,7},{2,0},{3,1},{4,2},{5,3},{6,4},{7,5},{8,14},{9,15},{10,... | collective-permute-start | bytes 3145736 | tf_op jit(solution)/shard_map/ppermute | solution.py:45
  90.8 26.0 %collective-permute-start.18 = (bf16[2,1024,256]{2,1,0:T(8,128)(2,1)}, bf16[2,1024,256]{2,1,0:T(8,128)(2,1)}, u32[]{:S(2)}, u32[]{:S(2)}) collective-permute-start(bf16[2,1024,256]{2,1,0:T(8,128)(2,1)} %get-tuple-element.110), channel_id=1, source_target_pairs={{0,2},{1,3},{2,4},{3,5},{4,6},{5,7},{6,0},{7,1},{8,10},{9,11},{10,... | collective-permute-start | bytes 3145736 | tf_op jit(solution)/shard_map/ppermute | solution.py:45
  90.8 47.3 %all-to-all-start = ((bf16[16,64,1024]{2,1,0:T(8,128)(2,1)}), bf16[16,64,1024]{2,1,0:T(8,128)(2,1)S(1)}, u32[]{:S(2)}, u32[]{:S(2)}) async-start(bf16[16,64,1024]{2,1,0:T(8,128)(2,1)} %bitcast.65), calls=%async_computation | async-start | bytes 4194304 | tf_op jit(solution)/shard_map/all_to_all | solution.py:226
  119.6 12.6 %collective-permute-start.19 = (bf16[1024,256]{1,0:T(8,128)(2,1)}, bf16[1024,256]{1,0:T(8,128)(2,1)}, u32[]{:S(2)}, u32[]{:S(2)}) collective-permute-start(bf16[1024,256]{1,0:T(8,128)(2,1)} %get-tuple-element.114), channel_id=1, source_target_pairs={{0,6},{1,7},{2,0},{3,1},{4,2},{5,3},{6,4},{7,5},{8,14},{9,15},{10,... | collective-permute-start | bytes 1572872 | tf_op jit(solution)/shard_map/ppermute | solution.py:45
  119.8 13.8 %collective-permute-start.20 = (bf16[1024,256]{1,0:T(8,128)(2,1)}, bf16[1024,256]{1,0:T(8,128)(2,1)}, u32[]{:S(2)}, u32[]{:S(2)}) collective-permute-start(bf16[1024,256]{1,0:T(8,128)(2,1)} %get-tuple-element.115), channel_id=1, source_target_pairs={{0,2},{1,3},{2,4},{3,5},{4,6},{5,7},{6,0},{7,1},{8,10},{9,11},{10,... | collective-permute-start | bytes 1572872 | tf_op jit(solution)/shard_map/ppermute | solution.py:45
  138.2 9.3 %collective-permute-start.21 = (bf16[512,256]{1,0:T(8,128)(2,1)}, bf16[512,256]{1,0:T(8,128)(2,1)}, u32[]{:S(2)}, u32[]{:S(2)}) collective-permute-start(bf16[512,256]{1,0:T(8,128)(2,1)} %pad_maximum_fusion.3), channel_id=1, source_target_pairs={{0,1},{1,17},{2,3},{3,19},{4,5},{5,21},{6,7},{7,23},{8,9},{9,25},{... | collective-permute-start | bytes 786440 | tf_op jit(solution)/shard_map/ppermute | solution.py:45
  139.0 9.8 %collective-permute-start.22 = (bf16[512,256]{1,0:T(8,128)(2,1)}, bf16[512,256]{1,0:T(8,128)(2,1)}, u32[]{:S(2)}, u32[]{:S(2)}) collective-permute-start(bf16[512,256]{1,0:T(8,128)(2,1)} %pad_maximum_fusion.4), channel_id=1, source_target_pairs={{0,9},{1,25},{2,11},{3,27},{4,13},{5,29},{6,15},{7,31},{8,1},{9,17... | collective-permute-start | bytes 786440 | tf_op jit(solution)/shard_map/ppermute | solution.py:45
  139.0 11.7 %collective-permute-start.23 = (bf16[512,256]{1,0:T(8,128)(2,1)}, bf16[512,256]{1,0:T(8,128)(2,1)}, u32[]{:S(2)}, u32[]{:S(2)}) collective-permute-start(bf16[512,256]{1,0:T(8,128)(2,1)} %pad_maximum_fusion.5), channel_id=1, source_target_pairs={{0,17},{1,1},{2,19},{3,3},{4,21},{5,5},{6,23},{7,7},{8,25},{9,9},{... | collective-permute-start | bytes 786440 | tf_op jit(solution)/shard_map/ppermute | solution.py:45
  143.1 14.1 %collective-permute-start.24 = (bf16[512,256]{1,0:T(8,128)(2,1)S(1)}, bf16[512,256]{1,0:T(8,128)(2,1)}, u32[]{:S(2)}, u32[]{:S(2)}) collective-permute-start(bf16[512,256]{1,0:T(8,128)(2,1)S(1)} %pad_maximum_fusion.6), channel_id=1, source_target_pairs={{0,25},{1,9},{2,27},{3,11},{4,29},{5,13},{6,31},{7,15},{8,17},{9,1... | collective-permute-start | bytes 786440 | tf_op jit(solution)/shard_map/ppermute | solution.py:45
  (8 other events, 50.2 us)

commit v8 on v7

--- a/solution.py
+++ b/solution.py
@@ -9,6 +9,7 @@
 
 SIZES = (4, 2, 2, 4, 2)
 AXES = ("feat", "batch")
+LATE = 60
 
 
 def flat(place):
@@ -67,8 +68,12 @@
     place, refs = refs[0], refs[1:]
     n_in = plan["inputs"]
     inputs, refs = refs[:n_in], refs[n_in + plan["kept"] :]
-    home, up, down, middle = refs[:4]
-    targets, refs = ((home, up, down, middle), (home, middle, up, down)), refs[4:]
+    if plan["messages"] == 4:
+        home, up, down, middle = refs[:4]
+    else:
+        (home, middle), up, down = refs[:2], None, None
+    targets = ((home, up, down, middle), (home, middle, up, down))
+    refs = refs[plan["messages"] :]
     left, columns_in, result, left_sem, column_sem, out_sem = refs
     shift, high = place[0], place[1]
     rows = columns_in.shape[2]
@@ -97,37 +102,53 @@
         copy.start()
     outs = []
     arrived = set()
+    slot = 0
     for side, (cc, wanted) in enumerate(plan["sides"]):
         for copy in lefts[8 * side : 8 * side + 8]:
             copy.wait()
-        for n, dx in wanted:
-            if n not in arrived:
-                arrived.add(n)
-                for copy in rights[2 * n : 2 * n + 2]:
-                    copy.wait()
+        for kind, which in wanted:
+            if kind == "dz":
+                block = (which + 4 - shift) % 4
+                needed = range(len(plan["blocks"]))
+                options = [(None, which)]
+            else:
+                block = plan["order"].index(which)
+                needed = (block,)
+                dz = (shift + which) % 4
+                options = [(dz == d, d) for d in range(4)]
+            for n in needed:
+                if n not in arrived:
+                    arrived.add(n)
+                    for copy in rights[2 * n : 2 * n + 2]:
+                        copy.wait()
             total = None
             for i in range(2):
                 term = lax.dot_general(
                     left[side, i],
-                    columns_in[n, i],
+                    columns_in[block, i],
                     (((1,), (1,)), ((), ())),
                     preferred_element_type=jnp.float32,
                 )
                 total = term if total is None else total + term
-            slot = len(outs) // 4
             result[slot] = total.astype(jnp.bfloat16)
-            dz = (shift + dx) % 4
-            for d in range(4):
+            for here, d in options:
                 copy = pltpu.make_async_copy(
                     result.at[slot], targets[cc][d].at[cc], out_sem.at[slot]
                 )
-                outs.append((dz == d, copy))
-                pl.when(dz == d)(copy.start)
+                outs.append((here, copy))
+                if here is None:
+                    copy.start()
+                else:
+                    pl.when(here)(copy.start)
+            slot += 1
     for here, copy in outs:
-        pl.when(here)(copy.wait)
-
-
-def block_product(place, sides, blocks, kept=()):
+        if here is None:
+            copy.wait()
+        else:
+            pl.when(here)(copy.wait)
+
+
+def block_product(place, sides, blocks, kept=(), limit=60):
     inputs = []
 
     def enter(piece):
@@ -141,18 +162,25 @@
     groups = [[enter(piece) for piece in pair] for side, _ in sides.values() for pair in side]
     names = [[enter(piece) for piece in pair] for pair in blocks.values()]
     half, items = inputs[0].shape[-2:]
-    order = list(blocks)
-    wanted = tuple((cc, tuple((order.index(dx), dx) for dx in dxs)) for cc, (_, dxs) in sides.items())
-    n_results = sum(len(dxs) for _, dxs in wanted)
-    plan = {"inputs": len(inputs), "kept": len(kept), "sides": wanted, "blocks": names}
+    wanted = tuple((cc, jobs) for cc, (_, jobs) in sides.items())
+    n_results = sum(len(jobs) for _, jobs in wanted)
+    n_messages = len(kept) or 4
+    plan = {
+        "inputs": len(inputs),
+        "kept": len(kept),
+        "messages": n_messages,
+        "sides": wanted,
+        "blocks": names,
+        "order": tuple(blocks),
+    }
     outside = pl.BlockSpec(memory_space=pltpu.HBM)
     n_blocks = len(blocks)
     return pl.pallas_call(
         functools.partial(block_kernel, plan, groups),
-        out_shape=[jax.ShapeDtypeStruct((2, 4 * half, half), jnp.bfloat16)] * 4,
+        out_shape=[jax.ShapeDtypeStruct((2, 4 * half, half), jnp.bfloat16)] * n_messages,
         in_specs=[pl.BlockSpec(memory_space=pltpu.SMEM)]
         + [outside] * (len(inputs) + len(kept)),
-        out_specs=[outside] * 4,
+        out_specs=[outside] * n_messages,
         input_output_aliases={1 + len(inputs) + n: n for n in range(len(kept))},
         scratch_shapes=[
             pltpu.VMEM((len(sides), 2, 4 * half, items), jnp.bfloat16),
@@ -162,7 +190,7 @@
             pltpu.SemaphoreType.DMA((2 * n_blocks,)),
             pltpu.SemaphoreType.DMA((n_results,)),
         ],
-        compiler_params=pltpu.CompilerParams(vmem_limit_bytes=60 * 1024 * 1024),
+        compiler_params=pltpu.CompilerParams(vmem_limit_bytes=limit * 1024 * 1024),
         cost_estimate=pl.CostEstimate(
             flops=half * half, bytes_accessed=half * items, transcendentals=0
         ),
@@ -217,9 +245,13 @@
         ((rim_c, 0), (rim_c, 1)),
     )
     early = {0: (near, far), 1: (above_n, above_f), 3: (below_n, below_f)}
-    kept = block_product(place, {0: (side, (0, 1, 3))}, early)
+    every = {0: (near, far), 1: (above_n, above_f), 2: tuple(across), 3: (below_n, below_f)}
+    kept = block_product(place, {0: (side, (("dx", 0), ("dx", 1), ("dx", 3)))}, early)
     home, up, down, middle = block_product(
-        place, {1: (side_c, (0, 1, 3, 2)), 0: (side, (2,))}, {**early, 2: tuple(across)}, kept
+        place, {1: (side_c, (("dz", 2), ("dz", 3))), 0: (side, (("dx", 2),))}, every, kept
+    )
+    home, middle = block_product(
+        place, {1: (side_c, (("dz", 1), ("dz", 0)))}, every, (home, middle), LATE
     )
 
     share, down, up = lax.optimization_barrier((share, down, up))
@@ -232,23 +264,25 @@
         ]
     )
     total = [
-        narrow(wide(home[0]) + wide(up[0]) + wide(first)).reshape(2, 2, half, half),
-        narrow(wide(home[1]) + wide(down[1]) + wide(second)).reshape(2, 2, half, half),
+        narrow(wide(home[0]) + wide(up[0]) + wide(first)).reshape(2, 2 * half, half),
+        narrow(wide(home[1]) + wide(down[1]) + wide(second)).reshape(2, 2 * half, half),
     ]
-    homeward = []
-    for s in range(2):
-        for t in range(2):
-            chosen = pick(total[t], yl ^ yh ^ s)
-            value = jnp.concatenate([pick(chosen, yh ^ i) for i in range(2)], 0)
-            homeward.append(value)
+    homeward = [pick(total[t], yl ^ yh ^ s) for s in range(2) for t in range(2)]
     shares, homeward = lax.optimization_barrier((shares, homeward))
     projected = narrow(jnp.sum(wide(shares), 0))
     arrived = [send(v, HOME[s // 2, s % 2]) for s, v in enumerate(homeward)]
     *arrived, projected = lax.optimization_barrier((*arrived, projected))
-    arrived = jnp.stack(arrived)
-    gram = jnp.concatenate(
-        [pick(arrived, (q % 2 ^ yl) * 2 + (q // 2 ^ c)) for q in range(4)], 1
-    )
+
+    def quarter(q):
+        t, s = q // 2, q % 2
+        value = jnp.where(
+            c == 0,
+            jnp.where(yl == 0, arrived[2 * s + t], arrived[2 - 2 * s + t]),
+            jnp.where(yl == 0, arrived[2 * s + 1 - t], arrived[3 - 2 * s - t]),
+        )
+        return jnp.concatenate([value[half:], value[:half]], 0) if s else value
+
+    gram = jnp.concatenate([quarter(q) for q in range(4)], 1)
     covariance = 0.9 * cov_prior + wide(gram) / items_total
     return (covariance, projected)
 

time: 161 us -> 156 us (0.969)
  waiting for transfers between devices: 79.6 us -> 69 us
  Pallas kernels: 25.9 us -> 30 us
  other arithmetic: 13.1 us -> 10.6 us
  starting transfers between devices: 36.4 us -> 38.3 us
    ppermute x25, waiting for transfers between devices: 79.6 us -> 69 us  [send(): return lax.ppermute(value, AXES, pairs)]
    pallas_call x2 -> x3, Pallas kernels: 25.9 us -> 30 us  [block_product(): pl.pallas_call(functools.partial(block_kernel, plan, groups), out_shape=[...]
    concatenate x4 -> x0, other arithmetic: 2.17 us -> none  [on_device(): value = jnp.concatenate([pick(chosen, yh ^ i) for i in range(2)], 0)]
    ppermute x25, starting transfers between devices: 32.2 us -> 33.9 us  [send(): return lax.ppermute(value, AXES, pairs)]
    reduce_sum x1, other arithmetic: 1.06 us -> 2.68 us  [on_device(): projected = narrow(jnp.sum(wide(shares), 0))]
  transfers between devices with their start and end apart: 26 -> 26, of which waited for: 17 -> 16; matrix products, arithmetic and copies ran while one was open for 8% -> 7% of each run, Pallas kernels for 7% -> 12%
where the time goes in v8:
time: 156 us; the launch traced here: 155 us
  waiting for transfers between devices  69 us (44%)
  starting transfers between devices  38.3 us (25%)
  Pallas kernels  30 us (19%)
  other arithmetic  10.6 us (7%)
  local copies, waits for them, and re-layouts  3.72 us (2%)
  matrix products  2.57 us (2%)
    ppermute x25, waiting for transfers between devices, send(): return lax.ppermute(value, AXES, pairs)  69 us
    ppermute x25, starting transfers between devices, send(): return lax.ppermute(value, AXES, pairs)  33.9 us
    pallas_call x3, Pallas kernels, block_product(): pl.pallas_call(functools.partial(block_kernel, plan, groups), out_shape=[...  30 us
    all_to_all x1, starting transfers between devices, on_device(): shares = lax.all_to_all(share, 'feat', 0, 0)  4.43 us
    convert_element_type x2, other arithmetic, narrow(): return value.astype(jnp.bfloat16)  4.38 us
  transfers between devices with their start and end apart: 26, of which 16 were waited for; matrix products, arithmetic and copies ran while one was open for 7% of the time, Pallas kernels for 12%

profile of v8, /device:TPU:0, one launch (start us, length us, event | category | flops | bytes accessed | tf_op | source)
XLA Modules:
  0.0 155.1 jit_solution(16339482101969407891)
XLA Ops:
  0.7 1.6 %copy.11 = bf16[512,1024]{1,0:T(8,128)(2,1)S(1)} copy(bf16[512,1024]{0,1:T(8,128)(2,1)} %bitcast.48) | data formatting | bytes 2097152 | tf_op jit(solution)/shard_map/transpose | solution.py:209
  2.5 1.7 %collective-permute-start = (bf16[256,1024]{1,0:T(8,128)(2,1)S(1)}, bf16[256,1024]{1,0:T(8,128)(2,1)S(1)}, u32[]{:S(2)}, u32[]{:S(2)}) collective-permute-start(bf16[256,1024]{1,0:T(8,128)(2,1)S(1)} %get-tuple-element.76), channel_id=1, source_target_pairs={{0,16},{1,17},{2,18},{3,19},{4,20},{5,21},{6,22},{7,23},{8,24},{9,... | collective-permute-start | bytes 1572872 | tf_op jit(solution)/shard_map/ppermute | solution.py:46
  4.2 2.2 %collective-permute-start.1 = (bf16[256,1024]{1,0:T(8,128)(2,1)S(1)}, bf16[256,1024]{1,0:T(8,128)(2,1)S(1)}, u32[]{:S(2)}, u32[]{:S(2)}) collective-permute-start(bf16[256,1024]{1,0:T(8,128)(2,1)S(1)} %get-tuple-element.75), channel_id=1, source_target_pairs={{0,17},{1,16},{2,19},{3,18},{4,21},{5,20},{6,23},{7,22},{8,25},{9,... | collective-permute-start | bytes 1572872 | tf_op jit(solution)/shard_map/ppermute | solution.py:46
  6.4 2.6 %convolution_convert_fusion = bf16[1024,1024]{1,0:T(8,128)(2,1)} fusion(bf16[1024,512]{1,0:T(8,128)(2,1)S(1)} %copy-done.13, bf16[512,1024]{1,0:T(8,128)(2,1)S(1)} %copy-done), kind=kOutput, calls=%fused_computation.1 | convolution fusion | flops 1074790400 | bytes 4194304 | tf_op jit(solution)/shard_map/dot_general | solution.py:213
  9.0 7.8 %collective-permute-done.refs_4_.refs_9_.refs_6_ = bf16[256,1024]{1,0:T(8,128)(2,1)S(1)} collective-permute-done((bf16[256,1024]{1,0:T(8,128)(2,1)S(1)}, bf16[256,1024]{1,0:T(8,128)(2,1)S(1)}, u32[]{:S(2)}, u32[]{:S(2)}) %collective-permute-start) | collective-permute-done | bytes 524320 | tf_op jit(solution)/shard_map/ppermute | solution.py:46
  16.9 2.6 %collective-permute-done.1.refs_5_.refs_10_.refs_7_ = bf16[256,1024]{1,0:T(8,128)(2,1)S(1)} collective-permute-done((bf16[256,1024]{1,0:T(8,128)(2,1)S(1)}, bf16[256,1024]{1,0:T(8,128)(2,1)S(1)}, u32[]{:S(2)}, u32[]{:S(2)}) %collective-permute-start.1) | collective-permute-done | bytes 524320 | tf_op jit(solution)/shard_map/ppermute | solution.py:46
  21.0 1.7 %collective-permute-start.4 = (bf16[256,1024]{1,0:T(8,128)(2,1)S(1)}, bf16[256,1024]{1,0:T(8,128)(2,1)}, u32[]{:S(2)}, u32[]{:S(2)}) collective-permute-start(bf16[256,1024]{1,0:T(8,128)(2,1)S(1)} %collective-permute-done.1.refs_5_.refs_10_.refs_7_), channel_id=1, source_target_pairs={{0,96},{1,97},{2,98},{3,99},{4,100},{5,101},{6,102},{7,103},{8,104... | collective-permute-start | bytes 1572872 | tf_op jit(solution)/shard_map/ppermute | solution.py:46
  22.8 2.3 %collective-permute-start.6 = (bf16[256,1024]{1,0:T(8,128)(2,1)S(1)}, bf16[256,1024]{1,0:T(8,128)(2,1)S(1)}, u32[]{:S(2)}, u32[]{:S(2)}) collective-permute-start(bf16[256,1024]{1,0:T(8,128)(2,1)S(1)} %get-tuple-element.76), channel_id=1, source_target_pairs={{0,17},{1,16},{2,19},{3,18},{4,21},{5,20},{6,23},{7,22},{8,25},{9,... | collective-permute-start | bytes 1572872 | tf_op jit(solution)/shard_map/ppermute | solution.py:46
  25.1 8.9 %collective-permute-done.3.refs_10_.refs_17_.refs_12_ = bf16[256,1024]{1,0:T(8,128)(2,1)} collective-permute-done((bf16[256,1024]{1,0:T(8,128)(2,1)S(1)}, bf16[256,1024]{1,0:T(8,128)(2,1)}, u32[]{:S(2)}, u32[]{:S(2)}) %collective-permute-start.3) | collective-permute-done | bytes 524320 | tf_op jit(solution)/shard_map/ppermute | solution.py:46
  36.8 3.0 %collective-permute-start.8 = (bf16[256,1024]{1,0:T(8,128)(2,1)S(1)}, bf16[256,1024]{1,0:T(8,128)(2,1)S(1)}, u32[]{:S(2)}, u32[]{:S(2)}) collective-permute-start(bf16[256,1024]{1,0:T(8,128)(2,1)S(1)} %collective-permute-done.refs_4_.refs_9_.refs_6_), channel_id=1, source_target_pairs={{0,96},{1,97},{2,98},{3,99},{4,100},{5,101},{6,102},{7,103},{8,104... | collective-permute-start | bytes 1572872 | tf_op jit(solution)/shard_map/ppermute | solution.py:46
  40.3 2.2 %collective-permute-start.10 = (bf16[256,1024]{1,0:T(8,128)(2,1)S(1)}, bf16[256,1024]{1,0:T(8,128)(2,1)}, u32[]{:S(2)}, u32[]{:S(2)}) collective-permute-start(bf16[256,1024]{1,0:T(8,128)(2,1)S(1)} %collective-permute-done.refs_4_.refs_9_.refs_6_), channel_id=1, source_target_pairs={{0,17},{1,16},{2,19},{3,18},{4,21},{5,20},{6,23},{7,22},{8,25},{9,... | collective-permute-start | bytes 1572872 | tf_op jit(solution)/shard_map/ppermute | solution.py:46
  43.6 8.5 %collective-permute-done.7.refs_11_.refs_18_.refs_13_ = bf16[256,1024]{1,0:T(8,128)(2,1)S(1)} collective-permute-done((bf16[256,1024]{1,0:T(8,128)(2,1)S(1)}, bf16[256,1024]{1,0:T(8,128)(2,1)S(1)}, u32[]{:S(2)}, u32[]{:S(2)}) %collective-permute-start.7) | collective-permute-done | bytes 524320 | tf_op jit(solution)/shard_map/ppermute | solution.py:46
  52.1 1.6 %collective-permute-done.9.refs_2_.refs_7_ = bf16[256,1024]{1,0:T(8,128)(2,1)} collective-permute-done((bf16[256,1024]{1,0:T(8,128)(2,1)S(1)}, bf16[256,1024]{1,0:T(8,128)(2,1)}, u32[]{:S(2)}, u32[]{:S(2)}) %collective-permute-start.9) | collective-permute-done | bytes 524320 | tf_op jit(solution)/shard_map/ppermute | solution.py:46
  56.1 3.2 %collective-permute-start.16 = (bf16[256,1024]{1,0:T(8,128)(2,1)}, bf16[256,1024]{1,0:T(8,128)(2,1)}, u32[]{:S(2)}, u32[]{:S(2)}) collective-permute-start(bf16[256,1024]{1,0:T(8,128)(2,1)} %collective-permute-done.4.refs_9_.refs_14_), channel_id=1, source_target_pairs={{0,96},{1,97},{2,98},{3,99},{4,100},{5,101},{6,102},{7,103},{8,104... | collective-permute-start | bytes 1572872 | tf_op jit(solution)/shard_map/ppermute | solution.py:46
  60.5 10.5 %shard_map.50 = (bf16[2,1024,256]{2,1,0:T(8,128)(2,1)}, bf16[2,1024,256]{2,1,0:T(8,128)(2,1)}, bf16[2,1024,256]{2,1,0:T(8,128)(2,1)}, bf16[2,1024,256]{2,1,0:T(8,128)(2,1)}) custom-call(s32[2]{0:T(128)} %pad_add_fusion.refs_0_, bf16[2,256,1024]{2,1,0:T(8,128)(2,1)} %bitcast.39, bf16[256,1024]{1,0:T(8,128)(2,1)} %collective-permute-done.9.refs_2_.refs_7_, ...), custom_call_target="tpu_custom_call" | custom-call | flops 65536 | bytes 262144 | tf_op jit(solution)/shard_map/pallas_call | solution.py:178
  72.1 11.9 %shard_map.51 = (bf16[2,1024,256]{2,1,0:T(8,128)(2,1)}, bf16[2,1024,256]{2,1,0:T(8,128)(2,1)}, bf16[2,1024,256]{2,1,0:T(8,128)(2,1)}, bf16[2,1024,256]{2,1,0:T(8,128)(2,1)}) custom-call(s32[2]{0:T(128)} %pad_add_fusion.refs_0_, bf16[2,256,1024]{2,1,0:T(8,128)(2,1)} %copy-done.9, ...), custom_call_target="tpu_custom_call", output_to_operand_aliasing={{0}: (19, {}), {1}: (20, {}), {2}: (21, {}), {3}: (22, {})} | custom-call | flops 65536 | bytes 262144 | tf_op jit(solution)/shard_map/pallas_call | solution.py:178
  84.0 4.1 %collective-permute-start.17 = (bf16[2,1024,256]{2,1,0:T(8,128)(2,1)}, bf16[2,1024,256]{2,1,0:T(8,128)(2,1)S(1)}, u32[]{:S(2)}, u32[]{:S(2)}) collective-permute-start(bf16[2,1024,256]{2,1,0:T(8,128)(2,1)} %get-tuple-element.113), channel_id=1, source_target_pairs={{0,6},{1,7},{2,0},{3,1},{4,2},{5,3},{6,4},{7,5},{8,14},{9,15},{10,... | collective-permute-start | bytes 3145736 | tf_op jit(solution)/shard_map/ppermute | solution.py:46
  88.1 4.4 %all-to-all-start = ((bf16[16,64,1024]{2,1,0:T(8,128)(2,1)}), bf16[16,64,1024]{2,1,0:T(8,128)(2,1)}, u32[]{:S(2)}, u32[]{:S(2)}) async-start(bf16[16,64,1024]{2,1,0:T(8,128)(2,1)} %bitcast.45), calls=%async_computation | async-start | bytes 4194304 | tf_op jit(solution)/shard_map/all_to_all | solution.py:258
  92.6 7.5 %shard_map.52 = (bf16[2,1024,256]{2,1,0:T(8,128)(2,1)}, bf16[2,1024,256]{2,1,0:T(8,128)(2,1)}) custom-call(s32[2]{0:T(128)} %pad_add_fusion.refs_0_, bf16[2,256,1024]{2,1,0:T(8,128)(2,1)} %copy-done.9, bf16[256,1024]{1,0:T(8,128)(2,1)} %collective-permute-done.13.refs_2_, ...), custom_call_target="tpu_custom_call", output_to_operand_aliasing={{0}: (14, {}), {1}: (15, {})} | custom-call | flops 65536 | bytes 262144 | tf_op jit(solution)/shard_map/pallas_call | solution.py:178
  100.2 10.9 %collective-permute-done.17 = bf16[2,1024,256]{2,1,0:T(8,128)(2,1)S(1)} collective-permute-done((bf16[2,1024,256]{2,1,0:T(8,128)(2,1)}, bf16[2,1024,256]{2,1,0:T(8,128)(2,1)S(1)}, u32[]{:S(2)}, u32[]{:S(2)}) %collective-permute-start.17) | collective-permute-done | bytes 1048608 | tf_op jit(solution)/shard_map/ppermute | solution.py:46
  111.0 3.4 %collective-permute-done.18 = bf16[2,1024,256]{2,1,0:T(8,128)(2,1)} collective-permute-done((bf16[2,1024,256]{2,1,0:T(8,128)(2,1)}, bf16[2,1024,256]{2,1,0:T(8,128)(2,1)}, u32[]{:S(2)}, u32[]{:S(2)}) %collective-permute-start.18) | collective-permute-done | bytes 1048608 | tf_op jit(solution)/shard_map/ppermute | solution.py:46
  114.4 2.6 %fusion.3 = (bf16[1024,256]{1,0:T(8,128)(2,1)}, bf16[1024,256]{1,0:T(8,128)(2,1)}) fusion(bf16[2,1024,256]{2,1,0:T(8,128)(2,1)} %get-tuple-element.117, bf16[2,1024,256]{2,1,0:T(8,128)(2,1)} %collective-permute-done.18, bf16[2,1024,256]{2,1,0:T(8,128)(2,1)S(1)} %collective-permute-done.17), kind=kLoop, calls=%fused_computation.11 | loop fusion | flops 2097152 | bytes 3145728 | tf_op jit(solution)/shard_map/convert_element_type | solution.py:58
  117.2 1.8 %collective-permute-start.20 = (bf16[1024,256]{1,0:T(8,128)(2,1)}, bf16[1024,256]{1,0:T(8,128)(2,1)}, u32[]{:S(2)}, u32[]{:S(2)}) collective-permute-start(bf16[1024,256]{1,0:T(8,128)(2,1)} %get-tuple-element.119), channel_id=1, source_target_pairs={{0,2},{1,3},{2,4},{3,5},{4,6},{5,7},{6,0},{7,1},{8,10},{9,11},{10,... | collective-permute-start | bytes 1572872 | tf_op jit(solution)/shard_map/ppermute | solution.py:46
  119.1 10.9 %collective-permute-done.19 = bf16[1024,256]{1,0:T(8,128)(2,1)} collective-permute-done((bf16[1024,256]{1,0:T(8,128)(2,1)}, bf16[1024,256]{1,0:T(8,128)(2,1)}, u32[]{:S(2)}, u32[]{:S(2)}) %collective-permute-start.19) | collective-permute-done | bytes 524320 | tf_op jit(solution)/shard_map/ppermute | solution.py:46
  131.5 1.8 %fusion = (bf16[1024,256]{1,0:T(8,128)(2,1)S(1)}, bf16[1024,256]{1,0:T(8,128)(2,1)S(1)}) fusion(bf16[1024,256]{1,0:T(8,128)(2,1)} %collective-permute-done.20, bf16[2,1024,256]{2,1,0:T(8,128)(2,1)S(1)} %collective-permute-done.17, bf16[2,1024,256]{2,1,0:T(8,128)(2,1)S(1)} %copy-done.2, bf16[1024,256]{1,0:T(8,128)(2,1)} %collective-permute-done.19, ...), kind=kLoop, calls=%fused_computation.5 | loop fusion | flops 3145728 | bytes 4194304 | tf_op jit(solution)/shard_map/convert_element_type | solution.py:58
  133.4 2.0 %collective-permute-start.21 = (bf16[512,256]{1,0:T(8,128)(2,1)S(1)}, bf16[512,256]{1,0:T(8,128)(2,1)S(1)}, u32[]{:S(2)}, u32[]{:S(2)}) collective-permute-start(bf16[512,256]{1,0:T(8,128)(2,1)S(1)} %get-tuple-element.122), channel_id=1, source_target_pairs={{0,1},{1,17},{2,3},{3,19},{4,5},{5,21},{6,7},{7,23},{8,9},{9,25},{... | collective-permute-start | bytes 786440 | tf_op jit(solution)/shard_map/ppermute | solution.py:46
  135.4 3.0 %collective-permute-start.23 = (bf16[512,256]{1,0:T(8,128)(2,1)S(1)}, bf16[512,256]{1,0:T(8,128)(2,1)S(1)}, u32[]{:S(2)}, u32[]{:S(2)}) collective-permute-start(bf16[512,256]{1,0:T(8,128)(2,1)S(1)} %get-tuple-element.124), channel_id=1, source_target_pairs={{0,17},{1,1},{2,19},{3,3},{4,21},{5,5},{6,23},{7,7},{8,25},{9,9},{... | collective-permute-start | bytes 786440 | tf_op jit(solution)/shard_map/ppermute | solution.py:46
  138.3 3.4 %collective-permute-start.24 = (bf16[512,256]{1,0:T(8,128)(2,1)S(1)}, bf16[512,256]{1,0:T(8,128)(2,1)S(1)}, u32[]{:S(2)}, u32[]{:S(2)}) collective-permute-start(bf16[512,256]{1,0:T(8,128)(2,1)S(1)} %get-tuple-element.125), channel_id=1, source_target_pairs={{0,25},{1,9},{2,27},{3,11},{4,29},{5,13},{6,31},{7,15},{8,17},{9,1... | collective-permute-start | bytes 786440 | tf_op jit(solution)/shard_map/ppermute | solution.py:46
  141.8 2.7 %reduce_sum.12 = bf16[64,1024]{1,0:T(8,128)(2,1)} reduce(bf16[16,64,1024]{2,1,0:T(8,128)(2,1)} %all-to-all-done, bf16[]{:T(256)} %constant.91.clone.1), dimensions={0}, to_apply=%region_0.1 | reduce | flops 983040 | bytes 2228226 | tf_op jit(solution)/shard_map/reduce_sum | solution.py:272
  144.9 1.9 %collective-permute-done.23 = bf16[512,256]{1,0:T(8,128)(2,1)S(1)} collective-permute-done((bf16[512,256]{1,0:T(8,128)(2,1)S(1)}, bf16[512,256]{1,0:T(8,128)(2,1)S(1)}, u32[]{:S(2)}, u32[]{:S(2)}) %collective-permute-start.23) | collective-permute-done | bytes 262176 | tf_op jit(solution)/shard_map/ppermute | solution.py:46
  146.8 6.5 %collective-permute-done.24 = bf16[512,256]{1,0:T(8,128)(2,1)S(1)} collective-permute-done((bf16[512,256]{1,0:T(8,128)(2,1)S(1)}, bf16[512,256]{1,0:T(8,128)(2,1)S(1)}, u32[]{:S(2)}, u32[]{:S(2)}) %collective-permute-start.24) | collective-permute-done | bytes 262176 | tf_op jit(solution)/shard_map/ppermute | solution.py:46
  153.4 1.7 %multiply_add_fusion = f32[512,1024]{1,0:T(8,128)} fusion(f32[512,1024]{1,0:T(8,128)S(1)} %copy-done.12, bf16[256,256]{1,0:T(8,128)(2,1)S(1)} %get-tuple-element.149, bf16[256,256]{1,0:T(8,128)(2,1)S(1)} %get-tuple-element.148, bf16[512,256]{1,0:T(8,128)(2,1)S(1)} %get-tuple-element.134, bf16[256,256]{1,0:T(8,128)(2,1)S(1)} %get-tuple-element.147, ...), kind=kLoop, calls=%fused_computation | loop fusion | flops 7864320 | bytes 5242880 | tf_op jit(solution)/shard_map/add | solution.py:286
  (65 shorter events, 13.3 us)
Async XLA Ops:
  2.4 17.0 %collective-permute-start.2 = (bf16[2,256,1024]{2,1,0:T(8,128)(2,1)S(1)}, bf16[2,256,1024]{2,1,0:T(8,128)(2,1)S(1)}, u32[]{:S(2)}, u32[]{:S(2)}) collective-permute-start(bf16[2,256,1024]{2,1,0:T(8,128)(2,1)S(1)} %bitcast.38), channel_id=1, source_target_pairs={{0,8},{1,9},{2,10},{3,11},{4,12},{5,13},{6,14},{7,15},{8,0},{9,1},... | collective-permute-start | bytes 3145736 | tf_op jit(solution)/shard_map/ppermute | solution.py:46
  2.5 14.3 %collective-permute-start = (bf16[256,1024]{1,0:T(8,128)(2,1)S(1)}, bf16[256,1024]{1,0:T(8,128)(2,1)S(1)}, u32[]{:S(2)}, u32[]{:S(2)}) collective-permute-start(bf16[256,1024]{1,0:T(8,128)(2,1)S(1)} %get-tuple-element.76), channel_id=1, source_target_pairs={{0,16},{1,17},{2,18},{3,19},{4,20},{5,21},{6,22},{7,23},{8,24},{9,... | collective-permute-start | bytes 1572872 | tf_op jit(solution)/shard_map/ppermute | solution.py:46
  4.2 15.2 %collective-permute-start.1 = (bf16[256,1024]{1,0:T(8,128)(2,1)S(1)}, bf16[256,1024]{1,0:T(8,128)(2,1)S(1)}, u32[]{:S(2)}, u32[]{:S(2)}) collective-permute-start(bf16[256,1024]{1,0:T(8,128)(2,1)S(1)} %get-tuple-element.75), channel_id=1, source_target_pairs={{0,17},{1,16},{2,19},{3,18},{4,21},{5,20},{6,23},{7,22},{8,25},{9,... | collective-permute-start | bytes 1572872 | tf_op jit(solution)/shard_map/ppermute | solution.py:46
  16.9 26.7 %copy-start.3 = (bf16[256,1024]{1,0:T(8,128)(2,1)}, bf16[256,1024]{1,0:T(8,128)(2,1)S(1)}, u32[]{:S(2)}) copy-start(bf16[256,1024]{1,0:T(8,128)(2,1)S(1)} %collective-permute-done.refs_4_.refs_9_.refs_6_) | copy-start | bytes 1572868
  19.4 24.1 %copy-start.4 = (bf16[256,1024]{1,0:T(8,128)(2,1)}, bf16[256,1024]{1,0:T(8,128)(2,1)S(1)}, u32[]{:S(2)}) copy-start(bf16[256,1024]{1,0:T(8,128)(2,1)S(1)} %collective-permute-done.1.refs_5_.refs_10_.refs_7_) | copy-start | bytes 1572868
  19.4 24.1 %copy-start.9 = (bf16[2,256,1024]{2,1,0:T(8,128)(2,1)}, bf16[2,256,1024]{2,1,0:T(8,128)(2,1)S(1)}, u32[]{:S(2)}) copy-start(bf16[2,256,1024]{2,1,0:T(8,128)(2,1)S(1)} %collective-permute-done.2.refs_1_) | copy-start | bytes 3145732
  19.4 14.5 %collective-permute-start.3 = (bf16[256,1024]{1,0:T(8,128)(2,1)S(1)}, bf16[256,1024]{1,0:T(8,128)(2,1)}, u32[]{:S(2)}, u32[]{:S(2)}) collective-permute-start(bf16[256,1024]{1,0:T(8,128)(2,1)S(1)} %collective-permute-done.refs_4_.refs_9_.refs_6_), channel_id=1, source_target_pairs={{0,32},{1,33},{2,34},{3,35},{4,36},{5,37},{6,38},{7,39},{8,40},{9,... | collective-permute-start | bytes 1572872 | tf_op jit(solution)/shard_map/ppermute | solution.py:46
  21.0 13.0 %collective-permute-start.4 = (bf16[256,1024]{1,0:T(8,128)(2,1)S(1)}, bf16[256,1024]{1,0:T(8,128)(2,1)}, u32[]{:S(2)}, u32[]{:S(2)}) collective-permute-start(bf16[256,1024]{1,0:T(8,128)(2,1)S(1)} %collective-permute-done.1.refs_5_.refs_10_.refs_7_), channel_id=1, source_target_pairs={{0,96},{1,97},{2,98},{3,99},{4,100},{5,101},{6,102},{7,103},{8,104... | collective-permute-start | bytes 1572872 | tf_op jit(solution)/shard_map/ppermute | solution.py:46
  22.8 12.6 %collective-permute-start.5 = (bf16[256,1024]{1,0:T(8,128)(2,1)S(1)}, bf16[256,1024]{1,0:T(8,128)(2,1)S(1)}, u32[]{:S(2)}, u32[]{:S(2)}) collective-permute-start(bf16[256,1024]{1,0:T(8,128)(2,1)S(1)} %get-tuple-element.75), channel_id=1, source_target_pairs={{0,16},{1,17},{2,18},{3,19},{4,20},{5,21},{6,22},{7,23},{8,24},{9,... | collective-permute-start | bytes 1572872 | tf_op jit(solution)/shard_map/ppermute | solution.py:46
  22.8 13.8 %collective-permute-start.6 = (bf16[256,1024]{1,0:T(8,128)(2,1)S(1)}, bf16[256,1024]{1,0:T(8,128)(2,1)S(1)}, u32[]{:S(2)}, u32[]{:S(2)}) collective-permute-start(bf16[256,1024]{1,0:T(8,128)(2,1)S(1)} %get-tuple-element.76), channel_id=1, source_target_pairs={{0,17},{1,16},{2,19},{3,18},{4,21},{5,20},{6,23},{7,22},{8,25},{9,... | collective-permute-start | bytes 1572872 | tf_op jit(solution)/shard_map/ppermute | solution.py:46
  35.3 25.2 %copy-start.5 = (bf16[256,1024]{1,0:T(8,128)(2,1)}, bf16[256,1024]{1,0:T(8,128)(2,1)S(1)}, u32[]{:S(2)}) copy-start(bf16[256,1024]{1,0:T(8,128)(2,1)S(1)} %collective-permute-done.5.refs_6_.refs_11_) | copy-start | bytes 1572868
  36.6 24.0 %copy-start.6 = (bf16[256,1024]{1,0:T(8,128)(2,1)}, bf16[256,1024]{1,0:T(8,128)(2,1)S(1)}, u32[]{:S(2)}) copy-start(bf16[256,1024]{1,0:T(8,128)(2,1)S(1)} %collective-permute-done.6.refs_7_.refs_12_) | copy-start | bytes 1572868
  36.6 18.6 %collective-permute-start.11 = (bf16[2,256,1024]{2,1,0:T(8,128)(2,1)S(1)}, bf16[2,256,1024]{2,1,0:T(8,128)(2,1)S(1)}, u32[]{:S(2)}, u32[]{:S(2)}) collective-permute-start(bf16[2,256,1024]{2,1,0:T(8,128)(2,1)S(1)} %pad_maximum_fusion.1), channel_id=1, source_target_pairs={{0,8},{1,9},{2,10},{3,11},{4,12},{5,13},{6,14},{7,15},{8,0},{9,1},... | collective-permute-start | bytes 3145736 | tf_op jit(solution)/shard_map/ppermute | solution.py:46
  36.6 15.5 %collective-permute-start.7 = (bf16[256,1024]{1,0:T(8,128)(2,1)S(1)}, bf16[256,1024]{1,0:T(8,128)(2,1)S(1)}, u32[]{:S(2)}, u32[]{:S(2)}) collective-permute-start(bf16[256,1024]{1,0:T(8,128)(2,1)S(1)} %collective-permute-done.1.refs_5_.refs_10_.refs_7_), channel_id=1, source_target_pairs={{0,32},{1,33},{2,34},{3,35},{4,36},{5,37},{6,38},{7,39},{8,40},{9,... | collective-permute-start | bytes 1572872 | tf_op jit(solution)/shard_map/ppermute | solution.py:46
  36.8 15.3 %collective-permute-start.8 = (bf16[256,1024]{1,0:T(8,128)(2,1)S(1)}, bf16[256,1024]{1,0:T(8,128)(2,1)S(1)}, u32[]{:S(2)}, u32[]{:S(2)}) collective-permute-start(bf16[256,1024]{1,0:T(8,128)(2,1)S(1)} %collective-permute-done.refs_4_.refs_9_.refs_6_), channel_id=1, source_target_pairs={{0,96},{1,97},{2,98},{3,99},{4,100},{5,101},{6,102},{7,103},{8,104... | collective-permute-start | bytes 1572872 | tf_op jit(solution)/shard_map/ppermute | solution.py:46
  39.8 13.9 %collective-permute-start.9 = (bf16[256,1024]{1,0:T(8,128)(2,1)S(1)}, bf16[256,1024]{1,0:T(8,128)(2,1)}, u32[]{:S(2)}, u32[]{:S(2)}) collective-permute-start(bf16[256,1024]{1,0:T(8,128)(2,1)S(1)} %collective-permute-done.1.refs_5_.refs_10_.refs_7_), channel_id=1, source_target_pairs={{0,16},{1,17},{2,18},{3,19},{4,20},{5,21},{6,22},{7,23},{8,24},{9,... | collective-permute-start | bytes 1572872 | tf_op jit(solution)/shard_map/ppermute | solution.py:46
  40.3 14.8 %collective-permute-start.10 = (bf16[256,1024]{1,0:T(8,128)(2,1)S(1)}, bf16[256,1024]{1,0:T(8,128)(2,1)}, u32[]{:S(2)}, u32[]{:S(2)}) collective-permute-start(bf16[256,1024]{1,0:T(8,128)(2,1)S(1)} %collective-permute-done.refs_4_.refs_9_.refs_6_), channel_id=1, source_target_pairs={{0,17},{1,16},{2,19},{3,18},{4,21},{5,20},{6,23},{7,22},{8,25},{9,... | collective-permute-start | bytes 1572872 | tf_op jit(solution)/shard_map/ppermute | solution.py:46
  55.2 16.0 %collective-permute-start.12 = (bf16[2,256,1024]{2,1,0:T(8,128)(2,1)}, bf16[2,256,1024]{2,1,0:T(8,128)(2,1)S(1)}, u32[]{:S(2)}, u32[]{:S(2)}) collective-permute-start(bf16[2,256,1024]{2,1,0:T(8,128)(2,1)} %pad_maximum_fusion), channel_id=1, source_target_pairs={{0,8},{1,9},{2,10},{3,11},{4,12},{5,13},{6,14},{7,15},{8,0},{9,1},... | collective-permute-start | bytes 3145736 | tf_op jit(solution)/shard_map/ppermute | solution.py:46
  56.1 15.0 %collective-permute-start.15 = (bf16[256,1024]{1,0:T(8,128)(2,1)}, bf16[256,1024]{1,0:T(8,128)(2,1)}, u32[]{:S(2)}, u32[]{:S(2)}) collective-permute-start(bf16[256,1024]{1,0:T(8,128)(2,1)} %collective-permute-done.3.refs_10_.refs_17_.refs_12_), channel_id=1, source_target_pairs={{0,32},{1,33},{2,34},{3,35},{4,36},{5,37},{6,38},{7,39},{8,40},{9,... | collective-permute-start | bytes 1572872 | tf_op jit(solution)/shard_map/ppermute | solution.py:46
  56.1 15.0 %collective-permute-start.16 = (bf16[256,1024]{1,0:T(8,128)(2,1)}, bf16[256,1024]{1,0:T(8,128)(2,1)}, u32[]{:S(2)}, u32[]{:S(2)}) collective-permute-start(bf16[256,1024]{1,0:T(8,128)(2,1)} %collective-permute-done.4.refs_9_.refs_14_), channel_id=1, source_target_pairs={{0,96},{1,97},{2,98},{3,99},{4,100},{5,101},{6,102},{7,103},{8,104... | collective-permute-start | bytes 1572872 | tf_op jit(solution)/shard_map/ppermute | solution.py:46
  59.4 11.7 %collective-permute-start.13 = (bf16[256,1024]{1,0:T(8,128)(2,1)}, bf16[256,1024]{1,0:T(8,128)(2,1)}, u32[]{:S(2)}, u32[]{:S(2)}) collective-permute-start(bf16[256,1024]{1,0:T(8,128)(2,1)} %collective-permute-done.9.refs_2_.refs_7_), channel_id=1, source_target_pairs={{0,8},{1,9},{2,10},{3,11},{4,12},{5,13},{6,14},{7,15},{8,0},{9,1},... | collective-permute-start | bytes 1572872 | tf_op jit(solution)/shard_map/ppermute | solution.py:46
  59.4 11.7 %collective-permute-start.14 = (bf16[256,1024]{1,0:T(8,128)(2,1)}, bf16[256,1024]{1,0:T(8,128)(2,1)}, u32[]{:S(2)}, u32[]{:S(2)}) collective-permute-start(bf16[256,1024]{1,0:T(8,128)(2,1)} %collective-permute-done.10.refs_3_.refs_8_), channel_id=1, source_target_pairs={{0,8},{1,9},{2,10},{3,11},{4,12},{5,13},{6,14},{7,15},{8,0},{9,1},... | collective-permute-start | bytes 1572872 | tf_op jit(solution)/shard_map/ppermute | solution.py:46
  84.0 27.0 %collective-permute-start.17 = (bf16[2,1024,256]{2,1,0:T(8,128)(2,1)}, bf16[2,1024,256]{2,1,0:T(8,128)(2,1)S(1)}, u32[]{:S(2)}, u32[]{:S(2)}) collective-permute-start(bf16[2,1024,256]{2,1,0:T(8,128)(2,1)} %get-tuple-element.113), channel_id=1, source_target_pairs={{0,6},{1,7},{2,0},{3,1},{4,2},{5,3},{6,4},{7,5},{8,14},{9,15},{10,... | collective-permute-start | bytes 3145736 | tf_op jit(solution)/shard_map/ppermute | solution.py:46
  88.1 26.3 %collective-permute-start.18 = (bf16[2,1024,256]{2,1,0:T(8,128)(2,1)}, bf16[2,1024,256]{2,1,0:T(8,128)(2,1)}, u32[]{:S(2)}, u32[]{:S(2)}) collective-permute-start(bf16[2,1024,256]{2,1,0:T(8,128)(2,1)} %get-tuple-element.114), channel_id=1, source_target_pairs={{0,2},{1,3},{2,4},{3,5},{4,6},{5,7},{6,0},{7,1},{8,10},{9,11},{10,... | collective-permute-start | bytes 3145736 | tf_op jit(solution)/shard_map/ppermute | solution.py:46
  88.1 45.2 %all-to-all-start = ((bf16[16,64,1024]{2,1,0:T(8,128)(2,1)}), bf16[16,64,1024]{2,1,0:T(8,128)(2,1)}, u32[]{:S(2)}, u32[]{:S(2)}) async-start(bf16[16,64,1024]{2,1,0:T(8,128)(2,1)} %bitcast.45), calls=%async_computation | async-start | bytes 4194304 | tf_op jit(solution)/shard_map/all_to_all | solution.py:258
  100.1 31.4 %copy-start.2 = (bf16[2,1024,256]{2,1,0:T(8,128)(2,1)S(1)}, bf16[2,1024,256]{2,1,0:T(8,128)(2,1)}, u32[]{:S(2)}) copy-start(bf16[2,1024,256]{2,1,0:T(8,128)(2,1)} %get-tuple-element.110) | copy-start | bytes 3145732
  117.1 12.9 %collective-permute-start.19 = (bf16[1024,256]{1,0:T(8,128)(2,1)}, bf16[1024,256]{1,0:T(8,128)(2,1)}, u32[]{:S(2)}, u32[]{:S(2)}) collective-permute-start(bf16[1024,256]{1,0:T(8,128)(2,1)} %get-tuple-element.118), channel_id=1, source_target_pairs={{0,6},{1,7},{2,0},{3,1},{4,2},{5,3},{6,4},{7,5},{8,14},{9,15},{10,... | collective-permute-start | bytes 1572872 | tf_op jit(solution)/shard_map/ppermute | solution.py:46
  117.2 14.3 %collective-permute-start.20 = (bf16[1024,256]{1,0:T(8,128)(2,1)}, bf16[1024,256]{1,0:T(8,128)(2,1)}, u32[]{:S(2)}, u32[]{:S(2)}) collective-permute-start(bf16[1024,256]{1,0:T(8,128)(2,1)} %get-tuple-element.119), channel_id=1, source_target_pairs={{0,2},{1,3},{2,4},{3,5},{4,6},{5,7},{6,0},{7,1},{8,10},{9,11},{10,... | collective-permute-start | bytes 1572872 | tf_op jit(solution)/shard_map/ppermute | solution.py:46
  133.4 11.1 %collective-permute-start.21 = (bf16[512,256]{1,0:T(8,128)(2,1)S(1)}, bf16[512,256]{1,0:T(8,128)(2,1)S(1)}, u32[]{:S(2)}, u32[]{:S(2)}) collective-permute-start(bf16[512,256]{1,0:T(8,128)(2,1)S(1)} %get-tuple-element.122), channel_id=1, source_target_pairs={{0,1},{1,17},{2,3},{3,19},{4,5},{5,21},{6,7},{7,23},{8,9},{9,25},{... | collective-permute-start | bytes 786440 | tf_op jit(solution)/shard_map/ppermute | solution.py:46
  135.4 9.5 %collective-permute-start.22 = (bf16[512,256]{1,0:T(8,128)(2,1)S(1)}, bf16[512,256]{1,0:T(8,128)(2,1)S(1)}, u32[]{:S(2)}, u32[]{:S(2)}) collective-permute-start(bf16[512,256]{1,0:T(8,128)(2,1)S(1)} %get-tuple-element.123), channel_id=1, source_target_pairs={{0,9},{1,25},{2,11},{3,27},{4,13},{5,29},{6,15},{7,31},{8,1},{9,17... | collective-permute-start | bytes 786440 | tf_op jit(solution)/shard_map/ppermute | solution.py:46
  135.4 11.4 %collective-permute-start.23 = (bf16[512,256]{1,0:T(8,128)(2,1)S(1)}, bf16[512,256]{1,0:T(8,128)(2,1)S(1)}, u32[]{:S(2)}, u32[]{:S(2)}) collective-permute-start(bf16[512,256]{1,0:T(8,128)(2,1)S(1)} %get-tuple-element.124), channel_id=1, source_target_pairs={{0,17},{1,1},{2,19},{3,3},{4,21},{5,5},{6,23},{7,7},{8,25},{9,9},{... | collective-permute-start | bytes 786440 | tf_op jit(solution)/shard_map/ppermute | solution.py:46
  138.3 14.9 %collective-permute-start.24 = (bf16[512,256]{1,0:T(8,128)(2,1)S(1)}, bf16[512,256]{1,0:T(8,128)(2,1)S(1)}, u32[]{:S(2)}, u32[]{:S(2)}) collective-permute-start(bf16[512,256]{1,0:T(8,128)(2,1)S(1)} %get-tuple-element.125), channel_id=1, source_target_pairs={{0,25},{1,9},{2,27},{3,11},{4,29},{5,13},{6,31},{7,15},{8,17},{9,1... | collective-permute-start | bytes 786440 | tf_op jit(solution)/shard_map/ppermute | solution.py:46
  (8 other events, 35.3 us)

commit v9 on v8

--- a/solution.py
+++ b/solution.py
@@ -84,11 +84,32 @@
             return inputs[index]
         return inputs[index].at[part if isinstance(part, int) else (high ^ int(part))]
 
-    rights = [
-        pltpu.make_async_copy(view(name), columns_in.at[n, i], column_sem.at[2 * n + i])
-        for n, names in enumerate(plan["blocks"])
-        for i, name in enumerate(names)
+    jobs = [
+        (side, cc, kind, which)
+        for side, (cc, wanted) in enumerate(plan["sides"])
+        for kind, which in wanted
     ]
+    rights = []
+    for slot, (_, _, kind, which) in enumerate(jobs):
+        if kind == "dx":
+            options = [(None, which)]
+        else:
+            dx = (which + 4 - shift) % 4
+            options = [(dx == k, k) for k in plan["order"]]
+        rights.append(
+            [
+                (
+                    here,
+                    pltpu.make_async_copy(
+                        view(plan["blocks"][plan["order"].index(k)][i]),
+                        columns_in.at[slot, i],
+                        column_sem.at[2 * slot + i],
+                    ),
+                )
+                for here, k in options
+                for i in range(2)
+            ]
+        )
     lefts = [
         pltpu.make_async_copy(
             view(name),
@@ -98,54 +119,47 @@
         for k, names in enumerate(sides)
         for i, name in enumerate(names)
     ]
-    for copy in rights[:2] + lefts[:8] + rights[2:] + lefts[8:]:
-        copy.start()
+
+    def each(copies, act):
+        for here, copy in copies:
+            if here is None:
+                getattr(copy, act)()
+            else:
+                pl.when(here)(getattr(copy, act))
+
+    for slot, (side, *_) in enumerate(jobs):
+        each(rights[slot], "start")
+        if slot == 0 or jobs[slot - 1][0] != side:
+            each([(None, copy) for copy in lefts[8 * side : 8 * side + 8]], "start")
     outs = []
-    arrived = set()
-    slot = 0
-    for side, (cc, wanted) in enumerate(plan["sides"]):
-        for copy in lefts[8 * side : 8 * side + 8]:
-            copy.wait()
-        for kind, which in wanted:
-            if kind == "dz":
-                block = (which + 4 - shift) % 4
-                needed = range(len(plan["blocks"]))
-                options = [(None, which)]
-            else:
-                block = plan["order"].index(which)
-                needed = (block,)
-                dz = (shift + which) % 4
-                options = [(dz == d, d) for d in range(4)]
-            for n in needed:
-                if n not in arrived:
-                    arrived.add(n)
-                    for copy in rights[2 * n : 2 * n + 2]:
-                        copy.wait()
-            total = None
-            for i in range(2):
-                term = lax.dot_general(
-                    left[side, i],
-                    columns_in[block, i],
-                    (((1,), (1,)), ((), ())),
-                    preferred_element_type=jnp.float32,
-                )
-                total = term if total is None else total + term
-            result[slot] = total.astype(jnp.bfloat16)
-            for here, d in options:
-                copy = pltpu.make_async_copy(
+    for slot, (side, cc, kind, which) in enumerate(jobs):
+        if slot == 0 or jobs[slot - 1][0] != side:
+            each([(None, copy) for copy in lefts[8 * side : 8 * side + 8]], "wait")
+        each(rights[slot], "wait")
+        total = None
+        for i in range(2):
+            term = lax.dot_general(
+                left[side, i],
+                columns_in[slot, i],
+                (((1,), (1,)), ((), ())),
+                preferred_element_type=jnp.float32,
+            )
+            total = term if total is None else total + term
+        result[slot] = total.astype(jnp.bfloat16)
+        dz = (shift + which) % 4
+        options = [(dz == d, d) for d in range(4)] if kind == "dx" else [(None, which)]
+        copies = [
+            (
+                here,
+                pltpu.make_async_copy(
                     result.at[slot], targets[cc][d].at[cc], out_sem.at[slot]
-                )
-                outs.append((here, copy))
-                if here is None:
-                    copy.start()
-                else:
-                    pl.when(here)(copy.start)
-            slot += 1
-    for here, copy in outs:
-        if here is None:
-            copy.wait()
-        else:
-            pl.when(here)(copy.wait)
+                ),
+            )
+            for here, d in options
+        ]
+        each(copies, "start")
+        outs += copies
+    each(outs, "wait")
 
 
 def block_product(place, sides, blocks, kept=(), limit=60):
@@ -184,10 +198,10 @@
         input_output_aliases={1 + len(inputs) + n: n for n in range(len(kept))},
         scratch_shapes=[
             pltpu.VMEM((len(sides), 2, 4 * half, items), jnp.bfloat16),
-            pltpu.VMEM((n_blocks, 2, half, items), jnp.bfloat16),
+            pltpu.VMEM((n_results, 2, half, items), jnp.bfloat16),
             pltpu.VMEM((n_results, 4 * half, half), jnp.bfloat16),
             pltpu.SemaphoreType.DMA((2 * len(groups),)),
-            pltpu.SemaphoreType.DMA((2 * n_blocks,)),
+            pltpu.SemaphoreType.DMA((2 * n_results,)),
             pltpu.SemaphoreType.DMA((n_results,)),
         ],
         compiler_params=pltpu.CompilerParams(vmem_limit_bytes=limit * 1024 * 1024),
@@ -214,24 +228,16 @@
     width = share.shape[1]
     share = share.reshape(16, items // 16, width)
 
-    below_n, above_f, near1, far1 = together(
-        [
-            (near, X_STEP[1]),
-            (far, X_STEP[3]),
-            (outer, NEAR),
-            (inner, FAR),
-        ],
-        (share,),
-    )
-    below_f, above_n, two0, two1, right_c = together(
-        [(far, X_STEP[1]), (near, X_STEP[3]), (far, NEAR), (near, FAR), (right, CORE)],
-        (below_n, above_f),
+    below_n, above_f = together([(near, X_STEP[1]), (far, X_STEP[3])], (share,))
+    near1, far1 = together([(outer, NEAR), (inner, FAR)], (near, far, share))
+    below_f, above_n = together([(far, X_STEP[1]), (near, X_STEP[3])], (below_n, above_f))
+    two0, two1, right_c = together(
+        [(far, NEAR), (near, FAR), (right, CORE)], (near1, far1)
     )
     rim = jnp.stack([near1, far1])
-    rim_c, two0_c, two1_c = together(
-        [(rim, CORE), (two0, CORE), (two1, CORE)], (below_f, above_n)
-    )
     across = together([(below_n, X_STEP[1]), (above_f, X_STEP[3])], (below_f, above_n))
+    (rim_c,) = together([(rim, CORE)])
+    two0_c, two1_c = together([(two0, CORE), (two1, CORE)])
     side = (
         ((whole, "0"), two0),
         ((whole, "1"), two1),

time: 156 us -> 152 us (0.974)
  waiting for transfers between devices: 69 us -> 67 us
    ppermute x25, waiting for transfers between devices: 69 us -> 67 us  [send(): return lax.ppermute(value, AXES, pairs)]
  transfers between devices with their start and end apart: 26 -> 26, of which waited for: 16 -> 14; matrix products, arithmetic and copies ran while one was open for 7% -> 8% of each run, Pallas kernels for 12% -> 13%
where the time goes in v9:
time: 152 us
  waiting for transfers between devices  67 us (44%)
  starting transfers between devices  37.3 us (25%)
  Pallas kernels  29.9 us (20%)
  other arithmetic  10.6 us (7%)
  local copies, waits for them, and re-layouts  3.71 us (2%)
  matrix products  2.57 us (2%)
    ppermute x25, waiting for transfers between devices, send(): return lax.ppermute(value, AXES, pairs)  67 us
    ppermute x25, starting transfers between devices, send(): return lax.ppermute(value, AXES, pairs)  32.8 us
    pallas_call x3, Pallas kernels, block_product(): pl.pallas_call(functools.partial(block_kernel, plan, groups), out_shape=[...  29.9 us
    all_to_all x1, starting transfers between devices, on_device(): shares = lax.all_to_all(share, 'feat', 0, 0)  4.44 us
    convert_element_type x2, other arithmetic, narrow(): return value.astype(jnp.bfloat16)  4.35 us
  transfers between devices with their start and end apart: 26, of which 14 were waited for; matrix products, arithmetic and copies ran while one was open for 8% of the time, Pallas kernels for 13%

profile of v9, /device:TPU:0, one launch (start us, length us, event | category | flops | bytes accessed | tf_op | source)
XLA Modules:
  0.0 152.0 jit_solution(11827692424034526545)
XLA Ops:
  0.7 1.6 %copy.11 = bf16[512,1024]{1,0:T(8,128)(2,1)S(1)} copy(bf16[512,1024]{0,1:T(8,128)(2,1)} %bitcast.47) | data formatting | bytes 2097152 | tf_op jit(solution)/shard_map/transpose | solution.py:223
  2.5 1.7 %collective-permute-start = (bf16[256,1024]{1,0:T(8,128)(2,1)S(1)}, bf16[256,1024]{1,0:T(8,128)(2,1)S(1)}, u32[]{:S(2)}, u32[]{:S(2)}) collective-permute-start(bf16[256,1024]{1,0:T(8,128)(2,1)S(1)} %get-tuple-element.72), channel_id=1, source_target_pairs={{0,16},{1,17},{2,18},{3,19},{4,20},{5,21},{6,22},{7,23},{8,24},{9,... | collective-permute-start | bytes 1572872 | tf_op jit(solution)/shard_map/ppermute | solution.py:46
  4.2 2.2 %collective-permute-start.1 = (bf16[256,1024]{1,0:T(8,128)(2,1)S(1)}, bf16[256,1024]{1,0:T(8,128)(2,1)S(1)}, u32[]{:S(2)}, u32[]{:S(2)}) collective-permute-start(bf16[256,1024]{1,0:T(8,128)(2,1)S(1)} %get-tuple-element.71), channel_id=1, source_target_pairs={{0,17},{1,16},{2,19},{3,18},{4,21},{5,20},{6,23},{7,22},{8,25},{9,... | collective-permute-start | bytes 1572872 | tf_op jit(solution)/shard_map/ppermute | solution.py:46
  6.4 2.6 %convolution_convert_fusion = bf16[1024,1024]{1,0:T(8,128)(2,1)} fusion(bf16[1024,512]{1,0:T(8,128)(2,1)S(1)} %copy-done.14, bf16[512,1024]{1,0:T(8,128)(2,1)S(1)} %copy-done), kind=kOutput, calls=%fused_computation.1 | convolution fusion | flops 1074790400 | bytes 4194304 | tf_op jit(solution)/shard_map/dot_general | solution.py:227
  9.0 7.8 %collective-permute-done.refs_4_.refs_9_.refs_6_ = bf16[256,1024]{1,0:T(8,128)(2,1)S(1)} collective-permute-done((bf16[256,1024]{1,0:T(8,128)(2,1)S(1)}, bf16[256,1024]{1,0:T(8,128)(2,1)S(1)}, u32[]{:S(2)}, u32[]{:S(2)}) %collective-permute-start) | collective-permute-done | bytes 524320 | tf_op jit(solution)/shard_map/ppermute | solution.py:46
  16.9 2.6 %collective-permute-done.1.refs_5_.refs_10_.refs_7_ = bf16[256,1024]{1,0:T(8,128)(2,1)S(1)} collective-permute-done((bf16[256,1024]{1,0:T(8,128)(2,1)S(1)}, bf16[256,1024]{1,0:T(8,128)(2,1)S(1)}, u32[]{:S(2)}, u32[]{:S(2)}) %collective-permute-start.1) | collective-permute-done | bytes 524320 | tf_op jit(solution)/shard_map/ppermute | solution.py:46
  19.5 2.3 %collective-permute-start.4 = (bf16[256,1024]{1,0:T(8,128)(2,1)S(1)}, bf16[256,1024]{1,0:T(8,128)(2,1)S(1)}, u32[]{:S(2)}, u32[]{:S(2)}) collective-permute-start(bf16[256,1024]{1,0:T(8,128)(2,1)S(1)} %get-tuple-element.72), channel_id=1, source_target_pairs={{0,17},{1,16},{2,19},{3,18},{4,21},{5,20},{6,23},{7,22},{8,25},{9,... | collective-permute-start | bytes 1572872 | tf_op jit(solution)/shard_map/ppermute | solution.py:46
  23.3 1.7 %collective-permute-start.12 = (bf16[256,1024]{1,0:T(8,128)(2,1)S(1)}, bf16[256,1024]{1,0:T(8,128)(2,1)}, u32[]{:S(2)}, u32[]{:S(2)}) collective-permute-start(bf16[256,1024]{1,0:T(8,128)(2,1)S(1)} %collective-permute-done.1.refs_5_.refs_10_.refs_7_), channel_id=1, source_target_pairs={{0,96},{1,97},{2,98},{3,99},{4,100},{5,101},{6,102},{7,103},{8,104... | collective-permute-start | bytes 1572872 | tf_op jit(solution)/shard_map/ppermute | solution.py:46
  25.1 7.5 %collective-permute-done.3.refs_6_.refs_11_ = bf16[256,1024]{1,0:T(8,128)(2,1)S(1)} collective-permute-done((bf16[256,1024]{1,0:T(8,128)(2,1)S(1)}, bf16[256,1024]{1,0:T(8,128)(2,1)S(1)}, u32[]{:S(2)}, u32[]{:S(2)}) %collective-permute-start.3) | collective-permute-done | bytes 524320 | tf_op jit(solution)/shard_map/ppermute | solution.py:46
  34.0 2.0 %collective-permute-done.11.refs_10_.refs_17_.refs_12_ = bf16[256,1024]{1,0:T(8,128)(2,1)} collective-permute-done((bf16[256,1024]{1,0:T(8,128)(2,1)S(1)}, bf16[256,1024]{1,0:T(8,128)(2,1)}, u32[]{:S(2)}, u32[]{:S(2)}) %collective-permute-start.11) | collective-permute-done | bytes 524320 | tf_op jit(solution)/shard_map/ppermute | solution.py:46
  39.6 1.7 %collective-permute-start.14 = (bf16[256,1024]{1,0:T(8,128)(2,1)S(1)}, bf16[256,1024]{1,0:T(8,128)(2,1)S(1)}, u32[]{:S(2)}, u32[]{:S(2)}) collective-permute-start(bf16[256,1024]{1,0:T(8,128)(2,1)S(1)} %collective-permute-done.refs_4_.refs_9_.refs_6_), channel_id=1, source_target_pairs={{0,96},{1,97},{2,98},{3,99},{4,100},{5,101},{6,102},{7,103},{8,104... | collective-permute-start | bytes 1572872 | tf_op jit(solution)/shard_map/ppermute | solution.py:46
  42.4 9.1 %collective-permute-done.13.refs_11_.refs_18_.refs_13_ = bf16[256,1024]{1,0:T(8,128)(2,1)S(1)} collective-permute-done((bf16[256,1024]{1,0:T(8,128)(2,1)S(1)}, bf16[256,1024]{1,0:T(8,128)(2,1)S(1)}, u32[]{:S(2)}, u32[]{:S(2)}) %collective-permute-start.13) | collective-permute-done | bytes 524320 | tf_op jit(solution)/shard_map/ppermute | solution.py:46
  51.5 1.5 %collective-permute-done.14.refs_8_.refs_13_ = bf16[256,1024]{1,0:T(8,128)(2,1)S(1)} collective-permute-done((bf16[256,1024]{1,0:T(8,128)(2,1)S(1)}, bf16[256,1024]{1,0:T(8,128)(2,1)S(1)}, u32[]{:S(2)}, u32[]{:S(2)}) %collective-permute-start.14) | collective-permute-done | bytes 524320 | tf_op jit(solution)/shard_map/ppermute | solution.py:46
  54.3 2.0 %collective-permute-start.16 = (bf16[256,1024]{1,0:T(8,128)(2,1)}, bf16[256,1024]{1,0:T(8,128)(2,1)S(1)}, u32[]{:S(2)}, u32[]{:S(2)}) collective-permute-start(bf16[256,1024]{1,0:T(8,128)(2,1)} %collective-permute-done.12.refs_9_.refs_14_), channel_id=1, source_target_pairs={{0,96},{1,97},{2,98},{3,99},{4,100},{5,101},{6,102},{7,103},{8,104... | collective-permute-start | bytes 1572872 | tf_op jit(solution)/shard_map/ppermute | solution.py:46
  58.0 10.7 %shard_map.50 = (bf16[2,1024,256]{2,1,0:T(8,128)(2,1)}, bf16[2,1024,256]{2,1,0:T(8,128)(2,1)}, bf16[2,1024,256]{2,1,0:T(8,128)(2,1)}, bf16[2,1024,256]{2,1,0:T(8,128)(2,1)}) custom-call(s32[2]{0:T(128)} %pad_add_fusion.refs_0_, bf16[2,256,1024]{2,1,0:T(8,128)(2,1)} %bitcast.39, bf16[256,1024]{1,0:T(8,128)(2,1)} %collective-permute-done.5.refs_2_.refs_7_, ...), custom_call_target="tpu_custom_call" | custom-call | flops 65536 | bytes 262144 | tf_op jit(solution)/shard_map/pallas_call | solution.py:192
  69.7 10.2 %shard_map.51 = (bf16[2,1024,256]{2,1,0:T(8,128)(2,1)}, bf16[2,1024,256]{2,1,0:T(8,128)(2,1)}, bf16[2,1024,256]{2,1,0:T(8,128)(2,1)}, bf16[2,1024,256]{2,1,0:T(8,128)(2,1)}) custom-call(s32[2]{0:T(128)} %pad_add_fusion.refs_0_, bf16[2,256,1024]{2,1,0:T(8,128)(2,1)} %copy-done.9, ...), custom_call_target="tpu_custom_call", output_to_operand_aliasing={{0}: (19, {}), {1}: (20, {}), {2}: (21, {}), {3}: (22, {})} | custom-call | flops 65536 | bytes 262144 | tf_op jit(solution)/shard_map/pallas_call | solution.py:192
  79.9 4.1 %collective-permute-start.17 = (bf16[2,1024,256]{2,1,0:T(8,128)(2,1)}, bf16[2,1024,256]{2,1,0:T(8,128)(2,1)S(1)}, u32[]{:S(2)}, u32[]{:S(2)}) collective-permute-start(bf16[2,1024,256]{2,1,0:T(8,128)(2,1)} %get-tuple-element.109), channel_id=1, source_target_pairs={{0,6},{1,7},{2,0},{3,1},{4,2},{5,3},{6,4},{7,5},{8,14},{9,15},{10,... | collective-permute-start | bytes 3145736 | tf_op jit(solution)/shard_map/ppermute | solution.py:46
  83.9 4.4 %all-to-all-start = ((bf16[16,64,1024]{2,1,0:T(8,128)(2,1)}), bf16[16,64,1024]{2,1,0:T(8,128)(2,1)}, u32[]{:S(2)}, u32[]{:S(2)}) async-start(bf16[16,64,1024]{2,1,0:T(8,128)(2,1)} %bitcast), calls=%async_computation | async-start | bytes 4194304 | tf_op jit(solution)/shard_map/all_to_all | solution.py:264
  88.4 9.1 %shard_map.52 = (bf16[2,1024,256]{2,1,0:T(8,128)(2,1)}, bf16[2,1024,256]{2,1,0:T(8,128)(2,1)}) custom-call(s32[2]{0:T(128)} %pad_add_fusion.refs_0_, bf16[2,256,1024]{2,1,0:T(8,128)(2,1)} %copy-done.9, bf16[256,1024]{1,0:T(8,128)(2,1)} %copy-done.13, ...), custom_call_target="tpu_custom_call", output_to_operand_aliasing={{0}: (14, {}), {1}: (15, {})} | custom-call | flops 65536 | bytes 262144 | tf_op jit(solution)/shard_map/pallas_call | solution.py:192
  97.5 9.9 %collective-permute-done.17 = bf16[2,1024,256]{2,1,0:T(8,128)(2,1)S(1)} collective-permute-done((bf16[2,1024,256]{2,1,0:T(8,128)(2,1)}, bf16[2,1024,256]{2,1,0:T(8,128)(2,1)S(1)}, u32[]{:S(2)}, u32[]{:S(2)}) %collective-permute-start.17) | collective-permute-done | bytes 1048608 | tf_op jit(solution)/shard_map/ppermute | solution.py:46
  107.3 3.4 %collective-permute-done.18 = bf16[2,1024,256]{2,1,0:T(8,128)(2,1)} collective-permute-done((bf16[2,1024,256]{2,1,0:T(8,128)(2,1)}, bf16[2,1024,256]{2,1,0:T(8,128)(2,1)}, u32[]{:S(2)}, u32[]{:S(2)}) %collective-permute-start.18) | collective-permute-done | bytes 1048608 | tf_op jit(solution)/shard_map/ppermute | solution.py:46
  110.8 2.6 %fusion.3 = (bf16[1024,256]{1,0:T(8,128)(2,1)}, bf16[1024,256]{1,0:T(8,128)(2,1)}) fusion(bf16[2,1024,256]{2,1,0:T(8,128)(2,1)} %get-tuple-element.113, bf16[2,1024,256]{2,1,0:T(8,128)(2,1)} %collective-permute-done.18, bf16[2,1024,256]{2,1,0:T(8,128)(2,1)S(1)} %collective-permute-done.17), kind=kLoop, calls=%fused_computation.11 | loop fusion | flops 2097152 | bytes 3145728 | tf_op jit(solution)/shard_map/convert_element_type | solution.py:58
  113.5 1.8 %collective-permute-start.20 = (bf16[1024,256]{1,0:T(8,128)(2,1)}, bf16[1024,256]{1,0:T(8,128)(2,1)}, u32[]{:S(2)}, u32[]{:S(2)}) collective-permute-start(bf16[1024,256]{1,0:T(8,128)(2,1)} %get-tuple-element.115), channel_id=1, source_target_pairs={{0,2},{1,3},{2,4},{3,5},{4,6},{5,7},{6,0},{7,1},{8,10},{9,11},{10,... | collective-permute-start | bytes 1572872 | tf_op jit(solution)/shard_map/ppermute | solution.py:46
  115.4 11.5 %collective-permute-done.19 = bf16[1024,256]{1,0:T(8,128)(2,1)} collective-permute-done((bf16[1024,256]{1,0:T(8,128)(2,1)}, bf16[1024,256]{1,0:T(8,128)(2,1)}, u32[]{:S(2)}, u32[]{:S(2)}) %collective-permute-start.19) | collective-permute-done | bytes 524320 | tf_op jit(solution)/shard_map/ppermute | solution.py:46
  128.3 1.8 %fusion = (bf16[1024,256]{1,0:T(8,128)(2,1)S(1)}, bf16[1024,256]{1,0:T(8,128)(2,1)S(1)}) fusion(bf16[1024,256]{1,0:T(8,128)(2,1)} %collective-permute-done.20, bf16[2,1024,256]{2,1,0:T(8,128)(2,1)S(1)} %collective-permute-done.17, bf16[2,1024,256]{2,1,0:T(8,128)(2,1)S(1)} %copy-done.2, bf16[1024,256]{1,0:T(8,128)(2,1)} %collective-permute-done.19, ...), kind=kLoop, calls=%fused_computation.5 | loop fusion | flops 3145728 | bytes 4194304 | tf_op jit(solution)/shard_map/convert_element_type | solution.py:58
  130.2 2.1 %collective-permute-start.21 = (bf16[512,256]{1,0:T(8,128)(2,1)S(1)}, bf16[512,256]{1,0:T(8,128)(2,1)S(1)}, u32[]{:S(2)}, u32[]{:S(2)}) collective-permute-start(bf16[512,256]{1,0:T(8,128)(2,1)S(1)} %get-tuple-element.118), channel_id=1, source_target_pairs={{0,1},{1,17},{2,3},{3,19},{4,5},{5,21},{6,7},{7,23},{8,9},{9,25},{... | collective-permute-start | bytes 786440 | tf_op jit(solution)/shard_map/ppermute | solution.py:46
  132.3 3.1 %collective-permute-start.23 = (bf16[512,256]{1,0:T(8,128)(2,1)S(1)}, bf16[512,256]{1,0:T(8,128)(2,1)S(1)}, u32[]{:S(2)}, u32[]{:S(2)}) collective-permute-start(bf16[512,256]{1,0:T(8,128)(2,1)S(1)} %get-tuple-element.120), channel_id=1, source_target_pairs={{0,17},{1,1},{2,19},{3,3},{4,21},{5,5},{6,23},{7,7},{8,25},{9,9},{... | collective-permute-start | bytes 786440 | tf_op jit(solution)/shard_map/ppermute | solution.py:46
  135.3 3.4 %collective-permute-start.24 = (bf16[512,256]{1,0:T(8,128)(2,1)S(1)}, bf16[512,256]{1,0:T(8,128)(2,1)S(1)}, u32[]{:S(2)}, u32[]{:S(2)}) collective-permute-start(bf16[512,256]{1,0:T(8,128)(2,1)S(1)} %get-tuple-element.121), channel_id=1, source_target_pairs={{0,25},{1,9},{2,27},{3,11},{4,29},{5,13},{6,31},{7,15},{8,17},{9,1... | collective-permute-start | bytes 786440 | tf_op jit(solution)/shard_map/ppermute | solution.py:46
  138.7 2.7 %reduce_sum.12 = bf16[64,1024]{1,0:T(8,128)(2,1)} reduce(bf16[16,64,1024]{2,1,0:T(8,128)(2,1)} %all-to-all-done, bf16[]{:T(256)} %constant.91.clone.1), dimensions={0}, to_apply=%region_0.1 | reduce | flops 983040 | bytes 2228226 | tf_op jit(solution)/shard_map/reduce_sum | solution.py:278
  142.1 1.5 collective-permute-done.23
  143.6 6.5 %collective-permute-done.24 = bf16[512,256]{1,0:T(8,128)(2,1)S(1)} collective-permute-done((bf16[512,256]{1,0:T(8,128)(2,1)S(1)}, bf16[512,256]{1,0:T(8,128)(2,1)S(1)}, u32[]{:S(2)}, u32[]{:S(2)}) %collective-permute-start.24) | collective-permute-done | bytes 262176 | tf_op jit(solution)/shard_map/ppermute | solution.py:46
  150.3 1.7 %multiply_add_fusion = f32[512,1024]{1,0:T(8,128)} fusion(f32[512,1024]{1,0:T(8,128)S(1)} %copy-done.11, bf16[256,256]{1,0:T(8,128)(2,1)S(1)} %get-tuple-element.145, bf16[256,256]{1,0:T(8,128)(2,1)S(1)} %get-tuple-element.144, bf16[512,256]{1,0:T(8,128)(2,1)S(1)} %get-tuple-element.130, bf16[256,256]{1,0:T(8,128)(2,1)S(1)} %get-tuple-element.143, ...), kind=kLoop, calls=%fused_computation | loop fusion | flops 7864320 | bytes 5242880 | tf_op jit(solution)/shard_map/add | solution.py:292
  (67 shorter events, 14.3 us)
Async XLA Ops:
  2.4 17.0 %collective-permute-start.2 = (bf16[2,256,1024]{2,1,0:T(8,128)(2,1)S(1)}, bf16[2,256,1024]{2,1,0:T(8,128)(2,1)S(1)}, u32[]{:S(2)}, u32[]{:S(2)}) collective-permute-start(bf16[2,256,1024]{2,1,0:T(8,128)(2,1)S(1)} %bitcast.38), channel_id=1, source_target_pairs={{0,8},{1,9},{2,10},{3,11},{4,12},{5,13},{6,14},{7,15},{8,0},{9,1},... | collective-permute-start | bytes 3145736 | tf_op jit(solution)/shard_map/ppermute | solution.py:46
  2.5 14.3 %collective-permute-start = (bf16[256,1024]{1,0:T(8,128)(2,1)S(1)}, bf16[256,1024]{1,0:T(8,128)(2,1)S(1)}, u32[]{:S(2)}, u32[]{:S(2)}) collective-permute-start(bf16[256,1024]{1,0:T(8,128)(2,1)S(1)} %get-tuple-element.72), channel_id=1, source_target_pairs={{0,16},{1,17},{2,18},{3,19},{4,20},{5,21},{6,22},{7,23},{8,24},{9,... | collective-permute-start | bytes 1572872 | tf_op jit(solution)/shard_map/ppermute | solution.py:46
  4.2 15.2 %collective-permute-start.1 = (bf16[256,1024]{1,0:T(8,128)(2,1)S(1)}, bf16[256,1024]{1,0:T(8,128)(2,1)S(1)}, u32[]{:S(2)}, u32[]{:S(2)}) collective-permute-start(bf16[256,1024]{1,0:T(8,128)(2,1)S(1)} %get-tuple-element.71), channel_id=1, source_target_pairs={{0,17},{1,16},{2,19},{3,18},{4,21},{5,20},{6,23},{7,22},{8,25},{9,... | collective-permute-start | bytes 1572872 | tf_op jit(solution)/shard_map/ppermute | solution.py:46
  16.9 25.6 %copy-start.3 = (bf16[256,1024]{1,0:T(8,128)(2,1)}, bf16[256,1024]{1,0:T(8,128)(2,1)S(1)}, u32[]{:S(2)}) copy-start(bf16[256,1024]{1,0:T(8,128)(2,1)S(1)} %collective-permute-done.refs_4_.refs_9_.refs_6_) | copy-start | bytes 1572868
  19.4 23.0 %copy-start.4 = (bf16[256,1024]{1,0:T(8,128)(2,1)}, bf16[256,1024]{1,0:T(8,128)(2,1)S(1)}, u32[]{:S(2)}) copy-start(bf16[256,1024]{1,0:T(8,128)(2,1)S(1)} %collective-permute-done.1.refs_5_.refs_10_.refs_7_) | copy-start | bytes 1572868
  19.4 23.0 %copy-start.9 = (bf16[2,256,1024]{2,1,0:T(8,128)(2,1)}, bf16[2,256,1024]{2,1,0:T(8,128)(2,1)S(1)}, u32[]{:S(2)}) copy-start(bf16[2,256,1024]{2,1,0:T(8,128)(2,1)S(1)} %collective-permute-done.2.refs_1_) | copy-start | bytes 3145732
  19.4 13.2 %collective-permute-start.3 = (bf16[256,1024]{1,0:T(8,128)(2,1)S(1)}, bf16[256,1024]{1,0:T(8,128)(2,1)S(1)}, u32[]{:S(2)}, u32[]{:S(2)}) collective-permute-start(bf16[256,1024]{1,0:T(8,128)(2,1)S(1)} %get-tuple-element.71), channel_id=1, source_target_pairs={{0,16},{1,17},{2,18},{3,19},{4,20},{5,21},{6,22},{7,23},{8,24},{9,... | collective-permute-start | bytes 1572872 | tf_op jit(solution)/shard_map/ppermute | solution.py:46
  19.5 14.4 %collective-permute-start.4 = (bf16[256,1024]{1,0:T(8,128)(2,1)S(1)}, bf16[256,1024]{1,0:T(8,128)(2,1)S(1)}, u32[]{:S(2)}, u32[]{:S(2)}) collective-permute-start(bf16[256,1024]{1,0:T(8,128)(2,1)S(1)} %get-tuple-element.72), channel_id=1, source_target_pairs={{0,17},{1,16},{2,19},{3,18},{4,21},{5,20},{6,23},{7,22},{8,25},{9,... | collective-permute-start | bytes 1572872 | tf_op jit(solution)/shard_map/ppermute | solution.py:46
  21.8 14.2 %collective-permute-start.11 = (bf16[256,1024]{1,0:T(8,128)(2,1)S(1)}, bf16[256,1024]{1,0:T(8,128)(2,1)}, u32[]{:S(2)}, u32[]{:S(2)}) collective-permute-start(bf16[256,1024]{1,0:T(8,128)(2,1)S(1)} %collective-permute-done.refs_4_.refs_9_.refs_6_), channel_id=1, source_target_pairs={{0,32},{1,33},{2,34},{3,35},{4,36},{5,37},{6,38},{7,39},{8,40},{9,... | collective-permute-start | bytes 1572872 | tf_op jit(solution)/shard_map/ppermute | solution.py:46
  23.3 12.7 %collective-permute-start.12 = (bf16[256,1024]{1,0:T(8,128)(2,1)S(1)}, bf16[256,1024]{1,0:T(8,128)(2,1)}, u32[]{:S(2)}, u32[]{:S(2)}) collective-permute-start(bf16[256,1024]{1,0:T(8,128)(2,1)S(1)} %collective-permute-done.1.refs_5_.refs_10_.refs_7_), channel_id=1, source_target_pairs={{0,96},{1,97},{2,98},{3,99},{4,100},{5,101},{6,102},{7,103},{8,104... | collective-permute-start | bytes 1572872 | tf_op jit(solution)/shard_map/ppermute | solution.py:46
  32.7 25.3 %copy-start.5 = (bf16[256,1024]{1,0:T(8,128)(2,1)}, bf16[256,1024]{1,0:T(8,128)(2,1)S(1)}, u32[]{:S(2)}) copy-start(bf16[256,1024]{1,0:T(8,128)(2,1)S(1)} %collective-permute-done.3.refs_6_.refs_11_) | copy-start | bytes 1572868
  34.0 24.0 %copy-start.6 = (bf16[256,1024]{1,0:T(8,128)(2,1)}, bf16[256,1024]{1,0:T(8,128)(2,1)S(1)}, u32[]{:S(2)}) copy-start(bf16[256,1024]{1,0:T(8,128)(2,1)S(1)} %collective-permute-done.4.refs_7_.refs_12_) | copy-start | bytes 1572868
  36.0 20.3 %collective-permute-start.7 = (bf16[2,256,1024]{2,1,0:T(8,128)(2,1)S(1)}, bf16[2,256,1024]{2,1,0:T(8,128)(2,1)S(1)}, u32[]{:S(2)}, u32[]{:S(2)}) collective-permute-start(bf16[2,256,1024]{2,1,0:T(8,128)(2,1)S(1)} %pad_maximum_fusion), channel_id=1, source_target_pairs={{0,8},{1,9},{2,10},{3,11},{4,12},{5,13},{6,14},{7,15},{8,0},{9,1},... | collective-permute-start | bytes 3145736 | tf_op jit(solution)/shard_map/ppermute | solution.py:46
  36.0 15.5 %collective-permute-start.13 = (bf16[256,1024]{1,0:T(8,128)(2,1)S(1)}, bf16[256,1024]{1,0:T(8,128)(2,1)S(1)}, u32[]{:S(2)}, u32[]{:S(2)}) collective-permute-start(bf16[256,1024]{1,0:T(8,128)(2,1)S(1)} %collective-permute-done.1.refs_5_.refs_10_.refs_7_), channel_id=1, source_target_pairs={{0,32},{1,33},{2,34},{3,35},{4,36},{5,37},{6,38},{7,39},{8,40},{9,... | collective-permute-start | bytes 1572872 | tf_op jit(solution)/shard_map/ppermute | solution.py:46
  37.5 16.8 %collective-permute-start.5 = (bf16[256,1024]{1,0:T(8,128)(2,1)S(1)}, bf16[256,1024]{1,0:T(8,128)(2,1)}, u32[]{:S(2)}, u32[]{:S(2)}) collective-permute-start(bf16[256,1024]{1,0:T(8,128)(2,1)S(1)} %collective-permute-done.1.refs_5_.refs_10_.refs_7_), channel_id=1, source_target_pairs={{0,16},{1,17},{2,18},{3,19},{4,20},{5,21},{6,22},{7,23},{8,24},{9,... | collective-permute-start | bytes 1572872 | tf_op jit(solution)/shard_map/ppermute | solution.py:46
  38.5 17.8 %collective-permute-start.6 = (bf16[256,1024]{1,0:T(8,128)(2,1)S(1)}, bf16[256,1024]{1,0:T(8,128)(2,1)}, u32[]{:S(2)}, u32[]{:S(2)}) collective-permute-start(bf16[256,1024]{1,0:T(8,128)(2,1)S(1)} %collective-permute-done.refs_4_.refs_9_.refs_6_), channel_id=1, source_target_pairs={{0,17},{1,16},{2,19},{3,18},{4,21},{5,20},{6,23},{7,22},{8,25},{9,... | collective-permute-start | bytes 1572872 | tf_op jit(solution)/shard_map/ppermute | solution.py:46
  39.6 13.5 %collective-permute-start.14 = (bf16[256,1024]{1,0:T(8,128)(2,1)S(1)}, bf16[256,1024]{1,0:T(8,128)(2,1)S(1)}, u32[]{:S(2)}, u32[]{:S(2)}) collective-permute-start(bf16[256,1024]{1,0:T(8,128)(2,1)S(1)} %collective-permute-done.refs_4_.refs_9_.refs_6_), channel_id=1, source_target_pairs={{0,96},{1,97},{2,98},{3,99},{4,100},{5,101},{6,102},{7,103},{8,104... | collective-permute-start | bytes 1572872 | tf_op jit(solution)/shard_map/ppermute | solution.py:46
  51.5 17.1 %collective-permute-start.10 = (bf16[2,256,1024]{2,1,0:T(8,128)(2,1)}, bf16[2,256,1024]{2,1,0:T(8,128)(2,1)}, u32[]{:S(2)}, u32[]{:S(2)}) collective-permute-start(bf16[2,256,1024]{2,1,0:T(8,128)(2,1)} %pad_maximum_fusion.1), channel_id=1, source_target_pairs={{0,8},{1,9},{2,10},{3,11},{4,12},{5,13},{6,14},{7,15},{8,0},{9,1},... | collective-permute-start | bytes 3145736 | tf_op jit(solution)/shard_map/ppermute | solution.py:46
  53.1 15.6 %collective-permute-start.15 = (bf16[256,1024]{1,0:T(8,128)(2,1)}, bf16[256,1024]{1,0:T(8,128)(2,1)}, u32[]{:S(2)}, u32[]{:S(2)}) collective-permute-start(bf16[256,1024]{1,0:T(8,128)(2,1)} %collective-permute-done.11.refs_10_.refs_17_.refs_12_), channel_id=1, source_target_pairs={{0,32},{1,33},{2,34},{3,35},{4,36},{5,37},{6,38},{7,39},{8,40},{9,... | collective-permute-start | bytes 1572872 | tf_op jit(solution)/shard_map/ppermute | solution.py:46
  54.3 14.4 %collective-permute-start.16 = (bf16[256,1024]{1,0:T(8,128)(2,1)}, bf16[256,1024]{1,0:T(8,128)(2,1)S(1)}, u32[]{:S(2)}, u32[]{:S(2)}) collective-permute-start(bf16[256,1024]{1,0:T(8,128)(2,1)} %collective-permute-done.12.refs_9_.refs_14_), channel_id=1, source_target_pairs={{0,96},{1,97},{2,98},{3,99},{4,100},{5,101},{6,102},{7,103},{8,104... | collective-permute-start | bytes 1572872 | tf_op jit(solution)/shard_map/ppermute | solution.py:46
  56.4 12.3 %collective-permute-start.8 = (bf16[256,1024]{1,0:T(8,128)(2,1)}, bf16[256,1024]{1,0:T(8,128)(2,1)S(1)}, u32[]{:S(2)}, u32[]{:S(2)}) collective-permute-start(bf16[256,1024]{1,0:T(8,128)(2,1)} %collective-permute-done.5.refs_2_.refs_7_), channel_id=1, source_target_pairs={{0,8},{1,9},{2,10},{3,11},{4,12},{5,13},{6,14},{7,15},{8,0},{9,1},... | collective-permute-start | bytes 1572872 | tf_op jit(solution)/shard_map/ppermute | solution.py:46
  57.3 11.4 %collective-permute-start.9 = (bf16[256,1024]{1,0:T(8,128)(2,1)}, bf16[256,1024]{1,0:T(8,128)(2,1)}, u32[]{:S(2)}, u32[]{:S(2)}) collective-permute-start(bf16[256,1024]{1,0:T(8,128)(2,1)} %collective-permute-done.6.refs_3_.refs_8_), channel_id=1, source_target_pairs={{0,8},{1,9},{2,10},{3,11},{4,12},{5,13},{6,14},{7,15},{8,0},{9,1},... | collective-permute-start | bytes 1572872 | tf_op jit(solution)/shard_map/ppermute | solution.py:46
  79.9 27.5 %collective-permute-start.17 = (bf16[2,1024,256]{2,1,0:T(8,128)(2,1)}, bf16[2,1024,256]{2,1,0:T(8,128)(2,1)S(1)}, u32[]{:S(2)}, u32[]{:S(2)}) collective-permute-start(bf16[2,1024,256]{2,1,0:T(8,128)(2,1)} %get-tuple-element.109), channel_id=1, source_target_pairs={{0,6},{1,7},{2,0},{3,1},{4,2},{5,3},{6,4},{7,5},{8,14},{9,15},{10,... | collective-permute-start | bytes 3145736 | tf_op jit(solution)/shard_map/ppermute | solution.py:46
  83.9 26.8 %collective-permute-start.18 = (bf16[2,1024,256]{2,1,0:T(8,128)(2,1)}, bf16[2,1024,256]{2,1,0:T(8,128)(2,1)}, u32[]{:S(2)}, u32[]{:S(2)}) collective-permute-start(bf16[2,1024,256]{2,1,0:T(8,128)(2,1)} %get-tuple-element.110), channel_id=1, source_target_pairs={{0,2},{1,3},{2,4},{3,5},{4,6},{5,7},{6,0},{7,1},{8,10},{9,11},{10,... | collective-permute-start | bytes 3145736 | tf_op jit(solution)/shard_map/ppermute | solution.py:46
  83.9 46.2 %all-to-all-start = ((bf16[16,64,1024]{2,1,0:T(8,128)(2,1)}), bf16[16,64,1024]{2,1,0:T(8,128)(2,1)}, u32[]{:S(2)}, u32[]{:S(2)}) async-start(bf16[16,64,1024]{2,1,0:T(8,128)(2,1)} %bitcast), calls=%async_computation | async-start | bytes 4194304 | tf_op jit(solution)/shard_map/all_to_all | solution.py:264
  97.5 30.9 %copy-start.2 = (bf16[2,1024,256]{2,1,0:T(8,128)(2,1)S(1)}, bf16[2,1024,256]{2,1,0:T(8,128)(2,1)}, u32[]{:S(2)}) copy-start(bf16[2,1024,256]{2,1,0:T(8,128)(2,1)} %get-tuple-element.106) | copy-start | bytes 3145732
  113.3 13.6 %collective-permute-start.19 = (bf16[1024,256]{1,0:T(8,128)(2,1)}, bf16[1024,256]{1,0:T(8,128)(2,1)}, u32[]{:S(2)}, u32[]{:S(2)}) collective-permute-start(bf16[1024,256]{1,0:T(8,128)(2,1)} %get-tuple-element.114), channel_id=1, source_target_pairs={{0,6},{1,7},{2,0},{3,1},{4,2},{5,3},{6,4},{7,5},{8,14},{9,15},{10,... | collective-permute-start | bytes 1572872 | tf_op jit(solution)/shard_map/ppermute | solution.py:46
  113.5 14.8 %collective-permute-start.20 = (bf16[1024,256]{1,0:T(8,128)(2,1)}, bf16[1024,256]{1,0:T(8,128)(2,1)}, u32[]{:S(2)}, u32[]{:S(2)}) collective-permute-start(bf16[1024,256]{1,0:T(8,128)(2,1)} %get-tuple-element.115), channel_id=1, source_target_pairs={{0,2},{1,3},{2,4},{3,5},{4,6},{5,7},{6,0},{7,1},{8,10},{9,11},{10,... | collective-permute-start | bytes 1572872 | tf_op jit(solution)/shard_map/ppermute | solution.py:46
  130.2 11.2 %collective-permute-start.21 = (bf16[512,256]{1,0:T(8,128)(2,1)S(1)}, bf16[512,256]{1,0:T(8,128)(2,1)S(1)}, u32[]{:S(2)}, u32[]{:S(2)}) collective-permute-start(bf16[512,256]{1,0:T(8,128)(2,1)S(1)} %get-tuple-element.118), channel_id=1, source_target_pairs={{0,1},{1,17},{2,3},{3,19},{4,5},{5,21},{6,7},{7,23},{8,9},{9,25},{... | collective-permute-start | bytes 786440 | tf_op jit(solution)/shard_map/ppermute | solution.py:46
  132.3 9.9 %collective-permute-start.22 = (bf16[512,256]{1,0:T(8,128)(2,1)S(1)}, bf16[512,256]{1,0:T(8,128)(2,1)S(1)}, u32[]{:S(2)}, u32[]{:S(2)}) collective-permute-start(bf16[512,256]{1,0:T(8,128)(2,1)S(1)} %get-tuple-element.119), channel_id=1, source_target_pairs={{0,9},{1,25},{2,11},{3,27},{4,13},{5,29},{6,15},{7,31},{8,1},{9,17... | collective-permute-start | bytes 786440 | tf_op jit(solution)/shard_map/ppermute | solution.py:46
  132.3 11.4 %collective-permute-start.23 = (bf16[512,256]{1,0:T(8,128)(2,1)S(1)}, bf16[512,256]{1,0:T(8,128)(2,1)S(1)}, u32[]{:S(2)}, u32[]{:S(2)}) collective-permute-start(bf16[512,256]{1,0:T(8,128)(2,1)S(1)} %get-tuple-element.120), channel_id=1, source_target_pairs={{0,17},{1,1},{2,19},{3,3},{4,21},{5,5},{6,23},{7,7},{8,25},{9,9},{... | collective-permute-start | bytes 786440 | tf_op jit(solution)/shard_map/ppermute | solution.py:46
  135.3 14.8 %collective-permute-start.24 = (bf16[512,256]{1,0:T(8,128)(2,1)S(1)}, bf16[512,256]{1,0:T(8,128)(2,1)S(1)}, u32[]{:S(2)}, u32[]{:S(2)}) collective-permute-start(bf16[512,256]{1,0:T(8,128)(2,1)S(1)} %get-tuple-element.121), channel_id=1, source_target_pairs={{0,25},{1,9},{2,27},{3,11},{4,29},{5,13},{6,31},{7,15},{8,17},{9,1... | collective-permute-start | bytes 786440 | tf_op jit(solution)/shard_map/ppermute | solution.py:46
  (9 other events, 38.1 us)

commit v10 on v9

--- a/solution.py
+++ b/solution.py
@@ -132,33 +132,42 @@
         if slot == 0 or jobs[slot - 1][0] != side:
             each([(None, copy) for copy in lefts[8 * side : 8 * side + 8]], "start")
     outs = []
-    for slot, (side, cc, kind, which) in enumerate(jobs):
-        if slot == 0 or jobs[slot - 1][0] != side:
-            each([(None, copy) for copy in lefts[8 * side : 8 * side + 8]], "wait")
-        each(rights[slot], "wait")
-        total = None
-        for i in range(2):
-            term = lax.dot_general(
-                left[side, i],
-                columns_in[slot, i],
-                (((1,), (1,)), ((), ())),
-                preferred_element_type=jnp.float32,
-            )
-            total = term if total is None else total + term
-        result[slot] = total.astype(jnp.bfloat16)
-        dz = (shift + which) % 4
-        options = [(dz == d, d) for d in range(4)] if kind == "dx" else [(None, which)]
-        copies = [
-            (
-                here,
-                pltpu.make_async_copy(
-                    result.at[slot], targets[cc][d].at[cc], out_sem.at[slot]
-                ),
-            )
-            for here, d in options
-        ]
-        each(copies, "start")
-        outs += copies
+    for side, (cc, wanted) in enumerate(plan["sides"]):
+        slots = [slot for slot, job in enumerate(jobs) if job[0] == side]
+        each([(None, copy) for copy in lefts[8 * side : 8 * side + 8]], "wait")
+        for slot in slots:
+            each(rights[slot], "wait")
+
+        def multiply(slot, carry):
+            for group in range(4):
+                here = slice(group * rows, (group + 1) * rows)
+                total = None
+                for i in range(2):
+                    term = lax.dot_general(
+                        left[side, i, here],
+                        columns_in[slot, i],
+                        (((1,), (1,)), ((), ())),
+                        preferred_element_type=jnp.float32,
+                    )
+                    total = term if total is None else total + term
+                result[slot, here] = total.astype(jnp.bfloat16)
+            return carry
+
+        lax.fori_loop(slots[0], slots[-1] + 1, multiply, 0)
+        for slot, (kind, which) in zip(slots, wanted):
+            dz = (shift + which) % 4
+            options = [(dz == d, d) for d in range(4)] if kind == "dx" else [(None, which)]
+            copies = [
+                (
+                    here,
+                    pltpu.make_async_copy(
+                        result.at[slot], targets[cc][d].at[cc], out_sem.at[slot]
+                    ),
+                )
+                for here, d in options
+            ]
+            each(copies, "start")
+            outs += copies
     each(outs, "wait")
 
 

time: 152 us -> 149 us (0.980)
  Pallas kernels: 29.9 us -> 25 us
    pallas_call x3, Pallas kernels: 29.9 us -> 25 us  [block_product(): pl.pallas_call(functools.partial(block_kernel, plan, groups), out_shape=[...]
  transfers between devices with their start and end apart: 26 -> 26, of which waited for: 14 -> 15; matrix products, arithmetic and copies ran while one was open for 8% -> 8% of each run, Pallas kernels for 13% -> 11%
where the time goes in v10:
time: 149 us
  waiting for transfers between devices  68.1 us (46%)
  starting transfers between devices  37.7 us (25%)
  Pallas kernels  25 us (17%)
  other arithmetic  10.6 us (7%)
  local copies, waits for them, and re-layouts  3.72 us (2%)
  matrix products  2.57 us (2%)
    ppermute x25, waiting for transfers between devices, send(): return lax.ppermute(value, AXES, pairs)  68.1 us
    ppermute x25, starting transfers between devices, send(): return lax.ppermute(value, AXES, pairs)  32.7 us
    pallas_call x3, Pallas kernels, block_product(): pl.pallas_call(functools.partial(block_kernel, plan, groups), out_shape=[...  25 us
    all_to_all x1, starting transfers between devices, on_device(): shares = lax.all_to_all(share, 'feat', 0, 0)  4.96 us
    convert_element_type x2, other arithmetic, narrow(): return value.astype(jnp.bfloat16)  4.35 us
  transfers between devices with their start and end apart: 26, of which 15 were waited for; matrix products, arithmetic and copies ran while one was open for 8% of the time, Pallas kernels for 11%

profile of v10, /device:TPU:0, one launch (start us, length us, event | category | flops | bytes accessed | tf_op | source)
XLA Modules:
  0.0 148.5 jit_solution(2643641876199926881)
XLA Ops:
  0.7 1.6 %copy.11 = bf16[512,1024]{1,0:T(8,128)(2,1)S(1)} copy(bf16[512,1024]{0,1:T(8,128)(2,1)} %bitcast.47) | data formatting | bytes 2097152 | tf_op jit(solution)/shard_map/transpose | solution.py:232
  2.5 1.7 %collective-permute-start = (bf16[256,1024]{1,0:T(8,128)(2,1)S(1)}, bf16[256,1024]{1,0:T(8,128)(2,1)S(1)}, u32[]{:S(2)}, u32[]{:S(2)}) collective-permute-start(bf16[256,1024]{1,0:T(8,128)(2,1)S(1)} %get-tuple-element.72), channel_id=1, source_target_pairs={{0,16},{1,17},{2,18},{3,19},{4,20},{5,21},{6,22},{7,23},{8,24},{9,... | collective-permute-start | bytes 1572872 | tf_op jit(solution)/shard_map/ppermute | solution.py:46
  4.2 2.2 %collective-permute-start.1 = (bf16[256,1024]{1,0:T(8,128)(2,1)S(1)}, bf16[256,1024]{1,0:T(8,128)(2,1)S(1)}, u32[]{:S(2)}, u32[]{:S(2)}) collective-permute-start(bf16[256,1024]{1,0:T(8,128)(2,1)S(1)} %get-tuple-element.71), channel_id=1, source_target_pairs={{0,17},{1,16},{2,19},{3,18},{4,21},{5,20},{6,23},{7,22},{8,25},{9,... | collective-permute-start | bytes 1572872 | tf_op jit(solution)/shard_map/ppermute | solution.py:46
  6.4 2.6 %convolution_convert_fusion = bf16[1024,1024]{1,0:T(8,128)(2,1)} fusion(bf16[1024,512]{1,0:T(8,128)(2,1)S(1)} %copy-done.14, bf16[512,1024]{1,0:T(8,128)(2,1)S(1)} %copy-done), kind=kOutput, calls=%fused_computation.1 | convolution fusion | flops 1074790400 | bytes 4194304 | tf_op jit(solution)/shard_map/dot_general | solution.py:236
  9.0 7.8 %collective-permute-done.refs_4_.refs_9_.refs_6_ = bf16[256,1024]{1,0:T(8,128)(2,1)S(1)} collective-permute-done((bf16[256,1024]{1,0:T(8,128)(2,1)S(1)}, bf16[256,1024]{1,0:T(8,128)(2,1)S(1)}, u32[]{:S(2)}, u32[]{:S(2)}) %collective-permute-start) | collective-permute-done | bytes 524320 | tf_op jit(solution)/shard_map/ppermute | solution.py:46
  16.9 2.6 %collective-permute-done.1.refs_5_.refs_10_.refs_7_ = bf16[256,1024]{1,0:T(8,128)(2,1)S(1)} collective-permute-done((bf16[256,1024]{1,0:T(8,128)(2,1)S(1)}, bf16[256,1024]{1,0:T(8,128)(2,1)S(1)}, u32[]{:S(2)}, u32[]{:S(2)}) %collective-permute-start.1) | collective-permute-done | bytes 524320 | tf_op jit(solution)/shard_map/ppermute | solution.py:46
  19.5 2.3 %collective-permute-start.4 = (bf16[256,1024]{1,0:T(8,128)(2,1)S(1)}, bf16[256,1024]{1,0:T(8,128)(2,1)S(1)}, u32[]{:S(2)}, u32[]{:S(2)}) collective-permute-start(bf16[256,1024]{1,0:T(8,128)(2,1)S(1)} %get-tuple-element.72), channel_id=1, source_target_pairs={{0,17},{1,16},{2,19},{3,18},{4,21},{5,20},{6,23},{7,22},{8,25},{9,... | collective-permute-start | bytes 1572872 | tf_op jit(solution)/shard_map/ppermute | solution.py:46
  23.3 1.7 %collective-permute-start.12 = (bf16[256,1024]{1,0:T(8,128)(2,1)S(1)}, bf16[256,1024]{1,0:T(8,128)(2,1)}, u32[]{:S(2)}, u32[]{:S(2)}) collective-permute-start(bf16[256,1024]{1,0:T(8,128)(2,1)S(1)} %collective-permute-done.1.refs_5_.refs_10_.refs_7_), channel_id=1, source_target_pairs={{0,96},{1,97},{2,98},{3,99},{4,100},{5,101},{6,102},{7,103},{8,104... | collective-permute-start | bytes 1572872 | tf_op jit(solution)/shard_map/ppermute | solution.py:46
  25.1 7.5 %collective-permute-done.3.refs_6_.refs_11_ = bf16[256,1024]{1,0:T(8,128)(2,1)S(1)} collective-permute-done((bf16[256,1024]{1,0:T(8,128)(2,1)S(1)}, bf16[256,1024]{1,0:T(8,128)(2,1)S(1)}, u32[]{:S(2)}, u32[]{:S(2)}) %collective-permute-start.3) | collective-permute-done | bytes 524320 | tf_op jit(solution)/shard_map/ppermute | solution.py:46
  34.0 2.0 %collective-permute-done.11.refs_10_.refs_17_.refs_12_ = bf16[256,1024]{1,0:T(8,128)(2,1)} collective-permute-done((bf16[256,1024]{1,0:T(8,128)(2,1)S(1)}, bf16[256,1024]{1,0:T(8,128)(2,1)}, u32[]{:S(2)}, u32[]{:S(2)}) %collective-permute-start.11) | collective-permute-done | bytes 524320 | tf_op jit(solution)/shard_map/ppermute | solution.py:46
  39.6 1.7 %collective-permute-start.14 = (bf16[256,1024]{1,0:T(8,128)(2,1)S(1)}, bf16[256,1024]{1,0:T(8,128)(2,1)S(1)}, u32[]{:S(2)}, u32[]{:S(2)}) collective-permute-start(bf16[256,1024]{1,0:T(8,128)(2,1)S(1)} %collective-permute-done.refs_4_.refs_9_.refs_6_), channel_id=1, source_target_pairs={{0,96},{1,97},{2,98},{3,99},{4,100},{5,101},{6,102},{7,103},{8,104... | collective-permute-start | bytes 1572872 | tf_op jit(solution)/shard_map/ppermute | solution.py:46
  42.4 9.1 %collective-permute-done.13.refs_11_.refs_18_.refs_13_ = bf16[256,1024]{1,0:T(8,128)(2,1)S(1)} collective-permute-done((bf16[256,1024]{1,0:T(8,128)(2,1)S(1)}, bf16[256,1024]{1,0:T(8,128)(2,1)S(1)}, u32[]{:S(2)}, u32[]{:S(2)}) %collective-permute-start.13) | collective-permute-done | bytes 524320 | tf_op jit(solution)/shard_map/ppermute | solution.py:46
  51.5 1.5 %collective-permute-done.14.refs_8_.refs_13_ = bf16[256,1024]{1,0:T(8,128)(2,1)S(1)} collective-permute-done((bf16[256,1024]{1,0:T(8,128)(2,1)S(1)}, bf16[256,1024]{1,0:T(8,128)(2,1)S(1)}, u32[]{:S(2)}, u32[]{:S(2)}) %collective-permute-start.14) | collective-permute-done | bytes 524320 | tf_op jit(solution)/shard_map/ppermute | solution.py:46
  54.3 2.0 %collective-permute-start.16 = (bf16[256,1024]{1,0:T(8,128)(2,1)}, bf16[256,1024]{1,0:T(8,128)(2,1)S(1)}, u32[]{:S(2)}, u32[]{:S(2)}) collective-permute-start(bf16[256,1024]{1,0:T(8,128)(2,1)} %collective-permute-done.12.refs_9_.refs_14_), channel_id=1, source_target_pairs={{0,96},{1,97},{2,98},{3,99},{4,100},{5,101},{6,102},{7,103},{8,104... | collective-permute-start | bytes 1572872 | tf_op jit(solution)/shard_map/ppermute | solution.py:46
  58.0 9.0 %shard_map.50 = (bf16[2,1024,256]{2,1,0:T(8,128)(2,1)}, bf16[2,1024,256]{2,1,0:T(8,128)(2,1)}, bf16[2,1024,256]{2,1,0:T(8,128)(2,1)}, bf16[2,1024,256]{2,1,0:T(8,128)(2,1)}) custom-call(s32[2]{0:T(128)} %pad_add_fusion.refs_0_, bf16[2,256,1024]{2,1,0:T(8,128)(2,1)} %bitcast.39, bf16[256,1024]{1,0:T(8,128)(2,1)} %collective-permute-done.5.refs_2_.refs_7_, ...), custom_call_target="tpu_custom_call" | custom-call | flops 65536 | bytes 262144 | tf_op jit(solution)/shard_map/pallas_call | solution.py:201
  68.4 8.8 %shard_map.51 = (bf16[2,1024,256]{2,1,0:T(8,128)(2,1)}, bf16[2,1024,256]{2,1,0:T(8,128)(2,1)}, bf16[2,1024,256]{2,1,0:T(8,128)(2,1)}, bf16[2,1024,256]{2,1,0:T(8,128)(2,1)}) custom-call(s32[2]{0:T(128)} %pad_add_fusion.refs_0_, bf16[2,256,1024]{2,1,0:T(8,128)(2,1)} %copy-done.9, ...), custom_call_target="tpu_custom_call", output_to_operand_aliasing={{0}: (19, {}), {1}: (20, {}), {2}: (21, {}), {3}: (22, {})} | custom-call | flops 65536 | bytes 262144 | tf_op jit(solution)/shard_map/pallas_call | solution.py:201
  77.2 3.9 %collective-permute-start.17 = (bf16[2,1024,256]{2,1,0:T(8,128)(2,1)}, bf16[2,1024,256]{2,1,0:T(8,128)(2,1)S(1)}, u32[]{:S(2)}, u32[]{:S(2)}) collective-permute-start(bf16[2,1024,256]{2,1,0:T(8,128)(2,1)} %get-tuple-element.109), channel_id=1, source_target_pairs={{0,6},{1,7},{2,0},{3,1},{4,2},{5,3},{6,4},{7,5},{8,14},{9,15},{10,... | collective-permute-start | bytes 3145736 | tf_op jit(solution)/shard_map/ppermute | solution.py:46
  81.2 5.0 %all-to-all-start = ((bf16[16,64,1024]{2,1,0:T(8,128)(2,1)}), bf16[16,64,1024]{2,1,0:T(8,128)(2,1)}, u32[]{:S(2)}, u32[]{:S(2)}) async-start(bf16[16,64,1024]{2,1,0:T(8,128)(2,1)} %bitcast), calls=%async_computation | async-start | bytes 4194304 | tf_op jit(solution)/shard_map/all_to_all | solution.py:273
  86.2 7.1 %shard_map.52 = (bf16[2,1024,256]{2,1,0:T(8,128)(2,1)}, bf16[2,1024,256]{2,1,0:T(8,128)(2,1)}) custom-call(s32[2]{0:T(128)} %pad_add_fusion.refs_0_, bf16[2,256,1024]{2,1,0:T(8,128)(2,1)} %copy-done.9, bf16[256,1024]{1,0:T(8,128)(2,1)} %copy-done.13, ...), custom_call_target="tpu_custom_call", output_to_operand_aliasing={{0}: (14, {}), {1}: (15, {})} | custom-call | flops 65536 | bytes 262144 | tf_op jit(solution)/shard_map/pallas_call | solution.py:201
  93.3 10.8 %collective-permute-done.17 = bf16[2,1024,256]{2,1,0:T(8,128)(2,1)S(1)} collective-permute-done((bf16[2,1024,256]{2,1,0:T(8,128)(2,1)}, bf16[2,1024,256]{2,1,0:T(8,128)(2,1)S(1)}, u32[]{:S(2)}, u32[]{:S(2)}) %collective-permute-start.17) | collective-permute-done | bytes 1048608 | tf_op jit(solution)/shard_map/ppermute | solution.py:46
  104.2 3.4 %collective-permute-done.18 = bf16[2,1024,256]{2,1,0:T(8,128)(2,1)} collective-permute-done((bf16[2,1024,256]{2,1,0:T(8,128)(2,1)}, bf16[2,1024,256]{2,1,0:T(8,128)(2,1)}, u32[]{:S(2)}, u32[]{:S(2)}) %collective-permute-start.18) | collective-permute-done | bytes 1048608 | tf_op jit(solution)/shard_map/ppermute | solution.py:46
  107.6 2.6 %fusion.3 = (bf16[1024,256]{1,0:T(8,128)(2,1)}, bf16[1024,256]{1,0:T(8,128)(2,1)}) fusion(bf16[2,1024,256]{2,1,0:T(8,128)(2,1)} %get-tuple-element.113, bf16[2,1024,256]{2,1,0:T(8,128)(2,1)} %collective-permute-done.18, bf16[2,1024,256]{2,1,0:T(8,128)(2,1)S(1)} %collective-permute-done.17), kind=kLoop, calls=%fused_computation.11 | loop fusion | flops 2097152 | bytes 3145728 | tf_op jit(solution)/shard_map/convert_element_type | solution.py:58
  110.3 1.8 %collective-permute-start.20 = (bf16[1024,256]{1,0:T(8,128)(2,1)}, bf16[1024,256]{1,0:T(8,128)(2,1)}, u32[]{:S(2)}, u32[]{:S(2)}) collective-permute-start(bf16[1024,256]{1,0:T(8,128)(2,1)} %get-tuple-element.115), channel_id=1, source_target_pairs={{0,2},{1,3},{2,4},{3,5},{4,6},{5,7},{6,0},{7,1},{8,10},{9,11},{10,... | collective-permute-start | bytes 1572872 | tf_op jit(solution)/shard_map/ppermute | solution.py:46
  112.2 11.0 %collective-permute-done.19 = bf16[1024,256]{1,0:T(8,128)(2,1)} collective-permute-done((bf16[1024,256]{1,0:T(8,128)(2,1)}, bf16[1024,256]{1,0:T(8,128)(2,1)}, u32[]{:S(2)}, u32[]{:S(2)}) %collective-permute-start.19) | collective-permute-done | bytes 524320 | tf_op jit(solution)/shard_map/ppermute | solution.py:46
  124.8 1.8 %fusion = (bf16[1024,256]{1,0:T(8,128)(2,1)S(1)}, bf16[1024,256]{1,0:T(8,128)(2,1)S(1)}) fusion(bf16[1024,256]{1,0:T(8,128)(2,1)} %collective-permute-done.20, bf16[2,1024,256]{2,1,0:T(8,128)(2,1)S(1)} %collective-permute-done.17, bf16[2,1024,256]{2,1,0:T(8,128)(2,1)S(1)} %copy-done.2, bf16[1024,256]{1,0:T(8,128)(2,1)} %collective-permute-done.19, ...), kind=kLoop, calls=%fused_computation.5 | loop fusion | flops 3145728 | bytes 4194304 | tf_op jit(solution)/shard_map/convert_element_type | solution.py:58
  126.6 2.2 %collective-permute-start.21 = (bf16[512,256]{1,0:T(8,128)(2,1)S(1)}, bf16[512,256]{1,0:T(8,128)(2,1)S(1)}, u32[]{:S(2)}, u32[]{:S(2)}) collective-permute-start(bf16[512,256]{1,0:T(8,128)(2,1)S(1)} %get-tuple-element.118), channel_id=1, source_target_pairs={{0,1},{1,17},{2,3},{3,19},{4,5},{5,21},{6,7},{7,23},{8,9},{9,25},{... | collective-permute-start | bytes 786440 | tf_op jit(solution)/shard_map/ppermute | solution.py:46
  128.8 2.2 %collective-permute-start.23 = (bf16[512,256]{1,0:T(8,128)(2,1)S(1)}, bf16[512,256]{1,0:T(8,128)(2,1)S(1)}, u32[]{:S(2)}, u32[]{:S(2)}) collective-permute-start(bf16[512,256]{1,0:T(8,128)(2,1)S(1)} %get-tuple-element.120), channel_id=1, source_target_pairs={{0,17},{1,1},{2,19},{3,3},{4,21},{5,5},{6,23},{7,7},{8,25},{9,9},{... | collective-permute-start | bytes 786440 | tf_op jit(solution)/shard_map/ppermute | solution.py:46
  131.0 4.1 %collective-permute-start.24 = (bf16[512,256]{1,0:T(8,128)(2,1)S(1)}, bf16[512,256]{1,0:T(8,128)(2,1)S(1)}, u32[]{:S(2)}, u32[]{:S(2)}) collective-permute-start(bf16[512,256]{1,0:T(8,128)(2,1)S(1)} %get-tuple-element.121), channel_id=1, source_target_pairs={{0,25},{1,9},{2,27},{3,11},{4,29},{5,13},{6,31},{7,15},{8,17},{9,1... | collective-permute-start | bytes 786440 | tf_op jit(solution)/shard_map/ppermute | solution.py:46
  135.1 2.7 %reduce_sum.12 = bf16[64,1024]{1,0:T(8,128)(2,1)} reduce(bf16[16,64,1024]{2,1,0:T(8,128)(2,1)} %all-to-all-done, bf16[]{:T(256)} %constant.91.clone.1), dimensions={0}, to_apply=%region_0.1 | reduce | flops 983040 | bytes 2228226 | tf_op jit(solution)/shard_map/reduce_sum | solution.py:287
  138.4 1.9 %collective-permute-done.23 = bf16[512,256]{1,0:T(8,128)(2,1)S(1)} collective-permute-done((bf16[512,256]{1,0:T(8,128)(2,1)S(1)}, bf16[512,256]{1,0:T(8,128)(2,1)S(1)}, u32[]{:S(2)}, u32[]{:S(2)}) %collective-permute-start.23) | collective-permute-done | bytes 262176 | tf_op jit(solution)/shard_map/ppermute | solution.py:46
  140.3 6.4 %collective-permute-done.24 = bf16[512,256]{1,0:T(8,128)(2,1)S(1)} collective-permute-done((bf16[512,256]{1,0:T(8,128)(2,1)S(1)}, bf16[512,256]{1,0:T(8,128)(2,1)S(1)}, u32[]{:S(2)}, u32[]{:S(2)}) %collective-permute-start.24) | collective-permute-done | bytes 262176 | tf_op jit(solution)/shard_map/ppermute | solution.py:46
  146.9 1.7 %multiply_add_fusion = f32[512,1024]{1,0:T(8,128)} fusion(f32[512,1024]{1,0:T(8,128)S(1)} %copy-done.11, bf16[256,256]{1,0:T(8,128)(2,1)S(1)} %get-tuple-element.145, bf16[256,256]{1,0:T(8,128)(2,1)S(1)} %get-tuple-element.144, bf16[512,256]{1,0:T(8,128)(2,1)S(1)} %get-tuple-element.130, bf16[256,256]{1,0:T(8,128)(2,1)S(1)} %get-tuple-element.143, ...), kind=kLoop, calls=%fused_computation | loop fusion | flops 7864320 | bytes 5242880 | tf_op jit(solution)/shard_map/add | solution.py:301
  (67 shorter events, 14.6 us)
Async XLA Ops:
  2.4 17.0 %collective-permute-start.2 = (bf16[2,256,1024]{2,1,0:T(8,128)(2,1)S(1)}, bf16[2,256,1024]{2,1,0:T(8,128)(2,1)S(1)}, u32[]{:S(2)}, u32[]{:S(2)}) collective-permute-start(bf16[2,256,1024]{2,1,0:T(8,128)(2,1)S(1)} %bitcast.38), channel_id=1, source_target_pairs={{0,8},{1,9},{2,10},{3,11},{4,12},{5,13},{6,14},{7,15},{8,0},{9,1},... | collective-permute-start | bytes 3145736 | tf_op jit(solution)/shard_map/ppermute | solution.py:46
  2.5 14.3 %collective-permute-start = (bf16[256,1024]{1,0:T(8,128)(2,1)S(1)}, bf16[256,1024]{1,0:T(8,128)(2,1)S(1)}, u32[]{:S(2)}, u32[]{:S(2)}) collective-permute-start(bf16[256,1024]{1,0:T(8,128)(2,1)S(1)} %get-tuple-element.72), channel_id=1, source_target_pairs={{0,16},{1,17},{2,18},{3,19},{4,20},{5,21},{6,22},{7,23},{8,24},{9,... | collective-permute-start | bytes 1572872 | tf_op jit(solution)/shard_map/ppermute | solution.py:46
  4.2 15.2 %collective-permute-start.1 = (bf16[256,1024]{1,0:T(8,128)(2,1)S(1)}, bf16[256,1024]{1,0:T(8,128)(2,1)S(1)}, u32[]{:S(2)}, u32[]{:S(2)}) collective-permute-start(bf16[256,1024]{1,0:T(8,128)(2,1)S(1)} %get-tuple-element.71), channel_id=1, source_target_pairs={{0,17},{1,16},{2,19},{3,18},{4,21},{5,20},{6,23},{7,22},{8,25},{9,... | collective-permute-start | bytes 1572872 | tf_op jit(solution)/shard_map/ppermute | solution.py:46
  16.9 25.6 %copy-start.3 = (bf16[256,1024]{1,0:T(8,128)(2,1)}, bf16[256,1024]{1,0:T(8,128)(2,1)S(1)}, u32[]{:S(2)}) copy-start(bf16[256,1024]{1,0:T(8,128)(2,1)S(1)} %collective-permute-done.refs_4_.refs_9_.refs_6_) | copy-start | bytes 1572868
  19.4 23.0 %copy-start.4 = (bf16[256,1024]{1,0:T(8,128)(2,1)}, bf16[256,1024]{1,0:T(8,128)(2,1)S(1)}, u32[]{:S(2)}) copy-start(bf16[256,1024]{1,0:T(8,128)(2,1)S(1)} %collective-permute-done.1.refs_5_.refs_10_.refs_7_) | copy-start | bytes 1572868
  19.4 23.0 %copy-start.9 = (bf16[2,256,1024]{2,1,0:T(8,128)(2,1)}, bf16[2,256,1024]{2,1,0:T(8,128)(2,1)S(1)}, u32[]{:S(2)}) copy-start(bf16[2,256,1024]{2,1,0:T(8,128)(2,1)S(1)} %collective-permute-done.2.refs_1_) | copy-start | bytes 3145732
  19.4 13.2 %collective-permute-start.3 = (bf16[256,1024]{1,0:T(8,128)(2,1)S(1)}, bf16[256,1024]{1,0:T(8,128)(2,1)S(1)}, u32[]{:S(2)}, u32[]{:S(2)}) collective-permute-start(bf16[256,1024]{1,0:T(8,128)(2,1)S(1)} %get-tuple-element.71), channel_id=1, source_target_pairs={{0,16},{1,17},{2,18},{3,19},{4,20},{5,21},{6,22},{7,23},{8,24},{9,... | collective-permute-start | bytes 1572872 | tf_op jit(solution)/shard_map/ppermute | solution.py:46
  19.5 14.4 %collective-permute-start.4 = (bf16[256,1024]{1,0:T(8,128)(2,1)S(1)}, bf16[256,1024]{1,0:T(8,128)(2,1)S(1)}, u32[]{:S(2)}, u32[]{:S(2)}) collective-permute-start(bf16[256,1024]{1,0:T(8,128)(2,1)S(1)} %get-tuple-element.72), channel_id=1, source_target_pairs={{0,17},{1,16},{2,19},{3,18},{4,21},{5,20},{6,23},{7,22},{8,25},{9,... | collective-permute-start | bytes 1572872 | tf_op jit(solution)/shard_map/ppermute | solution.py:46
  21.8 14.2 %collective-permute-start.11 = (bf16[256,1024]{1,0:T(8,128)(2,1)S(1)}, bf16[256,1024]{1,0:T(8,128)(2,1)}, u32[]{:S(2)}, u32[]{:S(2)}) collective-permute-start(bf16[256,1024]{1,0:T(8,128)(2,1)S(1)} %collective-permute-done.refs_4_.refs_9_.refs_6_), channel_id=1, source_target_pairs={{0,32},{1,33},{2,34},{3,35},{4,36},{5,37},{6,38},{7,39},{8,40},{9,... | collective-permute-start | bytes 1572872 | tf_op jit(solution)/shard_map/ppermute | solution.py:46
  23.3 12.7 %collective-permute-start.12 = (bf16[256,1024]{1,0:T(8,128)(2,1)S(1)}, bf16[256,1024]{1,0:T(8,128)(2,1)}, u32[]{:S(2)}, u32[]{:S(2)}) collective-permute-start(bf16[256,1024]{1,0:T(8,128)(2,1)S(1)} %collective-permute-done.1.refs_5_.refs_10_.refs_7_), channel_id=1, source_target_pairs={{0,96},{1,97},{2,98},{3,99},{4,100},{5,101},{6,102},{7,103},{8,104... | collective-permute-start | bytes 1572872 | tf_op jit(solution)/shard_map/ppermute | solution.py:46
  32.7 25.3 %copy-start.5 = (bf16[256,1024]{1,0:T(8,128)(2,1)}, bf16[256,1024]{1,0:T(8,128)(2,1)S(1)}, u32[]{:S(2)}) copy-start(bf16[256,1024]{1,0:T(8,128)(2,1)S(1)} %collective-permute-done.3.refs_6_.refs_11_) | copy-start | bytes 1572868
  34.0 24.0 %copy-start.6 = (bf16[256,1024]{1,0:T(8,128)(2,1)}, bf16[256,1024]{1,0:T(8,128)(2,1)S(1)}, u32[]{:S(2)}) copy-start(bf16[256,1024]{1,0:T(8,128)(2,1)S(1)} %collective-permute-done.4.refs_7_.refs_12_) | copy-start | bytes 1572868
  36.0 20.3 %collective-permute-start.7 = (bf16[2,256,1024]{2,1,0:T(8,128)(2,1)S(1)}, bf16[2,256,1024]{2,1,0:T(8,128)(2,1)S(1)}, u32[]{:S(2)}, u32[]{:S(2)}) collective-permute-start(bf16[2,256,1024]{2,1,0:T(8,128)(2,1)S(1)} %pad_maximum_fusion), channel_id=1, source_target_pairs={{0,8},{1,9},{2,10},{3,11},{4,12},{5,13},{6,14},{7,15},{8,0},{9,1},... | collective-permute-start | bytes 3145736 | tf_op jit(solution)/shard_map/ppermute | solution.py:46
  36.0 15.5 %collective-permute-start.13 = (bf16[256,1024]{1,0:T(8,128)(2,1)S(1)}, bf16[256,1024]{1,0:T(8,128)(2,1)S(1)}, u32[]{:S(2)}, u32[]{:S(2)}) collective-permute-start(bf16[256,1024]{1,0:T(8,128)(2,1)S(1)} %collective-permute-done.1.refs_5_.refs_10_.refs_7_), channel_id=1, source_target_pairs={{0,32},{1,33},{2,34},{3,35},{4,36},{5,37},{6,38},{7,39},{8,40},{9,... | collective-permute-start | bytes 1572872 | tf_op jit(solution)/shard_map/ppermute | solution.py:46
  37.5 16.8 %collective-permute-start.5 = (bf16[256,1024]{1,0:T(8,128)(2,1)S(1)}, bf16[256,1024]{1,0:T(8,128)(2,1)}, u32[]{:S(2)}, u32[]{:S(2)}) collective-permute-start(bf16[256,1024]{1,0:T(8,128)(2,1)S(1)} %collective-permute-done.1.refs_5_.refs_10_.refs_7_), channel_id=1, source_target_pairs={{0,16},{1,17},{2,18},{3,19},{4,20},{5,21},{6,22},{7,23},{8,24},{9,... | collective-permute-start | bytes 1572872 | tf_op jit(solution)/shard_map/ppermute | solution.py:46
  38.5 17.8 %collective-permute-start.6 = (bf16[256,1024]{1,0:T(8,128)(2,1)S(1)}, bf16[256,1024]{1,0:T(8,128)(2,1)}, u32[]{:S(2)}, u32[]{:S(2)}) collective-permute-start(bf16[256,1024]{1,0:T(8,128)(2,1)S(1)} %collective-permute-done.refs_4_.refs_9_.refs_6_), channel_id=1, source_target_pairs={{0,17},{1,16},{2,19},{3,18},{4,21},{5,20},{6,23},{7,22},{8,25},{9,... | collective-permute-start | bytes 1572872 | tf_op jit(solution)/shard_map/ppermute | solution.py:46
  39.6 13.5 %collective-permute-start.14 = (bf16[256,1024]{1,0:T(8,128)(2,1)S(1)}, bf16[256,1024]{1,0:T(8,128)(2,1)S(1)}, u32[]{:S(2)}, u32[]{:S(2)}) collective-permute-start(bf16[256,1024]{1,0:T(8,128)(2,1)S(1)} %collective-permute-done.refs_4_.refs_9_.refs_6_), channel_id=1, source_target_pairs={{0,96},{1,97},{2,98},{3,99},{4,100},{5,101},{6,102},{7,103},{8,104... | collective-permute-start | bytes 1572872 | tf_op jit(solution)/shard_map/ppermute | solution.py:46
  51.5 15.9 %collective-permute-start.10 = (bf16[2,256,1024]{2,1,0:T(8,128)(2,1)}, bf16[2,256,1024]{2,1,0:T(8,128)(2,1)}, u32[]{:S(2)}, u32[]{:S(2)}) collective-permute-start(bf16[2,256,1024]{2,1,0:T(8,128)(2,1)} %pad_maximum_fusion.1), channel_id=1, source_target_pairs={{0,8},{1,9},{2,10},{3,11},{4,12},{5,13},{6,14},{7,15},{8,0},{9,1},... | collective-permute-start | bytes 3145736 | tf_op jit(solution)/shard_map/ppermute | solution.py:46
  53.1 14.3 %collective-permute-start.15 = (bf16[256,1024]{1,0:T(8,128)(2,1)}, bf16[256,1024]{1,0:T(8,128)(2,1)}, u32[]{:S(2)}, u32[]{:S(2)}) collective-permute-start(bf16[256,1024]{1,0:T(8,128)(2,1)} %collective-permute-done.11.refs_10_.refs_17_.refs_12_), channel_id=1, source_target_pairs={{0,32},{1,33},{2,34},{3,35},{4,36},{5,37},{6,38},{7,39},{8,40},{9,... | collective-permute-start | bytes 1572872 | tf_op jit(solution)/shard_map/ppermute | solution.py:46
  54.3 13.1 %collective-permute-start.16 = (bf16[256,1024]{1,0:T(8,128)(2,1)}, bf16[256,1024]{1,0:T(8,128)(2,1)S(1)}, u32[]{:S(2)}, u32[]{:S(2)}) collective-permute-start(bf16[256,1024]{1,0:T(8,128)(2,1)} %collective-permute-done.12.refs_9_.refs_14_), channel_id=1, source_target_pairs={{0,96},{1,97},{2,98},{3,99},{4,100},{5,101},{6,102},{7,103},{8,104... | collective-permute-start | bytes 1572872 | tf_op jit(solution)/shard_map/ppermute | solution.py:46
  56.4 11.1 %collective-permute-start.8 = (bf16[256,1024]{1,0:T(8,128)(2,1)}, bf16[256,1024]{1,0:T(8,128)(2,1)S(1)}, u32[]{:S(2)}, u32[]{:S(2)}) collective-permute-start(bf16[256,1024]{1,0:T(8,128)(2,1)} %collective-permute-done.5.refs_2_.refs_7_), channel_id=1, source_target_pairs={{0,8},{1,9},{2,10},{3,11},{4,12},{5,13},{6,14},{7,15},{8,0},{9,1},... | collective-permute-start | bytes 1572872 | tf_op jit(solution)/shard_map/ppermute | solution.py:46
  57.3 10.1 %collective-permute-start.9 = (bf16[256,1024]{1,0:T(8,128)(2,1)}, bf16[256,1024]{1,0:T(8,128)(2,1)}, u32[]{:S(2)}, u32[]{:S(2)}) collective-permute-start(bf16[256,1024]{1,0:T(8,128)(2,1)} %collective-permute-done.6.refs_3_.refs_8_), channel_id=1, source_target_pairs={{0,8},{1,9},{2,10},{3,11},{4,12},{5,13},{6,14},{7,15},{8,0},{9,1},... | collective-permute-start | bytes 1572872 | tf_op jit(solution)/shard_map/ppermute | solution.py:46
  77.2 26.9 %collective-permute-start.17 = (bf16[2,1024,256]{2,1,0:T(8,128)(2,1)}, bf16[2,1024,256]{2,1,0:T(8,128)(2,1)S(1)}, u32[]{:S(2)}, u32[]{:S(2)}) collective-permute-start(bf16[2,1024,256]{2,1,0:T(8,128)(2,1)} %get-tuple-element.109), channel_id=1, source_target_pairs={{0,6},{1,7},{2,0},{3,1},{4,2},{5,3},{6,4},{7,5},{8,14},{9,15},{10,... | collective-permute-start | bytes 3145736 | tf_op jit(solution)/shard_map/ppermute | solution.py:46
  81.2 26.4 %collective-permute-start.18 = (bf16[2,1024,256]{2,1,0:T(8,128)(2,1)}, bf16[2,1024,256]{2,1,0:T(8,128)(2,1)}, u32[]{:S(2)}, u32[]{:S(2)}) collective-permute-start(bf16[2,1024,256]{2,1,0:T(8,128)(2,1)} %get-tuple-element.110), channel_id=1, source_target_pairs={{0,2},{1,3},{2,4},{3,5},{4,6},{5,7},{6,0},{7,1},{8,10},{9,11},{10,... | collective-permute-start | bytes 3145736 | tf_op jit(solution)/shard_map/ppermute | solution.py:46
  81.2 45.4 %all-to-all-start = ((bf16[16,64,1024]{2,1,0:T(8,128)(2,1)}), bf16[16,64,1024]{2,1,0:T(8,128)(2,1)}, u32[]{:S(2)}, u32[]{:S(2)}) async-start(bf16[16,64,1024]{2,1,0:T(8,128)(2,1)} %bitcast), calls=%async_computation | async-start | bytes 4194304 | tf_op jit(solution)/shard_map/all_to_all | solution.py:273
  93.3 31.5 %copy-start.2 = (bf16[2,1024,256]{2,1,0:T(8,128)(2,1)S(1)}, bf16[2,1024,256]{2,1,0:T(8,128)(2,1)}, u32[]{:S(2)}) copy-start(bf16[2,1024,256]{2,1,0:T(8,128)(2,1)} %get-tuple-element.106) | copy-start | bytes 3145732
  110.2 13.1 %collective-permute-start.19 = (bf16[1024,256]{1,0:T(8,128)(2,1)}, bf16[1024,256]{1,0:T(8,128)(2,1)}, u32[]{:S(2)}, u32[]{:S(2)}) collective-permute-start(bf16[1024,256]{1,0:T(8,128)(2,1)} %get-tuple-element.114), channel_id=1, source_target_pairs={{0,6},{1,7},{2,0},{3,1},{4,2},{5,3},{6,4},{7,5},{8,14},{9,15},{10,... | collective-permute-start | bytes 1572872 | tf_op jit(solution)/shard_map/ppermute | solution.py:46
  110.3 14.4 %collective-permute-start.20 = (bf16[1024,256]{1,0:T(8,128)(2,1)}, bf16[1024,256]{1,0:T(8,128)(2,1)}, u32[]{:S(2)}, u32[]{:S(2)}) collective-permute-start(bf16[1024,256]{1,0:T(8,128)(2,1)} %get-tuple-element.115), channel_id=1, source_target_pairs={{0,2},{1,3},{2,4},{3,5},{4,6},{5,7},{6,0},{7,1},{8,10},{9,11},{10,... | collective-permute-start | bytes 1572872 | tf_op jit(solution)/shard_map/ppermute | solution.py:46
  126.6 11.2 %collective-permute-start.21 = (bf16[512,256]{1,0:T(8,128)(2,1)S(1)}, bf16[512,256]{1,0:T(8,128)(2,1)S(1)}, u32[]{:S(2)}, u32[]{:S(2)}) collective-permute-start(bf16[512,256]{1,0:T(8,128)(2,1)S(1)} %get-tuple-element.118), channel_id=1, source_target_pairs={{0,1},{1,17},{2,3},{3,19},{4,5},{5,21},{6,7},{7,23},{8,9},{9,25},{... | collective-permute-start | bytes 786440 | tf_op jit(solution)/shard_map/ppermute | solution.py:46
  128.8 9.6 %collective-permute-start.22 = (bf16[512,256]{1,0:T(8,128)(2,1)S(1)}, bf16[512,256]{1,0:T(8,128)(2,1)S(1)}, u32[]{:S(2)}, u32[]{:S(2)}) collective-permute-start(bf16[512,256]{1,0:T(8,128)(2,1)S(1)} %get-tuple-element.119), channel_id=1, source_target_pairs={{0,9},{1,25},{2,11},{3,27},{4,13},{5,29},{6,15},{7,31},{8,1},{9,17... | collective-permute-start | bytes 786440 | tf_op jit(solution)/shard_map/ppermute | solution.py:46
  128.8 11.5 %collective-permute-start.23 = (bf16[512,256]{1,0:T(8,128)(2,1)S(1)}, bf16[512,256]{1,0:T(8,128)(2,1)S(1)}, u32[]{:S(2)}, u32[]{:S(2)}) collective-permute-start(bf16[512,256]{1,0:T(8,128)(2,1)S(1)} %get-tuple-element.120), channel_id=1, source_target_pairs={{0,17},{1,1},{2,19},{3,3},{4,21},{5,5},{6,23},{7,7},{8,25},{9,9},{... | collective-permute-start | bytes 786440 | tf_op jit(solution)/shard_map/ppermute | solution.py:46
  131.0 15.7 %collective-permute-start.24 = (bf16[512,256]{1,0:T(8,128)(2,1)S(1)}, bf16[512,256]{1,0:T(8,128)(2,1)S(1)}, u32[]{:S(2)}, u32[]{:S(2)}) collective-permute-start(bf16[512,256]{1,0:T(8,128)(2,1)S(1)} %get-tuple-element.121), channel_id=1, source_target_pairs={{0,25},{1,9},{2,27},{3,11},{4,29},{5,13},{6,31},{7,15},{8,17},{9,1... | collective-permute-start | bytes 786440 | tf_op jit(solution)/shard_map/ppermute | solution.py:46
  (9 other events, 38.2 us)

commit v11 on v10

--- a/solution.py
+++ b/solution.py
@@ -35,11 +35,8 @@
 FAR = table(lambda x, yl, c, z, yh: (x, 1 - yl, c, z, 1 - yh))
 X_STEP = {d: table(lambda x, yl, c, z, yh, d=d: (x + d, yl, c, z, yh)) for d in (1, 2, 3)}
 Z_STEP = {d: table(lambda x, yl, c, z, yh, d=d: (x, yl, c, z + d, yh)) for d in (1, 3)}
-HOME = {
-    (s, t): table(lambda x, yl, c, z, yh, s=s, t=t: (x, yh ^ s, c ^ t, z, 1 - yl))
-    for s in range(2)
-    for t in range(2)
-}
+Z_CROSS = {d: table(lambda x, yl, c, z, yh, d=d: (x, yl, 1 - c, z + d, yh)) for d in (1, 3)}
+HOME = [table(lambda x, yl, c, z, yh, s=s: (x, yh ^ s, c, z, 1 - yl)) for s in range(2)]
 
 
 def send(value, pairs):
@@ -68,11 +65,15 @@
     place, refs = refs[0], refs[1:]
     n_in = plan["inputs"]
     inputs, refs = refs[:n_in], refs[n_in + plan["kept"] :]
-    if plan["messages"] == 4:
-        home, up, down, middle = refs[:4]
+    if plan["messages"] == 6:
+        home_a, home_b, up, down_a, down_b, middle = refs[:6]
+        targets = (
+            (home_a, up.at[0], down_a, middle.at[0]),
+            (home_b, middle.at[1], up.at[1], down_b),
+        )
     else:
-        (home, middle), up, down = refs[:2], None, None
-    targets = ((home, up, down, middle), (home, middle, up, down))
+        home_b, middle = refs[:2]
+        targets = ((), (home_b, middle.at[1]))
     refs = refs[plan["messages"] :]
     left, columns_in, result, left_sem, column_sem, out_sem = refs
     shift, high = place[0], place[1]
@@ -161,7 +162,7 @@
                 (
                     here,
                     pltpu.make_async_copy(
-                        result.at[slot], targets[cc][d].at[cc], out_sem.at[slot]
+                        result.at[slot], targets[cc][d], out_sem.at[slot]
                     ),
                 )
                 for here, d in options
@@ -187,7 +188,12 @@
     half, items = inputs[0].shape[-2:]
     wanted = tuple((cc, jobs) for cc, (_, jobs) in sides.items())
     n_results = sum(len(jobs) for _, jobs in wanted)
-    n_messages = len(kept) or 4
+    single = jax.ShapeDtypeStruct((4 * half, half), jnp.bfloat16)
+    double = jax.ShapeDtypeStruct((2, 4 * half, half), jnp.bfloat16)
+    messages = [single, single, double, single, single, double]
+    if len(kept) == 2:
+        messages = [single, double]
+    n_messages = len(messages)
     plan = {
         "inputs": len(inputs),
         "kept": len(kept),
@@ -200,7 +206,7 @@
     n_blocks = len(blocks)
     return pl.pallas_call(
         functools.partial(block_kernel, plan, groups),
-        out_shape=[jax.ShapeDtypeStruct((2, 4 * half, half), jnp.bfloat16)] * n_messages,
+        out_shape=messages,
         in_specs=[pl.BlockSpec(memory_space=pltpu.SMEM)]
         + [outside] * (len(inputs) + len(kept)),
         out_specs=[outside] * n_messages,
@@ -262,38 +268,44 @@
     early = {0: (near, far), 1: (above_n, above_f), 3: (below_n, below_f)}
     every = {0: (near, far), 1: (above_n, above_f), 2: tuple(across), 3: (below_n, below_f)}
     kept = block_product(place, {0: (side, (("dx", 0), ("dx", 1), ("dx", 3)))}, early)
-    home, up, down, middle = block_product(
+    home_a, home_b, up, down_a, down_b, middle = block_product(
         place, {1: (side_c, (("dz", 2), ("dz", 3))), 0: (side, (("dx", 2),))}, every, kept
     )
-    home, middle = block_product(
-        place, {1: (side_c, (("dz", 1), ("dz", 0)))}, every, (home, middle), LATE
-    )
-
-    share, down, up = lax.optimization_barrier((share, down, up))
+    home_b, middle = block_product(
+        place, {1: (side_c, (("dz", 1), ("dz", 0)))}, every, (home_b, middle), LATE
+    )
+
+    share, down_a, down_b, up = lax.optimization_barrier((share, down_a, down_b, up))
     shares = lax.all_to_all(share, "feat", 0, 0)
-    down, up = together([(down, Z_STEP[3]), (up, Z_STEP[1])])
+    down_a, up, down_b = together(
+        [(down_a, Z_STEP[3]), (up, Z_STEP[1]), (down_b, Z_CROSS[3])]
+    )
+    (home_b,) = together([(home_b, CORE)])
     first, second = together(
         [
-            (narrow(wide(down[0]) + wide(middle[0])), Z_STEP[3]),
-            (narrow(wide(up[1]) + wide(middle[1])), Z_STEP[1]),
+            (narrow(wide(down_a) + wide(middle[0])), Z_STEP[3]),
+            (narrow(wide(up[1]) + wide(middle[1])), Z_CROSS[1]),
         ]
     )
-    total = [
-        narrow(wide(home[0]) + wide(up[0]) + wide(first)).reshape(2, 2 * half, half),
-        narrow(wide(home[1]) + wide(down[1]) + wide(second)).reshape(2, 2 * half, half),
-    ]
-    homeward = [pick(total[t], yl ^ yh ^ s) for s in range(2) for t in range(2)]
+    total = jnp.stack(
+        [
+            narrow(wide(home_a) + wide(up[0]) + wide(first)).reshape(2, 2 * half, half),
+            narrow(wide(home_b) + wide(down_b) + wide(second)).reshape(2, 2 * half, half),
+        ],
+        1,
+    )
+    homeward = [pick(total, yl ^ yh ^ s) for s in range(2)]
     shares, homeward = lax.optimization_barrier((shares, homeward))
     projected = narrow(jnp.sum(wide(shares), 0))
-    arrived = [send(v, HOME[s // 2, s % 2]) for s, v in enumerate(homeward)]
+    arrived = [send(v, HOME[s]) for s, v in enumerate(homeward)]
     *arrived, projected = lax.optimization_barrier((*arrived, projected))
 
     def quarter(q):
         t, s = q // 2, q % 2
         value = jnp.where(
             c == 0,
-            jnp.where(yl == 0, arrived[2 * s + t], arrived[2 - 2 * s + t]),
-            jnp.where(yl == 0, arrived[2 * s + 1 - t], arrived[3 - 2 * s - t]),
+            jnp.where(yl == 0, arrived[s][t], arrived[1 - s][t]),
+            jnp.where(yl == 0, arrived[s][1 - t], arrived[1 - s][1 - t]),
         )
         return jnp.concatenate([value[half:], value[:half]], 0) if s else value
 

time: 149 us -> 154 us (1.034)
  other arithmetic: 10.6 us -> 14.2 us
  waiting for transfers between devices: 68.1 us -> 70.4 us
    convert_element_type x2 -> x4, other arithmetic: 4.35 us -> 7.38 us  [narrow(): return value.astype(jnp.bfloat16)]
    ppermute x25, waiting for transfers between devices: 68.1 us -> 70.4 us  [send(): return lax.ppermute(value, AXES, pairs)]
    ppermute x25, starting transfers between devices: 32.7 us -> 31 us  [send(): return lax.ppermute(value, AXES, pairs)]
    reduce_sum x1, other arithmetic: 2.68 us -> 1.06 us  [on_device(): projected = narrow(jnp.sum(wide(shares), 0))]
  transfers between devices with their start and end apart: 26 -> 26, of which waited for: 15 -> 14; matrix products, arithmetic and copies ran while one was open for 8% -> 9% of each run, Pallas kernels for 11% -> 11%
where the time goes in v11:
time: 154 us; the launch traced here: 153 us
  waiting for transfers between devices  70.4 us (46%)
  starting transfers between devices  36.5 us (24%)
  Pallas kernels  25.3 us (16%)
  other arithmetic  14.2 us (9%)
  local copies, waits for them, and re-layouts  3.62 us (2%)
  matrix products  2.57 us (2%)
    ppermute x25, waiting for transfers between devices, send(): return lax.ppermute(value, AXES, pairs)  70.4 us
    ppermute x25, starting transfers between devices, send(): return lax.ppermute(value, AXES, pairs)  31 us
    pallas_call x3, Pallas kernels, block_product(): pl.pallas_call(functools.partial(block_kernel, plan, groups), out_shape=m...  25.3 us
    convert_element_type x4, other arithmetic, narrow(): return value.astype(jnp.bfloat16)  7.38 us
    all_to_all x1, starting transfers between devices, on_device(): shares = lax.all_to_all(share, 'feat', 0, 0)  5.49 us
  transfers between devices with their start and end apart: 26, of which 14 were waited for; matrix products, arithmetic and copies ran while one was open for 9% of the time, Pallas kernels for 11%

profile of v11, /device:TPU:0, one launch (start us, length us, event | category | flops | bytes accessed | tf_op | source)
XLA Modules:
  0.0 153.5 jit_solution(6006455158120359012)
XLA Ops:
  0.7 1.6 %copy.13 = bf16[512,1024]{1,0:T(8,128)(2,1)S(1)} copy(bf16[512,1024]{0,1:T(8,128)(2,1)} %bitcast.52) | data formatting | bytes 2097152 | tf_op jit(solution)/shard_map/transpose | solution.py:238
  2.5 1.7 %collective-permute-start = (bf16[256,1024]{1,0:T(8,128)(2,1)S(1)}, bf16[256,1024]{1,0:T(8,128)(2,1)S(1)}, u32[]{:S(2)}, u32[]{:S(2)}) collective-permute-start(bf16[256,1024]{1,0:T(8,128)(2,1)S(1)} %get-tuple-element.75), channel_id=1, source_target_pairs={{0,16},{1,17},{2,18},{3,19},{4,20},{5,21},{6,22},{7,23},{8,24},{9,... | collective-permute-start | bytes 1572872 | tf_op jit(solution)/shard_map/ppermute | solution.py:43
  4.2 2.2 %collective-permute-start.1 = (bf16[256,1024]{1,0:T(8,128)(2,1)S(1)}, bf16[256,1024]{1,0:T(8,128)(2,1)S(1)}, u32[]{:S(2)}, u32[]{:S(2)}) collective-permute-start(bf16[256,1024]{1,0:T(8,128)(2,1)S(1)} %get-tuple-element.74), channel_id=1, source_target_pairs={{0,17},{1,16},{2,19},{3,18},{4,21},{5,20},{6,23},{7,22},{8,25},{9,... | collective-permute-start | bytes 1572872 | tf_op jit(solution)/shard_map/ppermute | solution.py:43
  6.4 2.6 %convolution_convert_fusion = bf16[1024,1024]{1,0:T(8,128)(2,1)} fusion(bf16[1024,512]{1,0:T(8,128)(2,1)S(1)} %copy-done.15, bf16[512,1024]{1,0:T(8,128)(2,1)S(1)} %copy-done), kind=kOutput, calls=%fused_computation.1 | convolution fusion | flops 1074790400 | bytes 4194304 | tf_op jit(solution)/shard_map/dot_general | solution.py:242
  9.0 7.8 %collective-permute-done.refs_4_.refs_9_.refs_6_ = bf16[256,1024]{1,0:T(8,128)(2,1)S(1)} collective-permute-done((bf16[256,1024]{1,0:T(8,128)(2,1)S(1)}, bf16[256,1024]{1,0:T(8,128)(2,1)S(1)}, u32[]{:S(2)}, u32[]{:S(2)}) %collective-permute-start) | collective-permute-done | bytes 524320 | tf_op jit(solution)/shard_map/ppermute | solution.py:43
  16.9 2.6 %collective-permute-done.1.refs_5_.refs_10_.refs_7_ = bf16[256,1024]{1,0:T(8,128)(2,1)S(1)} collective-permute-done((bf16[256,1024]{1,0:T(8,128)(2,1)S(1)}, bf16[256,1024]{1,0:T(8,128)(2,1)S(1)}, u32[]{:S(2)}, u32[]{:S(2)}) %collective-permute-start.1) | collective-permute-done | bytes 524320 | tf_op jit(solution)/shard_map/ppermute | solution.py:43
  19.5 2.3 %collective-permute-start.4 = (bf16[256,1024]{1,0:T(8,128)(2,1)S(1)}, bf16[256,1024]{1,0:T(8,128)(2,1)S(1)}, u32[]{:S(2)}, u32[]{:S(2)}) collective-permute-start(bf16[256,1024]{1,0:T(8,128)(2,1)S(1)} %get-tuple-element.75), channel_id=1, source_target_pairs={{0,17},{1,16},{2,19},{3,18},{4,21},{5,20},{6,23},{7,22},{8,25},{9,... | collective-permute-start | bytes 1572872 | tf_op jit(solution)/shard_map/ppermute | solution.py:43
  23.3 1.7 %collective-permute-start.12 = (bf16[256,1024]{1,0:T(8,128)(2,1)S(1)}, bf16[256,1024]{1,0:T(8,128)(2,1)S(1)}, u32[]{:S(2)}, u32[]{:S(2)}) collective-permute-start(bf16[256,1024]{1,0:T(8,128)(2,1)S(1)} %collective-permute-done.1.refs_5_.refs_10_.refs_7_), channel_id=1, source_target_pairs={{0,96},{1,97},{2,98},{3,99},{4,100},{5,101},{6,102},{7,103},{8,104... | collective-permute-start | bytes 1572872 | tf_op jit(solution)/shard_map/ppermute | solution.py:43
  25.1 7.5 %collective-permute-done.3.refs_6_.refs_11_ = bf16[256,1024]{1,0:T(8,128)(2,1)S(1)} collective-permute-done((bf16[256,1024]{1,0:T(8,128)(2,1)S(1)}, bf16[256,1024]{1,0:T(8,128)(2,1)S(1)}, u32[]{:S(2)}, u32[]{:S(2)}) %collective-permute-start.3) | collective-permute-done | bytes 524320 | tf_op jit(solution)/shard_map/ppermute | solution.py:43
  34.0 1.9 %collective-permute-done.11.refs_10_.refs_17_.refs_12_ = bf16[256,1024]{1,0:T(8,128)(2,1)S(1)} collective-permute-done((bf16[256,1024]{1,0:T(8,128)(2,1)S(1)}, bf16[256,1024]{1,0:T(8,128)(2,1)S(1)}, u32[]{:S(2)}, u32[]{:S(2)}) %collective-permute-start.11) | collective-permute-done | bytes 524320 | tf_op jit(solution)/shard_map/ppermute | solution.py:43
  39.5 1.9 %collective-permute-start.14 = (bf16[256,1024]{1,0:T(8,128)(2,1)S(1)}, bf16[256,1024]{1,0:T(8,128)(2,1)S(1)}, u32[]{:S(2)}, u32[]{:S(2)}) collective-permute-start(bf16[256,1024]{1,0:T(8,128)(2,1)S(1)} %collective-permute-done.refs_4_.refs_9_.refs_6_), channel_id=1, source_target_pairs={{0,96},{1,97},{2,98},{3,99},{4,100},{5,101},{6,102},{7,103},{8,104... | collective-permute-start | bytes 1572872 | tf_op jit(solution)/shard_map/ppermute | solution.py:43
  42.4 9.1 %collective-permute-done.13.refs_11_.refs_18_.refs_13_ = bf16[256,1024]{1,0:T(8,128)(2,1)S(1)} collective-permute-done((bf16[256,1024]{1,0:T(8,128)(2,1)S(1)}, bf16[256,1024]{1,0:T(8,128)(2,1)S(1)}, u32[]{:S(2)}, u32[]{:S(2)}) %collective-permute-start.13) | collective-permute-done | bytes 524320 | tf_op jit(solution)/shard_map/ppermute | solution.py:43
  54.2 2.0 %collective-permute-start.16 = (bf16[256,1024]{1,0:T(8,128)(2,1)S(1)}, bf16[256,1024]{1,0:T(8,128)(2,1)S(1)}, u32[]{:S(2)}, u32[]{:S(2)}) collective-permute-start(bf16[256,1024]{1,0:T(8,128)(2,1)S(1)} %collective-permute-done.12.refs_9_.refs_14_), channel_id=1, source_target_pairs={{0,96},{1,97},{2,98},{3,99},{4,100},{5,101},{6,102},{7,103},{8,104... | collective-permute-start | bytes 1572872 | tf_op jit(solution)/shard_map/ppermute | solution.py:43
  57.8 9.0 %shard_map.50 = (bf16[1024,256]{1,0:T(8,128)(2,1)}, bf16[1024,256]{1,0:T(8,128)(2,1)}, bf16[2,1024,256]{2,1,0:T(8,128)(2,1)}, bf16[1024,256]{1,0:T(8,128)(2,1)},...) custom-call(s32[2]{0:T(128)} %pad_add_fusion.refs_0_, bf16[2,256,1024]{2,1,0:T(8,128)(2,1)} %bitcast.43, ...), custom_call_target="tpu_custom_call" | custom-call | flops 65536 | bytes 262144 | tf_op jit(solution)/shard_map/pallas_call | solution.py:207
  68.2 9.1 %shard_map.51 = (bf16[1024,256]{1,0:T(8,128)(2,1)}, bf16[1024,256]{1,0:T(8,128)(2,1)}, bf16[2,1024,256]{2,1,0:T(8,128)(2,1)}, bf16[1024,256]{1,0:T(8,128)(2,1)},...) custom-call(s32[2]{0:T(128)} %pad_add_fusion.refs_0_, ...), custom_call_target="tpu_custom_call", output_to_operand_aliasing={{0}: (19, {}), {1}: (20, {}), {2}: (21, {}), {3}: (22, {}),... | custom-call | flops 65536 | bytes 262144 | tf_op jit(solution)/shard_map/pallas_call | solution.py:207
  77.3 1.6 %collective-permute-start.18 = (bf16[2,1024,256]{2,1,0:T(8,128)(2,1)}, bf16[2,1024,256]{2,1,0:T(8,128)(2,1)}, u32[]{:S(2)}, u32[]{:S(2)}) collective-permute-start(bf16[2,1024,256]{2,1,0:T(8,128)(2,1)} %get-tuple-element.115), channel_id=1, source_target_pairs={{0,2},{1,3},{2,4},{3,5},{4,6},{5,7},{6,0},{7,1},{8,10},{9,11},{10,... | collective-permute-start | bytes 3145736 | tf_op jit(solution)/shard_map/ppermute | solution.py:43
  78.9 2.3 %collective-permute-start.17 = (bf16[1024,256]{1,0:T(8,128)(2,1)}, bf16[1024,256]{1,0:T(8,128)(2,1)}, u32[]{:S(2)}, u32[]{:S(2)}) collective-permute-start(bf16[1024,256]{1,0:T(8,128)(2,1)} %get-tuple-element.114), channel_id=1, source_target_pairs={{0,6},{1,7},{2,0},{3,1},{4,2},{5,3},{6,4},{7,5},{8,14},{9,15},{10,... | collective-permute-start | bytes 1572872 | tf_op jit(solution)/shard_map/ppermute | solution.py:43
  82.4 5.5 %all-to-all-start = ((bf16[16,64,1024]{2,1,0:T(8,128)(2,1)}), bf16[16,64,1024]{2,1,0:T(8,128)(2,1)S(1)}, u32[]{:S(2)}, u32[]{:S(2)}) async-start(bf16[16,64,1024]{2,1,0:T(8,128)(2,1)} %bitcast.49), calls=%async_computation | async-start | bytes 4194304 | tf_op jit(solution)/shard_map/all_to_all | solution.py:279
  87.9 7.2 %shard_map.52 = (bf16[1024,256]{1,0:T(8,128)(2,1)}, bf16[2,1024,256]{2,1,0:T(8,128)(2,1)}) custom-call(s32[2]{0:T(128)} %pad_add_fusion.refs_0_, bf16[2,256,1024]{2,1,0:T(8,128)(2,1)} %copy-done.10, bf16[256,1024]{1,0:T(8,128)(2,1)} %copy-done.13, bf16[256,1024]{1,0:T(8,128)(2,1)} %collective-permute-done.9.refs_3_, ...), custom_call_target="tpu_custom_call", output_to_operand_aliasing={{0}: (14, {}), {1}: (15, {})} | custom-call | flops 65536 | bytes 262144 | tf_op jit(solution)/shard_map/pallas_call | solution.py:207
  95.6 8.8 %collective-permute-done.19 = bf16[1024,256]{1,0:T(8,128)(2,1)} collective-permute-done((bf16[1024,256]{1,0:T(8,128)(2,1)}, bf16[1024,256]{1,0:T(8,128)(2,1)}, u32[]{:S(2)}, u32[]{:S(2)}) %collective-permute-start.19) | collective-permute-done | bytes 524320 | tf_op jit(solution)/shard_map/ppermute | solution.py:43
  105.0 2.2 %fusion = bf16[1024,256]{1,0:T(8,128)(2,1)} fusion(bf16[1024,256]{1,0:T(8,128)(2,1)} %collective-permute-done.17, bf16[2,1024,256]{2,1,0:T(8,128)(2,1)} %get-tuple-element.121), kind=kLoop, calls=%fused_computation.9 | loop fusion | flops 1048576 | bytes 1572864 | tf_op jit(solution)/shard_map/convert_element_type | solution.py:55
  107.1 2.1 %fusion.3 = bf16[1024,256]{1,0:T(8,128)(2,1)} fusion(bf16[2,1024,256]{2,1,0:T(8,128)(2,1)} %get-tuple-element.121, bf16[2,1024,256]{2,1,0:T(8,128)(2,1)} %collective-permute-done.18), kind=kLoop, calls=%fused_computation.15 | loop fusion | flops 1048576 | bytes 1572864 | tf_op jit(solution)/shard_map/convert_element_type | solution.py:55
  109.3 2.3 %collective-permute-start.20 = (bf16[1024,256]{1,0:T(8,128)(2,1)}, bf16[1024,256]{1,0:T(8,128)(2,1)}, u32[]{:S(2)}, u32[]{:S(2)}) collective-permute-start(bf16[1024,256]{1,0:T(8,128)(2,1)} %fusion), channel_id=1, source_target_pairs={{0,6},{1,7},{2,0},{3,1},{4,2},{5,3},{6,4},{7,5},{8,14},{9,15},{10,... | collective-permute-start | bytes 1572872 | tf_op jit(solution)/shard_map/ppermute | solution.py:43
  111.6 12.4 %collective-permute-done.20 = bf16[1024,256]{1,0:T(8,128)(2,1)} collective-permute-done((bf16[1024,256]{1,0:T(8,128)(2,1)}, bf16[1024,256]{1,0:T(8,128)(2,1)}, u32[]{:S(2)}, u32[]{:S(2)}) %collective-permute-start.20) | collective-permute-done | bytes 524320 | tf_op jit(solution)/shard_map/ppermute | solution.py:43
  124.0 2.7 %collective-permute-done.21 = bf16[1024,256]{1,0:T(8,128)(2,1)} collective-permute-done((bf16[1024,256]{1,0:T(8,128)(2,1)}, bf16[1024,256]{1,0:T(8,128)(2,1)}, u32[]{:S(2)}, u32[]{:S(2)}) %collective-permute-start.21) | collective-permute-done | bytes 524320 | tf_op jit(solution)/shard_map/ppermute | solution.py:43
  126.7 1.5 %fusion.2 = bf16[1024,256]{1,0:T(8,128)(2,1)S(1)} fusion(bf16[1024,256]{1,0:T(8,128)(2,1)} %collective-permute-done.20, bf16[1024,256]{1,0:T(8,128)(2,1)} %get-tuple-element.110, bf16[2,1024,256]{2,1,0:T(8,128)(2,1)} %collective-permute-done.18), kind=kLoop, calls=%fused_computation.12 | loop fusion | flops 1572864 | bytes 2097152 | tf_op jit(solution)/shard_map/convert_element_type | solution.py:55
  128.2 1.5 %add_convert_fusion = bf16[1024,256]{1,0:T(8,128)(2,1)S(1)} fusion(bf16[1024,256]{1,0:T(8,128)(2,1)} %collective-permute-done.21, bf16[1024,256]{1,0:T(8,128)(2,1)} %collective-permute-done.19, bf16[1024,256]{1,0:T(8,128)(2,1)} %collective-permute-done.22), kind=kLoop, calls=%fused_computation.13 | loop fusion | flops 1572864 | bytes 2097152 | tf_op jit(solution)/shard_map/convert_element_type | solution.py:55
  130.9 2.4 %collective-permute-start.23 = (bf16[2,512,256]{2,1,0:T(8,128)(2,1)}, bf16[2,512,256]{2,1,0:T(8,128)(2,1)}, u32[]{:S(2)}, u32[]{:S(2)}) collective-permute-start(bf16[2,512,256]{2,1,0:T(8,128)(2,1)} %get-tuple-element.128), channel_id=1, source_target_pairs={{0,1},{1,17},{2,3},{3,19},{4,5},{5,21},{6,7},{7,23},{8,9},{9,25},{... | collective-permute-start | bytes 1572872 | tf_op jit(solution)/shard_map/ppermute | solution.py:43
  133.3 2.3 %collective-permute-start.24 = (bf16[2,512,256]{2,1,0:T(8,128)(2,1)}, bf16[2,512,256]{2,1,0:T(8,128)(2,1)}, u32[]{:S(2)}, u32[]{:S(2)}) collective-permute-start(bf16[2,512,256]{2,1,0:T(8,128)(2,1)} %get-tuple-element.129), channel_id=1, source_target_pairs={{0,17},{1,1},{2,19},{3,3},{4,21},{5,5},{6,23},{7,7},{8,25},{9,9},{... | collective-permute-start | bytes 1572872 | tf_op jit(solution)/shard_map/ppermute | solution.py:43
  136.7 8.8 %collective-permute-done.23 = bf16[2,512,256]{2,1,0:T(8,128)(2,1)} collective-permute-done((bf16[2,512,256]{2,1,0:T(8,128)(2,1)}, bf16[2,512,256]{2,1,0:T(8,128)(2,1)}, u32[]{:S(2)}, u32[]{:S(2)}) %collective-permute-start.23) | collective-permute-done | bytes 524320 | tf_op jit(solution)/shard_map/ppermute | solution.py:43
  145.5 5.0 %collective-permute-done.24 = bf16[2,512,256]{2,1,0:T(8,128)(2,1)} collective-permute-done((bf16[2,512,256]{2,1,0:T(8,128)(2,1)}, bf16[2,512,256]{2,1,0:T(8,128)(2,1)}, u32[]{:S(2)}, u32[]{:S(2)}) %collective-permute-start.24) | collective-permute-done | bytes 524320 | tf_op jit(solution)/shard_map/ppermute | solution.py:43
  151.8 1.7 %multiply_add_fusion = f32[512,1024]{1,0:T(8,128)} fusion(f32[512,1024]{1,0:T(8,128)S(1)} %copy-done.14, bf16[256,256]{1,0:T(8,128)(2,1)S(1)} %get-tuple-element.145, bf16[256,256]{1,0:T(8,128)(2,1)S(1)} %get-tuple-element.144, bf16[512,256]{1,0:T(8,128)(2,1)S(1)} %get-tuple-element.136, bf16[256,256]{1,0:T(8,128)(2,1)S(1)} %get-tuple-element.146, ...), kind=kLoop, calls=%fused_computation | loop fusion | flops 7864320 | bytes 5242880 | tf_op jit(solution)/shard_map/add | solution.py:313
  (70 shorter events, 19.2 us)
Async XLA Ops:
  2.4 17.0 %collective-permute-start.2 = (bf16[2,256,1024]{2,1,0:T(8,128)(2,1)S(1)}, bf16[2,256,1024]{2,1,0:T(8,128)(2,1)S(1)}, u32[]{:S(2)}, u32[]{:S(2)}) collective-permute-start(bf16[2,256,1024]{2,1,0:T(8,128)(2,1)S(1)} %bitcast.42), channel_id=1, source_target_pairs={{0,8},{1,9},{2,10},{3,11},{4,12},{5,13},{6,14},{7,15},{8,0},{9,1},... | collective-permute-start | bytes 3145736 | tf_op jit(solution)/shard_map/ppermute | solution.py:43
  2.5 14.3 %collective-permute-start = (bf16[256,1024]{1,0:T(8,128)(2,1)S(1)}, bf16[256,1024]{1,0:T(8,128)(2,1)S(1)}, u32[]{:S(2)}, u32[]{:S(2)}) collective-permute-start(bf16[256,1024]{1,0:T(8,128)(2,1)S(1)} %get-tuple-element.75), channel_id=1, source_target_pairs={{0,16},{1,17},{2,18},{3,19},{4,20},{5,21},{6,22},{7,23},{8,24},{9,... | collective-permute-start | bytes 1572872 | tf_op jit(solution)/shard_map/ppermute | solution.py:43
  4.2 15.2 %collective-permute-start.1 = (bf16[256,1024]{1,0:T(8,128)(2,1)S(1)}, bf16[256,1024]{1,0:T(8,128)(2,1)S(1)}, u32[]{:S(2)}, u32[]{:S(2)}) collective-permute-start(bf16[256,1024]{1,0:T(8,128)(2,1)S(1)} %get-tuple-element.74), channel_id=1, source_target_pairs={{0,17},{1,16},{2,19},{3,18},{4,21},{5,20},{6,23},{7,22},{8,25},{9,... | collective-permute-start | bytes 1572872 | tf_op jit(solution)/shard_map/ppermute | solution.py:43
  16.9 25.6 %copy-start.2 = (bf16[256,1024]{1,0:T(8,128)(2,1)}, bf16[256,1024]{1,0:T(8,128)(2,1)S(1)}, u32[]{:S(2)}) copy-start(bf16[256,1024]{1,0:T(8,128)(2,1)S(1)} %collective-permute-done.refs_4_.refs_9_.refs_6_) | copy-start | bytes 1572868
  19.4 23.0 %copy-start.3 = (bf16[256,1024]{1,0:T(8,128)(2,1)}, bf16[256,1024]{1,0:T(8,128)(2,1)S(1)}, u32[]{:S(2)}) copy-start(bf16[256,1024]{1,0:T(8,128)(2,1)S(1)} %collective-permute-done.1.refs_5_.refs_10_.refs_7_) | copy-start | bytes 1572868
  19.4 23.0 %copy-start.10 = (bf16[2,256,1024]{2,1,0:T(8,128)(2,1)}, bf16[2,256,1024]{2,1,0:T(8,128)(2,1)S(1)}, u32[]{:S(2)}) copy-start(bf16[2,256,1024]{2,1,0:T(8,128)(2,1)S(1)} %collective-permute-done.2.refs_1_) | copy-start | bytes 3145732
  19.4 13.2 %collective-permute-start.3 = (bf16[256,1024]{1,0:T(8,128)(2,1)S(1)}, bf16[256,1024]{1,0:T(8,128)(2,1)S(1)}, u32[]{:S(2)}, u32[]{:S(2)}) collective-permute-start(bf16[256,1024]{1,0:T(8,128)(2,1)S(1)} %get-tuple-element.74), channel_id=1, source_target_pairs={{0,16},{1,17},{2,18},{3,19},{4,20},{5,21},{6,22},{7,23},{8,24},{9,... | collective-permute-start | bytes 1572872 | tf_op jit(solution)/shard_map/ppermute | solution.py:43
  19.5 14.4 %collective-permute-start.4 = (bf16[256,1024]{1,0:T(8,128)(2,1)S(1)}, bf16[256,1024]{1,0:T(8,128)(2,1)S(1)}, u32[]{:S(2)}, u32[]{:S(2)}) collective-permute-start(bf16[256,1024]{1,0:T(8,128)(2,1)S(1)} %get-tuple-element.75), channel_id=1, source_target_pairs={{0,17},{1,16},{2,19},{3,18},{4,21},{5,20},{6,23},{7,22},{8,25},{9,... | collective-permute-start | bytes 1572872 | tf_op jit(solution)/shard_map/ppermute | solution.py:43
  21.8 14.1 %collective-permute-start.11 = (bf16[256,1024]{1,0:T(8,128)(2,1)S(1)}, bf16[256,1024]{1,0:T(8,128)(2,1)S(1)}, u32[]{:S(2)}, u32[]{:S(2)}) collective-permute-start(bf16[256,1024]{1,0:T(8,128)(2,1)S(1)} %collective-permute-done.refs_4_.refs_9_.refs_6_), channel_id=1, source_target_pairs={{0,32},{1,33},{2,34},{3,35},{4,36},{5,37},{6,38},{7,39},{8,40},{9,... | collective-permute-start | bytes 1572872 | tf_op jit(solution)/shard_map/ppermute | solution.py:43
  23.3 12.6 %collective-permute-start.12 = (bf16[256,1024]{1,0:T(8,128)(2,1)S(1)}, bf16[256,1024]{1,0:T(8,128)(2,1)S(1)}, u32[]{:S(2)}, u32[]{:S(2)}) collective-permute-start(bf16[256,1024]{1,0:T(8,128)(2,1)S(1)} %collective-permute-done.1.refs_5_.refs_10_.refs_7_), channel_id=1, source_target_pairs={{0,96},{1,97},{2,98},{3,99},{4,100},{5,101},{6,102},{7,103},{8,104... | collective-permute-start | bytes 1572872 | tf_op jit(solution)/shard_map/ppermute | solution.py:43
  32.7 23.7 %copy-start.8 = (bf16[256,1024]{1,0:T(8,128)(2,1)}, bf16[256,1024]{1,0:T(8,128)(2,1)S(1)}, u32[]{:S(2)}) copy-start(bf16[256,1024]{1,0:T(8,128)(2,1)S(1)} %collective-permute-done.3.refs_6_.refs_11_) | copy-start | bytes 1572868
  34.0 22.4 %copy-start.9 = (bf16[256,1024]{1,0:T(8,128)(2,1)}, bf16[256,1024]{1,0:T(8,128)(2,1)S(1)}, u32[]{:S(2)}) copy-start(bf16[256,1024]{1,0:T(8,128)(2,1)S(1)} %collective-permute-done.4.refs_7_.refs_12_) | copy-start | bytes 1572868
  35.9 22.0 %copy-start.4 = (bf16[256,1024]{1,0:T(8,128)(2,1)}, bf16[256,1024]{1,0:T(8,128)(2,1)S(1)}, u32[]{:S(2)}) copy-start(bf16[256,1024]{1,0:T(8,128)(2,1)S(1)} %collective-permute-done.11.refs_10_.refs_17_.refs_12_) | copy-start | bytes 1572868
  35.9 20.3 %collective-permute-start.7 = (bf16[2,256,1024]{2,1,0:T(8,128)(2,1)S(1)}, bf16[2,256,1024]{2,1,0:T(8,128)(2,1)S(1)}, u32[]{:S(2)}, u32[]{:S(2)}) collective-permute-start(bf16[2,256,1024]{2,1,0:T(8,128)(2,1)S(1)} %pad_maximum_fusion), channel_id=1, source_target_pairs={{0,8},{1,9},{2,10},{3,11},{4,12},{5,13},{6,14},{7,15},{8,0},{9,1},... | collective-permute-start | bytes 3145736 | tf_op jit(solution)/shard_map/ppermute | solution.py:43
  36.0 15.6 %collective-permute-start.13 = (bf16[256,1024]{1,0:T(8,128)(2,1)S(1)}, bf16[256,1024]{1,0:T(8,128)(2,1)S(1)}, u32[]{:S(2)}, u32[]{:S(2)}) collective-permute-start(bf16[256,1024]{1,0:T(8,128)(2,1)S(1)} %collective-permute-done.1.refs_5_.refs_10_.refs_7_), channel_id=1, source_target_pairs={{0,32},{1,33},{2,34},{3,35},{4,36},{5,37},{6,38},{7,39},{8,40},{9,... | collective-permute-start | bytes 1572872 | tf_op jit(solution)/shard_map/ppermute | solution.py:43
  37.4 16.8 %collective-permute-start.5 = (bf16[256,1024]{1,0:T(8,128)(2,1)S(1)}, bf16[256,1024]{1,0:T(8,128)(2,1)}, u32[]{:S(2)}, u32[]{:S(2)}) collective-permute-start(bf16[256,1024]{1,0:T(8,128)(2,1)S(1)} %collective-permute-done.1.refs_5_.refs_10_.refs_7_), channel_id=1, source_target_pairs={{0,16},{1,17},{2,18},{3,19},{4,20},{5,21},{6,22},{7,23},{8,24},{9,... | collective-permute-start | bytes 1572872 | tf_op jit(solution)/shard_map/ppermute | solution.py:43
  38.4 17.8 %collective-permute-start.6 = (bf16[256,1024]{1,0:T(8,128)(2,1)S(1)}, bf16[256,1024]{1,0:T(8,128)(2,1)}, u32[]{:S(2)}, u32[]{:S(2)}) collective-permute-start(bf16[256,1024]{1,0:T(8,128)(2,1)S(1)} %collective-permute-done.refs_4_.refs_9_.refs_6_), channel_id=1, source_target_pairs={{0,17},{1,16},{2,19},{3,18},{4,21},{5,20},{6,23},{7,22},{8,25},{9,... | collective-permute-start | bytes 1572872 | tf_op jit(solution)/shard_map/ppermute | solution.py:43
  39.5 13.5 %collective-permute-start.14 = (bf16[256,1024]{1,0:T(8,128)(2,1)S(1)}, bf16[256,1024]{1,0:T(8,128)(2,1)S(1)}, u32[]{:S(2)}, u32[]{:S(2)}) collective-permute-start(bf16[256,1024]{1,0:T(8,128)(2,1)S(1)} %collective-permute-done.refs_4_.refs_9_.refs_6_), channel_id=1, source_target_pairs={{0,96},{1,97},{2,98},{3,99},{4,100},{5,101},{6,102},{7,103},{8,104... | collective-permute-start | bytes 1572872 | tf_op jit(solution)/shard_map/ppermute | solution.py:43
  51.5 15.7 %collective-permute-start.10 = (bf16[2,256,1024]{2,1,0:T(8,128)(2,1)}, bf16[2,256,1024]{2,1,0:T(8,128)(2,1)}, u32[]{:S(2)}, u32[]{:S(2)}) collective-permute-start(bf16[2,256,1024]{2,1,0:T(8,128)(2,1)} %pad_maximum_fusion.1), channel_id=1, source_target_pairs={{0,8},{1,9},{2,10},{3,11},{4,12},{5,13},{6,14},{7,15},{8,0},{9,1},... | collective-permute-start | bytes 3145736 | tf_op jit(solution)/shard_map/ppermute | solution.py:43
  53.0 14.2 %collective-permute-start.15 = (bf16[256,1024]{1,0:T(8,128)(2,1)S(1)}, bf16[256,1024]{1,0:T(8,128)(2,1)}, u32[]{:S(2)}, u32[]{:S(2)}) collective-permute-start(bf16[256,1024]{1,0:T(8,128)(2,1)S(1)} %collective-permute-done.11.refs_10_.refs_17_.refs_12_), channel_id=1, source_target_pairs={{0,32},{1,33},{2,34},{3,35},{4,36},{5,37},{6,38},{7,39},{8,40},{9,... | collective-permute-start | bytes 1572872 | tf_op jit(solution)/shard_map/ppermute | solution.py:43
  54.2 13.0 %collective-permute-start.16 = (bf16[256,1024]{1,0:T(8,128)(2,1)S(1)}, bf16[256,1024]{1,0:T(8,128)(2,1)S(1)}, u32[]{:S(2)}, u32[]{:S(2)}) collective-permute-start(bf16[256,1024]{1,0:T(8,128)(2,1)S(1)} %collective-permute-done.12.refs_9_.refs_14_), channel_id=1, source_target_pairs={{0,96},{1,97},{2,98},{3,99},{4,100},{5,101},{6,102},{7,103},{8,104... | collective-permute-start | bytes 1572872 | tf_op jit(solution)/shard_map/ppermute | solution.py:43
  56.3 11.0 %collective-permute-start.8 = (bf16[256,1024]{1,0:T(8,128)(2,1)}, bf16[256,1024]{1,0:T(8,128)(2,1)S(1)}, u32[]{:S(2)}, u32[]{:S(2)}) collective-permute-start(bf16[256,1024]{1,0:T(8,128)(2,1)} %collective-permute-done.5.refs_2_.refs_7_), channel_id=1, source_target_pairs={{0,8},{1,9},{2,10},{3,11},{4,12},{5,13},{6,14},{7,15},{8,0},{9,1},... | collective-permute-start | bytes 1572872 | tf_op jit(solution)/shard_map/ppermute | solution.py:43
  57.2 10.0 %collective-permute-start.9 = (bf16[256,1024]{1,0:T(8,128)(2,1)}, bf16[256,1024]{1,0:T(8,128)(2,1)}, u32[]{:S(2)}, u32[]{:S(2)}) collective-permute-start(bf16[256,1024]{1,0:T(8,128)(2,1)} %collective-permute-done.6.refs_3_.refs_8_), channel_id=1, source_target_pairs={{0,8},{1,9},{2,10},{3,11},{4,12},{5,13},{6,14},{7,15},{8,0},{9,1},... | collective-permute-start | bytes 1572872 | tf_op jit(solution)/shard_map/ppermute | solution.py:43
  77.3 27.7 %collective-permute-start.18 = (bf16[2,1024,256]{2,1,0:T(8,128)(2,1)}, bf16[2,1024,256]{2,1,0:T(8,128)(2,1)}, u32[]{:S(2)}, u32[]{:S(2)}) collective-permute-start(bf16[2,1024,256]{2,1,0:T(8,128)(2,1)} %get-tuple-element.115), channel_id=1, source_target_pairs={{0,2},{1,3},{2,4},{3,5},{4,6},{5,7},{6,0},{7,1},{8,10},{9,11},{10,... | collective-permute-start | bytes 3145736 | tf_op jit(solution)/shard_map/ppermute | solution.py:43
  78.9 16.6 %collective-permute-start.17 = (bf16[1024,256]{1,0:T(8,128)(2,1)}, bf16[1024,256]{1,0:T(8,128)(2,1)}, u32[]{:S(2)}, u32[]{:S(2)}) collective-permute-start(bf16[1024,256]{1,0:T(8,128)(2,1)} %get-tuple-element.114), channel_id=1, source_target_pairs={{0,6},{1,7},{2,0},{3,1},{4,2},{5,3},{6,4},{7,5},{8,14},{9,15},{10,... | collective-permute-start | bytes 1572872 | tf_op jit(solution)/shard_map/ppermute | solution.py:43
  81.2 23.1 %collective-permute-start.19 = (bf16[1024,256]{1,0:T(8,128)(2,1)}, bf16[1024,256]{1,0:T(8,128)(2,1)}, u32[]{:S(2)}, u32[]{:S(2)}) collective-permute-start(bf16[1024,256]{1,0:T(8,128)(2,1)} %get-tuple-element.116), channel_id=1, source_target_pairs={{0,14},{1,15},{2,8},{3,9},{4,10},{5,11},{6,12},{7,13},{8,6},{9,7},... | collective-permute-start | bytes 1572872 | tf_op jit(solution)/shard_map/ppermute | solution.py:43
  82.4 48.5 %all-to-all-start = ((bf16[16,64,1024]{2,1,0:T(8,128)(2,1)}), bf16[16,64,1024]{2,1,0:T(8,128)(2,1)S(1)}, u32[]{:S(2)}, u32[]{:S(2)}) async-start(bf16[16,64,1024]{2,1,0:T(8,128)(2,1)} %bitcast.49), calls=%async_computation | async-start | bytes 4194304 | tf_op jit(solution)/shard_map/all_to_all | solution.py:279
  95.1 16.5 %collective-permute-start.22 = (bf16[1024,256]{1,0:T(8,128)(2,1)}, bf16[1024,256]{1,0:T(8,128)(2,1)}, u32[]{:S(2)}, u32[]{:S(2)}) collective-permute-start(bf16[1024,256]{1,0:T(8,128)(2,1)} %get-tuple-element.125), channel_id=1, source_target_pairs={{0,8},{1,9},{2,10},{3,11},{4,12},{5,13},{6,14},{7,15},{8,0},{9,1},... | collective-permute-start | bytes 1572872 | tf_op jit(solution)/shard_map/ppermute | solution.py:43
  109.3 14.7 %collective-permute-start.20 = (bf16[1024,256]{1,0:T(8,128)(2,1)}, bf16[1024,256]{1,0:T(8,128)(2,1)}, u32[]{:S(2)}, u32[]{:S(2)}) collective-permute-start(bf16[1024,256]{1,0:T(8,128)(2,1)} %fusion), channel_id=1, source_target_pairs={{0,6},{1,7},{2,0},{3,1},{4,2},{5,3},{6,4},{7,5},{8,14},{9,15},{10,... | collective-permute-start | bytes 1572872 | tf_op jit(solution)/shard_map/ppermute | solution.py:43
  111.6 15.1 %collective-permute-start.21 = (bf16[1024,256]{1,0:T(8,128)(2,1)}, bf16[1024,256]{1,0:T(8,128)(2,1)}, u32[]{:S(2)}, u32[]{:S(2)}) collective-permute-start(bf16[1024,256]{1,0:T(8,128)(2,1)} %fusion.3), channel_id=1, source_target_pairs={{0,10},{1,11},{2,12},{3,13},{4,14},{5,15},{6,8},{7,9},{8,2},{9,3},... | collective-permute-start | bytes 1572872 | tf_op jit(solution)/shard_map/ppermute | solution.py:43
  130.9 14.6 %collective-permute-start.23 = (bf16[2,512,256]{2,1,0:T(8,128)(2,1)}, bf16[2,512,256]{2,1,0:T(8,128)(2,1)}, u32[]{:S(2)}, u32[]{:S(2)}) collective-permute-start(bf16[2,512,256]{2,1,0:T(8,128)(2,1)} %get-tuple-element.128), channel_id=1, source_target_pairs={{0,1},{1,17},{2,3},{3,19},{4,5},{5,21},{6,7},{7,23},{8,9},{9,25},{... | collective-permute-start | bytes 1572872 | tf_op jit(solution)/shard_map/ppermute | solution.py:43
  133.3 17.2 %collective-permute-start.24 = (bf16[2,512,256]{2,1,0:T(8,128)(2,1)}, bf16[2,512,256]{2,1,0:T(8,128)(2,1)}, u32[]{:S(2)}, u32[]{:S(2)}) collective-permute-start(bf16[2,512,256]{2,1,0:T(8,128)(2,1)} %get-tuple-element.129), channel_id=1, source_target_pairs={{0,17},{1,1},{2,19},{3,3},{4,21},{5,5},{6,23},{7,7},{8,25},{9,9},{... | collective-permute-start | bytes 1572872 | tf_op jit(solution)/shard_map/ppermute | solution.py:43
  (10 other events, 66.1 us)

commit v12 on v10

--- a/solution.py
+++ b/solution.py
@@ -9,7 +9,7 @@
 
 SIZES = (4, 2, 2, 4, 2)
 AXES = ("feat", "batch")
-LATE = 60
+LATE = 30
 
 
 def flat(place):

time: 149 us -> 149 us (level)
  local copies, waits for them, and re-layouts: 3.72 us -> 14.5 us
  waiting for transfers between devices: 68.1 us -> 59.5 us
  Pallas kernels: 25 us -> 22.7 us
    unnamed x30 -> x58, local copies, waits for them, and re-layouts: 1.9 us -> 12.7 us
    ppermute x25, waiting for transfers between devices: 68.1 us -> 59.5 us  [send(): return lax.ppermute(value, AXES, pairs)]
    pallas_call x3, Pallas kernels: 25 us -> 22.7 us  [block_product(): pl.pallas_call(functools.partial(block_kernel, plan, groups), out_shape=[...]
  transfers between devices with their start and end apart: 26 -> 26, of which waited for: 15 -> 15; matrix products, arithmetic and copies ran while one was open for 8% -> 8% of each run, Pallas kernels for 11% -> 9%
where the time goes in v12:
time: 149 us; the launch traced here: 148 us
  waiting for transfers between devices  59.5 us (40%)
  starting transfers between devices  37.8 us (25%)
  Pallas kernels  22.7 us (15%)
  local copies, waits for them, and re-layouts  14.5 us (10%)
  other arithmetic  10.2 us (7%)
  matrix products  2.57 us (2%)
    ppermute x25, waiting for transfers between devices, send(): return lax.ppermute(value, AXES, pairs)  59.5 us
    ppermute x25, starting transfers between devices, send(): return lax.ppermute(value, AXES, pairs)  32.8 us
    pallas_call x3, Pallas kernels, block_product(): pl.pallas_call(functools.partial(block_kernel, plan, groups), out_shape=[...  22.7 us
    unnamed x58, local copies, waits for them, and re-layouts  12.7 us
    all_to_all x1, starting transfers between devices, on_device(): shares = lax.all_to_all(share, 'feat', 0, 0)  5 us
    convert_element_type x2, other arithmetic, narrow(): return value.astype(jnp.bfloat16)  4.05 us
  transfers between devices with their start and end apart: 26, of which 15 were waited for; matrix products, arithmetic and copies ran while one was open for 8% of the time, Pallas kernels for 9%

profile of v12, /device:TPU:0, one launch (start us, length us, event | category | flops | bytes accessed | tf_op | source)
XLA Modules:
  0.0 148.3 jit_solution(10888249802544731632)
XLA Ops:
  0.7 1.6 %copy.11 = bf16[512,1024]{1,0:T(8,128)(2,1)S(1)} copy(bf16[512,1024]{0,1:T(8,128)(2,1)} %bitcast.48) | data formatting | bytes 2097152 | tf_op jit(solution)/shard_map/transpose | solution.py:232
  2.5 1.7 %collective-permute-start = (bf16[256,1024]{1,0:T(8,128)(2,1)S(1)}, bf16[256,1024]{1,0:T(8,128)(2,1)S(1)}, u32[]{:S(2)}, u32[]{:S(2)}) collective-permute-start(bf16[256,1024]{1,0:T(8,128)(2,1)S(1)} %get-tuple-element.72), channel_id=1, source_target_pairs={{0,16},{1,17},{2,18},{3,19},{4,20},{5,21},{6,22},{7,23},{8,24},{9,... | collective-permute-start | bytes 1572872 | tf_op jit(solution)/shard_map/ppermute | solution.py:46
  4.2 2.2 %collective-permute-start.1 = (bf16[256,1024]{1,0:T(8,128)(2,1)S(1)}, bf16[256,1024]{1,0:T(8,128)(2,1)S(1)}, u32[]{:S(2)}, u32[]{:S(2)}) collective-permute-start(bf16[256,1024]{1,0:T(8,128)(2,1)S(1)} %get-tuple-element.71), channel_id=1, source_target_pairs={{0,17},{1,16},{2,19},{3,18},{4,21},{5,20},{6,23},{7,22},{8,25},{9,... | collective-permute-start | bytes 1572872 | tf_op jit(solution)/shard_map/ppermute | solution.py:46
  6.4 2.6 %convolution_convert_fusion = bf16[1024,1024]{1,0:T(8,128)(2,1)} fusion(bf16[1024,512]{1,0:T(8,128)(2,1)S(1)} %copy-done.28, bf16[512,1024]{1,0:T(8,128)(2,1)S(1)} %copy-done), kind=kOutput, calls=%fused_computation.1 | convolution fusion | flops 1074790400 | bytes 4194304 | tf_op jit(solution)/shard_map/dot_general | solution.py:236
  9.0 7.8 %collective-permute-done.refs_4_.refs_9_.refs_6_ = bf16[256,1024]{1,0:T(8,128)(2,1)S(1)} collective-permute-done((bf16[256,1024]{1,0:T(8,128)(2,1)S(1)}, bf16[256,1024]{1,0:T(8,128)(2,1)S(1)}, u32[]{:S(2)}, u32[]{:S(2)}) %collective-permute-start) | collective-permute-done | bytes 524320 | tf_op jit(solution)/shard_map/ppermute | solution.py:46
  16.9 2.6 %collective-permute-done.1.refs_5_.refs_10_.refs_7_ = bf16[256,1024]{1,0:T(8,128)(2,1)S(1)} collective-permute-done((bf16[256,1024]{1,0:T(8,128)(2,1)S(1)}, bf16[256,1024]{1,0:T(8,128)(2,1)S(1)}, u32[]{:S(2)}, u32[]{:S(2)}) %collective-permute-start.1) | collective-permute-done | bytes 524320 | tf_op jit(solution)/shard_map/ppermute | solution.py:46
  19.5 2.3 %collective-permute-start.4 = (bf16[256,1024]{1,0:T(8,128)(2,1)S(1)}, bf16[256,1024]{1,0:T(8,128)(2,1)S(1)}, u32[]{:S(2)}, u32[]{:S(2)}) collective-permute-start(bf16[256,1024]{1,0:T(8,128)(2,1)S(1)} %get-tuple-element.72), channel_id=1, source_target_pairs={{0,17},{1,16},{2,19},{3,18},{4,21},{5,20},{6,23},{7,22},{8,25},{9,... | collective-permute-start | bytes 1572872 | tf_op jit(solution)/shard_map/ppermute | solution.py:46
  23.3 1.7 %collective-permute-start.12 = (bf16[256,1024]{1,0:T(8,128)(2,1)S(1)}, bf16[256,1024]{1,0:T(8,128)(2,1)S(1)}, u32[]{:S(2)}, u32[]{:S(2)}) collective-permute-start(bf16[256,1024]{1,0:T(8,128)(2,1)S(1)} %collective-permute-done.1.refs_5_.refs_10_.refs_7_), channel_id=1, source_target_pairs={{0,96},{1,97},{2,98},{3,99},{4,100},{5,101},{6,102},{7,103},{8,104... | collective-permute-start | bytes 1572872 | tf_op jit(solution)/shard_map/ppermute | solution.py:46
  25.1 7.5 %collective-permute-done.3.refs_6_.refs_11_ = bf16[256,1024]{1,0:T(8,128)(2,1)S(1)} collective-permute-done((bf16[256,1024]{1,0:T(8,128)(2,1)S(1)}, bf16[256,1024]{1,0:T(8,128)(2,1)S(1)}, u32[]{:S(2)}, u32[]{:S(2)}) %collective-permute-start.3) | collective-permute-done | bytes 524320 | tf_op jit(solution)/shard_map/ppermute | solution.py:46
  34.0 1.9 %collective-permute-done.11.refs_10_.refs_17_.refs_12_ = bf16[256,1024]{1,0:T(8,128)(2,1)S(1)} collective-permute-done((bf16[256,1024]{1,0:T(8,128)(2,1)S(1)}, bf16[256,1024]{1,0:T(8,128)(2,1)S(1)}, u32[]{:S(2)}, u32[]{:S(2)}) %collective-permute-start.11) | collective-permute-done | bytes 524320 | tf_op jit(solution)/shard_map/ppermute | solution.py:46
  39.5 1.9 %collective-permute-start.14 = (bf16[256,1024]{1,0:T(8,128)(2,1)S(1)}, bf16[256,1024]{1,0:T(8,128)(2,1)S(1)}, u32[]{:S(2)}, u32[]{:S(2)}) collective-permute-start(bf16[256,1024]{1,0:T(8,128)(2,1)S(1)} %collective-permute-done.refs_4_.refs_9_.refs_6_), channel_id=1, source_target_pairs={{0,96},{1,97},{2,98},{3,99},{4,100},{5,101},{6,102},{7,103},{8,104... | collective-permute-start | bytes 1572872 | tf_op jit(solution)/shard_map/ppermute | solution.py:46
  42.5 9.1 %collective-permute-done.13.refs_11_.refs_18_.refs_13_ = bf16[256,1024]{1,0:T(8,128)(2,1)S(1)} collective-permute-done((bf16[256,1024]{1,0:T(8,128)(2,1)S(1)}, bf16[256,1024]{1,0:T(8,128)(2,1)S(1)}, u32[]{:S(2)}, u32[]{:S(2)}) %collective-permute-start.13) | collective-permute-done | bytes 524320 | tf_op jit(solution)/shard_map/ppermute | solution.py:46
  54.2 2.0 %collective-permute-start.16 = (bf16[256,1024]{1,0:T(8,128)(2,1)S(1)}, bf16[256,1024]{1,0:T(8,128)(2,1)S(1)}, u32[]{:S(2)}, u32[]{:S(2)}) collective-permute-start(bf16[256,1024]{1,0:T(8,128)(2,1)S(1)} %collective-permute-done.12.refs_9_.refs_14_), channel_id=1, source_target_pairs={{0,96},{1,97},{2,98},{3,99},{4,100},{5,101},{6,102},{7,103},{8,104... | collective-permute-start | bytes 1572872 | tf_op jit(solution)/shard_map/ppermute | solution.py:46
  57.9 8.9 %shard_map.50 = (bf16[2,1024,256]{2,1,0:T(8,128)(2,1)}, bf16[2,1024,256]{2,1,0:T(8,128)(2,1)}, bf16[2,1024,256]{2,1,0:T(8,128)(2,1)}, bf16[2,1024,256]{2,1,0:T(8,128)(2,1)}) custom-call(s32[2]{0:T(128)} %pad_add_fusion.refs_0_, bf16[2,256,1024]{2,1,0:T(8,128)(2,1)} %bitcast.41, bf16[256,1024]{1,0:T(8,128)(2,1)} %collective-permute-done.5.refs_2_.refs_7_, ...), custom_call_target="tpu_custom_call" | custom-call | flops 65536 | bytes 262144 | tf_op jit(solution)/shard_map/pallas_call | solution.py:201
  68.2 8.8 %shard_map.51 = (bf16[2,1024,256]{2,1,0:T(8,128)(2,1)}, bf16[2,1024,256]{2,1,0:T(8,128)(2,1)}, bf16[2,1024,256]{2,1,0:T(8,128)(2,1)}, bf16[2,1024,256]{2,1,0:T(8,128)(2,1)}) custom-call(s32[2]{0:T(128)} %pad_add_fusion.refs_0_, bf16[2,256,1024]{2,1,0:T(8,128)(2,1)} %copy-done.15, ...), custom_call_target="tpu_custom_call", output_to_operand_aliasing={{0}: (19, {}), {1}: (20, {}), {2}: (21, {}), {3}: (22, {})} | custom-call | flops 65536 | bytes 262144 | tf_op jit(solution)/shard_map/pallas_call | solution.py:201
  77.1 3.9 %collective-permute-start.17 = (bf16[2,1024,256]{2,1,0:T(8,128)(2,1)}, bf16[2,1024,256]{2,1,0:T(8,128)(2,1)}, u32[]{:S(2)}, u32[]{:S(2)}) collective-permute-start(bf16[2,1024,256]{2,1,0:T(8,128)(2,1)} %get-tuple-element.109), channel_id=1, source_target_pairs={{0,6},{1,7},{2,0},{3,1},{4,2},{5,3},{6,4},{7,5},{8,14},{9,15},{10,... | collective-permute-start | bytes 3145736 | tf_op jit(solution)/shard_map/ppermute | solution.py:46
  80.9 5.0 %all-to-all-start = ((bf16[16,64,1024]{2,1,0:T(8,128)(2,1)}), bf16[16,64,1024]{2,1,0:T(8,128)(2,1)}, u32[]{:S(2)}, u32[]{:S(2)}) async-start(bf16[16,64,1024]{2,1,0:T(8,128)(2,1)} %bitcast.45), calls=%async_computation | async-start | bytes 4194304 | tf_op jit(solution)/shard_map/all_to_all | solution.py:273
  96.8 4.9 %shard_map.52 = (bf16[2,1024,256]{2,1,0:T(8,128)(2,1)S(1)}, bf16[2,1024,256]{2,1,0:T(8,128)(2,1)S(1)}) custom-call(s32[2]{0:T(128)S(1)} %copy-done.23, bf16[2,256,1024]{2,1,0:T(8,128)(2,1)S(1)} %copy-done.16, bf16[256,1024]{1,0:T(8,128)(2,1)S(1)} %copy-done.22, ...), custom_call_target="tpu_custom_call", output_to_operand_aliasing={{0}: (14, {}), {1}: (15, {})} | custom-call | flops 65536 | bytes 262144 | tf_op jit(solution)/shard_map/pallas_call | solution.py:201
  101.7 2.4 %collective-permute-done.17 = bf16[2,1024,256]{2,1,0:T(8,128)(2,1)} collective-permute-done((bf16[2,1024,256]{2,1,0:T(8,128)(2,1)}, bf16[2,1024,256]{2,1,0:T(8,128)(2,1)}, u32[]{:S(2)}, u32[]{:S(2)}) %collective-permute-start.17) | collective-permute-done | bytes 1048608 | tf_op jit(solution)/shard_map/ppermute | solution.py:46
  104.1 3.4 %collective-permute-done.18 = bf16[2,1024,256]{2,1,0:T(8,128)(2,1)} collective-permute-done((bf16[2,1024,256]{2,1,0:T(8,128)(2,1)}, bf16[2,1024,256]{2,1,0:T(8,128)(2,1)}, u32[]{:S(2)}, u32[]{:S(2)}) %collective-permute-start.18) | collective-permute-done | bytes 1048608 | tf_op jit(solution)/shard_map/ppermute | solution.py:46
  107.5 2.4 %fusion.3 = (bf16[1024,256]{1,0:T(8,128)(2,1)}, bf16[1024,256]{1,0:T(8,128)(2,1)}) fusion(bf16[2,1024,256]{2,1,0:T(8,128)(2,1)S(1)} %get-tuple-element.113, bf16[2,1024,256]{2,1,0:T(8,128)(2,1)} %collective-permute-done.18, bf16[2,1024,256]{2,1,0:T(8,128)(2,1)} %collective-permute-done.17), kind=kLoop, calls=%fused_computation.11 | loop fusion | flops 2097152 | bytes 3145728 | tf_op jit(solution)/shard_map/convert_element_type | solution.py:58
  110.2 1.7 %collective-permute-start.20 = (bf16[1024,256]{1,0:T(8,128)(2,1)}, bf16[1024,256]{1,0:T(8,128)(2,1)S(1)}, u32[]{:S(2)}, u32[]{:S(2)}) collective-permute-start(bf16[1024,256]{1,0:T(8,128)(2,1)} %get-tuple-element.115), channel_id=1, source_target_pairs={{0,2},{1,3},{2,4},{3,5},{4,6},{5,7},{6,0},{7,1},{8,10},{9,11},{10,... | collective-permute-start | bytes 1572872 | tf_op jit(solution)/shard_map/ppermute | solution.py:46
  112.0 11.1 %collective-permute-done.19 = bf16[1024,256]{1,0:T(8,128)(2,1)S(1)} collective-permute-done((bf16[1024,256]{1,0:T(8,128)(2,1)}, bf16[1024,256]{1,0:T(8,128)(2,1)S(1)}, u32[]{:S(2)}, u32[]{:S(2)}) %collective-permute-start.19) | collective-permute-done | bytes 524320 | tf_op jit(solution)/shard_map/ppermute | solution.py:46
  123.1 1.5 %collective-permute-done.20 = bf16[1024,256]{1,0:T(8,128)(2,1)S(1)} collective-permute-done((bf16[1024,256]{1,0:T(8,128)(2,1)}, bf16[1024,256]{1,0:T(8,128)(2,1)S(1)}, u32[]{:S(2)}, u32[]{:S(2)}) %collective-permute-start.20) | collective-permute-done | bytes 524320 | tf_op jit(solution)/shard_map/ppermute | solution.py:46
  124.6 1.6 %fusion = (bf16[1024,256]{1,0:T(8,128)(2,1)S(1)}, bf16[1024,256]{1,0:T(8,128)(2,1)S(1)}) fusion(bf16[1024,256]{1,0:T(8,128)(2,1)S(1)} %collective-permute-done.20, bf16[2,1024,256]{2,1,0:T(8,128)(2,1)} %collective-permute-done.17, bf16[2,1024,256]{2,1,0:T(8,128)(2,1)S(1)} %get-tuple-element.106, bf16[1024,256]{1,0:T(8,128)(2,1)S(1)} %collective-permute-done.19, ...), kind=kLoop, calls=%fused_computation.5 | loop fusion | flops 3145728 | bytes 4194304 | tf_op jit(solution)/shard_map/convert_element_type | solution.py:58
  126.3 2.3 %collective-permute-start.21 = (bf16[512,256]{1,0:T(8,128)(2,1)S(1)}, bf16[512,256]{1,0:T(8,128)(2,1)S(1)}, u32[]{:S(2)}, u32[]{:S(2)}) collective-permute-start(bf16[512,256]{1,0:T(8,128)(2,1)S(1)} %get-tuple-element.118), channel_id=1, source_target_pairs={{0,1},{1,17},{2,3},{3,19},{4,5},{5,21},{6,7},{7,23},{8,9},{9,25},{... | collective-permute-start | bytes 786440 | tf_op jit(solution)/shard_map/ppermute | solution.py:46
  128.6 2.1 %collective-permute-start.23 = (bf16[512,256]{1,0:T(8,128)(2,1)S(1)}, bf16[512,256]{1,0:T(8,128)(2,1)S(1)}, u32[]{:S(2)}, u32[]{:S(2)}) collective-permute-start(bf16[512,256]{1,0:T(8,128)(2,1)S(1)} %get-tuple-element.120), channel_id=1, source_target_pairs={{0,17},{1,1},{2,19},{3,3},{4,21},{5,5},{6,23},{7,7},{8,25},{9,9},{... | collective-permute-start | bytes 786440 | tf_op jit(solution)/shard_map/ppermute | solution.py:46
  130.7 4.1 %collective-permute-start.24 = (bf16[512,256]{1,0:T(8,128)(2,1)S(1)}, bf16[512,256]{1,0:T(8,128)(2,1)S(1)}, u32[]{:S(2)}, u32[]{:S(2)}) collective-permute-start(bf16[512,256]{1,0:T(8,128)(2,1)S(1)} %get-tuple-element.121), channel_id=1, source_target_pairs={{0,25},{1,9},{2,27},{3,11},{4,29},{5,13},{6,31},{7,15},{8,17},{9,1... | collective-permute-start | bytes 786440 | tf_op jit(solution)/shard_map/ppermute | solution.py:46
  134.8 2.7 %reduce_sum.12 = bf16[64,1024]{1,0:T(8,128)(2,1)} reduce(bf16[16,64,1024]{2,1,0:T(8,128)(2,1)} %all-to-all-done, bf16[]{:T(256)} %constant.91.clone.1), dimensions={0}, to_apply=%region_0.1 | reduce | flops 983040 | bytes 2228226 | tf_op jit(solution)/shard_map/reduce_sum | solution.py:287
  138.4 1.8 %collective-permute-done.23 = bf16[512,256]{1,0:T(8,128)(2,1)S(1)} collective-permute-done((bf16[512,256]{1,0:T(8,128)(2,1)S(1)}, bf16[512,256]{1,0:T(8,128)(2,1)S(1)}, u32[]{:S(2)}, u32[]{:S(2)}) %collective-permute-start.23) | collective-permute-done | bytes 262176 | tf_op jit(solution)/shard_map/ppermute | solution.py:46
  140.2 6.3 %collective-permute-done.24 = bf16[512,256]{1,0:T(8,128)(2,1)S(1)} collective-permute-done((bf16[512,256]{1,0:T(8,128)(2,1)S(1)}, bf16[512,256]{1,0:T(8,128)(2,1)S(1)}, u32[]{:S(2)}, u32[]{:S(2)}) %collective-permute-start.24) | collective-permute-done | bytes 262176 | tf_op jit(solution)/shard_map/ppermute | solution.py:46
  146.6 1.7 %multiply_add_fusion = f32[512,1024]{1,0:T(8,128)} fusion(f32[512,1024]{1,0:T(8,128)S(1)} %copy-done.27, bf16[256,256]{1,0:T(8,128)(2,1)S(1)} %get-tuple-element.145, bf16[256,256]{1,0:T(8,128)(2,1)S(1)} %get-tuple-element.144, bf16[512,256]{1,0:T(8,128)(2,1)S(1)} %get-tuple-element.130, bf16[256,256]{1,0:T(8,128)(2,1)S(1)} %get-tuple-element.143, ...), kind=kLoop, calls=%fused_computation | loop fusion | flops 7864320 | bytes 5242880 | tf_op jit(solution)/shard_map/add | solution.py:301
  (95 shorter events, 25.6 us)
Async XLA Ops:
  2.4 17.0 %collective-permute-start.2 = (bf16[2,256,1024]{2,1,0:T(8,128)(2,1)S(1)}, bf16[2,256,1024]{2,1,0:T(8,128)(2,1)S(1)}, u32[]{:S(2)}, u32[]{:S(2)}) collective-permute-start(bf16[2,256,1024]{2,1,0:T(8,128)(2,1)S(1)} %bitcast.40), channel_id=1, source_target_pairs={{0,8},{1,9},{2,10},{3,11},{4,12},{5,13},{6,14},{7,15},{8,0},{9,1},... | collective-permute-start | bytes 3145736 | tf_op jit(solution)/shard_map/ppermute | solution.py:46
  2.5 14.3 %collective-permute-start = (bf16[256,1024]{1,0:T(8,128)(2,1)S(1)}, bf16[256,1024]{1,0:T(8,128)(2,1)S(1)}, u32[]{:S(2)}, u32[]{:S(2)}) collective-permute-start(bf16[256,1024]{1,0:T(8,128)(2,1)S(1)} %get-tuple-element.72), channel_id=1, source_target_pairs={{0,16},{1,17},{2,18},{3,19},{4,20},{5,21},{6,22},{7,23},{8,24},{9,... | collective-permute-start | bytes 1572872 | tf_op jit(solution)/shard_map/ppermute | solution.py:46
  4.2 15.2 %collective-permute-start.1 = (bf16[256,1024]{1,0:T(8,128)(2,1)S(1)}, bf16[256,1024]{1,0:T(8,128)(2,1)S(1)}, u32[]{:S(2)}, u32[]{:S(2)}) collective-permute-start(bf16[256,1024]{1,0:T(8,128)(2,1)S(1)} %get-tuple-element.71), channel_id=1, source_target_pairs={{0,17},{1,16},{2,19},{3,18},{4,21},{5,20},{6,23},{7,22},{8,25},{9,... | collective-permute-start | bytes 1572872 | tf_op jit(solution)/shard_map/ppermute | solution.py:46
  16.9 25.6 %copy-start.3 = (bf16[256,1024]{1,0:T(8,128)(2,1)}, bf16[256,1024]{1,0:T(8,128)(2,1)S(1)}, u32[]{:S(2)}) copy-start(bf16[256,1024]{1,0:T(8,128)(2,1)S(1)} %collective-permute-done.refs_4_.refs_9_.refs_6_) | copy-start | bytes 1572868
  19.4 23.0 %copy-start.5 = (bf16[256,1024]{1,0:T(8,128)(2,1)}, bf16[256,1024]{1,0:T(8,128)(2,1)S(1)}, u32[]{:S(2)}) copy-start(bf16[256,1024]{1,0:T(8,128)(2,1)S(1)} %collective-permute-done.1.refs_5_.refs_10_.refs_7_) | copy-start | bytes 1572868
  19.4 23.0 %copy-start.15 = (bf16[2,256,1024]{2,1,0:T(8,128)(2,1)}, bf16[2,256,1024]{2,1,0:T(8,128)(2,1)S(1)}, u32[]{:S(2)}) copy-start(bf16[2,256,1024]{2,1,0:T(8,128)(2,1)S(1)} %collective-permute-done.2.refs_1_) | copy-start | bytes 3145732
  19.4 13.2 %collective-permute-start.3 = (bf16[256,1024]{1,0:T(8,128)(2,1)S(1)}, bf16[256,1024]{1,0:T(8,128)(2,1)S(1)}, u32[]{:S(2)}, u32[]{:S(2)}) collective-permute-start(bf16[256,1024]{1,0:T(8,128)(2,1)S(1)} %get-tuple-element.71), channel_id=1, source_target_pairs={{0,16},{1,17},{2,18},{3,19},{4,20},{5,21},{6,22},{7,23},{8,24},{9,... | collective-permute-start | bytes 1572872 | tf_op jit(solution)/shard_map/ppermute | solution.py:46
  19.5 14.4 %collective-permute-start.4 = (bf16[256,1024]{1,0:T(8,128)(2,1)S(1)}, bf16[256,1024]{1,0:T(8,128)(2,1)S(1)}, u32[]{:S(2)}, u32[]{:S(2)}) collective-permute-start(bf16[256,1024]{1,0:T(8,128)(2,1)S(1)} %get-tuple-element.72), channel_id=1, source_target_pairs={{0,17},{1,16},{2,19},{3,18},{4,21},{5,20},{6,23},{7,22},{8,25},{9,... | collective-permute-start | bytes 1572872 | tf_op jit(solution)/shard_map/ppermute | solution.py:46
  21.8 14.1 %collective-permute-start.11 = (bf16[256,1024]{1,0:T(8,128)(2,1)S(1)}, bf16[256,1024]{1,0:T(8,128)(2,1)S(1)}, u32[]{:S(2)}, u32[]{:S(2)}) collective-permute-start(bf16[256,1024]{1,0:T(8,128)(2,1)S(1)} %collective-permute-done.refs_4_.refs_9_.refs_6_), channel_id=1, source_target_pairs={{0,32},{1,33},{2,34},{3,35},{4,36},{5,37},{6,38},{7,39},{8,40},{9,... | collective-permute-start | bytes 1572872 | tf_op jit(solution)/shard_map/ppermute | solution.py:46
  23.3 12.6 %collective-permute-start.12 = (bf16[256,1024]{1,0:T(8,128)(2,1)S(1)}, bf16[256,1024]{1,0:T(8,128)(2,1)S(1)}, u32[]{:S(2)}, u32[]{:S(2)}) collective-permute-start(bf16[256,1024]{1,0:T(8,128)(2,1)S(1)} %collective-permute-done.1.refs_5_.refs_10_.refs_7_), channel_id=1, source_target_pairs={{0,96},{1,97},{2,98},{3,99},{4,100},{5,101},{6,102},{7,103},{8,104... | collective-permute-start | bytes 1572872 | tf_op jit(solution)/shard_map/ppermute | solution.py:46
  32.7 23.7 %copy-start.25 = (bf16[256,1024]{1,0:T(8,128)(2,1)}, bf16[256,1024]{1,0:T(8,128)(2,1)S(1)}, u32[]{:S(2)}) copy-start(bf16[256,1024]{1,0:T(8,128)(2,1)S(1)} %collective-permute-done.3.refs_6_.refs_11_) | copy-start | bytes 1572868
  34.0 22.4 %copy-start.26 = (bf16[256,1024]{1,0:T(8,128)(2,1)}, bf16[256,1024]{1,0:T(8,128)(2,1)S(1)}, u32[]{:S(2)}) copy-start(bf16[256,1024]{1,0:T(8,128)(2,1)S(1)} %collective-permute-done.4.refs_7_.refs_12_) | copy-start | bytes 1572868
  35.9 22.0 %copy-start.7 = (bf16[256,1024]{1,0:T(8,128)(2,1)}, bf16[256,1024]{1,0:T(8,128)(2,1)S(1)}, u32[]{:S(2)}) copy-start(bf16[256,1024]{1,0:T(8,128)(2,1)S(1)} %collective-permute-done.11.refs_10_.refs_17_.refs_12_) | copy-start | bytes 1572868
  35.9 20.3 %collective-permute-start.7 = (bf16[2,256,1024]{2,1,0:T(8,128)(2,1)S(1)}, bf16[2,256,1024]{2,1,0:T(8,128)(2,1)S(1)}, u32[]{:S(2)}, u32[]{:S(2)}) collective-permute-start(bf16[2,256,1024]{2,1,0:T(8,128)(2,1)S(1)} %pad_maximum_fusion), channel_id=1, source_target_pairs={{0,8},{1,9},{2,10},{3,11},{4,12},{5,13},{6,14},{7,15},{8,0},{9,1},... | collective-permute-start | bytes 3145736 | tf_op jit(solution)/shard_map/ppermute | solution.py:46
  36.0 15.6 %collective-permute-start.13 = (bf16[256,1024]{1,0:T(8,128)(2,1)S(1)}, bf16[256,1024]{1,0:T(8,128)(2,1)S(1)}, u32[]{:S(2)}, u32[]{:S(2)}) collective-permute-start(bf16[256,1024]{1,0:T(8,128)(2,1)S(1)} %collective-permute-done.1.refs_5_.refs_10_.refs_7_), channel_id=1, source_target_pairs={{0,32},{1,33},{2,34},{3,35},{4,36},{5,37},{6,38},{7,39},{8,40},{9,... | collective-permute-start | bytes 1572872 | tf_op jit(solution)/shard_map/ppermute | solution.py:46
  37.4 16.8 %collective-permute-start.5 = (bf16[256,1024]{1,0:T(8,128)(2,1)S(1)}, bf16[256,1024]{1,0:T(8,128)(2,1)}, u32[]{:S(2)}, u32[]{:S(2)}) collective-permute-start(bf16[256,1024]{1,0:T(8,128)(2,1)S(1)} %collective-permute-done.1.refs_5_.refs_10_.refs_7_), channel_id=1, source_target_pairs={{0,16},{1,17},{2,18},{3,19},{4,20},{5,21},{6,22},{7,23},{8,24},{9,... | collective-permute-start | bytes 1572872 | tf_op jit(solution)/shard_map/ppermute | solution.py:46
  38.4 17.8 %collective-permute-start.6 = (bf16[256,1024]{1,0:T(8,128)(2,1)S(1)}, bf16[256,1024]{1,0:T(8,128)(2,1)}, u32[]{:S(2)}, u32[]{:S(2)}) collective-permute-start(bf16[256,1024]{1,0:T(8,128)(2,1)S(1)} %collective-permute-done.refs_4_.refs_9_.refs_6_), channel_id=1, source_target_pairs={{0,17},{1,16},{2,19},{3,18},{4,21},{5,20},{6,23},{7,22},{8,25},{9,... | collective-permute-start | bytes 1572872 | tf_op jit(solution)/shard_map/ppermute | solution.py:46
  39.5 13.5 %collective-permute-start.14 = (bf16[256,1024]{1,0:T(8,128)(2,1)S(1)}, bf16[256,1024]{1,0:T(8,128)(2,1)S(1)}, u32[]{:S(2)}, u32[]{:S(2)}) collective-permute-start(bf16[256,1024]{1,0:T(8,128)(2,1)S(1)} %collective-permute-done.refs_4_.refs_9_.refs_6_), channel_id=1, source_target_pairs={{0,96},{1,97},{2,98},{3,99},{4,100},{5,101},{6,102},{7,103},{8,104... | collective-permute-start | bytes 1572872 | tf_op jit(solution)/shard_map/ppermute | solution.py:46
  51.5 15.7 %collective-permute-start.10 = (bf16[2,256,1024]{2,1,0:T(8,128)(2,1)}, bf16[2,256,1024]{2,1,0:T(8,128)(2,1)}, u32[]{:S(2)}, u32[]{:S(2)}) collective-permute-start(bf16[2,256,1024]{2,1,0:T(8,128)(2,1)} %pad_maximum_fusion.1), channel_id=1, source_target_pairs={{0,8},{1,9},{2,10},{3,11},{4,12},{5,13},{6,14},{7,15},{8,0},{9,1},... | collective-permute-start | bytes 3145736 | tf_op jit(solution)/shard_map/ppermute | solution.py:46
  53.0 14.2 %collective-permute-start.15 = (bf16[256,1024]{1,0:T(8,128)(2,1)S(1)}, bf16[256,1024]{1,0:T(8,128)(2,1)}, u32[]{:S(2)}, u32[]{:S(2)}) collective-permute-start(bf16[256,1024]{1,0:T(8,128)(2,1)S(1)} %collective-permute-done.11.refs_10_.refs_17_.refs_12_), channel_id=1, source_target_pairs={{0,32},{1,33},{2,34},{3,35},{4,36},{5,37},{6,38},{7,39},{8,40},{9,... | collective-permute-start | bytes 1572872 | tf_op jit(solution)/shard_map/ppermute | solution.py:46
  54.2 13.0 %collective-permute-start.16 = (bf16[256,1024]{1,0:T(8,128)(2,1)S(1)}, bf16[256,1024]{1,0:T(8,128)(2,1)S(1)}, u32[]{:S(2)}, u32[]{:S(2)}) collective-permute-start(bf16[256,1024]{1,0:T(8,128)(2,1)S(1)} %collective-permute-done.12.refs_9_.refs_14_), channel_id=1, source_target_pairs={{0,96},{1,97},{2,98},{3,99},{4,100},{5,101},{6,102},{7,103},{8,104... | collective-permute-start | bytes 1572872 | tf_op jit(solution)/shard_map/ppermute | solution.py:46
  56.3 11.0 %collective-permute-start.8 = (bf16[256,1024]{1,0:T(8,128)(2,1)}, bf16[256,1024]{1,0:T(8,128)(2,1)S(1)}, u32[]{:S(2)}, u32[]{:S(2)}) collective-permute-start(bf16[256,1024]{1,0:T(8,128)(2,1)} %collective-permute-done.5.refs_2_.refs_7_), channel_id=1, source_target_pairs={{0,8},{1,9},{2,10},{3,11},{4,12},{5,13},{6,14},{7,15},{8,0},{9,1},... | collective-permute-start | bytes 1572872 | tf_op jit(solution)/shard_map/ppermute | solution.py:46
  57.3 10.0 %collective-permute-start.9 = (bf16[256,1024]{1,0:T(8,128)(2,1)}, bf16[256,1024]{1,0:T(8,128)(2,1)}, u32[]{:S(2)}, u32[]{:S(2)}) collective-permute-start(bf16[256,1024]{1,0:T(8,128)(2,1)} %collective-permute-done.6.refs_3_.refs_8_), channel_id=1, source_target_pairs={{0,8},{1,9},{2,10},{3,11},{4,12},{5,13},{6,14},{7,15},{8,0},{9,1},... | collective-permute-start | bytes 1572872 | tf_op jit(solution)/shard_map/ppermute | solution.py:46
  77.1 27.0 %collective-permute-start.17 = (bf16[2,1024,256]{2,1,0:T(8,128)(2,1)}, bf16[2,1024,256]{2,1,0:T(8,128)(2,1)}, u32[]{:S(2)}, u32[]{:S(2)}) collective-permute-start(bf16[2,1024,256]{2,1,0:T(8,128)(2,1)} %get-tuple-element.109), channel_id=1, source_target_pairs={{0,6},{1,7},{2,0},{3,1},{4,2},{5,3},{6,4},{7,5},{8,14},{9,15},{10,... | collective-permute-start | bytes 3145736 | tf_op jit(solution)/shard_map/ppermute | solution.py:46
  80.9 26.5 %collective-permute-start.18 = (bf16[2,1024,256]{2,1,0:T(8,128)(2,1)}, bf16[2,1024,256]{2,1,0:T(8,128)(2,1)}, u32[]{:S(2)}, u32[]{:S(2)}) collective-permute-start(bf16[2,1024,256]{2,1,0:T(8,128)(2,1)} %get-tuple-element.110), channel_id=1, source_target_pairs={{0,2},{1,3},{2,4},{3,5},{4,6},{5,7},{6,0},{7,1},{8,10},{9,11},{10,... | collective-permute-start | bytes 3145736 | tf_op jit(solution)/shard_map/ppermute | solution.py:46
  80.9 45.3 %all-to-all-start = ((bf16[16,64,1024]{2,1,0:T(8,128)(2,1)}), bf16[16,64,1024]{2,1,0:T(8,128)(2,1)}, u32[]{:S(2)}, u32[]{:S(2)}) async-start(bf16[16,64,1024]{2,1,0:T(8,128)(2,1)} %bitcast.45), calls=%async_computation | async-start | bytes 4194304 | tf_op jit(solution)/shard_map/all_to_all | solution.py:273
  109.9 13.1 %collective-permute-start.19 = (bf16[1024,256]{1,0:T(8,128)(2,1)}, bf16[1024,256]{1,0:T(8,128)(2,1)S(1)}, u32[]{:S(2)}, u32[]{:S(2)}) collective-permute-start(bf16[1024,256]{1,0:T(8,128)(2,1)} %get-tuple-element.114), channel_id=1, source_target_pairs={{0,6},{1,7},{2,0},{3,1},{4,2},{5,3},{6,4},{7,5},{8,14},{9,15},{10,... | collective-permute-start | bytes 1572872 | tf_op jit(solution)/shard_map/ppermute | solution.py:46
  110.2 14.4 %collective-permute-start.20 = (bf16[1024,256]{1,0:T(8,128)(2,1)}, bf16[1024,256]{1,0:T(8,128)(2,1)S(1)}, u32[]{:S(2)}, u32[]{:S(2)}) collective-permute-start(bf16[1024,256]{1,0:T(8,128)(2,1)} %get-tuple-element.115), channel_id=1, source_target_pairs={{0,2},{1,3},{2,4},{3,5},{4,6},{5,7},{6,0},{7,1},{8,10},{9,11},{10,... | collective-permute-start | bytes 1572872 | tf_op jit(solution)/shard_map/ppermute | solution.py:46
  126.3 11.2 %collective-permute-start.21 = (bf16[512,256]{1,0:T(8,128)(2,1)S(1)}, bf16[512,256]{1,0:T(8,128)(2,1)S(1)}, u32[]{:S(2)}, u32[]{:S(2)}) collective-permute-start(bf16[512,256]{1,0:T(8,128)(2,1)S(1)} %get-tuple-element.118), channel_id=1, source_target_pairs={{0,1},{1,17},{2,3},{3,19},{4,5},{5,21},{6,7},{7,23},{8,9},{9,25},{... | collective-permute-start | bytes 786440 | tf_op jit(solution)/shard_map/ppermute | solution.py:46
  128.6 9.8 %collective-permute-start.22 = (bf16[512,256]{1,0:T(8,128)(2,1)S(1)}, bf16[512,256]{1,0:T(8,128)(2,1)S(1)}, u32[]{:S(2)}, u32[]{:S(2)}) collective-permute-start(bf16[512,256]{1,0:T(8,128)(2,1)S(1)} %get-tuple-element.119), channel_id=1, source_target_pairs={{0,9},{1,25},{2,11},{3,27},{4,13},{5,29},{6,15},{7,31},{8,1},{9,17... | collective-permute-start | bytes 786440 | tf_op jit(solution)/shard_map/ppermute | solution.py:46
  128.6 11.6 %collective-permute-start.23 = (bf16[512,256]{1,0:T(8,128)(2,1)S(1)}, bf16[512,256]{1,0:T(8,128)(2,1)S(1)}, u32[]{:S(2)}, u32[]{:S(2)}) collective-permute-start(bf16[512,256]{1,0:T(8,128)(2,1)S(1)} %get-tuple-element.120), channel_id=1, source_target_pairs={{0,17},{1,1},{2,19},{3,3},{4,21},{5,5},{6,23},{7,7},{8,25},{9,9},{... | collective-permute-start | bytes 786440 | tf_op jit(solution)/shard_map/ppermute | solution.py:46
  130.7 15.7 %collective-permute-start.24 = (bf16[512,256]{1,0:T(8,128)(2,1)S(1)}, bf16[512,256]{1,0:T(8,128)(2,1)S(1)}, u32[]{:S(2)}, u32[]{:S(2)}) collective-permute-start(bf16[512,256]{1,0:T(8,128)(2,1)S(1)} %get-tuple-element.121), channel_id=1, source_target_pairs={{0,25},{1,9},{2,27},{3,11},{4,29},{5,13},{6,31},{7,15},{8,17},{9,1... | collective-permute-start | bytes 786440 | tf_op jit(solution)/shard_map/ppermute | solution.py:46
  (23 other events, 97.7 us)

commit v13 on v10

--- a/solution.py
+++ b/solution.py
@@ -285,8 +285,9 @@
     homeward = [pick(total[t], yl ^ yh ^ s) for s in range(2) for t in range(2)]
     shares, homeward = lax.optimization_barrier((shares, homeward))
     projected = narrow(jnp.sum(wide(shares), 0))
-    arrived = [send(v, HOME[s // 2, s % 2]) for s, v in enumerate(homeward)]
-    *arrived, projected = lax.optimization_barrier((*arrived, projected))
+    sent = [send(homeward[n], HOME[n // 2, n % 2]) for n in (2, 0, 3, 1)]
+    *sent, projected = lax.optimization_barrier((*sent, projected))
+    arrived = [sent[n] for n in (1, 3, 0, 2)]
 
     def quarter(q):
         t, s = q // 2, q % 2

time: 149 us -> 146 us (0.980); the launches traced: 149 us -> 143 us
  waiting for transfers between devices: 68.1 us -> 64 us
  starting transfers between devices: 37.7 us -> 35.9 us
    ppermute x25, waiting for transfers between devices: 68.1 us -> 64 us  [send(): return lax.ppermute(value, AXES, pairs)]
    ppermute x25, starting transfers between devices: 32.7 us -> 31 us  [send(): return lax.ppermute(value, AXES, pairs)]
where the time goes in v13:
time: 146 us; the launch traced here: 143 us
  waiting for transfers between devices  64 us (44%)
  starting transfers between devices  35.9 us (25%)
  Pallas kernels  25 us (17%)
  other arithmetic  10.6 us (7%)
  local copies, waits for them, and re-layouts  3.72 us (3%)
  matrix products  2.57 us (2%)
    ppermute x25, waiting for transfers between devices, send(): return lax.ppermute(value, AXES, pairs)  64 us
    ppermute x25, starting transfers between devices, send(): return lax.ppermute(value, AXES, pairs)  31 us
    pallas_call x3, Pallas kernels, block_product(): pl.pallas_call(functools.partial(block_kernel, plan, groups), out_shape=[...  25 us
    all_to_all x1, starting transfers between devices, on_device(): shares = lax.all_to_all(share, 'feat', 0, 0)  4.96 us
    convert_element_type x2, other arithmetic, narrow(): return value.astype(jnp.bfloat16)  4.35 us
  transfers between devices with their start and end apart: 26, of which 15 were waited for; matrix products, arithmetic and copies ran while one was open for 8% of the time, Pallas kernels for 11%

profile of v13, /device:TPU:0, one launch (start us, length us, event | category | flops | bytes accessed | tf_op | source)
XLA Modules:
  0.0 142.7 jit_solution(17616532897814365446)
XLA Ops:
  0.7 1.6 %copy.11 = bf16[512,1024]{1,0:T(8,128)(2,1)S(1)} copy(bf16[512,1024]{0,1:T(8,128)(2,1)} %bitcast.47) | data formatting | bytes 2097152 | tf_op jit(solution)/shard_map/transpose | solution.py:232
  2.5 1.7 %collective-permute-start = (bf16[256,1024]{1,0:T(8,128)(2,1)S(1)}, bf16[256,1024]{1,0:T(8,128)(2,1)S(1)}, u32[]{:S(2)}, u32[]{:S(2)}) collective-permute-start(bf16[256,1024]{1,0:T(8,128)(2,1)S(1)} %get-tuple-element.72), channel_id=1, source_target_pairs={{0,16},{1,17},{2,18},{3,19},{4,20},{5,21},{6,22},{7,23},{8,24},{9,... | collective-permute-start | bytes 1572872 | tf_op jit(solution)/shard_map/ppermute | solution.py:46
  4.2 2.2 %collective-permute-start.1 = (bf16[256,1024]{1,0:T(8,128)(2,1)S(1)}, bf16[256,1024]{1,0:T(8,128)(2,1)S(1)}, u32[]{:S(2)}, u32[]{:S(2)}) collective-permute-start(bf16[256,1024]{1,0:T(8,128)(2,1)S(1)} %get-tuple-element.71), channel_id=1, source_target_pairs={{0,17},{1,16},{2,19},{3,18},{4,21},{5,20},{6,23},{7,22},{8,25},{9,... | collective-permute-start | bytes 1572872 | tf_op jit(solution)/shard_map/ppermute | solution.py:46
  6.4 2.6 %convolution_convert_fusion = bf16[1024,1024]{1,0:T(8,128)(2,1)} fusion(bf16[1024,512]{1,0:T(8,128)(2,1)S(1)} %copy-done.14, bf16[512,1024]{1,0:T(8,128)(2,1)S(1)} %copy-done), kind=kOutput, calls=%fused_computation.1 | convolution fusion | flops 1074790400 | bytes 4194304 | tf_op jit(solution)/shard_map/dot_general | solution.py:236
  9.0 7.8 %collective-permute-done.refs_4_.refs_9_.refs_6_ = bf16[256,1024]{1,0:T(8,128)(2,1)S(1)} collective-permute-done((bf16[256,1024]{1,0:T(8,128)(2,1)S(1)}, bf16[256,1024]{1,0:T(8,128)(2,1)S(1)}, u32[]{:S(2)}, u32[]{:S(2)}) %collective-permute-start) | collective-permute-done | bytes 524320 | tf_op jit(solution)/shard_map/ppermute | solution.py:46
  16.9 2.6 %collective-permute-done.1.refs_5_.refs_10_.refs_7_ = bf16[256,1024]{1,0:T(8,128)(2,1)S(1)} collective-permute-done((bf16[256,1024]{1,0:T(8,128)(2,1)S(1)}, bf16[256,1024]{1,0:T(8,128)(2,1)S(1)}, u32[]{:S(2)}, u32[]{:S(2)}) %collective-permute-start.1) | collective-permute-done | bytes 524320 | tf_op jit(solution)/shard_map/ppermute | solution.py:46
  19.5 2.3 %collective-permute-start.4 = (bf16[256,1024]{1,0:T(8,128)(2,1)S(1)}, bf16[256,1024]{1,0:T(8,128)(2,1)S(1)}, u32[]{:S(2)}, u32[]{:S(2)}) collective-permute-start(bf16[256,1024]{1,0:T(8,128)(2,1)S(1)} %get-tuple-element.72), channel_id=1, source_target_pairs={{0,17},{1,16},{2,19},{3,18},{4,21},{5,20},{6,23},{7,22},{8,25},{9,... | collective-permute-start | bytes 1572872 | tf_op jit(solution)/shard_map/ppermute | solution.py:46
  21.8 1.5 %collective-permute-start.11 = (bf16[256,1024]{1,0:T(8,128)(2,1)S(1)}, bf16[256,1024]{1,0:T(8,128)(2,1)}, u32[]{:S(2)}, u32[]{:S(2)}) collective-permute-start(bf16[256,1024]{1,0:T(8,128)(2,1)S(1)} %collective-permute-done.refs_4_.refs_9_.refs_6_), channel_id=1, source_target_pairs={{0,32},{1,33},{2,34},{3,35},{4,36},{5,37},{6,38},{7,39},{8,40},{9,... | collective-permute-start | bytes 1572872 | tf_op jit(solution)/shard_map/ppermute | solution.py:46
  23.3 1.7 %collective-permute-start.12 = (bf16[256,1024]{1,0:T(8,128)(2,1)S(1)}, bf16[256,1024]{1,0:T(8,128)(2,1)}, u32[]{:S(2)}, u32[]{:S(2)}) collective-permute-start(bf16[256,1024]{1,0:T(8,128)(2,1)S(1)} %collective-permute-done.1.refs_5_.refs_10_.refs_7_), channel_id=1, source_target_pairs={{0,96},{1,97},{2,98},{3,99},{4,100},{5,101},{6,102},{7,103},{8,104... | collective-permute-start | bytes 1572872 | tf_op jit(solution)/shard_map/ppermute | solution.py:46
  25.1 7.5 %collective-permute-done.3.refs_6_.refs_11_ = bf16[256,1024]{1,0:T(8,128)(2,1)S(1)} collective-permute-done((bf16[256,1024]{1,0:T(8,128)(2,1)S(1)}, bf16[256,1024]{1,0:T(8,128)(2,1)S(1)}, u32[]{:S(2)}, u32[]{:S(2)}) %collective-permute-start.3) | collective-permute-done | bytes 524320 | tf_op jit(solution)/shard_map/ppermute | solution.py:46
  34.0 2.0 %collective-permute-done.11.refs_10_.refs_17_.refs_12_ = bf16[256,1024]{1,0:T(8,128)(2,1)} collective-permute-done((bf16[256,1024]{1,0:T(8,128)(2,1)S(1)}, bf16[256,1024]{1,0:T(8,128)(2,1)}, u32[]{:S(2)}, u32[]{:S(2)}) %collective-permute-start.11) | collective-permute-done | bytes 524320 | tf_op jit(solution)/shard_map/ppermute | solution.py:46
  39.6 1.7 %collective-permute-start.14 = (bf16[256,1024]{1,0:T(8,128)(2,1)S(1)}, bf16[256,1024]{1,0:T(8,128)(2,1)S(1)}, u32[]{:S(2)}, u32[]{:S(2)}) collective-permute-start(bf16[256,1024]{1,0:T(8,128)(2,1)S(1)} %collective-permute-done.refs_4_.refs_9_.refs_6_), channel_id=1, source_target_pairs={{0,96},{1,97},{2,98},{3,99},{4,100},{5,101},{6,102},{7,103},{8,104... | collective-permute-start | bytes 1572872 | tf_op jit(solution)/shard_map/ppermute | solution.py:46
  42.4 9.1 %collective-permute-done.13.refs_11_.refs_18_.refs_13_ = bf16[256,1024]{1,0:T(8,128)(2,1)S(1)} collective-permute-done((bf16[256,1024]{1,0:T(8,128)(2,1)S(1)}, bf16[256,1024]{1,0:T(8,128)(2,1)S(1)}, u32[]{:S(2)}, u32[]{:S(2)}) %collective-permute-start.13) | collective-permute-done | bytes 524320 | tf_op jit(solution)/shard_map/ppermute | solution.py:46
  51.5 1.5 %collective-permute-done.14.refs_8_.refs_13_ = bf16[256,1024]{1,0:T(8,128)(2,1)S(1)} collective-permute-done((bf16[256,1024]{1,0:T(8,128)(2,1)S(1)}, bf16[256,1024]{1,0:T(8,128)(2,1)S(1)}, u32[]{:S(2)}, u32[]{:S(2)}) %collective-permute-start.14) | collective-permute-done | bytes 524320 | tf_op jit(solution)/shard_map/ppermute | solution.py:46
  54.3 2.0 %collective-permute-start.16 = (bf16[256,1024]{1,0:T(8,128)(2,1)}, bf16[256,1024]{1,0:T(8,128)(2,1)S(1)}, u32[]{:S(2)}, u32[]{:S(2)}) collective-permute-start(bf16[256,1024]{1,0:T(8,128)(2,1)} %collective-permute-done.12.refs_9_.refs_14_), channel_id=1, source_target_pairs={{0,96},{1,97},{2,98},{3,99},{4,100},{5,101},{6,102},{7,103},{8,104... | collective-permute-start | bytes 1572872 | tf_op jit(solution)/shard_map/ppermute | solution.py:46
  58.0 9.0 %shard_map.50 = (bf16[2,1024,256]{2,1,0:T(8,128)(2,1)}, bf16[2,1024,256]{2,1,0:T(8,128)(2,1)}, bf16[2,1024,256]{2,1,0:T(8,128)(2,1)}, bf16[2,1024,256]{2,1,0:T(8,128)(2,1)}) custom-call(s32[2]{0:T(128)} %pad_add_fusion.refs_0_, bf16[2,256,1024]{2,1,0:T(8,128)(2,1)} %bitcast.39, bf16[256,1024]{1,0:T(8,128)(2,1)} %collective-permute-done.5.refs_2_.refs_7_, ...), custom_call_target="tpu_custom_call" | custom-call | flops 65536 | bytes 262144 | tf_op jit(solution)/shard_map/pallas_call | solution.py:201
  68.4 8.8 %shard_map.51 = (bf16[2,1024,256]{2,1,0:T(8,128)(2,1)}, bf16[2,1024,256]{2,1,0:T(8,128)(2,1)}, bf16[2,1024,256]{2,1,0:T(8,128)(2,1)}, bf16[2,1024,256]{2,1,0:T(8,128)(2,1)}) custom-call(s32[2]{0:T(128)} %pad_add_fusion.refs_0_, bf16[2,256,1024]{2,1,0:T(8,128)(2,1)} %copy-done.9, ...), custom_call_target="tpu_custom_call", output_to_operand_aliasing={{0}: (19, {}), {1}: (20, {}), {2}: (21, {}), {3}: (22, {})} | custom-call | flops 65536 | bytes 262144 | tf_op jit(solution)/shard_map/pallas_call | solution.py:201
  77.2 3.9 %collective-permute-start.17 = (bf16[2,1024,256]{2,1,0:T(8,128)(2,1)}, bf16[2,1024,256]{2,1,0:T(8,128)(2,1)S(1)}, u32[]{:S(2)}, u32[]{:S(2)}) collective-permute-start(bf16[2,1024,256]{2,1,0:T(8,128)(2,1)} %get-tuple-element.109), channel_id=1, source_target_pairs={{0,6},{1,7},{2,0},{3,1},{4,2},{5,3},{6,4},{7,5},{8,14},{9,15},{10,... | collective-permute-start | bytes 3145736 | tf_op jit(solution)/shard_map/ppermute | solution.py:46
  81.2 5.0 %all-to-all-start = ((bf16[16,64,1024]{2,1,0:T(8,128)(2,1)}), bf16[16,64,1024]{2,1,0:T(8,128)(2,1)}, u32[]{:S(2)}, u32[]{:S(2)}) async-start(bf16[16,64,1024]{2,1,0:T(8,128)(2,1)} %bitcast), calls=%async_computation | async-start | bytes 4194304 | tf_op jit(solution)/shard_map/all_to_all | solution.py:273
  86.2 7.1 %shard_map.52 = (bf16[2,1024,256]{2,1,0:T(8,128)(2,1)}, bf16[2,1024,256]{2,1,0:T(8,128)(2,1)}) custom-call(s32[2]{0:T(128)} %pad_add_fusion.refs_0_, bf16[2,256,1024]{2,1,0:T(8,128)(2,1)} %copy-done.9, bf16[256,1024]{1,0:T(8,128)(2,1)} %copy-done.13, ...), custom_call_target="tpu_custom_call", output_to_operand_aliasing={{0}: (14, {}), {1}: (15, {})} | custom-call | flops 65536 | bytes 262144 | tf_op jit(solution)/shard_map/pallas_call | solution.py:201
  93.3 10.8 %collective-permute-done.17 = bf16[2,1024,256]{2,1,0:T(8,128)(2,1)S(1)} collective-permute-done((bf16[2,1024,256]{2,1,0:T(8,128)(2,1)}, bf16[2,1024,256]{2,1,0:T(8,128)(2,1)S(1)}, u32[]{:S(2)}, u32[]{:S(2)}) %collective-permute-start.17) | collective-permute-done | bytes 1048608 | tf_op jit(solution)/shard_map/ppermute | solution.py:46
  104.2 3.4 %collective-permute-done.18 = bf16[2,1024,256]{2,1,0:T(8,128)(2,1)} collective-permute-done((bf16[2,1024,256]{2,1,0:T(8,128)(2,1)}, bf16[2,1024,256]{2,1,0:T(8,128)(2,1)}, u32[]{:S(2)}, u32[]{:S(2)}) %collective-permute-start.18) | collective-permute-done | bytes 1048608 | tf_op jit(solution)/shard_map/ppermute | solution.py:46
  107.6 2.6 %fusion.3 = (bf16[1024,256]{1,0:T(8,128)(2,1)}, bf16[1024,256]{1,0:T(8,128)(2,1)}) fusion(bf16[2,1024,256]{2,1,0:T(8,128)(2,1)} %get-tuple-element.113, bf16[2,1024,256]{2,1,0:T(8,128)(2,1)} %collective-permute-done.18, bf16[2,1024,256]{2,1,0:T(8,128)(2,1)S(1)} %collective-permute-done.17), kind=kLoop, calls=%fused_computation.11 | loop fusion | flops 2097152 | bytes 3145728 | tf_op jit(solution)/shard_map/convert_element_type | solution.py:58
  110.3 1.8 %collective-permute-start.20 = (bf16[1024,256]{1,0:T(8,128)(2,1)}, bf16[1024,256]{1,0:T(8,128)(2,1)}, u32[]{:S(2)}, u32[]{:S(2)}) collective-permute-start(bf16[1024,256]{1,0:T(8,128)(2,1)} %get-tuple-element.115), channel_id=1, source_target_pairs={{0,2},{1,3},{2,4},{3,5},{4,6},{5,7},{6,0},{7,1},{8,10},{9,11},{10,... | collective-permute-start | bytes 1572872 | tf_op jit(solution)/shard_map/ppermute | solution.py:46
  112.2 11.0 %collective-permute-done.19 = bf16[1024,256]{1,0:T(8,128)(2,1)} collective-permute-done((bf16[1024,256]{1,0:T(8,128)(2,1)}, bf16[1024,256]{1,0:T(8,128)(2,1)}, u32[]{:S(2)}, u32[]{:S(2)}) %collective-permute-start.19) | collective-permute-done | bytes 524320 | tf_op jit(solution)/shard_map/ppermute | solution.py:46
  123.2 1.5 %collective-permute-done.20 = bf16[1024,256]{1,0:T(8,128)(2,1)} collective-permute-done((bf16[1024,256]{1,0:T(8,128)(2,1)}, bf16[1024,256]{1,0:T(8,128)(2,1)}, u32[]{:S(2)}, u32[]{:S(2)}) %collective-permute-start.20) | collective-permute-done | bytes 524320 | tf_op jit(solution)/shard_map/ppermute | solution.py:46
  124.8 1.8 %fusion = (bf16[1024,256]{1,0:T(8,128)(2,1)S(1)}, bf16[1024,256]{1,0:T(8,128)(2,1)S(1)}) fusion(bf16[1024,256]{1,0:T(8,128)(2,1)} %collective-permute-done.20, bf16[2,1024,256]{2,1,0:T(8,128)(2,1)S(1)} %collective-permute-done.17, bf16[2,1024,256]{2,1,0:T(8,128)(2,1)S(1)} %copy-done.2, bf16[1024,256]{1,0:T(8,128)(2,1)} %collective-permute-done.19, ...), kind=kLoop, calls=%fused_computation.5 | loop fusion | flops 3145728 | bytes 4194304 | tf_op jit(solution)/shard_map/convert_element_type | solution.py:58
  126.6 4.2 %collective-permute-start.21 = (bf16[512,256]{1,0:T(8,128)(2,1)S(1)}, bf16[512,256]{1,0:T(8,128)(2,1)S(1)}, u32[]{:S(2)}, u32[]{:S(2)}) collective-permute-start(bf16[512,256]{1,0:T(8,128)(2,1)S(1)} %get-tuple-element.118), channel_id=1, source_target_pairs={{0,17},{1,1},{2,19},{3,3},{4,21},{5,5},{6,23},{7,7},{8,25},{9,9},{... | collective-permute-start | bytes 786440 | tf_op jit(solution)/shard_map/ppermute | solution.py:46
  131.0 2.4 %collective-permute-start.24 = (bf16[512,256]{1,0:T(8,128)(2,1)S(1)}, bf16[512,256]{1,0:T(8,128)(2,1)S(1)}, u32[]{:S(2)}, u32[]{:S(2)}) collective-permute-start(bf16[512,256]{1,0:T(8,128)(2,1)S(1)} %get-tuple-element.121), channel_id=1, source_target_pairs={{0,9},{1,25},{2,11},{3,27},{4,13},{5,29},{6,15},{7,31},{8,1},{9,17... | collective-permute-start | bytes 786440 | tf_op jit(solution)/shard_map/ppermute | solution.py:46
  133.4 2.7 %reduce_sum.12 = bf16[64,1024]{1,0:T(8,128)(2,1)} reduce(bf16[16,64,1024]{2,1,0:T(8,128)(2,1)} %all-to-all-done, bf16[]{:T(256)} %constant.91.clone.1), dimensions={0}, to_apply=%region_0.1 | reduce | flops 983040 | bytes 2228226 | tf_op jit(solution)/shard_map/reduce_sum | solution.py:287
  137.2 2.7 %collective-permute-done.22 = bf16[512,256]{1,0:T(8,128)(2,1)S(1)} collective-permute-done((bf16[512,256]{1,0:T(8,128)(2,1)S(1)}, bf16[512,256]{1,0:T(8,128)(2,1)S(1)}, u32[]{:S(2)}, u32[]{:S(2)}) %collective-permute-start.22) | collective-permute-done | bytes 262176 | tf_op jit(solution)/shard_map/ppermute | solution.py:46
  141.1 1.7 %multiply_add_fusion = f32[512,1024]{1,0:T(8,128)} fusion(f32[512,1024]{1,0:T(8,128)S(1)} %copy-done.11, bf16[256,256]{1,0:T(8,128)(2,1)S(1)} %get-tuple-element.145, bf16[256,256]{1,0:T(8,128)(2,1)S(1)} %get-tuple-element.144, bf16[512,256]{1,0:T(8,128)(2,1)S(1)} %get-tuple-element.130, bf16[256,256]{1,0:T(8,128)(2,1)S(1)} %get-tuple-element.143, ...), kind=kLoop, calls=%fused_computation | loop fusion | flops 7864320 | bytes 5242880 | tf_op jit(solution)/shard_map/add | solution.py:302
  (67 shorter events, 13.2 us)
Async XLA Ops:
  2.4 17.0 %collective-permute-start.2 = (bf16[2,256,1024]{2,1,0:T(8,128)(2,1)S(1)}, bf16[2,256,1024]{2,1,0:T(8,128)(2,1)S(1)}, u32[]{:S(2)}, u32[]{:S(2)}) collective-permute-start(bf16[2,256,1024]{2,1,0:T(8,128)(2,1)S(1)} %bitcast.38), channel_id=1, source_target_pairs={{0,8},{1,9},{2,10},{3,11},{4,12},{5,13},{6,14},{7,15},{8,0},{9,1},... | collective-permute-start | bytes 3145736 | tf_op jit(solution)/shard_map/ppermute | solution.py:46
  2.5 14.3 %collective-permute-start = (bf16[256,1024]{1,0:T(8,128)(2,1)S(1)}, bf16[256,1024]{1,0:T(8,128)(2,1)S(1)}, u32[]{:S(2)}, u32[]{:S(2)}) collective-permute-start(bf16[256,1024]{1,0:T(8,128)(2,1)S(1)} %get-tuple-element.72), channel_id=1, source_target_pairs={{0,16},{1,17},{2,18},{3,19},{4,20},{5,21},{6,22},{7,23},{8,24},{9,... | collective-permute-start | bytes 1572872 | tf_op jit(solution)/shard_map/ppermute | solution.py:46
  4.2 15.2 %collective-permute-start.1 = (bf16[256,1024]{1,0:T(8,128)(2,1)S(1)}, bf16[256,1024]{1,0:T(8,128)(2,1)S(1)}, u32[]{:S(2)}, u32[]{:S(2)}) collective-permute-start(bf16[256,1024]{1,0:T(8,128)(2,1)S(1)} %get-tuple-element.71), channel_id=1, source_target_pairs={{0,17},{1,16},{2,19},{3,18},{4,21},{5,20},{6,23},{7,22},{8,25},{9,... | collective-permute-start | bytes 1572872 | tf_op jit(solution)/shard_map/ppermute | solution.py:46
  16.9 25.6 %copy-start.3 = (bf16[256,1024]{1,0:T(8,128)(2,1)}, bf16[256,1024]{1,0:T(8,128)(2,1)S(1)}, u32[]{:S(2)}) copy-start(bf16[256,1024]{1,0:T(8,128)(2,1)S(1)} %collective-permute-done.refs_4_.refs_9_.refs_6_) | copy-start | bytes 1572868
  19.4 23.0 %copy-start.4 = (bf16[256,1024]{1,0:T(8,128)(2,1)}, bf16[256,1024]{1,0:T(8,128)(2,1)S(1)}, u32[]{:S(2)}) copy-start(bf16[256,1024]{1,0:T(8,128)(2,1)S(1)} %collective-permute-done.1.refs_5_.refs_10_.refs_7_) | copy-start | bytes 1572868
  19.4 23.0 %copy-start.9 = (bf16[2,256,1024]{2,1,0:T(8,128)(2,1)}, bf16[2,256,1024]{2,1,0:T(8,128)(2,1)S(1)}, u32[]{:S(2)}) copy-start(bf16[2,256,1024]{2,1,0:T(8,128)(2,1)S(1)} %collective-permute-done.2.refs_1_) | copy-start | bytes 3145732
  19.4 13.2 %collective-permute-start.3 = (bf16[256,1024]{1,0:T(8,128)(2,1)S(1)}, bf16[256,1024]{1,0:T(8,128)(2,1)S(1)}, u32[]{:S(2)}, u32[]{:S(2)}) collective-permute-start(bf16[256,1024]{1,0:T(8,128)(2,1)S(1)} %get-tuple-element.71), channel_id=1, source_target_pairs={{0,16},{1,17},{2,18},{3,19},{4,20},{5,21},{6,22},{7,23},{8,24},{9,... | collective-permute-start | bytes 1572872 | tf_op jit(solution)/shard_map/ppermute | solution.py:46
  19.5 14.4 %collective-permute-start.4 = (bf16[256,1024]{1,0:T(8,128)(2,1)S(1)}, bf16[256,1024]{1,0:T(8,128)(2,1)S(1)}, u32[]{:S(2)}, u32[]{:S(2)}) collective-permute-start(bf16[256,1024]{1,0:T(8,128)(2,1)S(1)} %get-tuple-element.72), channel_id=1, source_target_pairs={{0,17},{1,16},{2,19},{3,18},{4,21},{5,20},{6,23},{7,22},{8,25},{9,... | collective-permute-start | bytes 1572872 | tf_op jit(solution)/shard_map/ppermute | solution.py:46
  21.8 14.2 %collective-permute-start.11 = (bf16[256,1024]{1,0:T(8,128)(2,1)S(1)}, bf16[256,1024]{1,0:T(8,128)(2,1)}, u32[]{:S(2)}, u32[]{:S(2)}) collective-permute-start(bf16[256,1024]{1,0:T(8,128)(2,1)S(1)} %collective-permute-done.refs_4_.refs_9_.refs_6_), channel_id=1, source_target_pairs={{0,32},{1,33},{2,34},{3,35},{4,36},{5,37},{6,38},{7,39},{8,40},{9,... | collective-permute-start | bytes 1572872 | tf_op jit(solution)/shard_map/ppermute | solution.py:46
  23.3 12.7 %collective-permute-start.12 = (bf16[256,1024]{1,0:T(8,128)(2,1)S(1)}, bf16[256,1024]{1,0:T(8,128)(2,1)}, u32[]{:S(2)}, u32[]{:S(2)}) collective-permute-start(bf16[256,1024]{1,0:T(8,128)(2,1)S(1)} %collective-permute-done.1.refs_5_.refs_10_.refs_7_), channel_id=1, source_target_pairs={{0,96},{1,97},{2,98},{3,99},{4,100},{5,101},{6,102},{7,103},{8,104... | collective-permute-start | bytes 1572872 | tf_op jit(solution)/shard_map/ppermute | solution.py:46
  32.7 25.3 %copy-start.5 = (bf16[256,1024]{1,0:T(8,128)(2,1)}, bf16[256,1024]{1,0:T(8,128)(2,1)S(1)}, u32[]{:S(2)}) copy-start(bf16[256,1024]{1,0:T(8,128)(2,1)S(1)} %collective-permute-done.3.refs_6_.refs_11_) | copy-start | bytes 1572868
  34.0 24.0 %copy-start.6 = (bf16[256,1024]{1,0:T(8,128)(2,1)}, bf16[256,1024]{1,0:T(8,128)(2,1)S(1)}, u32[]{:S(2)}) copy-start(bf16[256,1024]{1,0:T(8,128)(2,1)S(1)} %collective-permute-done.4.refs_7_.refs_12_) | copy-start | bytes 1572868
  36.0 20.3 %collective-permute-start.7 = (bf16[2,256,1024]{2,1,0:T(8,128)(2,1)S(1)}, bf16[2,256,1024]{2,1,0:T(8,128)(2,1)S(1)}, u32[]{:S(2)}, u32[]{:S(2)}) collective-permute-start(bf16[2,256,1024]{2,1,0:T(8,128)(2,1)S(1)} %pad_maximum_fusion), channel_id=1, source_target_pairs={{0,8},{1,9},{2,10},{3,11},{4,12},{5,13},{6,14},{7,15},{8,0},{9,1},... | collective-permute-start | bytes 3145736 | tf_op jit(solution)/shard_map/ppermute | solution.py:46
  36.0 15.5 %collective-permute-start.13 = (bf16[256,1024]{1,0:T(8,128)(2,1)S(1)}, bf16[256,1024]{1,0:T(8,128)(2,1)S(1)}, u32[]{:S(2)}, u32[]{:S(2)}) collective-permute-start(bf16[256,1024]{1,0:T(8,128)(2,1)S(1)} %collective-permute-done.1.refs_5_.refs_10_.refs_7_), channel_id=1, source_target_pairs={{0,32},{1,33},{2,34},{3,35},{4,36},{5,37},{6,38},{7,39},{8,40},{9,... | collective-permute-start | bytes 1572872 | tf_op jit(solution)/shard_map/ppermute | solution.py:46
  37.5 16.8 %collective-permute-start.5 = (bf16[256,1024]{1,0:T(8,128)(2,1)S(1)}, bf16[256,1024]{1,0:T(8,128)(2,1)}, u32[]{:S(2)}, u32[]{:S(2)}) collective-permute-start(bf16[256,1024]{1,0:T(8,128)(2,1)S(1)} %collective-permute-done.1.refs_5_.refs_10_.refs_7_), channel_id=1, source_target_pairs={{0,16},{1,17},{2,18},{3,19},{4,20},{5,21},{6,22},{7,23},{8,24},{9,... | collective-permute-start | bytes 1572872 | tf_op jit(solution)/shard_map/ppermute | solution.py:46
  38.5 17.8 %collective-permute-start.6 = (bf16[256,1024]{1,0:T(8,128)(2,1)S(1)}, bf16[256,1024]{1,0:T(8,128)(2,1)}, u32[]{:S(2)}, u32[]{:S(2)}) collective-permute-start(bf16[256,1024]{1,0:T(8,128)(2,1)S(1)} %collective-permute-done.refs_4_.refs_9_.refs_6_), channel_id=1, source_target_pairs={{0,17},{1,16},{2,19},{3,18},{4,21},{5,20},{6,23},{7,22},{8,25},{9,... | collective-permute-start | bytes 1572872 | tf_op jit(solution)/shard_map/ppermute | solution.py:46
  39.6 13.5 %collective-permute-start.14 = (bf16[256,1024]{1,0:T(8,128)(2,1)S(1)}, bf16[256,1024]{1,0:T(8,128)(2,1)S(1)}, u32[]{:S(2)}, u32[]{:S(2)}) collective-permute-start(bf16[256,1024]{1,0:T(8,128)(2,1)S(1)} %collective-permute-done.refs_4_.refs_9_.refs_6_), channel_id=1, source_target_pairs={{0,96},{1,97},{2,98},{3,99},{4,100},{5,101},{6,102},{7,103},{8,104... | collective-permute-start | bytes 1572872 | tf_op jit(solution)/shard_map/ppermute | solution.py:46
  51.5 15.9 %collective-permute-start.10 = (bf16[2,256,1024]{2,1,0:T(8,128)(2,1)}, bf16[2,256,1024]{2,1,0:T(8,128)(2,1)}, u32[]{:S(2)}, u32[]{:S(2)}) collective-permute-start(bf16[2,256,1024]{2,1,0:T(8,128)(2,1)} %pad_maximum_fusion.1), channel_id=1, source_target_pairs={{0,8},{1,9},{2,10},{3,11},{4,12},{5,13},{6,14},{7,15},{8,0},{9,1},... | collective-permute-start | bytes 3145736 | tf_op jit(solution)/shard_map/ppermute | solution.py:46
  53.1 14.3 %collective-permute-start.15 = (bf16[256,1024]{1,0:T(8,128)(2,1)}, bf16[256,1024]{1,0:T(8,128)(2,1)}, u32[]{:S(2)}, u32[]{:S(2)}) collective-permute-start(bf16[256,1024]{1,0:T(8,128)(2,1)} %collective-permute-done.11.refs_10_.refs_17_.refs_12_), channel_id=1, source_target_pairs={{0,32},{1,33},{2,34},{3,35},{4,36},{5,37},{6,38},{7,39},{8,40},{9,... | collective-permute-start | bytes 1572872 | tf_op jit(solution)/shard_map/ppermute | solution.py:46
  54.3 13.1 %collective-permute-start.16 = (bf16[256,1024]{1,0:T(8,128)(2,1)}, bf16[256,1024]{1,0:T(8,128)(2,1)S(1)}, u32[]{:S(2)}, u32[]{:S(2)}) collective-permute-start(bf16[256,1024]{1,0:T(8,128)(2,1)} %collective-permute-done.12.refs_9_.refs_14_), channel_id=1, source_target_pairs={{0,96},{1,97},{2,98},{3,99},{4,100},{5,101},{6,102},{7,103},{8,104... | collective-permute-start | bytes 1572872 | tf_op jit(solution)/shard_map/ppermute | solution.py:46
  56.4 11.1 %collective-permute-start.8 = (bf16[256,1024]{1,0:T(8,128)(2,1)}, bf16[256,1024]{1,0:T(8,128)(2,1)S(1)}, u32[]{:S(2)}, u32[]{:S(2)}) collective-permute-start(bf16[256,1024]{1,0:T(8,128)(2,1)} %collective-permute-done.5.refs_2_.refs_7_), channel_id=1, source_target_pairs={{0,8},{1,9},{2,10},{3,11},{4,12},{5,13},{6,14},{7,15},{8,0},{9,1},... | collective-permute-start | bytes 1572872 | tf_op jit(solution)/shard_map/ppermute | solution.py:46
  57.3 10.1 %collective-permute-start.9 = (bf16[256,1024]{1,0:T(8,128)(2,1)}, bf16[256,1024]{1,0:T(8,128)(2,1)}, u32[]{:S(2)}, u32[]{:S(2)}) collective-permute-start(bf16[256,1024]{1,0:T(8,128)(2,1)} %collective-permute-done.6.refs_3_.refs_8_), channel_id=1, source_target_pairs={{0,8},{1,9},{2,10},{3,11},{4,12},{5,13},{6,14},{7,15},{8,0},{9,1},... | collective-permute-start | bytes 1572872 | tf_op jit(solution)/shard_map/ppermute | solution.py:46
  77.2 26.9 %collective-permute-start.17 = (bf16[2,1024,256]{2,1,0:T(8,128)(2,1)}, bf16[2,1024,256]{2,1,0:T(8,128)(2,1)S(1)}, u32[]{:S(2)}, u32[]{:S(2)}) collective-permute-start(bf16[2,1024,256]{2,1,0:T(8,128)(2,1)} %get-tuple-element.109), channel_id=1, source_target_pairs={{0,6},{1,7},{2,0},{3,1},{4,2},{5,3},{6,4},{7,5},{8,14},{9,15},{10,... | collective-permute-start | bytes 3145736 | tf_op jit(solution)/shard_map/ppermute | solution.py:46
  81.2 26.4 %collective-permute-start.18 = (bf16[2,1024,256]{2,1,0:T(8,128)(2,1)}, bf16[2,1024,256]{2,1,0:T(8,128)(2,1)}, u32[]{:S(2)}, u32[]{:S(2)}) collective-permute-start(bf16[2,1024,256]{2,1,0:T(8,128)(2,1)} %get-tuple-element.110), channel_id=1, source_target_pairs={{0,2},{1,3},{2,4},{3,5},{4,6},{5,7},{6,0},{7,1},{8,10},{9,11},{10,... | collective-permute-start | bytes 3145736 | tf_op jit(solution)/shard_map/ppermute | solution.py:46
  81.2 45.4 %all-to-all-start = ((bf16[16,64,1024]{2,1,0:T(8,128)(2,1)}), bf16[16,64,1024]{2,1,0:T(8,128)(2,1)}, u32[]{:S(2)}, u32[]{:S(2)}) async-start(bf16[16,64,1024]{2,1,0:T(8,128)(2,1)} %bitcast), calls=%async_computation | async-start | bytes 4194304 | tf_op jit(solution)/shard_map/all_to_all | solution.py:273
  93.3 31.5 %copy-start.2 = (bf16[2,1024,256]{2,1,0:T(8,128)(2,1)S(1)}, bf16[2,1024,256]{2,1,0:T(8,128)(2,1)}, u32[]{:S(2)}) copy-start(bf16[2,1024,256]{2,1,0:T(8,128)(2,1)} %get-tuple-element.106) | copy-start | bytes 3145732
  110.2 13.1 %collective-permute-start.19 = (bf16[1024,256]{1,0:T(8,128)(2,1)}, bf16[1024,256]{1,0:T(8,128)(2,1)}, u32[]{:S(2)}, u32[]{:S(2)}) collective-permute-start(bf16[1024,256]{1,0:T(8,128)(2,1)} %get-tuple-element.114), channel_id=1, source_target_pairs={{0,6},{1,7},{2,0},{3,1},{4,2},{5,3},{6,4},{7,5},{8,14},{9,15},{10,... | collective-permute-start | bytes 1572872 | tf_op jit(solution)/shard_map/ppermute | solution.py:46
  110.3 14.4 %collective-permute-start.20 = (bf16[1024,256]{1,0:T(8,128)(2,1)}, bf16[1024,256]{1,0:T(8,128)(2,1)}, u32[]{:S(2)}, u32[]{:S(2)}) collective-permute-start(bf16[1024,256]{1,0:T(8,128)(2,1)} %get-tuple-element.115), channel_id=1, source_target_pairs={{0,2},{1,3},{2,4},{3,5},{4,6},{5,7},{6,0},{7,1},{8,10},{9,11},{10,... | collective-permute-start | bytes 1572872 | tf_op jit(solution)/shard_map/ppermute | solution.py:46
  126.6 10.6 %collective-permute-start.21 = (bf16[512,256]{1,0:T(8,128)(2,1)S(1)}, bf16[512,256]{1,0:T(8,128)(2,1)S(1)}, u32[]{:S(2)}, u32[]{:S(2)}) collective-permute-start(bf16[512,256]{1,0:T(8,128)(2,1)S(1)} %get-tuple-element.118), channel_id=1, source_target_pairs={{0,17},{1,1},{2,19},{3,3},{4,21},{5,5},{6,23},{7,7},{8,25},{9,9},{... | collective-permute-start | bytes 786440 | tf_op jit(solution)/shard_map/ppermute | solution.py:46
  130.8 9.1 %collective-permute-start.22 = (bf16[512,256]{1,0:T(8,128)(2,1)S(1)}, bf16[512,256]{1,0:T(8,128)(2,1)S(1)}, u32[]{:S(2)}, u32[]{:S(2)}) collective-permute-start(bf16[512,256]{1,0:T(8,128)(2,1)S(1)} %get-tuple-element.119), channel_id=1, source_target_pairs={{0,1},{1,17},{2,3},{3,19},{4,5},{5,21},{6,7},{7,23},{8,9},{9,25},{... | collective-permute-start | bytes 786440 | tf_op jit(solution)/shard_map/ppermute | solution.py:46
  130.9 10.0 %collective-permute-start.23 = (bf16[512,256]{1,0:T(8,128)(2,1)S(1)}, bf16[512,256]{1,0:T(8,128)(2,1)S(1)}, u32[]{:S(2)}, u32[]{:S(2)}) collective-permute-start(bf16[512,256]{1,0:T(8,128)(2,1)S(1)} %get-tuple-element.120), channel_id=1, source_target_pairs={{0,25},{1,9},{2,27},{3,11},{4,29},{5,13},{6,31},{7,15},{8,17},{9,1... | collective-permute-start | bytes 786440 | tf_op jit(solution)/shard_map/ppermute | solution.py:46
  131.0 9.9 %collective-permute-start.24 = (bf16[512,256]{1,0:T(8,128)(2,1)S(1)}, bf16[512,256]{1,0:T(8,128)(2,1)S(1)}, u32[]{:S(2)}, u32[]{:S(2)}) collective-permute-start(bf16[512,256]{1,0:T(8,128)(2,1)S(1)} %get-tuple-element.121), channel_id=1, source_target_pairs={{0,9},{1,25},{2,11},{3,27},{4,13},{5,29},{6,15},{7,31},{8,1},{9,17... | collective-permute-start | bytes 786440 | tf_op jit(solution)/shard_map/ppermute | solution.py:46
  (9 other events, 34.1 us)

commit v14 on v13

--- a/solution.py
+++ b/solution.py
@@ -285,9 +285,9 @@
     homeward = [pick(total[t], yl ^ yh ^ s) for s in range(2) for t in range(2)]
     shares, homeward = lax.optimization_barrier((shares, homeward))
     projected = narrow(jnp.sum(wide(shares), 0))
-    sent = [send(homeward[n], HOME[n // 2, n % 2]) for n in (2, 0, 3, 1)]
+    sent = [send(homeward[n], HOME[n // 2, n % 2]) for n in (2, 3, 0, 1)]
     *sent, projected = lax.optimization_barrier((*sent, projected))
-    arrived = [sent[n] for n in (1, 3, 0, 2)]
+    arrived = [sent[n] for n in (2, 3, 0, 1)]
 
     def quarter(q):
         t, s = q // 2, q % 2

time: 146 us -> 149 us (1.021); the launches traced: 143 us -> 148 us
  waiting for transfers between devices: 64 us -> 67.2 us
  starting transfers between devices: 35.9 us -> 37.6 us
    ppermute x25, waiting for transfers between devices: 64 us -> 67.2 us  [send(): return lax.ppermute(value, AXES, pairs)]
    ppermute x25, starting transfers between devices: 31 us -> 32.6 us  [send(): return lax.ppermute(value, AXES, pairs)]
  transfers between devices with their start and end apart: 26 -> 26, of which waited for: 15 -> 14; matrix products, arithmetic and copies ran while one was open for 8% -> 8% of each run, Pallas kernels for 11% -> 11%
where the time goes in v14:
time: 149 us; the launch traced here: 148 us
  waiting for transfers between devices  67.2 us (45%)
  starting transfers between devices  37.6 us (25%)
  Pallas kernels  25 us (17%)
  other arithmetic  10.6 us (7%)
  local copies, waits for them, and re-layouts  3.72 us (2%)
  matrix products  2.57 us (2%)
    ppermute x25, waiting for transfers between devices, send(): return lax.ppermute(value, AXES, pairs)  67.2 us
    ppermute x25, starting transfers between devices, send(): return lax.ppermute(value, AXES, pairs)  32.6 us
    pallas_call x3, Pallas kernels, block_product(): pl.pallas_call(functools.partial(block_kernel, plan, groups), out_shape=[...  25 us
    all_to_all x1, starting transfers between devices, on_device(): shares = lax.all_to_all(share, 'feat', 0, 0)  4.96 us
    convert_element_type x2, other arithmetic, narrow(): return value.astype(jnp.bfloat16)  4.35 us
  transfers between devices with their start and end apart: 26, of which 14 were waited for; matrix products, arithmetic and copies ran while one was open for 8% of the time, Pallas kernels for 11%

profile of v14, /device:TPU:0, one launch (start us, length us, event | category | flops | bytes accessed | tf_op | source)
XLA Modules:
  0.0 147.6 jit_solution(16478305778834188656)
XLA Ops:
  0.7 1.6 %copy.11 = bf16[512,1024]{1,0:T(8,128)(2,1)S(1)} copy(bf16[512,1024]{0,1:T(8,128)(2,1)} %bitcast.47) | data formatting | bytes 2097152 | tf_op jit(solution)/shard_map/transpose | solution.py:232
  2.5 1.7 %collective-permute-start = (bf16[256,1024]{1,0:T(8,128)(2,1)S(1)}, bf16[256,1024]{1,0:T(8,128)(2,1)S(1)}, u32[]{:S(2)}, u32[]{:S(2)}) collective-permute-start(bf16[256,1024]{1,0:T(8,128)(2,1)S(1)} %get-tuple-element.72), channel_id=1, source_target_pairs={{0,16},{1,17},{2,18},{3,19},{4,20},{5,21},{6,22},{7,23},{8,24},{9,... | collective-permute-start | bytes 1572872 | tf_op jit(solution)/shard_map/ppermute | solution.py:46
  4.2 2.2 %collective-permute-start.1 = (bf16[256,1024]{1,0:T(8,128)(2,1)S(1)}, bf16[256,1024]{1,0:T(8,128)(2,1)S(1)}, u32[]{:S(2)}, u32[]{:S(2)}) collective-permute-start(bf16[256,1024]{1,0:T(8,128)(2,1)S(1)} %get-tuple-element.71), channel_id=1, source_target_pairs={{0,17},{1,16},{2,19},{3,18},{4,21},{5,20},{6,23},{7,22},{8,25},{9,... | collective-permute-start | bytes 1572872 | tf_op jit(solution)/shard_map/ppermute | solution.py:46
  6.4 2.6 %convolution_convert_fusion = bf16[1024,1024]{1,0:T(8,128)(2,1)} fusion(bf16[1024,512]{1,0:T(8,128)(2,1)S(1)} %copy-done.14, bf16[512,1024]{1,0:T(8,128)(2,1)S(1)} %copy-done), kind=kOutput, calls=%fused_computation.1 | convolution fusion | flops 1074790400 | bytes 4194304 | tf_op jit(solution)/shard_map/dot_general | solution.py:236
  9.0 7.8 %collective-permute-done.refs_4_.refs_9_.refs_6_ = bf16[256,1024]{1,0:T(8,128)(2,1)S(1)} collective-permute-done((bf16[256,1024]{1,0:T(8,128)(2,1)S(1)}, bf16[256,1024]{1,0:T(8,128)(2,1)S(1)}, u32[]{:S(2)}, u32[]{:S(2)}) %collective-permute-start) | collective-permute-done | bytes 524320 | tf_op jit(solution)/shard_map/ppermute | solution.py:46
  16.9 2.6 %collective-permute-done.1.refs_5_.refs_10_.refs_7_ = bf16[256,1024]{1,0:T(8,128)(2,1)S(1)} collective-permute-done((bf16[256,1024]{1,0:T(8,128)(2,1)S(1)}, bf16[256,1024]{1,0:T(8,128)(2,1)S(1)}, u32[]{:S(2)}, u32[]{:S(2)}) %collective-permute-start.1) | collective-permute-done | bytes 524320 | tf_op jit(solution)/shard_map/ppermute | solution.py:46
  19.5 2.3 %collective-permute-start.4 = (bf16[256,1024]{1,0:T(8,128)(2,1)S(1)}, bf16[256,1024]{1,0:T(8,128)(2,1)S(1)}, u32[]{:S(2)}, u32[]{:S(2)}) collective-permute-start(bf16[256,1024]{1,0:T(8,128)(2,1)S(1)} %get-tuple-element.72), channel_id=1, source_target_pairs={{0,17},{1,16},{2,19},{3,18},{4,21},{5,20},{6,23},{7,22},{8,25},{9,... | collective-permute-start | bytes 1572872 | tf_op jit(solution)/shard_map/ppermute | solution.py:46
  23.3 1.7 %collective-permute-start.12 = (bf16[256,1024]{1,0:T(8,128)(2,1)S(1)}, bf16[256,1024]{1,0:T(8,128)(2,1)}, u32[]{:S(2)}, u32[]{:S(2)}) collective-permute-start(bf16[256,1024]{1,0:T(8,128)(2,1)S(1)} %collective-permute-done.1.refs_5_.refs_10_.refs_7_), channel_id=1, source_target_pairs={{0,96},{1,97},{2,98},{3,99},{4,100},{5,101},{6,102},{7,103},{8,104... | collective-permute-start | bytes 1572872 | tf_op jit(solution)/shard_map/ppermute | solution.py:46
  25.1 7.5 %collective-permute-done.3.refs_6_.refs_11_ = bf16[256,1024]{1,0:T(8,128)(2,1)S(1)} collective-permute-done((bf16[256,1024]{1,0:T(8,128)(2,1)S(1)}, bf16[256,1024]{1,0:T(8,128)(2,1)S(1)}, u32[]{:S(2)}, u32[]{:S(2)}) %collective-permute-start.3) | collective-permute-done | bytes 524320 | tf_op jit(solution)/shard_map/ppermute | solution.py:46
  34.0 2.0 %collective-permute-done.11.refs_10_.refs_17_.refs_12_ = bf16[256,1024]{1,0:T(8,128)(2,1)} collective-permute-done((bf16[256,1024]{1,0:T(8,128)(2,1)S(1)}, bf16[256,1024]{1,0:T(8,128)(2,1)}, u32[]{:S(2)}, u32[]{:S(2)}) %collective-permute-start.11) | collective-permute-done | bytes 524320 | tf_op jit(solution)/shard_map/ppermute | solution.py:46
  39.6 1.7 %collective-permute-start.14 = (bf16[256,1024]{1,0:T(8,128)(2,1)S(1)}, bf16[256,1024]{1,0:T(8,128)(2,1)S(1)}, u32[]{:S(2)}, u32[]{:S(2)}) collective-permute-start(bf16[256,1024]{1,0:T(8,128)(2,1)S(1)} %collective-permute-done.refs_4_.refs_9_.refs_6_), channel_id=1, source_target_pairs={{0,96},{1,97},{2,98},{3,99},{4,100},{5,101},{6,102},{7,103},{8,104... | collective-permute-start | bytes 1572872 | tf_op jit(solution)/shard_map/ppermute | solution.py:46
  42.4 9.1 %collective-permute-done.13.refs_11_.refs_18_.refs_13_ = bf16[256,1024]{1,0:T(8,128)(2,1)S(1)} collective-permute-done((bf16[256,1024]{1,0:T(8,128)(2,1)S(1)}, bf16[256,1024]{1,0:T(8,128)(2,1)S(1)}, u32[]{:S(2)}, u32[]{:S(2)}) %collective-permute-start.13) | collective-permute-done | bytes 524320 | tf_op jit(solution)/shard_map/ppermute | solution.py:46
  51.5 1.5 %collective-permute-done.14.refs_8_.refs_13_ = bf16[256,1024]{1,0:T(8,128)(2,1)S(1)} collective-permute-done((bf16[256,1024]{1,0:T(8,128)(2,1)S(1)}, bf16[256,1024]{1,0:T(8,128)(2,1)S(1)}, u32[]{:S(2)}, u32[]{:S(2)}) %collective-permute-start.14) | collective-permute-done | bytes 524320 | tf_op jit(solution)/shard_map/ppermute | solution.py:46
  54.3 2.0 %collective-permute-start.16 = (bf16[256,1024]{1,0:T(8,128)(2,1)}, bf16[256,1024]{1,0:T(8,128)(2,1)S(1)}, u32[]{:S(2)}, u32[]{:S(2)}) collective-permute-start(bf16[256,1024]{1,0:T(8,128)(2,1)} %collective-permute-done.12.refs_9_.refs_14_), channel_id=1, source_target_pairs={{0,96},{1,97},{2,98},{3,99},{4,100},{5,101},{6,102},{7,103},{8,104... | collective-permute-start | bytes 1572872 | tf_op jit(solution)/shard_map/ppermute | solution.py:46
  58.0 9.0 %shard_map.50 = (bf16[2,1024,256]{2,1,0:T(8,128)(2,1)}, bf16[2,1024,256]{2,1,0:T(8,128)(2,1)}, bf16[2,1024,256]{2,1,0:T(8,128)(2,1)}, bf16[2,1024,256]{2,1,0:T(8,128)(2,1)}) custom-call(s32[2]{0:T(128)} %pad_add_fusion.refs_0_, bf16[2,256,1024]{2,1,0:T(8,128)(2,1)} %bitcast.39, bf16[256,1024]{1,0:T(8,128)(2,1)} %collective-permute-done.5.refs_2_.refs_7_, ...), custom_call_target="tpu_custom_call" | custom-call | flops 65536 | bytes 262144 | tf_op jit(solution)/shard_map/pallas_call | solution.py:201
  68.4 8.8 %shard_map.51 = (bf16[2,1024,256]{2,1,0:T(8,128)(2,1)}, bf16[2,1024,256]{2,1,0:T(8,128)(2,1)}, bf16[2,1024,256]{2,1,0:T(8,128)(2,1)}, bf16[2,1024,256]{2,1,0:T(8,128)(2,1)}) custom-call(s32[2]{0:T(128)} %pad_add_fusion.refs_0_, bf16[2,256,1024]{2,1,0:T(8,128)(2,1)} %copy-done.9, ...), custom_call_target="tpu_custom_call", output_to_operand_aliasing={{0}: (19, {}), {1}: (20, {}), {2}: (21, {}), {3}: (22, {})} | custom-call | flops 65536 | bytes 262144 | tf_op jit(solution)/shard_map/pallas_call | solution.py:201
  77.2 3.9 %collective-permute-start.17 = (bf16[2,1024,256]{2,1,0:T(8,128)(2,1)}, bf16[2,1024,256]{2,1,0:T(8,128)(2,1)S(1)}, u32[]{:S(2)}, u32[]{:S(2)}) collective-permute-start(bf16[2,1024,256]{2,1,0:T(8,128)(2,1)} %get-tuple-element.109), channel_id=1, source_target_pairs={{0,6},{1,7},{2,0},{3,1},{4,2},{5,3},{6,4},{7,5},{8,14},{9,15},{10,... | collective-permute-start | bytes 3145736 | tf_op jit(solution)/shard_map/ppermute | solution.py:46
  81.2 5.0 %all-to-all-start = ((bf16[16,64,1024]{2,1,0:T(8,128)(2,1)}), bf16[16,64,1024]{2,1,0:T(8,128)(2,1)}, u32[]{:S(2)}, u32[]{:S(2)}) async-start(bf16[16,64,1024]{2,1,0:T(8,128)(2,1)} %bitcast), calls=%async_computation | async-start | bytes 4194304 | tf_op jit(solution)/shard_map/all_to_all | solution.py:273
  86.2 7.1 %shard_map.52 = (bf16[2,1024,256]{2,1,0:T(8,128)(2,1)}, bf16[2,1024,256]{2,1,0:T(8,128)(2,1)}) custom-call(s32[2]{0:T(128)} %pad_add_fusion.refs_0_, bf16[2,256,1024]{2,1,0:T(8,128)(2,1)} %copy-done.9, bf16[256,1024]{1,0:T(8,128)(2,1)} %copy-done.13, ...), custom_call_target="tpu_custom_call", output_to_operand_aliasing={{0}: (14, {}), {1}: (15, {})} | custom-call | flops 65536 | bytes 262144 | tf_op jit(solution)/shard_map/pallas_call | solution.py:201
  93.3 10.8 %collective-permute-done.17 = bf16[2,1024,256]{2,1,0:T(8,128)(2,1)S(1)} collective-permute-done((bf16[2,1024,256]{2,1,0:T(8,128)(2,1)}, bf16[2,1024,256]{2,1,0:T(8,128)(2,1)S(1)}, u32[]{:S(2)}, u32[]{:S(2)}) %collective-permute-start.17) | collective-permute-done | bytes 1048608 | tf_op jit(solution)/shard_map/ppermute | solution.py:46
  104.2 3.4 %collective-permute-done.18 = bf16[2,1024,256]{2,1,0:T(8,128)(2,1)} collective-permute-done((bf16[2,1024,256]{2,1,0:T(8,128)(2,1)}, bf16[2,1024,256]{2,1,0:T(8,128)(2,1)}, u32[]{:S(2)}, u32[]{:S(2)}) %collective-permute-start.18) | collective-permute-done | bytes 1048608 | tf_op jit(solution)/shard_map/ppermute | solution.py:46
  107.6 2.6 %fusion.3 = (bf16[1024,256]{1,0:T(8,128)(2,1)}, bf16[1024,256]{1,0:T(8,128)(2,1)}) fusion(bf16[2,1024,256]{2,1,0:T(8,128)(2,1)} %get-tuple-element.113, bf16[2,1024,256]{2,1,0:T(8,128)(2,1)} %collective-permute-done.18, bf16[2,1024,256]{2,1,0:T(8,128)(2,1)S(1)} %collective-permute-done.17), kind=kLoop, calls=%fused_computation.11 | loop fusion | flops 2097152 | bytes 3145728 | tf_op jit(solution)/shard_map/convert_element_type | solution.py:58
  110.3 1.8 %collective-permute-start.20 = (bf16[1024,256]{1,0:T(8,128)(2,1)}, bf16[1024,256]{1,0:T(8,128)(2,1)}, u32[]{:S(2)}, u32[]{:S(2)}) collective-permute-start(bf16[1024,256]{1,0:T(8,128)(2,1)} %get-tuple-element.115), channel_id=1, source_target_pairs={{0,2},{1,3},{2,4},{3,5},{4,6},{5,7},{6,0},{7,1},{8,10},{9,11},{10,... | collective-permute-start | bytes 1572872 | tf_op jit(solution)/shard_map/ppermute | solution.py:46
  112.2 11.0 %collective-permute-done.19 = bf16[1024,256]{1,0:T(8,128)(2,1)} collective-permute-done((bf16[1024,256]{1,0:T(8,128)(2,1)}, bf16[1024,256]{1,0:T(8,128)(2,1)}, u32[]{:S(2)}, u32[]{:S(2)}) %collective-permute-start.19) | collective-permute-done | bytes 524320 | tf_op jit(solution)/shard_map/ppermute | solution.py:46
  123.2 1.5 %collective-permute-done.20 = bf16[1024,256]{1,0:T(8,128)(2,1)} collective-permute-done((bf16[1024,256]{1,0:T(8,128)(2,1)}, bf16[1024,256]{1,0:T(8,128)(2,1)}, u32[]{:S(2)}, u32[]{:S(2)}) %collective-permute-start.20) | collective-permute-done | bytes 524320 | tf_op jit(solution)/shard_map/ppermute | solution.py:46
  124.8 1.8 %fusion = (bf16[1024,256]{1,0:T(8,128)(2,1)S(1)}, bf16[1024,256]{1,0:T(8,128)(2,1)S(1)}) fusion(bf16[1024,256]{1,0:T(8,128)(2,1)} %collective-permute-done.20, bf16[2,1024,256]{2,1,0:T(8,128)(2,1)S(1)} %collective-permute-done.17, bf16[2,1024,256]{2,1,0:T(8,128)(2,1)S(1)} %copy-done.2, bf16[1024,256]{1,0:T(8,128)(2,1)} %collective-permute-done.19, ...), kind=kLoop, calls=%fused_computation.5 | loop fusion | flops 3145728 | bytes 4194304 | tf_op jit(solution)/shard_map/convert_element_type | solution.py:58
  126.6 4.2 %collective-permute-start.21 = (bf16[512,256]{1,0:T(8,128)(2,1)S(1)}, bf16[512,256]{1,0:T(8,128)(2,1)S(1)}, u32[]{:S(2)}, u32[]{:S(2)}) collective-permute-start(bf16[512,256]{1,0:T(8,128)(2,1)S(1)} %get-tuple-element.118), channel_id=1, source_target_pairs={{0,17},{1,1},{2,19},{3,3},{4,21},{5,5},{6,23},{7,7},{8,25},{9,9},{... | collective-permute-start | bytes 786440 | tf_op jit(solution)/shard_map/ppermute | solution.py:46
  131.0 4.0 %collective-permute-start.24 = (bf16[512,256]{1,0:T(8,128)(2,1)S(1)}, bf16[512,256]{1,0:T(8,128)(2,1)S(1)}, u32[]{:S(2)}, u32[]{:S(2)}) collective-permute-start(bf16[512,256]{1,0:T(8,128)(2,1)S(1)} %get-tuple-element.121), channel_id=1, source_target_pairs={{0,9},{1,25},{2,11},{3,27},{4,13},{5,29},{6,15},{7,31},{8,1},{9,17... | collective-permute-start | bytes 786440 | tf_op jit(solution)/shard_map/ppermute | solution.py:46
  135.1 2.7 %reduce_sum.12 = bf16[64,1024]{1,0:T(8,128)(2,1)} reduce(bf16[16,64,1024]{2,1,0:T(8,128)(2,1)} %all-to-all-done, bf16[]{:T(256)} %constant.91.clone.1), dimensions={0}, to_apply=%region_0.1 | reduce | flops 983040 | bytes 2228226 | tf_op jit(solution)/shard_map/reduce_sum | solution.py:287
  137.8 3.1 %collective-permute-done.22 = bf16[512,256]{1,0:T(8,128)(2,1)S(1)} collective-permute-done((bf16[512,256]{1,0:T(8,128)(2,1)S(1)}, bf16[512,256]{1,0:T(8,128)(2,1)S(1)}, u32[]{:S(2)}, u32[]{:S(2)}) %collective-permute-start.22) | collective-permute-done | bytes 262176 | tf_op jit(solution)/shard_map/ppermute | solution.py:46
  140.8 5.0 %collective-permute-done.24 = bf16[512,256]{1,0:T(8,128)(2,1)S(1)} collective-permute-done((bf16[512,256]{1,0:T(8,128)(2,1)S(1)}, bf16[512,256]{1,0:T(8,128)(2,1)S(1)}, u32[]{:S(2)}, u32[]{:S(2)}) %collective-permute-start.24) | collective-permute-done | bytes 262176 | tf_op jit(solution)/shard_map/ppermute | solution.py:46
  145.9 1.7 %multiply_add_fusion = f32[512,1024]{1,0:T(8,128)} fusion(f32[512,1024]{1,0:T(8,128)S(1)} %copy-done.11, bf16[256,256]{1,0:T(8,128)(2,1)S(1)} %get-tuple-element.145, bf16[256,256]{1,0:T(8,128)(2,1)S(1)} %get-tuple-element.144, bf16[512,256]{1,0:T(8,128)(2,1)S(1)} %get-tuple-element.130, bf16[256,256]{1,0:T(8,128)(2,1)S(1)} %get-tuple-element.143, ...), kind=kLoop, calls=%fused_computation | loop fusion | flops 7864320 | bytes 5242880 | tf_op jit(solution)/shard_map/add | solution.py:302
  (67 shorter events, 12.6 us)
Async XLA Ops:
  2.4 17.0 %collective-permute-start.2 = (bf16[2,256,1024]{2,1,0:T(8,128)(2,1)S(1)}, bf16[2,256,1024]{2,1,0:T(8,128)(2,1)S(1)}, u32[]{:S(2)}, u32[]{:S(2)}) collective-permute-start(bf16[2,256,1024]{2,1,0:T(8,128)(2,1)S(1)} %bitcast.38), channel_id=1, source_target_pairs={{0,8},{1,9},{2,10},{3,11},{4,12},{5,13},{6,14},{7,15},{8,0},{9,1},... | collective-permute-start | bytes 3145736 | tf_op jit(solution)/shard_map/ppermute | solution.py:46
  2.5 14.3 %collective-permute-start = (bf16[256,1024]{1,0:T(8,128)(2,1)S(1)}, bf16[256,1024]{1,0:T(8,128)(2,1)S(1)}, u32[]{:S(2)}, u32[]{:S(2)}) collective-permute-start(bf16[256,1024]{1,0:T(8,128)(2,1)S(1)} %get-tuple-element.72), channel_id=1, source_target_pairs={{0,16},{1,17},{2,18},{3,19},{4,20},{5,21},{6,22},{7,23},{8,24},{9,... | collective-permute-start | bytes 1572872 | tf_op jit(solution)/shard_map/ppermute | solution.py:46
  4.2 15.2 %collective-permute-start.1 = (bf16[256,1024]{1,0:T(8,128)(2,1)S(1)}, bf16[256,1024]{1,0:T(8,128)(2,1)S(1)}, u32[]{:S(2)}, u32[]{:S(2)}) collective-permute-start(bf16[256,1024]{1,0:T(8,128)(2,1)S(1)} %get-tuple-element.71), channel_id=1, source_target_pairs={{0,17},{1,16},{2,19},{3,18},{4,21},{5,20},{6,23},{7,22},{8,25},{9,... | collective-permute-start | bytes 1572872 | tf_op jit(solution)/shard_map/ppermute | solution.py:46
  16.9 25.6 %copy-start.3 = (bf16[256,1024]{1,0:T(8,128)(2,1)}, bf16[256,1024]{1,0:T(8,128)(2,1)S(1)}, u32[]{:S(2)}) copy-start(bf16[256,1024]{1,0:T(8,128)(2,1)S(1)} %collective-permute-done.refs_4_.refs_9_.refs_6_) | copy-start | bytes 1572868
  19.4 23.0 %copy-start.4 = (bf16[256,1024]{1,0:T(8,128)(2,1)}, bf16[256,1024]{1,0:T(8,128)(2,1)S(1)}, u32[]{:S(2)}) copy-start(bf16[256,1024]{1,0:T(8,128)(2,1)S(1)} %collective-permute-done.1.refs_5_.refs_10_.refs_7_) | copy-start | bytes 1572868
  19.4 23.0 %copy-start.9 = (bf16[2,256,1024]{2,1,0:T(8,128)(2,1)}, bf16[2,256,1024]{2,1,0:T(8,128)(2,1)S(1)}, u32[]{:S(2)}) copy-start(bf16[2,256,1024]{2,1,0:T(8,128)(2,1)S(1)} %collective-permute-done.2.refs_1_) | copy-start | bytes 3145732
  19.4 13.2 %collective-permute-start.3 = (bf16[256,1024]{1,0:T(8,128)(2,1)S(1)}, bf16[256,1024]{1,0:T(8,128)(2,1)S(1)}, u32[]{:S(2)}, u32[]{:S(2)}) collective-permute-start(bf16[256,1024]{1,0:T(8,128)(2,1)S(1)} %get-tuple-element.71), channel_id=1, source_target_pairs={{0,16},{1,17},{2,18},{3,19},{4,20},{5,21},{6,22},{7,23},{8,24},{9,... | collective-permute-start | bytes 1572872 | tf_op jit(solution)/shard_map/ppermute | solution.py:46
  19.5 14.4 %collective-permute-start.4 = (bf16[256,1024]{1,0:T(8,128)(2,1)S(1)}, bf16[256,1024]{1,0:T(8,128)(2,1)S(1)}, u32[]{:S(2)}, u32[]{:S(2)}) collective-permute-start(bf16[256,1024]{1,0:T(8,128)(2,1)S(1)} %get-tuple-element.72), channel_id=1, source_target_pairs={{0,17},{1,16},{2,19},{3,18},{4,21},{5,20},{6,23},{7,22},{8,25},{9,... | collective-permute-start | bytes 1572872 | tf_op jit(solution)/shard_map/ppermute | solution.py:46
  21.8 14.2 %collective-permute-start.11 = (bf16[256,1024]{1,0:T(8,128)(2,1)S(1)}, bf16[256,1024]{1,0:T(8,128)(2,1)}, u32[]{:S(2)}, u32[]{:S(2)}) collective-permute-start(bf16[256,1024]{1,0:T(8,128)(2,1)S(1)} %collective-permute-done.refs_4_.refs_9_.refs_6_), channel_id=1, source_target_pairs={{0,32},{1,33},{2,34},{3,35},{4,36},{5,37},{6,38},{7,39},{8,40},{9,... | collective-permute-start | bytes 1572872 | tf_op jit(solution)/shard_map/ppermute | solution.py:46
  23.3 12.7 %collective-permute-start.12 = (bf16[256,1024]{1,0:T(8,128)(2,1)S(1)}, bf16[256,1024]{1,0:T(8,128)(2,1)}, u32[]{:S(2)}, u32[]{:S(2)}) collective-permute-start(bf16[256,1024]{1,0:T(8,128)(2,1)S(1)} %collective-permute-done.1.refs_5_.refs_10_.refs_7_), channel_id=1, source_target_pairs={{0,96},{1,97},{2,98},{3,99},{4,100},{5,101},{6,102},{7,103},{8,104... | collective-permute-start | bytes 1572872 | tf_op jit(solution)/shard_map/ppermute | solution.py:46
  32.7 25.3 %copy-start.5 = (bf16[256,1024]{1,0:T(8,128)(2,1)}, bf16[256,1024]{1,0:T(8,128)(2,1)S(1)}, u32[]{:S(2)}) copy-start(bf16[256,1024]{1,0:T(8,128)(2,1)S(1)} %collective-permute-done.3.refs_6_.refs_11_) | copy-start | bytes 1572868
  34.0 24.0 %copy-start.6 = (bf16[256,1024]{1,0:T(8,128)(2,1)}, bf16[256,1024]{1,0:T(8,128)(2,1)S(1)}, u32[]{:S(2)}) copy-start(bf16[256,1024]{1,0:T(8,128)(2,1)S(1)} %collective-permute-done.4.refs_7_.refs_12_) | copy-start | bytes 1572868
  36.0 20.3 %collective-permute-start.7 = (bf16[2,256,1024]{2,1,0:T(8,128)(2,1)S(1)}, bf16[2,256,1024]{2,1,0:T(8,128)(2,1)S(1)}, u32[]{:S(2)}, u32[]{:S(2)}) collective-permute-start(bf16[2,256,1024]{2,1,0:T(8,128)(2,1)S(1)} %pad_maximum_fusion), channel_id=1, source_target_pairs={{0,8},{1,9},{2,10},{3,11},{4,12},{5,13},{6,14},{7,15},{8,0},{9,1},... | collective-permute-start | bytes 3145736 | tf_op jit(solution)/shard_map/ppermute | solution.py:46
  36.0 15.5 %collective-permute-start.13 = (bf16[256,1024]{1,0:T(8,128)(2,1)S(1)}, bf16[256,1024]{1,0:T(8,128)(2,1)S(1)}, u32[]{:S(2)}, u32[]{:S(2)}) collective-permute-start(bf16[256,1024]{1,0:T(8,128)(2,1)S(1)} %collective-permute-done.1.refs_5_.refs_10_.refs_7_), channel_id=1, source_target_pairs={{0,32},{1,33},{2,34},{3,35},{4,36},{5,37},{6,38},{7,39},{8,40},{9,... | collective-permute-start | bytes 1572872 | tf_op jit(solution)/shard_map/ppermute | solution.py:46
  37.5 16.8 %collective-permute-start.5 = (bf16[256,1024]{1,0:T(8,128)(2,1)S(1)}, bf16[256,1024]{1,0:T(8,128)(2,1)}, u32[]{:S(2)}, u32[]{:S(2)}) collective-permute-start(bf16[256,1024]{1,0:T(8,128)(2,1)S(1)} %collective-permute-done.1.refs_5_.refs_10_.refs_7_), channel_id=1, source_target_pairs={{0,16},{1,17},{2,18},{3,19},{4,20},{5,21},{6,22},{7,23},{8,24},{9,... | collective-permute-start | bytes 1572872 | tf_op jit(solution)/shard_map/ppermute | solution.py:46
  38.5 17.8 %collective-permute-start.6 = (bf16[256,1024]{1,0:T(8,128)(2,1)S(1)}, bf16[256,1024]{1,0:T(8,128)(2,1)}, u32[]{:S(2)}, u32[]{:S(2)}) collective-permute-start(bf16[256,1024]{1,0:T(8,128)(2,1)S(1)} %collective-permute-done.refs_4_.refs_9_.refs_6_), channel_id=1, source_target_pairs={{0,17},{1,16},{2,19},{3,18},{4,21},{5,20},{6,23},{7,22},{8,25},{9,... | collective-permute-start | bytes 1572872 | tf_op jit(solution)/shard_map/ppermute | solution.py:46
  39.6 13.5 %collective-permute-start.14 = (bf16[256,1024]{1,0:T(8,128)(2,1)S(1)}, bf16[256,1024]{1,0:T(8,128)(2,1)S(1)}, u32[]{:S(2)}, u32[]{:S(2)}) collective-permute-start(bf16[256,1024]{1,0:T(8,128)(2,1)S(1)} %collective-permute-done.refs_4_.refs_9_.refs_6_), channel_id=1, source_target_pairs={{0,96},{1,97},{2,98},{3,99},{4,100},{5,101},{6,102},{7,103},{8,104... | collective-permute-start | bytes 1572872 | tf_op jit(solution)/shard_map/ppermute | solution.py:46
  51.5 15.9 %collective-permute-start.10 = (bf16[2,256,1024]{2,1,0:T(8,128)(2,1)}, bf16[2,256,1024]{2,1,0:T(8,128)(2,1)}, u32[]{:S(2)}, u32[]{:S(2)}) collective-permute-start(bf16[2,256,1024]{2,1,0:T(8,128)(2,1)} %pad_maximum_fusion.1), channel_id=1, source_target_pairs={{0,8},{1,9},{2,10},{3,11},{4,12},{5,13},{6,14},{7,15},{8,0},{9,1},... | collective-permute-start | bytes 3145736 | tf_op jit(solution)/shard_map/ppermute | solution.py:46
  53.1 14.3 %collective-permute-start.15 = (bf16[256,1024]{1,0:T(8,128)(2,1)}, bf16[256,1024]{1,0:T(8,128)(2,1)}, u32[]{:S(2)}, u32[]{:S(2)}) collective-permute-start(bf16[256,1024]{1,0:T(8,128)(2,1)} %collective-permute-done.11.refs_10_.refs_17_.refs_12_), channel_id=1, source_target_pairs={{0,32},{1,33},{2,34},{3,35},{4,36},{5,37},{6,38},{7,39},{8,40},{9,... | collective-permute-start | bytes 1572872 | tf_op jit(solution)/shard_map/ppermute | solution.py:46
  54.3 13.1 %collective-permute-start.16 = (bf16[256,1024]{1,0:T(8,128)(2,1)}, bf16[256,1024]{1,0:T(8,128)(2,1)S(1)}, u32[]{:S(2)}, u32[]{:S(2)}) collective-permute-start(bf16[256,1024]{1,0:T(8,128)(2,1)} %collective-permute-done.12.refs_9_.refs_14_), channel_id=1, source_target_pairs={{0,96},{1,97},{2,98},{3,99},{4,100},{5,101},{6,102},{7,103},{8,104... | collective-permute-start | bytes 1572872 | tf_op jit(solution)/shard_map/ppermute | solution.py:46
  56.4 11.1 %collective-permute-start.8 = (bf16[256,1024]{1,0:T(8,128)(2,1)}, bf16[256,1024]{1,0:T(8,128)(2,1)S(1)}, u32[]{:S(2)}, u32[]{:S(2)}) collective-permute-start(bf16[256,1024]{1,0:T(8,128)(2,1)} %collective-permute-done.5.refs_2_.refs_7_), channel_id=1, source_target_pairs={{0,8},{1,9},{2,10},{3,11},{4,12},{5,13},{6,14},{7,15},{8,0},{9,1},... | collective-permute-start | bytes 1572872 | tf_op jit(solution)/shard_map/ppermute | solution.py:46
  57.3 10.1 %collective-permute-start.9 = (bf16[256,1024]{1,0:T(8,128)(2,1)}, bf16[256,1024]{1,0:T(8,128)(2,1)}, u32[]{:S(2)}, u32[]{:S(2)}) collective-permute-start(bf16[256,1024]{1,0:T(8,128)(2,1)} %collective-permute-done.6.refs_3_.refs_8_), channel_id=1, source_target_pairs={{0,8},{1,9},{2,10},{3,11},{4,12},{5,13},{6,14},{7,15},{8,0},{9,1},... | collective-permute-start | bytes 1572872 | tf_op jit(solution)/shard_map/ppermute | solution.py:46
  77.2 26.9 %collective-permute-start.17 = (bf16[2,1024,256]{2,1,0:T(8,128)(2,1)}, bf16[2,1024,256]{2,1,0:T(8,128)(2,1)S(1)}, u32[]{:S(2)}, u32[]{:S(2)}) collective-permute-start(bf16[2,1024,256]{2,1,0:T(8,128)(2,1)} %get-tuple-element.109), channel_id=1, source_target_pairs={{0,6},{1,7},{2,0},{3,1},{4,2},{5,3},{6,4},{7,5},{8,14},{9,15},{10,... | collective-permute-start | bytes 3145736 | tf_op jit(solution)/shard_map/ppermute | solution.py:46
  81.2 26.4 %collective-permute-start.18 = (bf16[2,1024,256]{2,1,0:T(8,128)(2,1)}, bf16[2,1024,256]{2,1,0:T(8,128)(2,1)}, u32[]{:S(2)}, u32[]{:S(2)}) collective-permute-start(bf16[2,1024,256]{2,1,0:T(8,128)(2,1)} %get-tuple-element.110), channel_id=1, source_target_pairs={{0,2},{1,3},{2,4},{3,5},{4,6},{5,7},{6,0},{7,1},{8,10},{9,11},{10,... | collective-permute-start | bytes 3145736 | tf_op jit(solution)/shard_map/ppermute | solution.py:46
  81.2 45.4 %all-to-all-start = ((bf16[16,64,1024]{2,1,0:T(8,128)(2,1)}), bf16[16,64,1024]{2,1,0:T(8,128)(2,1)}, u32[]{:S(2)}, u32[]{:S(2)}) async-start(bf16[16,64,1024]{2,1,0:T(8,128)(2,1)} %bitcast), calls=%async_computation | async-start | bytes 4194304 | tf_op jit(solution)/shard_map/all_to_all | solution.py:273
  93.3 31.5 %copy-start.2 = (bf16[2,1024,256]{2,1,0:T(8,128)(2,1)S(1)}, bf16[2,1024,256]{2,1,0:T(8,128)(2,1)}, u32[]{:S(2)}) copy-start(bf16[2,1024,256]{2,1,0:T(8,128)(2,1)} %get-tuple-element.106) | copy-start | bytes 3145732
  110.2 13.1 %collective-permute-start.19 = (bf16[1024,256]{1,0:T(8,128)(2,1)}, bf16[1024,256]{1,0:T(8,128)(2,1)}, u32[]{:S(2)}, u32[]{:S(2)}) collective-permute-start(bf16[1024,256]{1,0:T(8,128)(2,1)} %get-tuple-element.114), channel_id=1, source_target_pairs={{0,6},{1,7},{2,0},{3,1},{4,2},{5,3},{6,4},{7,5},{8,14},{9,15},{10,... | collective-permute-start | bytes 1572872 | tf_op jit(solution)/shard_map/ppermute | solution.py:46
  110.3 14.4 %collective-permute-start.20 = (bf16[1024,256]{1,0:T(8,128)(2,1)}, bf16[1024,256]{1,0:T(8,128)(2,1)}, u32[]{:S(2)}, u32[]{:S(2)}) collective-permute-start(bf16[1024,256]{1,0:T(8,128)(2,1)} %get-tuple-element.115), channel_id=1, source_target_pairs={{0,2},{1,3},{2,4},{3,5},{4,6},{5,7},{6,0},{7,1},{8,10},{9,11},{10,... | collective-permute-start | bytes 1572872 | tf_op jit(solution)/shard_map/ppermute | solution.py:46
  126.6 11.1 %collective-permute-start.21 = (bf16[512,256]{1,0:T(8,128)(2,1)S(1)}, bf16[512,256]{1,0:T(8,128)(2,1)S(1)}, u32[]{:S(2)}, u32[]{:S(2)}) collective-permute-start(bf16[512,256]{1,0:T(8,128)(2,1)S(1)} %get-tuple-element.118), channel_id=1, source_target_pairs={{0,17},{1,1},{2,19},{3,3},{4,21},{5,5},{6,23},{7,7},{8,25},{9,9},{... | collective-permute-start | bytes 786440 | tf_op jit(solution)/shard_map/ppermute | solution.py:46
  130.8 10.0 %collective-permute-start.22 = (bf16[512,256]{1,0:T(8,128)(2,1)S(1)}, bf16[512,256]{1,0:T(8,128)(2,1)S(1)}, u32[]{:S(2)}, u32[]{:S(2)}) collective-permute-start(bf16[512,256]{1,0:T(8,128)(2,1)S(1)} %get-tuple-element.119), channel_id=1, source_target_pairs={{0,25},{1,9},{2,27},{3,11},{4,29},{5,13},{6,31},{7,15},{8,17},{9,1... | collective-permute-start | bytes 786440 | tf_op jit(solution)/shard_map/ppermute | solution.py:46
  130.9 9.9 %collective-permute-start.23 = (bf16[512,256]{1,0:T(8,128)(2,1)S(1)}, bf16[512,256]{1,0:T(8,128)(2,1)S(1)}, u32[]{:S(2)}, u32[]{:S(2)}) collective-permute-start(bf16[512,256]{1,0:T(8,128)(2,1)S(1)} %get-tuple-element.120), channel_id=1, source_target_pairs={{0,1},{1,17},{2,3},{3,19},{4,5},{5,21},{6,7},{7,23},{8,9},{9,25},{... | collective-permute-start | bytes 786440 | tf_op jit(solution)/shard_map/ppermute | solution.py:46
  131.0 14.8 %collective-permute-start.24 = (bf16[512,256]{1,0:T(8,128)(2,1)S(1)}, bf16[512,256]{1,0:T(8,128)(2,1)S(1)}, u32[]{:S(2)}, u32[]{:S(2)}) collective-permute-start(bf16[512,256]{1,0:T(8,128)(2,1)S(1)} %get-tuple-element.121), channel_id=1, source_target_pairs={{0,9},{1,25},{2,11},{3,27},{4,13},{5,29},{6,15},{7,31},{8,1},{9,17... | collective-permute-start | bytes 786440 | tf_op jit(solution)/shard_map/ppermute | solution.py:46
  (9 other events, 37.3 us)
